TPU v7x, 32 devices: a whole 2x2x4 slice. The times are simulated.
32 devices in a mesh: seq: 8 (over y, x, core), fsdp: 4 (over z).
Axes of the slice: x: 2, y: 2, z: 4, core: 2. Of those that a mesh axis runs over, the one named last changes fastest.
Arguments:
- tokens: bfloat16 [4, 2048, 2048], P('fsdp', 'seq'), may hold values from -6 to 6
- lengths: int32 [4], replicated, may hold values from 1793 to 2048, as said below
- norm_attn: bfloat16 [2048], replicated, may hold values from 0.099609375 to 1.8984375
- norm_ffn: bfloat16 [2048], replicated, may hold values from 0.099609375 to 1.8984375
- w_query: bfloat16 [2048, 2048], P(('seq', 'fsdp')), may hold values from -0.125 to 0.125
- key_projection: bfloat16 [2048, 512], P(('seq', 'fsdp')), may hold values from -0.125 to 0.125
- value_projection: bfloat16 [2048, 512], P(('seq', 'fsdp')), may hold values from -0.125 to 0.125
- w_output: bfloat16 [2048, 2048], P(('seq', 'fsdp')), may hold values from -0.75 to 0.75
- w_gate: bfloat16 [2048, 8192], P('seq', 'fsdp'), may hold values from -0.125 to 0.125
- w_up: bfloat16 [2048, 8192], P('seq', 'fsdp'), may hold values from -0.125 to 0.125
- w_down: bfloat16 [2048, 8192], P('seq', 'fsdp'), may hold values from -0.0625 to 0.0625
- down_query: bfloat16 [2048, 8], replicated, may hold values from -0.125 to 0.125
- up_query: bfloat16 [2048, 8], replicated, may hold values from -1 to 1
- key_down_matrix: bfloat16 [2048, 8], replicated, may hold values from -0.125 to 0.125
- key_up_matrix: bfloat16 [512, 8], replicated, may hold values from -1 to 1
- value_down_matrix: bfloat16 [2048, 8], replicated, may hold values from -0.125 to 0.125
- value_up_matrix: bfloat16 [512, 8], replicated, may hold values from -1 to 1
- down_output: bfloat16 [2048, 8], replicated, may hold values from -0.75 to 0.75
- up_output: bfloat16 [2048, 8], replicated, may hold values from -1 to 1
- feature_query: bfloat16 [2048, 64], replicated, may hold values from -0.75 to 0.75
- key_feature_weight: bfloat16 [512, 64], replicated, may hold values from -0.75 to 0.75
- cotangent: bfloat16 [4, 2048, 2048], P('fsdp', 'seq'), may hold values from -6 to 6
Outputs:
- output: bfloat16 [4, 2048, 2048], P('fsdp', 'seq')
- grad_tokens: bfloat16 [4, 2048, 2048], P('fsdp', 'seq')
- grad_down_query: float32 [2048, 8], P(('seq', 'fsdp'))
- grad_up_query: float32 [2048, 8], P(('seq', 'fsdp'))
- grad_down_key: float32 [2048, 8], P(('seq', 'fsdp'))
- grad_up_key: float32 [512, 8], P(('seq', 'fsdp'))
- grad_down_value: float32 [2048, 8], P(('seq', 'fsdp'))
- grad_up_value: float32 [512, 8], P(('seq', 'fsdp'))
- grad_down_output: float32 [2048, 8], P(('seq', 'fsdp'))
- grad_up_output: float32 [2048, 8], P(('seq', 'fsdp'))
- grad_feature_query: float32 [2048, 64], P(('seq', 'fsdp'))
- key_feature_gradient: float32 [512, 64], P(('seq', 'fsdp'))
- transfer_loss: float32 [32], P(('seq', 'fsdp'))
Inputs may be any that keep to these rules, and one draw needn't show every extreme that they name: lengths holds the real tokens of each lane; every lane's sequence reaches into the last 256 positions of its lane.
All inputs are finite; a program needn't handle non-finite values.
Results may differ from a plain program's by a relative error of at most 0.015.
Values may be sent and summed in bfloat16 or wider, within the bound.
No kernel may reach another device: no remote copies, remote signals or barrier semaphores. Data moves between devices by JAX's collectives and lax.ppermute only.
A program may use at most 320 MiB of HBM per device.

v0:
```python
import math

import jax
import jax.numpy as jnp
from jax import lax
from jax.sharding import PartitionSpec as P

QUERY_HEADS = 32
KEY_VALUE_HEADS = 8
HEAD_SIZE = 64
WINDOW_KEYS = 64


epsilon = 1e-05
rope_base = 500000.0
precise = lax.Precision.HIGHEST
lowest_precision = -1e30


def prefix(x, axis, join, neutral, backward):
    count = lax.axis_size(axis)
    place = lax.axis_index(axis)
    ahead = count - 1 - place if backward else place
    gathered = jax.tree.map(
        lambda a, kind: lax.all_gather(a.astype(kind), axis), x, (jnp.bfloat16, jnp.bfloat16)
    )
    state = jax.tree.map(lambda a, e: jnp.zeros_like(a) + jnp.asarray(e, a.dtype), x, neutral)

    def one(hop, state):
        source = count - 1 - hop if backward else hop
        return join(
            state,
            jax.tree.map(
                lambda a, own: lax.dynamic_index_in_dim(a, source, 0, False).astype(own.dtype),
                gathered,
                x,
            ),
        )

    return lax.fori_loop(0, ahead, one, state)


def as_sent(x):

    def short(part):
        return part.astype(jnp.bfloat16) if part.dtype == jnp.float32 else part

    return jax.tree.map(short, x)


def shifted(value, axis, steps):
    count = lax.axis_size(axis)
    first, last = (max(0, -steps), min(count, count - steps))
    return lax.ppermute(value, axis, [(source, source + steps) for source in range(first, last)])


def rotary(positions):
    half_dim = HEAD_SIZE // 2
    inverse = rope_base ** (-(jnp.arange(half_dim, dtype=jnp.float32) * 2.0) / HEAD_SIZE)
    phase = positions.astype(jnp.float32)[:, None] * inverse[None, :]
    return (jnp.cos(phase)[:, None, :], jnp.sin(phase)[:, None, :])


def apply_rotary(vectors, cosine_lookup, sine_lookup):
    half_dim = vectors.shape[-1] // 2
    first_half = vectors[..., :half_dim]
    second_half = vectors[..., half_dim:]
    return jnp.concatenate(
        [
            first_half * cosine_lookup - second_half * sine_lookup,
            second_half * cosine_lookup + first_half * sine_lookup,
        ],
        axis=-1,
    )


def inverse_rotary(gradient, cosine_lookup, sine_lookup):
    half_dim = gradient.shape[-1] // 2
    first_half = gradient[..., :half_dim]
    second_half = gradient[..., half_dim:]
    return jnp.concatenate(
        [
            first_half * cosine_lookup + second_half * sine_lookup,
            second_half * cosine_lookup - first_half * sine_lookup,
        ],
        axis=-1,
    )


def apply_feature_map(vectors, weights):
    logits_map = jnp.einsum("thd,hde->the", vectors, weights, preferred_element_type=jnp.float32)
    return jnp.concatenate(
        [jax.nn.softmax(logits_map, axis=-1), jax.nn.softmax(-logits_map, axis=-1)], axis=-1
    )


def feature_back(vectors, weights, gradient):
    logits_map = jnp.einsum("thd,hde->the", vectors, weights, preferred_element_type=jnp.float32)
    plus_soft = jax.nn.softmax(logits_map, axis=-1)
    minus_soft = jax.nn.softmax(-logits_map, axis=-1)
    grad_plus = gradient[..., :HEAD_SIZE]
    grad_minus = gradient[..., HEAD_SIZE:]
    grad_logits = plus_soft * (
        grad_plus - jnp.sum(grad_plus * plus_soft, axis=-1, keepdims=True)
    ) - minus_soft * (grad_minus - jnp.sum(grad_minus * minus_soft, axis=-1, keepdims=True))
    grad_vectors = jnp.einsum(
        "the,hde->thd", grad_logits, weights, preferred_element_type=jnp.float32
    )
    grad_weights = jnp.einsum(
        "thd,the->hde", vectors, grad_logits, preferred_element_type=jnp.float32
    )
    return (grad_vectors, grad_weights)


def norm_back(values, inverse, gain, gradient):
    scaled = gradient * gain
    return inverse * scaled - values * inverse * inverse * inverse * jnp.mean(
        scaled * values, axis=-1, keepdims=True
    )


def coefficients(query_rows, query_feature_maps, keys_ext, key_maps, key_valid):
    row_count = query_rows.shape[0]
    key_count = keys_ext.shape[0]
    offset = (
        jnp.arange(row_count)[:, None] + (key_count - row_count) - jnp.arange(key_count)[None, :]
    )
    window = ((offset >= 0) & (offset < WINDOW_KEYS) & key_valid[None, :])[None]
    linear = ((offset >= WINDOW_KEYS) & key_valid[None, :])[None]
    scores = jnp.einsum(
        "tjd,sd->jts", query_rows, keys_ext, preferred_element_type=jnp.float32
    ) / math.sqrt(HEAD_SIZE)
    exp_scores = jnp.exp(scores)
    near_terms = lax.optimization_barrier(exp_scores.astype(jnp.bfloat16)).astype(jnp.float32)
    far_terms = jnp.einsum(
        "tjf,sf->jts", query_feature_maps, key_maps, preferred_element_type=jnp.float32
    )
    weights = jnp.where(window, near_terms, 0.0) + jnp.where(linear, far_terms, 0.0)
    return (weights, exp_scores, window, linear)


def attend_group(operands, key_valid):
    query_rows, query_feature_maps, keys_ext, values_ext, key_maps, carry_state, carry_total = (
        operands
    )
    weights, exp_scores, window, linear = coefficients(
        query_rows, query_feature_maps, keys_ext, key_maps, key_valid
    )
    maps_wide = query_feature_maps.astype(jnp.float32)
    numerator = jnp.einsum(
        "jts,sd->tjd", weights, values_ext.astype(jnp.float32), precision=precise
    ) + jnp.einsum("tjf,fd->tjd", maps_wide, carry_state, precision=precise)
    denominator = jnp.transpose(jnp.sum(weights, axis=-1)) + jnp.einsum(
        "tjf,f->tj", maps_wide, carry_total, precision=precise
    )
    return (numerator, denominator)


def attend_back(operands, key_valid):
    (
        query_rows,
        query_feature_maps,
        keys_ext,
        values_ext,
        key_maps,
        carry_state,
        carry_total,
        numerator,
        denominator,
        grad_out,
    ) = operands
    weights, exp_scores, window, linear = coefficients(
        query_rows, query_feature_maps, keys_ext, key_maps, key_valid
    )
    grad_numer = grad_out / denominator[..., None]
    grad_denom = -jnp.sum(grad_out * numerator, axis=-1) / (denominator * denominator)
    grad_weights = (
        jnp.einsum("tjd,sd->jts", grad_numer, values_ext, preferred_element_type=jnp.float32)
        + jnp.transpose(grad_denom)[:, :, None]
    )
    grad_scores = jnp.where(window, grad_weights * exp_scores, 0.0) / math.sqrt(HEAD_SIZE)
    grad_far = jnp.where(linear, grad_weights, 0.0)
    grad_queries = jnp.einsum(
        "jts,sd->tjd", grad_scores, keys_ext, preferred_element_type=jnp.float32
    )
    grad_keys = jnp.einsum(
        "jts,tjd->sd", grad_scores, query_rows, preferred_element_type=jnp.float32
    )
    grad_qmaps = (
        jnp.einsum("jts,sf->tjf", grad_far, key_maps, preferred_element_type=jnp.float32)
        + jnp.einsum("tjd,fd->tjf", grad_numer, carry_state, preferred_element_type=jnp.float32)
        + grad_denom[..., None] * carry_total
    )
    grad_kmaps = jnp.einsum(
        "jts,tjf->sf", grad_far, query_feature_maps, preferred_element_type=jnp.float32
    )
    grad_values = jnp.einsum("jts,tjd->sd", weights, grad_numer, preferred_element_type=jnp.float32)
    grad_state = jnp.einsum(
        "tjf,tjd->fd", query_feature_maps, grad_numer, preferred_element_type=jnp.float32
    )
    grad_total = jnp.einsum(
        "tjf,tj->f", query_feature_maps, grad_denom, preferred_element_type=jnp.float32
    )
    return (grad_queries, grad_keys, grad_values, grad_qmaps, grad_kmaps, grad_state, grad_total)


def add_pair(earlier, later_part):
    return (earlier[0] + later_part[0], earlier[1] + later_part[1])


def local(
    tokens,
    lengths,
    norm_attn,
    norm_ffn,
    w_query,
    key_projection,
    value_projection,
    w_output,
    w_gate,
    w_up,
    w_down,
    down_query,
    up_query,
    key_down_matrix,
    key_up_matrix,
    value_down_matrix,
    value_up_matrix,
    down_output,
    up_output,
    feature_query,
    key_feature_weight,
    cotangent,
):
    rows_per_block = tokens.shape[1]
    ext_rows = rows_per_block + WINDOW_KEYS
    heads_per_group = QUERY_HEADS // KEY_VALUE_HEADS
    feature_width = 2 * HEAD_SIZE
    inputs_wide = tokens[0].astype(jnp.float32)
    cot_narrow = cotangent[0]
    cot_wide = cot_narrow.astype(jnp.float32)
    seq_index = lax.axis_index("seq")
    lane_length = lengths[lax.axis_index("fsdp")]
    positions = seq_index * rows_per_block + jnp.arange(rows_per_block)
    cosine_lookup, sine_lookup = rotary(positions)
    gain_attn = norm_attn.astype(jnp.float32)
    gain_ffn = norm_ffn.astype(jnp.float32)
    inverse_attn = lax.rsqrt(jnp.mean(inputs_wide * inputs_wide, axis=-1, keepdims=True) + epsilon)
    normed = (inputs_wide * inverse_attn * gain_attn).astype(jnp.bfloat16)
    pieces = (
        lax.all_gather(w_query, ("seq", "fsdp"), axis=0, tiled=True),
        lax.all_gather(key_projection, ("seq", "fsdp"), axis=0, tiled=True),
        lax.all_gather(value_projection, ("seq", "fsdp"), axis=0, tiled=True),
    )
    sliced = normed
    query_pre, key_before_rotation, value_before_adapter = tuple(
        (jnp.dot(sliced, block_piece, preferred_element_type=jnp.float32) for block_piece in pieces)
    )
    narrow_query = jnp.dot(normed, down_query, preferred_element_type=jnp.float32).astype(
        jnp.bfloat16
    )
    narrow_key = jnp.dot(normed, key_down_matrix, preferred_element_type=jnp.float32).astype(
        jnp.bfloat16
    )
    narrow_value = jnp.dot(normed, value_down_matrix, preferred_element_type=jnp.float32).astype(
        jnp.bfloat16
    )
    query_pre = query_pre + jnp.dot(narrow_query, up_query.T, preferred_element_type=jnp.float32)
    key_before_rotation = key_before_rotation + jnp.dot(
        narrow_key, key_up_matrix.T, preferred_element_type=jnp.float32
    )
    value_before_adapter = value_before_adapter + jnp.dot(
        narrow_value, value_up_matrix.T, preferred_element_type=jnp.float32
    )
    query_rows = apply_rotary(
        query_pre.reshape(rows_per_block, QUERY_HEADS, HEAD_SIZE), cosine_lookup, sine_lookup
    ).astype(jnp.bfloat16)
    device_keys = apply_rotary(
        key_before_rotation.reshape(rows_per_block, KEY_VALUE_HEADS, HEAD_SIZE),
        cosine_lookup,
        sine_lookup,
    ).astype(jnp.bfloat16)
    device_values = value_before_adapter.reshape(rows_per_block, KEY_VALUE_HEADS, HEAD_SIZE).astype(
        jnp.bfloat16
    )
    softmax_query_rows = query_rows.reshape(
        rows_per_block, KEY_VALUE_HEADS, heads_per_group, HEAD_SIZE
    )
    teacher_init = (
        jnp.full((KEY_VALUE_HEADS, heads_per_group, rows_per_block), lowest_precision, jnp.float32),
        jnp.zeros((KEY_VALUE_HEADS, heads_per_group, rows_per_block), jnp.float32),
        jnp.zeros((KEY_VALUE_HEADS, heads_per_group, rows_per_block, HEAD_SIZE), jnp.float32),
        jnp.zeros((WINDOW_KEYS, KEY_VALUE_HEADS, HEAD_SIZE), jnp.bfloat16),
        jnp.zeros((WINDOW_KEYS, KEY_VALUE_HEADS, HEAD_SIZE), jnp.bfloat16),
    )
    portion_keys = lax.all_gather(
        device_keys.reshape(rows_per_block, KEY_VALUE_HEADS * HEAD_SIZE), "seq", axis=0, tiled=True
    )
    portion_values = lax.all_gather(
        device_values.reshape(rows_per_block, KEY_VALUE_HEADS * HEAD_SIZE),
        "seq",
        axis=0,
        tiled=True,
    )
    count_of_shards = portion_keys.shape[0] // rows_per_block
    sharded_keys = portion_keys.reshape(count_of_shards, rows_per_block, KEY_VALUE_HEADS, HEAD_SIZE)
    sharded_values = portion_values.reshape(
        count_of_shards, rows_per_block, KEY_VALUE_HEADS, HEAD_SIZE
    )

    def one_shard(inner, item):
        best, total, accum, rim_keys, rim_values = inner
        shard_number, shard_keys, shard_values = item
        shard_start = shard_number * rows_per_block
        scores = jnp.einsum(
            "tgjd,sgd->gjts", softmax_query_rows, shard_keys, preferred_element_type=jnp.float32
        ) / math.sqrt(HEAD_SIZE)
        allowed = (positions[:, None] >= (shard_start + jnp.arange(rows_per_block))[None, :])[
            None, None
        ]
        masked = jnp.where(allowed, scores, lowest_precision)
        new_best = jnp.maximum(best, jnp.max(masked, axis=-1))
        probs = jnp.where(allowed, jnp.exp(masked - new_best[..., None]), 0.0)
        factor = jnp.exp(best - new_best)
        total = total * factor + jnp.sum(probs, axis=-1)
        accum = accum * factor[..., None] + jnp.einsum(
            "gjts,sgd->gjtd", probs, shard_values.astype(jnp.float32)
        )
        is_before = shard_start // rows_per_block == seq_index - 1
        rim_keys = jnp.where(is_before, shard_keys[rows_per_block - WINDOW_KEYS :], rim_keys)
        rim_values = jnp.where(is_before, shard_values[rows_per_block - WINDOW_KEYS :], rim_values)
        return ((new_best, total, accum, rim_keys, rim_values), None)

    result, unused = lax.scan(
        one_shard, teacher_init, (jnp.arange(count_of_shards), sharded_keys, sharded_values)
    )
    best_all, total_all, accum_all, rim_keys, rim_values = result
    teacher = jnp.transpose(accum_all / total_all[..., None], (2, 0, 1, 3)).reshape(
        rows_per_block, QUERY_HEADS * HEAD_SIZE
    )
    keys_ext = jnp.concatenate([rim_keys, device_keys], axis=0)
    values_ext = jnp.concatenate([rim_values, device_values], axis=0)
    query_features = feature_query.reshape(QUERY_HEADS, HEAD_SIZE, HEAD_SIZE)
    key_features = key_feature_weight.reshape(KEY_VALUE_HEADS, HEAD_SIZE, HEAD_SIZE)
    query_feature_maps = apply_feature_map(query_rows, query_features).astype(jnp.bfloat16)
    key_maps = apply_feature_map(keys_ext, key_features).astype(jnp.bfloat16)
    ext_positions = seq_index * rows_per_block - WINDOW_KEYS + jnp.arange(ext_rows)
    key_valid = ext_positions >= 0
    valid_rows = key_valid[:rows_per_block].astype(jnp.float32)
    used_maps = key_maps[:rows_per_block].astype(jnp.float32) * valid_rows[:, None, None]
    values_head = values_ext[:rows_per_block].astype(jnp.float32)
    local_state = jnp.einsum("sgf,sgd->gfd", used_maps, values_head, precision=precise)
    local_total = jnp.sum(used_maps, axis=0)
    zero_pair = (
        jnp.zeros((KEY_VALUE_HEADS, feature_width, HEAD_SIZE), jnp.float32),
        jnp.zeros((KEY_VALUE_HEADS, feature_width), jnp.float32),
    )
    state_in, total_in = prefix((local_state, local_total), "seq", add_pair, zero_pair, False)
    queries_by_group = jnp.moveaxis(
        query_rows.reshape(rows_per_block, KEY_VALUE_HEADS, heads_per_group, HEAD_SIZE), 1, 0
    )
    query_maps_by_group = jnp.moveaxis(
        query_feature_maps.reshape(rows_per_block, KEY_VALUE_HEADS, heads_per_group, feature_width),
        1,
        0,
    )
    grouped_keys = jnp.moveaxis(keys_ext, 1, 0)
    grouped_values = jnp.moveaxis(values_ext, 1, 0)
    grouped_kmaps = jnp.moveaxis(key_maps, 1, 0)

    def forward_group(operands):
        return attend_group(operands, key_valid)

    numerator, denominator = lax.map(
        forward_group,
        (
            queries_by_group,
            query_maps_by_group,
            grouped_keys,
            grouped_values,
            grouped_kmaps,
            state_in,
            total_in,
        ),
    )
    row_mask = (positions < lane_length).astype(jnp.float32)
    attn_mixed = jnp.moveaxis(numerator / denominator[..., None], 0, 1).reshape(
        rows_per_block, QUERY_HEADS * HEAD_SIZE
    )
    attended = (attn_mixed * row_mask[:, None]).astype(jnp.bfloat16)
    difference = attended.astype(jnp.float32) - teacher * row_mask[:, None]
    local_loss = jnp.sum(difference * difference)
    sliced = attended
    branch = jnp.dot(
        sliced,
        lax.all_gather(w_output, ("seq", "fsdp"), axis=0, tiled=True),
        preferred_element_type=jnp.float32,
    )
    narrow_out = jnp.dot(attended, down_output, preferred_element_type=jnp.float32).astype(
        jnp.bfloat16
    )
    branch = branch + jnp.dot(narrow_out, up_output.T, preferred_element_type=jnp.float32)
    residual = inputs_wide + branch
    inverse_ffn = lax.rsqrt(jnp.mean(residual * residual, axis=-1, keepdims=True) + epsilon)
    normed_ffn = (residual * inverse_ffn * gain_ffn).astype(jnp.bfloat16)
    ffn_weights = (
        lax.all_gather(w_gate, "fsdp", axis=1, tiled=True),
        lax.all_gather(w_up, "fsdp", axis=1, tiled=True),
        lax.all_gather(w_down, "fsdp", axis=1, tiled=True),
    )
    pieces = (
        lax.all_gather(ffn_weights[0], "seq", axis=0, tiled=True),
        lax.all_gather(ffn_weights[1], "seq", axis=0, tiled=True),
    )
    sliced = normed_ffn
    gate_pre = jnp.dot(sliced, pieces[0], preferred_element_type=jnp.float32)
    up_pre = jnp.dot(sliced, pieces[1], preferred_element_type=jnp.float32)
    sigmoid_gate = jax.nn.sigmoid(gate_pre)
    silu_gate = gate_pre * sigmoid_gate
    hidden = (silu_gate * up_pre).astype(jnp.bfloat16)
    ffn_part = jnp.dot(
        hidden,
        lax.all_gather(ffn_weights[2], "seq", axis=0, tiled=True).T,
        preferred_element_type=jnp.float32,
    )
    output = (residual + ffn_part).astype(jnp.bfloat16)
    sliced = cot_narrow
    grad_hidden = jnp.dot(
        sliced,
        lax.all_gather(ffn_weights[2], "seq", axis=0, tiled=True),
        preferred_element_type=jnp.float32,
    )
    grad_gate = (
        grad_hidden * up_pre * sigmoid_gate * (1.0 + gate_pre * (1.0 - sigmoid_gate))
    ).astype(jnp.bfloat16)
    grad_up = (grad_hidden * silu_gate).astype(jnp.bfloat16)
    pieces = lax.all_gather((ffn_weights[0], ffn_weights[1]), "seq", axis=0, tiled=True)
    grad_part = jnp.dot(grad_gate, pieces[0].T, preferred_element_type=jnp.float32) + jnp.dot(
        grad_up, pieces[1].T, preferred_element_type=jnp.float32
    )
    grad_residual = cot_wide + norm_back(residual, inverse_ffn, gain_ffn, grad_part)
    grad_branch = grad_residual.astype(jnp.bfloat16)
    grad_narrow_out = jnp.dot(grad_branch, up_output, preferred_element_type=jnp.float32)
    grad_up_output = jnp.dot(grad_branch.T, narrow_out, preferred_element_type=jnp.float32)
    grad_down_output = jnp.dot(attended.T, grad_narrow_out, preferred_element_type=jnp.float32)
    attended_gradient = (
        jnp.dot(
            grad_branch,
            lax.all_gather(w_output, ("seq", "fsdp"), axis=0, tiled=True).T,
            preferred_element_type=jnp.float32,
        )
        + jnp.dot(grad_narrow_out, down_output.T, preferred_element_type=jnp.float32)
        + 2.0 * difference
    )
    attended_gradient = (
        lax.optimization_barrier(attended_gradient.astype(jnp.bfloat16)).astype(jnp.float32)
        * row_mask[:, None]
    )
    gradient_by_group = jnp.moveaxis(
        attended_gradient.reshape(rows_per_block, KEY_VALUE_HEADS, heads_per_group, HEAD_SIZE), 1, 0
    )

    def backward_group(operands):
        return attend_back(operands, key_valid)

    grad_q, grad_k, grad_v, grad_qm, grad_km, grad_state, grad_total = lax.map(
        backward_group,
        (
            queries_by_group,
            query_maps_by_group,
            grouped_keys,
            grouped_values,
            grouped_kmaps,
            state_in,
            total_in,
            numerator,
            denominator,
            gradient_by_group,
        ),
    )
    later_state, later_total = prefix((grad_state, grad_total), "seq", add_pair, zero_pair, True)
    values_grouped_head = jnp.moveaxis(values_head, 1, 0)
    used_grouped = jnp.moveaxis(used_maps, 1, 0)
    kmaps_head = grad_km[:, :rows_per_block] + valid_rows[None, :, None] * (
        jnp.einsum("gfd,gsd->gsf", later_state, values_grouped_head, precision=precise)
        + later_total[:, None, :]
    )
    grad_km = jnp.concatenate([kmaps_head, grad_km[:, rows_per_block:]], axis=1)
    values_grad_head = grad_v[:, :rows_per_block] + jnp.einsum(
        "gsf,gfd->gsd", used_grouped, later_state, precision=precise
    )
    grad_v = jnp.concatenate([values_grad_head, grad_v[:, rows_per_block:]], axis=1)
    grad_k_feat, key_feature_gradient = feature_back(
        keys_ext, key_features, jnp.moveaxis(grad_km, 0, 1)
    )
    gathered_key_gradient = jnp.moveaxis(grad_k, 0, 1) + grad_k_feat
    gathered_value_gradient = jnp.moveaxis(grad_v, 0, 1)
    grad_q_feat, grad_feature_query = feature_back(
        query_rows,
        query_features,
        jnp.moveaxis(grad_qm, 0, 1).reshape(rows_per_block, QUERY_HEADS, feature_width),
    )
    grad_queries_rot = (
        jnp.moveaxis(grad_q, 0, 1).reshape(rows_per_block, QUERY_HEADS, HEAD_SIZE) + grad_q_feat
    )
    back_keys, back_values = (
        shifted(
            gathered_key_gradient[:WINDOW_KEYS]
            .reshape(WINDOW_KEYS, KEY_VALUE_HEADS * HEAD_SIZE)
            .astype(jnp.bfloat16),
            "seq",
            -1,
        ).astype(jnp.float32),
        shifted(
            as_sent(
                gathered_value_gradient[:WINDOW_KEYS].reshape(
                    WINDOW_KEYS, KEY_VALUE_HEADS * HEAD_SIZE
                )
            ),
            "seq",
            -1,
        ),
    )
    trailing_keys = gathered_key_gradient[WINDOW_KEYS:].reshape(
        rows_per_block, KEY_VALUE_HEADS * HEAD_SIZE
    )
    trailing_values = gathered_value_gradient[WINDOW_KEYS:].reshape(
        rows_per_block, KEY_VALUE_HEADS * HEAD_SIZE
    )
    trailing_keys = jnp.concatenate(
        [
            trailing_keys[: rows_per_block - WINDOW_KEYS],
            trailing_keys[rows_per_block - WINDOW_KEYS :] + back_keys,
        ],
        axis=0,
    )
    trailing_values = jnp.concatenate(
        [
            trailing_values[: rows_per_block - WINDOW_KEYS],
            trailing_values[rows_per_block - WINDOW_KEYS :] + back_values,
        ],
        axis=0,
    )
    grad_query_pre = (
        inverse_rotary(grad_queries_rot, cosine_lookup, sine_lookup)
        .reshape(rows_per_block, QUERY_HEADS * HEAD_SIZE)
        .astype(jnp.bfloat16)
    )
    grad_key_pre = (
        inverse_rotary(
            trailing_keys.reshape(rows_per_block, KEY_VALUE_HEADS, HEAD_SIZE),
            cosine_lookup,
            sine_lookup,
        )
        .reshape(rows_per_block, KEY_VALUE_HEADS * HEAD_SIZE)
        .astype(jnp.bfloat16)
    )
    grad_value_pre = trailing_values.astype(jnp.bfloat16)
    grad_narrow_query = jnp.dot(grad_query_pre, up_query, preferred_element_type=jnp.float32)
    grad_narrow_key = jnp.dot(grad_key_pre, key_up_matrix, preferred_element_type=jnp.float32)
    grad_narrow_value = jnp.dot(grad_value_pre, value_up_matrix, preferred_element_type=jnp.float32)
    grad_up_query = jnp.dot(grad_query_pre.T, narrow_query, preferred_element_type=jnp.float32)
    grad_up_key = jnp.dot(grad_key_pre.T, narrow_key, preferred_element_type=jnp.float32)
    grad_up_value = jnp.dot(grad_value_pre.T, narrow_value, preferred_element_type=jnp.float32)
    grad_down_query = jnp.dot(normed.T, grad_narrow_query, preferred_element_type=jnp.float32)
    grad_down_key = jnp.dot(normed.T, grad_narrow_key, preferred_element_type=jnp.float32)
    grad_down_value = jnp.dot(normed.T, grad_narrow_value, preferred_element_type=jnp.float32)
    pieces = lax.all_gather(
        (w_query, key_projection, value_projection), ("seq", "fsdp"), axis=0, tiled=True
    )
    grad_normed = (
        jnp.dot(grad_query_pre, pieces[0].T, preferred_element_type=jnp.float32)
        + jnp.dot(grad_key_pre, pieces[1].T, preferred_element_type=jnp.float32)
        + jnp.dot(grad_value_pre, pieces[2].T, preferred_element_type=jnp.float32)
    )
    grad_normed = grad_normed + jnp.dot(
        grad_narrow_query, down_query.T, preferred_element_type=jnp.float32
    )
    grad_normed = grad_normed + jnp.dot(
        grad_narrow_key, key_down_matrix.T, preferred_element_type=jnp.float32
    )
    grad_normed = grad_normed + jnp.dot(
        grad_narrow_value, value_down_matrix.T, preferred_element_type=jnp.float32
    )
    grad_tokens = (
        grad_residual + norm_back(inputs_wide, inverse_attn, gain_attn, grad_normed)
    ).astype(jnp.bfloat16)
    device_count = lax.axis_size(("seq", "fsdp"))
    device_number = lax.axis_index(("seq", "fsdp"))
    loss_terms = jnp.where(jnp.arange(device_count) >= device_number, local_loss, 0.0)
    summed = (
        lax.psum_scatter(grad_down_query, ("seq", "fsdp"), scatter_dimension=0, tiled=True),
        lax.psum_scatter(grad_up_query, ("seq", "fsdp"), scatter_dimension=0, tiled=True),
        lax.psum_scatter(grad_down_key, ("seq", "fsdp"), scatter_dimension=0, tiled=True),
        lax.psum_scatter(grad_up_key, ("seq", "fsdp"), scatter_dimension=0, tiled=True),
        lax.psum_scatter(grad_down_value, ("seq", "fsdp"), scatter_dimension=0, tiled=True),
        lax.psum_scatter(grad_up_value, ("seq", "fsdp"), scatter_dimension=0, tiled=True),
        lax.psum_scatter(grad_down_output, ("seq", "fsdp"), scatter_dimension=0, tiled=True),
        lax.psum_scatter(grad_up_output, ("seq", "fsdp"), scatter_dimension=0, tiled=True),
        lax.psum_scatter(
            grad_feature_query.reshape(QUERY_HEADS * HEAD_SIZE, HEAD_SIZE),
            ("seq", "fsdp"),
            scatter_dimension=0,
            tiled=True,
        ),
        lax.psum_scatter(
            key_feature_gradient.reshape(KEY_VALUE_HEADS * HEAD_SIZE, HEAD_SIZE),
            ("seq", "fsdp"),
            scatter_dimension=0,
            tiled=True,
        ),
        lax.psum_scatter(loss_terms, ("seq", "fsdp"), scatter_dimension=0, tiled=True),
    )
    transfer_loss = summed[10] / jnp.sum(lengths).astype(jnp.float32)
    return (
        output[None],
        grad_tokens[None],
        summed[0],
        summed[1],
        summed[2],
        summed[3],
        summed[4],
        summed[5],
        summed[6],
        summed[7],
        summed[8],
        summed[9],
        transfer_loss,
    )


def solution(mesh):
    placed = (
        P("fsdp", "seq", None),
        P(),
        P(),
        P(),
        P(("seq", "fsdp"), None),
        P(("seq", "fsdp"), None),
        P(("seq", "fsdp"), None),
        P(("seq", "fsdp"), None),
        P("seq", "fsdp"),
        P("seq", "fsdp"),
        P("seq", "fsdp"),
        P(),
        P(),
        P(),
        P(),
        P(),
        P(),
        P(),
        P(),
        P(),
        P(),
        P("fsdp", "seq", None),
    )
    return jax.shard_map(
        local,
        mesh=mesh,
        in_specs=placed,
        out_specs=(
            P("fsdp", "seq", None),
            P("fsdp", "seq", None),
            P(("seq", "fsdp"), None),
            P(("seq", "fsdp"), None),
            P(("seq", "fsdp"), None),
            P(("seq", "fsdp"), None),
            P(("seq", "fsdp"), None),
            P(("seq", "fsdp"), None),
            P(("seq", "fsdp"), None),
            P(("seq", "fsdp"), None),
            P(("seq", "fsdp"), None),
            P(("seq", "fsdp"), None),
            P(("seq", "fsdp")),
        ),
        check_vma=False,
    )
```

profile of v0, /device:TPU:0, one launch (start us, length us, event | category | flops | bytes accessed | tf_op | source)
XLA Modules:
  0.0 2722.3 jit_solution(10484308370028619449)
XLA Ops:
  13.2 57.0 %all-gather.19.cloned.1.call-done = bf16[2048,512]{1,0:T(8,128)(2,1)} async-done(((bf16[64,512]{1,0:T(8,128)(2,1)}), bf16[2048,512]{1,0:T(8,128)(2,1)}) %all-gather.19.cloned.1.call-update) | async-done | bytes 2097168 | tf_op jit(solution)/shard_map/all_gather | solution.py:252
  74.4 54.1 %all-gather.25.cloned.1.call-done = bf16[2048,512]{1,0:T(8,128)(2,1)} async-done(((bf16[64,512]{1,0:T(8,128)(2,1)}), bf16[2048,512]{1,0:T(8,128)(2,1)}) %all-gather.25.cloned.1.call-update) | async-done | bytes 2097168 | tf_op jit(solution)/shard_map/all_gather | solution.py:253
  137.0 20.5 all-gather.21.cloned.1.call-done
  161.5 26.2 all-gather.27.cloned.1.call-done
  187.7 6.2 reshape.486
  193.9 5.1 copy.105
  198.9 69.0 %all-gather.23.cloned.1.call-done = bf16[2048,2048]{1,0:T(8,128)(2,1)} async-done(((bf16[64,2048]{1,0:T(8,128)(2,1)}), bf16[2048,2048]{1,0:T(8,128)(2,1)}) %all-gather.23.cloned.1.call-update) | async-done | bytes 8388624 | tf_op jit(solution)/shard_map/all_gather | solution.py:251
  267.9 5.7 fusion.260
  282.4 147.2 %while.88 = (s32[]{:T(128)}, f32[8,4,256]{2,1,0:T(4,128)S(1)}, f32[8,4,256]{2,1,0:T(4,128)S(1)}, f32[8,4,256,64]{2,3,1,0:T(8,128)}, bf16[64,8,64]{0,2,1:T(8,128)...) while((s32[]{:T(128)}, f32[8,4,256]{2,1,0:T(4,128)S(1)}, ...), condition=%wide.region_8.9_spmd.clone, body=%wide.region_5.8_spmd.clone.sunk | while | flops 563847680 | bytes 65671600 | solution.py:334
  283.8 5.6 fusion.436
  289.4 4.7 fusion.437
  301.9 5.6 fusion.436
  307.5 4.7 fusion.437
  313.5 4.3 fusion.439
  320.4 5.6 fusion.436
  326.0 4.7 fusion.437
  331.9 4.3 fusion.439
  338.8 5.6 fusion.436
  344.4 4.6 fusion.437
  350.3 4.3 fusion.439
  357.2 5.6 fusion.436
  362.9 4.7 fusion.437
  368.7 4.3 fusion.439
  375.7 5.6 fusion.436
  381.3 4.7 fusion.437
  387.2 4.3 fusion.439
  394.1 5.6 fusion.436
  399.8 4.7 fusion.437
  405.7 4.3 fusion.439
  412.6 5.6 fusion.436
  418.2 4.6 fusion.437
  439.4 71.1 %all-gather.39.cloned.1.call-done = bf16[256,8192]{1,0:T(8,128)(2,1)} async-done(((bf16[256,2048]{1,0:T(8,128)(2,1)}), bf16[256,8192]{1,0:T(8,128)(2,1)}) %all-gather.39.cloned.1.call-update) | async-done | bytes 4194320 | tf_op jit(solution)/shard_map/all_gather | solution.py:409
  533.6 8.8 all-gather.1
  542.8 4.8 maximum_bitcast_fusion
  549.5 61.9 %while.86 = (s32[]{:T(128)}, f32[8,256,4,64]{1,3,2,0:T(8,128)}, f32[8,256,4]{1,2,0:T(4,128)}, bf16[8,320,64]{1,2,0:T(8,128)(2,1)S(1)}, bf16[8,320,64]{1,2,0:T(8,...) while((s32[]{:T(128)}, f32[8,256,4,64]{1,3,2,0:T(8,128)}, ...), condition=%wide.region_18.19_spmd.clone, body=%wide.region_16.18_spmd.clone.sunk | while | flops 482657152 | bytes 6213385 | solution.py:374
  611.5 6.2 fusion.183
  618.3 46.2 %all-reduce = f32[32]{0:T(128)S(1)} all-reduce(f32[32]{0:T(128)S(1)} %compare_select_fusion), channel_id=16, replica_groups=mesh['seq'=8,'fsdp'=4] {'seq','fsdp'}, use_global_device_ids=true, to_apply=%region_42.43.clone | all-reduce | flops 32 | bytes 256
  674.4 5.7 fusion.273
  682.1 95.5 %all-gather.37.cloned.1.call-done = bf16[2048,8192]{1,0:T(8,128)(2,1)} async-done(((bf16[256,8192]{1,0:T(8,128)(2,1)}), bf16[2048,8192]{1,0:T(8,128)(2,1)}) %all-gather.37.cloned.1.call-update) | async-done | bytes 33554448 | tf_op jit(solution)/shard_map/all_gather | solution.py:413
  777.6 22.1 fusion.246
  799.7 140.5 %all-gather.33.cloned.1.call-done = bf16[2048,8192]{1,0:T(8,128)(2,1)} async-done(((bf16[256,8192]{1,0:T(8,128)(2,1)}), bf16[2048,8192]{1,0:T(8,128)(2,1)}) %all-gather.33.cloned.1.call-update) | async-done | bytes 33554448 | tf_op jit(solution)/shard_map/all_gather | solution.py:412
  940.2 20.2 fusion.247
  960.4 142.5 %all-gather.41.cloned.1.call-done = bf16[2048,8192]{1,0:T(8,128)(2,1)} async-done(((bf16[256,8192]{1,0:T(8,128)(2,1)}), bf16[2048,8192]{1,0:T(8,128)(2,1)}) %all-gather.41.cloned.1.call-update) | async-done | bytes 33554448 | tf_op jit(solution)/shard_map/all_gather | solution.py:423
  1102.9 17.6 fusion.202
  1120.5 20.1 fusion.161
  1140.6 23.4 multiply_reduce_fusion.2
  1167.5 5.9 fusion.234
  1180.1 165.7 %while.87 = (s32[]{:T(128)}, f32[8,256,4,64]{1,3,2,0:T(8,128)}, f32[8,320,64]{1,2,0:T(8,128)}, f32[8,320,64]{1,2,0:T(8,128)}, f32[8,256,4,128]{1,3,2,0:T(8,128)}...) while((s32[]{:T(128)}, f32[8,256,4,64]{1,3,2,0:T(8,128)}, ...), condition=%wide.region_23.24_spmd.clone, body=%wide.region_21.23_spmd.clone.sunk | while | flops 501468032 | bytes 18283644 | solution.py:466
  1345.8 4.8 multiply_reduce_fusion.1
  1350.7 4.9 multiply_subtract_fusion
  1372.2 9.0 all-gather.3
  1382.1 31.8 %while.85 = (s32[]{:T(128)}, f32[8,128,64]{2,1,0:T(8,128)}, f32[8,128]{1,0:T(8,128)S(1)}, s32[]{:T(128)}, bf16[8,8,128,64]{2,3,1,0:T(8,128)(2,1)}, /*index=5*/bf...) while((s32[]{:T(128)}, f32[8,128,64]{2,1,0:T(8,128)}, ...), condition=%wide.region_27.28_spmd, body=%wide.region_26.27_spmd.sunk | while | flops 133126 | bytes 1190051 | solution.py:40
  1439.0 21.0 fusion.172
  1460.0 7.2 fusion.274
  1467.3 44.9 %reduce-scatter.31.cloned.1.call-done = f32[64,8]{1,0:T(8,128)} async-done(((f32[2048,8]{1,0:T(8,128)}), f32[64,8]{1,0:T(8,128)}) %reduce-scatter.31.cloned.1.call-update) | async-done | bytes 2064
  1513.6 132.3 %reduce-scatter.33.cloned.1.call-done = f32[64,8]{1,0:T(8,128)} async-done(((f32[2048,8]{1,0:T(8,128)}), f32[64,8]{1,0:T(8,128)}) %reduce-scatter.33.cloned.1.call-update) | async-done | bytes 2064
  1647.4 132.7 %reduce-scatter.43.cloned.1.call-done = f32[64,8]{1,0:T(8,128)} async-done(((f32[2048,8]{1,0:T(8,128)}), f32[64,8]{1,0:T(8,128)}) %reduce-scatter.43.cloned.1.call-update) | async-done | bytes 2064
  1781.4 132.7 %reduce-scatter.45.cloned.1.call-done = f32[64,8]{1,0:T(8,128)} async-done(((f32[2048,8]{1,0:T(8,128)}), f32[64,8]{1,0:T(8,128)}) %reduce-scatter.45.cloned.1.call-update) | async-done | bytes 2064
  1925.7 120.8 %reduce-scatter.37.cloned.1.call-done = f32[16,8]{1,0:T(8,128)} async-done(((f32[512,8]{1,0:T(8,128)}), f32[16,8]{1,0:T(8,128)}) %reduce-scatter.37.cloned.1.call-update) | async-done | bytes 528
  2047.8 130.6 %reduce-scatter.41.cloned.1.call-done = f32[16,8]{1,0:T(8,128)} async-done(((f32[512,8]{1,0:T(8,128)}), f32[16,8]{1,0:T(8,128)}) %reduce-scatter.41.cloned.1.call-update) | async-done | bytes 528
  2179.7 132.5 %reduce-scatter.35.cloned.1.call-done = f32[64,8]{1,0:T(8,128)} async-done(((f32[2048,8]{1,0:T(8,128)}), f32[64,8]{1,0:T(8,128)}) %reduce-scatter.35.cloned.1.call-update) | async-done | bytes 2064
  2313.7 132.8 %reduce-scatter.39.cloned.1.call-done = f32[64,8]{1,0:T(8,128)} async-done(((f32[2048,8]{1,0:T(8,128)}), f32[64,8]{1,0:T(8,128)}) %reduce-scatter.39.cloned.1.call-update) | async-done | bytes 2064
  2448.0 133.3 %reduce-scatter.27.cloned.1.call-done = f32[64,64]{1,0:T(8,128)} async-done(((f32[2048,64]{1,0:T(8,128)}), f32[64,64]{1,0:T(8,128)}) %reduce-scatter.27.cloned.1.call-update) | async-done | bytes 16400 | tf_op jit(solution)/shard_map/reduce_scatter | solution.py:600
  2581.2 132.8 %reduce-scatter.29.cloned.1.call-done = f32[16,64]{1,0:T(8,128)} async-done(((f32[512,64]{1,0:T(8,128)}), f32[16,64]{1,0:T(8,128)}) %reduce-scatter.29.cloned.1.call-update) | async-done | bytes 4112 | tf_op jit(solution)/shard_map/reduce_scatter | solution.py:606
  (704 shorter events, 442.5 us)
Async XLA Ops:
  7.2 673.0 %copy-start = (bf16[2048,8]{0,1:T(8,128)(2,1)S(1)}, bf16[2048,8]{0,1:T(8,128)(2,1)}, u32[]{:S(2)}) copy-start(bf16[2048,8]{0,1:T(8,128)(2,1)} %param.50) | copy-start | bytes 98308
  7.2 63.0 %copy-start.2 = (bf16[1,256,2048]{2,1,0:T(8,128)(2,1)S(1)}, bf16[1,256,2048]{2,1,0:T(8,128)(2,1)}, u32[]{:S(2)}) copy-start(bf16[1,256,2048]{2,1,0:T(8,128)(2,1)} %param.32) | copy-start | bytes 3145732
  7.2 63.0 %all-gather.19.cloned.1.call-start = ((), (), s32[]{:S(2)}) async-start(), calls=%async_computation.10 | async-start | bytes 2162688 | tf_op jit(solution)/shard_map/all_gather | solution.py:252
  8.0 120.5 %all-gather.25.cloned.1.call-start = ((), (), s32[]{:S(2)}) async-start(), calls=%async_computation.13 | async-start | bytes 2162688 | tf_op jit(solution)/shard_map/all_gather | solution.py:253
  8.7 148.7 %all-gather.21.cloned.1.call-start = ((), (), s32[]{:S(2)}) async-start(), calls=%async_computation.11 | async-start | bytes 2359296 | tf_op jit(solution)/shard_map/all_gather | solution.py:296
  9.4 258.5 %copy-start.56 = (f32[2048]{0:T(1024)}, f32[2048]{0:T(1024)S(1)}, u32[]{:S(2)}) copy-start(f32[2048]{0:T(1024)S(1)} %convert_element_type.207) | copy-start | bytes 24580
  11.0 256.9 %copy-start.76 = (f32[256]{0:T(256)}, f32[256]{0:T(256)S(1)}, u32[]{:S(2)}) copy-start(f32[256]{0:T(256)S(1)} %add_rsqrt_fusion.1) | copy-start | bytes 3076
  11.2 267.3 %copy-start.45 = (f32[256,32]{0,1:T(8,128)}, f32[256,32]{0,1:T(8,128)S(1)}, u32[]{:S(2)}) copy-start(f32[256,32]{0,1:T(8,128)S(1)} %get-tuple-element.910) | copy-start | bytes 98308
  11.2 267.3 %copy-start.47 = (f32[256,32]{0,1:T(8,128)}, f32[256,32]{0,1:T(8,128)S(1)}, u32[]{:S(2)}) copy-start(f32[256,32]{0,1:T(8,128)S(1)} %get-tuple-element.911) | copy-start | bytes 98308
  12.9 57.3 %copy-start.78 = (bf16[256,8]{0,1:T(8,128)(2,1)}, bf16[256,8]{0,1:T(8,128)(2,1)S(1)}, u32[]{:S(2)}) copy-start(bf16[256,8]{0,1:T(8,128)(2,1)S(1)} %convolution_convert_fusion.4) | copy-start | bytes 12292
  73.6 114.1 %all-gather.27.cloned.1.call-start = ((), (), s32[]{:S(2)}) async-start(), calls=%async_computation.14 | async-start | bytes 2359296 | tf_op jit(solution)/shard_map/all_gather | solution.py:299
  74.1 57.4 %copy-start.80 = (bf16[256,8]{0,1:T(8,128)(2,1)}, bf16[256,8]{0,1:T(8,128)(2,1)S(1)}, u32[]{:S(2)}) copy-start(bf16[256,8]{0,1:T(8,128)(2,1)S(1)} %convolution_convert_fusion.2) | copy-start | bytes 12292
  131.6 136.3 %all-gather.23.cloned.1.call-start = ((), (), s32[]{:S(2)}) async-start(), calls=%async_computation.12 | async-start | bytes 8650752 | tf_op jit(solution)/shard_map/all_gather | solution.py:251
  132.2 306.0 %all-gather.35.cloned.1.call-start = ((), (), s32[]{:S(2)}) async-start(), calls=%async_computation.18 | async-start | bytes 5242880 | tf_op jit(solution)/shard_map/all_gather | solution.py:408
  132.8 306.3 %all-gather.31.cloned.1.call-start = ((), (), s32[]{:S(2)}) async-start(), calls=%async_computation.16 | async-start | bytes 5242880 | tf_op jit(solution)/shard_map/all_gather | solution.py:407
  133.5 377.0 %all-gather.39.cloned.1.call-start = ((), (), s32[]{:S(2)}) async-start(), calls=%async_computation.20 | async-start | bytes 5242880 | tf_op jit(solution)/shard_map/all_gather | solution.py:409
  134.3 413.4 %all-gather.43.cloned.1.call-start = ((), (), s32[]{:S(2)}) async-start(), calls=%async_computation.24 | async-start | bytes 1179648 | tf_op jit(solution)/shard_map/all_gather | solution.py:25
  135.3 138.3 %copy-start.82 = (bf16[256,8]{0,1:T(8,128)(2,1)}, bf16[256,8]{0,1:T(8,128)(2,1)S(1)}, u32[]{:S(2)}) copy-start(bf16[256,8]{0,1:T(8,128)(2,1)S(1)} %convolution_convert_fusion.3) | copy-start | bytes 12292
  136.1 299.6 %copy-start.84 = (f32[256]{0:T(256)}, f32[256]{0:T(256)S(1)}, u32[]{:S(2)}) copy-start(f32[256]{0:T(256)S(1)} %slice_convert_fusion.1) | copy-start | bytes 3076
  198.9 74.7 %copy-start.60 = (bf16[2048,8]{0,1:T(8,128)(2,1)S(1)}, bf16[2048,8]{0,1:T(8,128)(2,1)}, u32[]{:S(2)}) copy-start(bf16[2048,8]{0,1:T(8,128)(2,1)} %param.44) | copy-start | bytes 98308
  280.4 247.2 %copy-start.12 = (bf16[256,32,32]{0,2,1:T(8,128)(2,1)}, bf16[256,32,32]{0,2,1:T(8,128)(2,1)S(1)}, u32[]{:S(2)}) copy-start(bf16[256,32,32]{0,2,1:T(8,128)(2,1)S(1)} %get-tuple-element.902) | copy-start | bytes 1572868
  282.4 147.2 %copy-start.26 = (bf16[256,8,64]{0,2,1:T(8,128)(2,1)S(1)}, bf16[256,8,64]{0,2,1:T(8,128)(2,1)}, u32[]{:S(2)}) copy-start(bf16[256,8,64]{0,2,1:T(8,128)(2,1)} %maximum_convert_fusion) | copy-start | bytes 786436
  289.4 5.9 copy-start.1
  307.5 5.9 copy-start.1
  326.0 5.9 copy-start.1
  362.9 5.9 copy-start.1
  381.3 5.9 copy-start.1
  399.8 5.9 copy-start.1
  429.6 112.8 %copy-start.20 = (bf16[64,8,64]{0,2,1:T(8,128)(2,1)}, bf16[64,8,64]{0,2,1:T(8,128)(2,1)S(1)}, u32[]{:S(2)}) copy-start(bf16[64,8,64]{0,2,1:T(8,128)(2,1)S(1)} %get-tuple-element.478) | copy-start | bytes 196612
  429.6 112.8 %copy-start.21 = (bf16[64,8,64]{0,2,1:T(8,128)(2,1)}, bf16[64,8,64]{0,2,1:T(8,128)(2,1)S(1)}, u32[]{:S(2)}) copy-start(bf16[64,8,64]{0,2,1:T(8,128)(2,1)S(1)} %get-tuple-element.479) | copy-start | bytes 196612
  437.5 236.9 %all-gather.29.cloned.1.call-start = ((), (), s32[]{:S(2)}) async-start(), calls=%async_computation.15 | async-start | bytes 8650752 | tf_op jit(solution)/shard_map/all_gather | solution.py:396
  438.1 339.5 %all-gather.37.cloned.1.call-start = ((), (), s32[]{:S(2)}) async-start(), calls=%async_computation.19 | async-start | bytes 37748736 | tf_op jit(solution)/shard_map/all_gather | solution.py:413
  438.8 501.4 %all-gather.33.cloned.1.call-start = ((), (), s32[]{:S(2)}) async-start(), calls=%async_computation.17 | async-start | bytes 37748736 | tf_op jit(solution)/shard_map/all_gather | solution.py:412
  439.4 663.5 %all-gather.41.cloned.1.call-start = ((), (), s32[]{:S(2)}) async-start(), calls=%async_computation.21 | async-start | bytes 37748736 | tf_op jit(solution)/shard_map/all_gather | solution.py:423
  510.5 9.3 copy-start.14
  510.5 870.7 %all-gather.45.cloned.1.call-start = ((), (), s32[]{:S(2)}) async-start(), calls=%async_computation.25 | async-start | bytes 1179648 | tf_op jit(solution)/shard_map/all_gather | solution.py:25
  513.6 14.0 copy-start.23
  531.7 10.7 copy-start.27
  531.7 10.7 copy-start.35
  611.5 6.2 copy-start.39
  611.5 6.2 copy-start.40
  611.5 6.2 copy-start.58
  674.0 6.1 copy-start.6
  777.6 162.6 %copy-start.15 = (f32[256,2048]{1,0:T(8,128)S(1)}, f32[256,2048]{1,0:T(8,128)}, u32[]{:S(2)}) copy-start(f32[256,2048]{1,0:T(8,128)} %get-tuple-element.921) | copy-start | bytes 6291460
  799.7 303.2 %copy-start.44 = (bf16[1,256,2048]{2,1,0:T(8,128)(2,1)S(1)}, bf16[1,256,2048]{2,1,0:T(8,128)(2,1)}, u32[]{:S(2)}) copy-start(bf16[1,256,2048]{2,1,0:T(8,128)(2,1)} %param.53) | copy-start | bytes 3145732
  1167.5 5.9 copy-start.7
  1167.5 5.9 copy-start.11
  1350.6 161.6 %reduce-scatter.31.cloned.1.call-start = ((), (), s32[]{:S(2)}) async-start(), calls=%async_computation.26 | async-start | bytes 1081344
  1360.3 285.7 %reduce-scatter.33.cloned.1.call-start = ((), (), s32[]{:S(2)}) async-start(), calls=%async_computation.27 | async-start | bytes 1081344
  1363.0 417.0 %reduce-scatter.43.cloned.1.call-start = ((), (), s32[]{:S(2)}) async-start(), calls=%async_computation.32 | async-start | bytes 1081344
  1365.8 548.3 %reduce-scatter.45.cloned.1.call-start = ((), (), s32[]{:S(2)}) async-start(), calls=%async_computation.33 | async-start | bytes 1081344
  1381.1 665.3 %reduce-scatter.37.cloned.1.call-start = ((), (), s32[]{:S(2)}) async-start(), calls=%async_computation.29 | async-start | bytes 270336
  1382.1 31.8 %copy-start.85 = (f32[256]{0:T(256)S(1)}, f32[256]{0:T(256)}, u32[]{:S(2)}) copy-start(f32[256]{0:T(256)} %copy-done.84) | copy-start | bytes 3076
  1421.0 5.0 collective-permute-start
  1424.7 4.3 collective-permute-start.1
  1426.3 6.4 copy-start.25
  1426.5 6.3 copy-start.87
  1429.0 749.4 %reduce-scatter.41.cloned.1.call-start = ((), (), s32[]{:S(2)}) async-start(), calls=%async_computation.31 | async-start | bytes 270336
  1432.7 879.6 %reduce-scatter.35.cloned.1.call-start = ((), (), s32[]{:S(2)}) async-start(), calls=%async_computation.28 | async-start | bytes 1081344
  1434.0 1012.5 %reduce-scatter.39.cloned.1.call-start = ((), (), s32[]{:S(2)}) async-start(), calls=%async_computation.30 | async-start | bytes 1081344
  1435.7 1145.5 %reduce-scatter.27.cloned.1.call-start = ((), (), s32[]{:S(2)}) async-start(), calls=%async_computation.22 | async-start | bytes 1081344 | tf_op jit(solution)/shard_map/reduce_scatter | solution.py:600
  1438.7 1275.3 %reduce-scatter.29.cloned.1.call-start = ((), (), s32[]{:S(2)}) async-start(), calls=%async_computation.23 | async-start | bytes 270336 | tf_op jit(solution)/shard_map/reduce_scatter | solution.py:606
  1439.0 21.0 copy-start.10
  1460.0 455.5 %copy-start.22 = (bf16[64,8,64]{0,2,1:T(8,128)(2,1)S(1)}, bf16[64,8,64]{0,2,1:T(8,128)(2,1)}, u32[]{:S(2)}) copy-start(bf16[64,8,64]{0,2,1:T(8,128)(2,1)} %copy-done.21) | copy-start | bytes 196612
  (68 other events, 184.7 us)
Sparse Core Ops, SparseCore 0:
  11.0 59.1 all-gather.18
  73.1 55.3 all-gather.24
  130.4 27.0 all-gather.20
  159.8 27.8 all-gather.26
  190.5 77.3 all-gather.22
  269.3 79.3 all-gather.34
  350.3 79.2 all-gather.30
  431.2 79.2 all-gather.38
  512.4 22.0 all-gather.42
  537.2 77.9 all-gather.28
  617.2 160.4 all-gather.36
  779.4 160.7 all-gather.32
  942.1 160.7 all-gather.40
  1350.7 23.5 all-gather.44
  1376.4 135.7 reduce-scatter.30
  1514.4 131.5 reduce-scatter.32
  1648.0 131.9 reduce-scatter.42
  1782.2 131.8 reduce-scatter.44
  1916.3 130.0 reduce-scatter.36
  2048.6 129.7 reduce-scatter.40
  2180.6 131.5 reduce-scatter.34
  2314.6 131.8 reduce-scatter.38
  2449.4 131.8 reduce-scatter.26
  2584.0 130.0 reduce-scatter.28
where the time goes:
time: 2730 us; the launch traced here: 2720 us
  waiting for transfers between devices  1910 us (70%)
  matrix products  479 us (18%)
  other arithmetic  135 us (5%)
  local copies, waits for them, and re-layouts  108 us (4%)
  blocking collectives  64 us (2%)
    unnamed x32, waiting for transfers between devices  965 us
    all_gather x1, waiting for transfers between devices, local(): lax.all_gather(ffn_weights[2], 'seq', axis=0, tiled=True)  142 us
    all_gather x1, waiting for transfers between devices, local(): lax.all_gather(ffn_weights[0], 'seq', axis=0, tiled=True)  140 us
    reduce_scatter x1, waiting for transfers between devices, local(): lax.psum_scatter(grad_feature_query.reshape(QUERY_HEADS * HEAD_SIZE, HEAD...  133 us
    reduce_scatter x1, waiting for transfers between devices, local(): lax.psum_scatter(key_feature_gradient.reshape(KEY_VALUE_HEADS * HEAD_SIZE...  133 us
    all_gather x1, waiting for transfers between devices, local(): lax.all_gather(ffn_weights[1], 'seq', axis=0, tiled=True)  95.5 us
    all_gather x1, waiting for transfers between devices, local(): lax.all_gather(w_down, 'fsdp', axis=1, tiled=True)  71.1 us
    all_gather x1, waiting for transfers between devices, local(): lax.all_gather(w_query, ('seq', 'fsdp'), axis=0, tiled=True)  69 us
  transfers between devices with their start and end apart: 26, of which 19 were waited for; matrix products, arithmetic and copies ran while one was open for 17% of the time, Pallas kernels for 0%

commit v1 on v0

--- a/solution.py
+++ b/solution.py
@@ -3,6 +3,8 @@
 import jax
 import jax.numpy as jnp
 from jax import lax
+from jax.experimental import pallas as pl
+from jax.experimental.pallas import tpu as pltpu
 from jax.sharding import PartitionSpec as P
 
 QUERY_HEADS = 32
@@ -15,6 +17,8 @@
 rope_base = 500000.0
 precise = lax.Precision.HIGHEST
 lowest_precision = -1e30
+ONES = 16
+SUB = 128
 
 
 def prefix(x, axis, join, neutral, backward):
@@ -628,6 +632,764 @@
         transfer_loss,
     )
 
+def halves_rotated(first_half, second_half, cosine, sine):
+    return (
+        first_half * cosine - second_half * sine,
+        second_half * cosine + first_half * sine,
+    )
+
+
+def soft_pair(logits):
+    plus = jnp.exp(logits - jnp.max(logits, axis=0, keepdims=True))
+    minus = jnp.exp(jnp.min(logits, axis=0, keepdims=True) - logits)
+    plus = plus * (1.0 / jnp.sum(plus, axis=0, keepdims=True))
+    minus = minus * (1.0 / jnp.sum(minus, axis=0, keepdims=True))
+    return plus, minus
+
+
+def mm(a, b):
+    return jnp.dot(a, b, preferred_element_type=jnp.float32)
+
+
+def mm_nt(a, b):
+    return lax.dot_general(a, b, (((1,), (1,)), ((), ())), preferred_element_type=jnp.float32)
+
+
+def split_wide(x):
+    high = x.astype(jnp.bfloat16)
+    low = (x - high.astype(jnp.float32)).astype(jnp.bfloat16)
+    return high, low
+
+
+def project_kernel(
+    x_ref, w_ref, up_ref, map_ref, cos_ref, sin_ref,
+    q_ref, kt_ref, vt_ref, k_ref, v_ref, pq_ref, pkt_ref, pk_ref, narrow_ref,
+):
+    group = q_ref.shape[0] // HEAD_SIZE
+    half = HEAD_SIZE // 2
+    width = (group + 2) * HEAD_SIZE
+    full = mm_nt(w_ref[...], x_ref[...])
+    narrow = full[width:].astype(jnp.bfloat16)
+    narrow_ref[...] = narrow
+    pre = full[:width] + mm(up_ref[...], narrow)
+    cosine, sine = cos_ref[...], sin_ref[...]
+    for head in range(group + 1):
+        base = head * HEAD_SIZE
+        low_half, high_half = halves_rotated(
+            pre[base : base + half], pre[base + half : base + HEAD_SIZE], cosine, sine
+        )
+        wide = jnp.concatenate([low_half, high_half], axis=0)
+        vector = wide.astype(jnp.bfloat16)
+        logits = mm(map_ref[base : base + HEAD_SIZE], vector)
+        plus, minus = soft_pair(logits)
+        maps = jnp.concatenate([plus, minus], axis=0)
+        if head < group:
+            q_ref[base : base + HEAD_SIZE] = vector
+            pq_ref[2 * base : 2 * base + 2 * HEAD_SIZE] = maps.astype(jnp.bfloat16)
+        else:
+            kt_ref[...] = vector
+            k_ref[...] = jnp.transpose(wide).astype(jnp.bfloat16)
+            pkt_ref[...] = maps.astype(jnp.bfloat16)
+            pk_ref[...] = jnp.transpose(maps).astype(jnp.bfloat16)
+    values = pre[width - HEAD_SIZE : width]
+    vt_ref[:HEAD_SIZE] = values.astype(jnp.bfloat16)
+    vt_ref[HEAD_SIZE:] = jnp.ones((ONES, values.shape[1]), jnp.bfloat16)
+    v_ref[...] = jnp.transpose(values).astype(jnp.bfloat16)
+
+
+def side_by_side(ref, size, group, columns):
+    return jnp.concatenate(
+        [ref[head * size : (head + 1) * size, columns] for head in range(group)], axis=1
+    )
+
+
+def band(group):
+    shape = (2 * SUB, group * SUB)
+    query_at = lax.rem(lax.broadcasted_iota(jnp.int32, shape, 1), SUB)
+    key_at = lax.broadcasted_iota(jnp.int32, shape, 0) - SUB
+    return query_at - key_at, key_at
+
+
+def forward_kernel(
+    length_ref, q_ref, pq_ref, k_ref, k_before, pk_ref, pk_before, vt_ref, vt_before,
+    att_ref, out_ref, denom_ref, states_ref, state,
+):
+    step = pl.program_id(0)
+    group = q_ref.shape[0] // HEAD_SIZE
+    rows = q_ref.shape[1]
+
+    @pl.when(step == 0)
+    def _():
+        state[...] = jnp.zeros_like(state)
+
+    for sub in range(rows // SUB):
+        columns = slice(sub * SUB, (sub + 1) * SUB)
+        queries = side_by_side(q_ref, HEAD_SIZE, group, columns)
+        query_maps = side_by_side(pq_ref, 2 * HEAD_SIZE, group, columns)
+        if sub == 0:
+            keys = jnp.concatenate([k_before[...], k_ref[:SUB]], axis=0)
+            key_maps = jnp.concatenate([pk_before[...], pk_ref[:SUB]], axis=0)
+            values = jnp.concatenate([vt_before[...], vt_ref[:, :SUB]], axis=1)
+        else:
+            around = slice((sub - 1) * SUB, (sub + 1) * SUB)
+            keys, key_maps, values = k_ref[around], pk_ref[around], vt_ref[:, around]
+        distance, key_at = band(group)
+        window = (distance >= 0) & (distance < WINDOW_KEYS)
+        linear = distance >= WINDOW_KEYS
+        if sub == 0:
+            inside = (key_at >= 0) | (step > 0)
+            window, linear = window & inside, linear & inside
+        near = jnp.exp(mm(keys, queries) * (1.0 / math.sqrt(HEAD_SIZE)))
+        far = mm(key_maps, query_maps)
+        weights = jnp.where(window, near, jnp.where(linear, far, 0.0)).astype(jnp.bfloat16)
+        states_ref[sub] = state[...]
+        high, low = split_wide(state[...])
+        total = mm(values, weights) + mm(
+            jnp.concatenate([high, low], axis=1),
+            jnp.concatenate([query_maps, query_maps], axis=0),
+        )
+        denom = total[HEAD_SIZE : HEAD_SIZE + 1]
+        out = total[:HEAD_SIZE] * (1.0 / denom)
+        at = (
+            step * rows
+            + sub * SUB
+            + lax.rem(lax.broadcasted_iota(jnp.int32, out.shape, 1), SUB)
+        )
+        attended = jnp.where(at < length_ref[0], out, 0.0).astype(jnp.bfloat16)
+        for head in range(group):
+            lanes = slice(head * SUB, (head + 1) * SUB)
+            base = head * HEAD_SIZE
+            out_ref[base : base + HEAD_SIZE, columns] = out[:, lanes]
+            att_ref[base : base + HEAD_SIZE, columns] = attended[:, lanes]
+            denom_ref[head : head + 1, columns] = denom[:, lanes]
+        update = mm(values[:, :SUB], key_maps[:SUB])
+        if sub == 0:
+            update = jnp.where(step > 0, update, 0.0)
+        state[...] = state[...] + update
+
+
+def teacher_kernel(length_ref, q_ref, k_ref, vt_ref, att_ref, diff_ref, loss_ref):
+    step = pl.program_id(0)
+    group = q_ref.shape[0] // HEAD_SIZE
+    rows = q_ref.shape[1]
+    scale = 1.0 / math.sqrt(HEAD_SIZE)
+    queries = [q_ref[head * HEAD_SIZE : (head + 1) * HEAD_SIZE] for head in range(group)]
+
+    def one(block, carry, diagonal):
+        start = pl.multiple_of(block * rows, rows)
+        keys = k_ref[pl.ds(start, rows)]
+        values = vt_ref[:, pl.ds(start, rows)]
+        later = []
+        for head in range(group):
+            best, accum = carry[head]
+            scores = mm(keys, queries[head])
+            if diagonal:
+                ahead = lax.broadcasted_iota(jnp.int32, scores.shape, 0) > (
+                    lax.broadcasted_iota(jnp.int32, scores.shape, 1)
+                )
+                scores = jnp.where(ahead, lowest_precision, scores)
+            new_best = jnp.maximum(best, jnp.max(scores, axis=0, keepdims=True))
+            probs = jnp.exp((scores - new_best) * scale).astype(jnp.bfloat16)
+            factor = jnp.exp((best - new_best) * scale)
+            later.append((new_best, accum * factor + mm(values, probs)))
+        return tuple(later)
+
+    carry = tuple(
+        (
+            jnp.full((1, rows), lowest_precision, jnp.float32),
+            jnp.zeros((HEAD_SIZE + ONES, rows), jnp.float32),
+        )
+        for _ in range(group)
+    )
+    carry = one(step, carry, True)
+    carry = lax.fori_loop(0, step, lambda block, now: one(block, now, False), carry)
+    loss = jnp.zeros((1, rows), jnp.float32)
+    for head in range(group):
+        accum = carry[head][1]
+        taught = accum[:HEAD_SIZE] * (1.0 / accum[HEAD_SIZE : HEAD_SIZE + 1])
+        at = step * rows + lax.broadcasted_iota(jnp.int32, taught.shape, 1)
+        base = head * HEAD_SIZE
+        difference = att_ref[base : base + HEAD_SIZE].astype(jnp.float32) - jnp.where(
+            at < length_ref[0], taught, 0.0
+        )
+        diff_ref[base : base + HEAD_SIZE] = difference
+        loss = loss + jnp.sum(difference * difference, axis=0, keepdims=True)
+    loss_ref[...] = jnp.broadcast_to(loss, loss_ref.shape)
+
+
+def backward_kernel(
+    length_ref, grad_ref, diff_ref, out_ref, denom_ref, q_ref, pq_ref,
+    k_ref, k_before, pk_ref, pk_before, v_ref, v_before,
+    kt_ref, kt_before, pkt_ref, pkt_before, vt_ref, vt_before,
+    states_ref, map_ref, back_ref, cos_ref, sin_ref,
+    pre_ref, gain_ref, key_carry, value_carry, map_carry, later,
+):
+    blocks = pl.num_programs(0)
+    step = blocks - 1 - pl.program_id(0)
+    group = q_ref.shape[0] // HEAD_SIZE
+    rows = q_ref.shape[1]
+    half = HEAD_SIZE // 2
+    scale = 1.0 / math.sqrt(HEAD_SIZE)
+
+    @pl.when(pl.program_id(0) == 0)
+    def _():
+        gain_ref[...] = jnp.zeros_like(gain_ref)
+        key_carry[...] = jnp.zeros_like(key_carry)
+        value_carry[...] = jnp.zeros_like(value_carry)
+        map_carry[...] = jnp.zeros_like(map_carry)
+        later[...] = jnp.zeros_like(later)
+
+    def through_map(head, vector, grad_maps):
+        base = head * HEAD_SIZE
+        plus, minus = soft_pair(mm(map_ref[base : base + HEAD_SIZE], vector))
+        grad_plus, grad_minus = grad_maps[:HEAD_SIZE], grad_maps[HEAD_SIZE:]
+        grad_logits = plus * (
+            grad_plus - jnp.sum(grad_plus * plus, axis=0, keepdims=True)
+        ) - minus * (grad_minus - jnp.sum(grad_minus * minus, axis=0, keepdims=True))
+        grad_logits = grad_logits.astype(jnp.bfloat16)
+        gain_ref[base : base + HEAD_SIZE] += mm_nt(vector, grad_logits)
+        return mm(back_ref[base : base + HEAD_SIZE], grad_logits)
+
+    for sub in reversed(range(rows // SUB)):
+        columns = slice(sub * SUB, (sub + 1) * SUB)
+        queries = side_by_side(q_ref, HEAD_SIZE, group, columns)
+        query_maps = side_by_side(pq_ref, 2 * HEAD_SIZE, group, columns)
+        if sub == 0:
+            keys = jnp.concatenate([k_before[...], k_ref[:SUB]], axis=0)
+            key_maps = jnp.concatenate([pk_before[...], pk_ref[:SUB]], axis=0)
+            values = jnp.concatenate([v_before[...], v_ref[:SUB]], axis=0)
+            keys_t = jnp.concatenate([kt_before[...], kt_ref[:, :SUB]], axis=1)
+            key_maps_t = jnp.concatenate([pkt_before[...], pkt_ref[:, :SUB]], axis=1)
+            values_before = vt_before[...]
+        else:
+            around = slice((sub - 1) * SUB, (sub + 1) * SUB)
+            keys, key_maps, values = k_ref[around], pk_ref[around], v_ref[around]
+            keys_t, key_maps_t = kt_ref[:, around], pkt_ref[:, around]
+            values_before = vt_ref[:, (sub - 1) * SUB : sub * SUB]
+        distance, key_at = band(group)
+        window = (distance >= 0) & (distance < WINDOW_KEYS)
+        linear = distance >= WINDOW_KEYS
+        if sub == 0:
+            inside = (key_at >= 0) | (step > 0)
+            window, linear = window & inside, linear & inside
+        incoming = side_by_side(grad_ref, HEAD_SIZE, group, columns).astype(jnp.float32)
+        difference = side_by_side(diff_ref, HEAD_SIZE, group, columns)
+        out = side_by_side(out_ref, HEAD_SIZE, group, columns)
+        denom = side_by_side(denom_ref, 1, group, columns)
+        at = (
+            step * rows
+            + sub * SUB
+            + lax.rem(lax.broadcasted_iota(jnp.int32, out.shape, 1), SUB)
+        )
+        incoming = (incoming + 2.0 * difference).astype(jnp.bfloat16).astype(jnp.float32)
+        incoming = jnp.where(at < length_ref[0], incoming, 0.0)
+        inverse = 1.0 / denom
+        grad_numer = (incoming * inverse).astype(jnp.bfloat16)
+        grad_denom = -jnp.sum(incoming * out, axis=0, keepdims=True) * inverse
+        rank = lax.broadcasted_iota(jnp.int32, (ONES, group * SUB), 0)
+        denom_high = grad_denom.astype(jnp.bfloat16).astype(jnp.float32)
+        extra = jnp.where(
+            rank == 0, denom_high, jnp.where(rank == 1, grad_denom - denom_high, 0.0)
+        ).astype(jnp.bfloat16)
+        grad_both = jnp.concatenate([grad_numer, extra], axis=0)
+        near = jnp.exp(mm(keys, queries) * scale)
+        far = mm(key_maps, query_maps)
+        weights = jnp.where(window, near, jnp.where(linear, far, 0.0)).astype(jnp.bfloat16)
+        grad_weights = mm(values, grad_numer) + grad_denom
+        grad_scores = jnp.where(window, grad_weights * near * scale, 0.0).astype(jnp.bfloat16)
+        grad_far = jnp.where(linear, grad_weights, 0.0).astype(jnp.bfloat16)
+        state_high, state_low = split_wide(jnp.transpose(states_ref[sub]))
+        grad_queries = mm(keys_t, grad_scores)
+        grad_query_maps = mm(key_maps_t, grad_far) + mm(
+            jnp.concatenate([state_high, state_low], axis=1),
+            jnp.concatenate([grad_both, grad_both], axis=0),
+        )
+        grad_keys = mm_nt(queries, grad_scores)
+        grad_values = mm_nt(grad_numer, weights)
+        grad_key_maps = mm_nt(query_maps, grad_far)
+        own_keys = key_carry[...] + grad_keys[:, SUB:]
+        own_values = value_carry[...] + grad_values[:, SUB:]
+        own_maps = map_carry[...] + grad_key_maps[:, SUB:]
+        later_now = later[...]
+        later_high, later_low = split_wide(jnp.transpose(later_now))
+        key_carry[...] = grad_keys[:, :SUB]
+        value_carry[...] = grad_values[:, :SUB] + mm(
+            later_now[:HEAD_SIZE].astype(jnp.bfloat16), key_maps_t[:, :SUB]
+        )
+        map_carry[...] = grad_key_maps[:, :SUB] + mm(
+            jnp.concatenate([later_high, later_low], axis=1),
+            jnp.concatenate([values_before, values_before], axis=0),
+        )
+        later[...] = later_now + mm_nt(grad_both, query_maps)
+        cosine, sine = cos_ref[:, columns], sin_ref[:, columns]
+        for head in range(group + 1):
+            base = head * HEAD_SIZE
+            lanes = slice(head * SUB, (head + 1) * SUB)
+            if head < group:
+                total = grad_queries[:, lanes] + through_map(
+                    head, queries[:, lanes], grad_query_maps[:, lanes]
+                )
+            else:
+                total = own_keys + through_map(head, keys_t[:, SUB:], own_maps)
+            low_half, high_half = halves_rotated(total[:half], total[half:], cosine, -sine)
+            pre_ref[base : base + HEAD_SIZE, columns] = jnp.concatenate(
+                [low_half, high_half], axis=0
+            ).astype(jnp.bfloat16)
+        base = (group + 1) * HEAD_SIZE
+        pre_ref[base : base + HEAD_SIZE, columns] = own_values.astype(jnp.bfloat16)
+
+
+def exchanged(value, bits):
+    count = lax.axis_size("seq")
+    return lax.ppermute(value, "seq", [(place, place ^ bits) for place in range(count)])
+
+
+def plane_gather(value):
+    me = lax.axis_index("seq")
+    middle = value.shape[0] // 2
+    along_x, along_y = exchanged(value, 2), exchanged(value, 4)
+    across = jnp.concatenate(
+        [exchanged(along_x[:middle], 4), exchanged(along_y[middle:], 2)], axis=0
+    )
+    found = {0: value, 2: along_x, 4: along_y, 6: across}
+    for bits in (0, 2, 4, 6):
+        found[bits + 1] = exchanged(found[bits], 1)
+    whole = jnp.zeros((lax.axis_size("seq"),) + value.shape, value.dtype)
+    for bits in range(8):
+        whole = lax.dynamic_update_slice_in_dim(whole, found[bits][None], me ^ bits, 0)
+    return whole
+
+
+def plane_scatter(parts):
+    me = lax.axis_index("seq")
+    core, chip = me % 2, me // 2
+    shape = parts.shape[1:]
+    by_core = parts.reshape((parts.shape[0] // 2, 2) + shape)
+    keep = lax.dynamic_index_in_dim(by_core, core, 1, False)
+    give = lax.dynamic_index_in_dim(by_core, 1 - core, 1, False)
+    both = (keep.astype(jnp.float32) + exchanged(give, 1).astype(jnp.float32)).astype(jnp.bfloat16)
+    pieces = [lax.dynamic_index_in_dim(both, chip ^ bits, 0, False) for bits in range(4)]
+    total = pieces[0].astype(jnp.float32)
+    for bits in (1, 2, 3):
+        total = total + exchanged(pieces[bits], 2 * bits).astype(jnp.float32)
+    return total
+
+
+def ring(value):
+    count = lax.axis_size("fsdp")
+    found = [value]
+    for _ in range(count - 1):
+        found.append(
+            lax.ppermute(found[-1], "fsdp", [(at, (at + 1) % count) for at in range(count)])
+        )
+    return found
+
+
+def in_order(found):
+    count = len(found)
+    me = lax.axis_index("fsdp")
+    whole = jnp.zeros((count,) + found[0].shape, found[0].dtype)
+    for step in range(count):
+        whole = lax.dynamic_update_slice_in_dim(
+            whole, found[step][None], lax.rem(me - step + count, count), 0
+        )
+    return whole
+
+
+def call(kernel, grid, in_specs, out_specs, out_shape, scratch, flops, moved, mib, scalars=1):
+    spec = pltpu.PrefetchScalarGridSpec(
+        num_scalar_prefetch=scalars,
+        grid=grid,
+        in_specs=in_specs,
+        out_specs=out_specs,
+        scratch_shapes=scratch,
+    )
+    return pl.pallas_call(
+        kernel,
+        grid_spec=spec,
+        out_shape=out_shape,
+        compiler_params=pltpu.CompilerParams(vmem_limit_bytes=mib * 2**20),
+        cost_estimate=pl.CostEstimate(flops=flops, bytes_accessed=moved, transcendentals=0),
+    )
+
+
+def by_heads(
+    tokens,
+    lengths,
+    norm_attn,
+    norm_ffn,
+    w_query,
+    key_projection,
+    value_projection,
+    w_output,
+    w_gate,
+    w_up,
+    w_down,
+    down_query,
+    up_query,
+    key_down_matrix,
+    key_up_matrix,
+    value_down_matrix,
+    value_up_matrix,
+    down_output,
+    up_output,
+    feature_query,
+    key_feature_weight,
+    cotangent,
+):
+    places = lax.axis_size("seq")
+    lanes = lax.axis_size("fsdp")
+    rows = tokens.shape[1]
+    model = tokens.shape[2]
+    count = rows * places
+    group = QUERY_HEADS // KEY_VALUE_HEADS
+    query_width = group * HEAD_SIZE
+    width = query_width + 2 * HEAD_SIZE
+    rank = down_query.shape[1]
+    place = lax.axis_index("seq")
+    lane = lax.axis_index("fsdp")
+    length = lax.dynamic_slice_in_dim(lengths, lane, 1)
+    bf16, f32 = jnp.bfloat16, jnp.float32
+    inputs_wide = tokens[0].astype(f32)
+    cot_wide = cotangent[0].astype(f32)
+    gain_attn = norm_attn.astype(f32)
+    gain_ffn = norm_ffn.astype(f32)
+
+    inverse_attn = lax.rsqrt(jnp.mean(inputs_wide * inputs_wide, axis=-1, keepdims=True) + epsilon)
+    normed = (inputs_wide * inverse_attn * gain_attn).astype(bf16)
+    normed_all = plane_gather(normed).reshape(count, model)
+
+    shard = w_query.shape[0]
+    by_place = jnp.concatenate(
+        [
+            w_query.reshape(shard, places, query_width),
+            key_projection.reshape(shard, places, HEAD_SIZE),
+            value_projection.reshape(shard, places, HEAD_SIZE),
+        ],
+        axis=2,
+    )
+    by_place = lax.all_to_all(jnp.moveaxis(by_place, 1, 0), "seq", 0, 0, tiled=True)
+    own_weights = jnp.moveaxis(in_order(ring(by_place)), 0, 1).reshape(model, width)
+    spare = 128
+    own_weights_t = jnp.concatenate(
+        [
+            own_weights.T,
+            down_query.T,
+            key_down_matrix.T,
+            value_down_matrix.T,
+            jnp.zeros((spare - 3 * rank, model), bf16),
+        ],
+        axis=0,
+    )
+    output_rows = in_order(ring(w_output))
+    output_weights = jnp.moveaxis(
+        plane_gather(output_rows.reshape(lanes * shard, model)).reshape(
+            places, lanes, shard, model
+        ),
+        0,
+        0,
+    ).reshape(model, model)
+
+    def own_rows(matrix, size):
+        return lax.dynamic_slice_in_dim(matrix, place * size, size, 0)
+
+    up_own = (
+        own_rows(up_query, query_width),
+        own_rows(key_up_matrix, HEAD_SIZE),
+        own_rows(value_up_matrix, HEAD_SIZE),
+    )
+    up_block = jnp.concatenate(
+        [
+            jnp.pad(part, ((0, 0), (at * rank, spare - (at + 1) * rank)))
+            for at, part in enumerate(up_own)
+        ],
+        axis=0,
+    )
+    maps_back = jnp.concatenate(
+        [own_rows(feature_query, query_width), own_rows(key_feature_weight, HEAD_SIZE)], axis=0
+    )
+    maps_ahead = jnp.swapaxes(
+        maps_back.reshape(group + 1, HEAD_SIZE, HEAD_SIZE), 1, 2
+    ).reshape((group + 1) * HEAD_SIZE, HEAD_SIZE)
+    half = HEAD_SIZE // 2
+    frequency = rope_base ** (-(jnp.arange(half, dtype=f32) * 2.0) / HEAD_SIZE)
+    phase = jnp.arange(count, dtype=jnp.int32).astype(f32)[None, :] * frequency[:, None]
+    cosine, sine = jnp.cos(phase), jnp.sin(phase)
+
+    def whole(shape):
+        return pl.BlockSpec(shape, lambda i, *_: (0,) * len(shape))
+
+    def across(height):
+        return pl.BlockSpec((height, rows), lambda i, *_: (0, i))
+
+    def down(wide):
+        return pl.BlockSpec((rows, wide), lambda i, *_: (i, 0))
+
+    def shape(*dims, dtype=bf16):
+        return jax.ShapeDtypeStruct(dims, dtype)
+
+    value_rows = HEAD_SIZE + ONES
+    maps_height = 2 * HEAD_SIZE
+    q_t, k_t, v_t, keys, values, pq_t, pk_t, key_maps, narrow_t = call(
+        project_kernel,
+        (places,),
+        [
+            down(model),
+            whole((width + spare, model)),
+            whole((width, spare)),
+            whole(((group + 1) * HEAD_SIZE, HEAD_SIZE)),
+            across(half),
+            across(half),
+        ],
+        [
+            across(query_width),
+            across(HEAD_SIZE),
+            across(value_rows),
+            down(HEAD_SIZE),
+            down(HEAD_SIZE),
+            across(group * maps_height),
+            across(maps_height),
+            down(maps_height),
+            across(spare),
+        ],
+        [
+            shape(query_width, count),
+            shape(HEAD_SIZE, count),
+            shape(value_rows, count),
+            shape(count, HEAD_SIZE),
+            shape(count, HEAD_SIZE),
+            shape(group * maps_height, count),
+            shape(maps_height, count),
+            shape(count, maps_height),
+            shape(spare, count),
+        ],
+        [],
+        2 * count * model * (width + spare),
+        2 * count * model * 2,
+        32,
+        scalars=0,
+    )(normed_all, own_weights_t, up_block, maps_ahead, cosine, sine)
+
+    per_step = rows // SUB
+
+    def before_down(wide):
+        return pl.BlockSpec((SUB, wide), lambda i, *_: (jnp.maximum(per_step * i - 1, 0), 0))
+
+    def before_across(height):
+        return pl.BlockSpec((height, SUB), lambda i, *_: (0, jnp.maximum(per_step * i - 1, 0)))
+
+    states_shape = (count // SUB, value_rows, maps_height)
+    att_t, out_t, denom, states = call(
+        forward_kernel,
+        (places,),
+        [
+            across(query_width),
+            across(group * maps_height),
+            down(HEAD_SIZE),
+            before_down(HEAD_SIZE),
+            down(maps_height),
+            before_down(maps_height),
+            across(value_rows),
+            before_across(value_rows),
+        ],
+        [
+            across(query_width),
+            across(query_width),
+            across(group),
+            pl.BlockSpec((per_step,) + states_shape[1:], lambda i, *_: (i, 0, 0)),
+        ],
+        [
+            shape(query_width, count),
+            shape(query_width, count, dtype=f32),
+            shape(group, count, dtype=f32),
+            shape(*states_shape, dtype=f32),
+        ],
+        [pltpu.VMEM(states_shape[1:], f32)],
+        8 * count * SUB * 2 * group * HEAD_SIZE,
+        count * 4096,
+        32,
+    )(length, q_t, pq_t, keys, keys, key_maps, key_maps, v_t, v_t)
+
+    sent = jnp.moveaxis(att_t.reshape(query_width, places, rows), 1, 0)
+    att_all = lax.all_to_all(sent, "seq", 0, 0, tiled=True).reshape(places * query_width, rows)
+
+    difference, loss_rows = call(
+        teacher_kernel,
+        (places,),
+        [
+            across(query_width),
+            whole((count, HEAD_SIZE)),
+            whole((value_rows, count)),
+            across(query_width),
+        ],
+        [across(query_width), across(8)],
+        [shape(query_width, count, dtype=f32), shape(8, count, dtype=f32)],
+        [],
+        4 * count * count * group * HEAD_SIZE,
+        count * 4096,
+        32,
+    )(length, q_t, keys, v_t, att_t)
+    losses = jnp.sum(loss_rows[0].reshape(places, rows), axis=1)
+
+    def dot_tn(a, b):
+        return lax.dot_general(a, b, (((0,), (0,)), ((), ())), preferred_element_type=f32)
+
+    branch = dot_tn(att_all, output_weights)
+    narrow_out = dot_tn(att_all, down_output).astype(bf16)
+    branch = branch + mm_nt(narrow_out, up_output)
+    residual = inputs_wide + branch
+    inverse_ffn = lax.rsqrt(jnp.mean(residual * residual, axis=-1, keepdims=True) + epsilon)
+    normed_ffn = (residual * inverse_ffn * gain_ffn).astype(bf16)
+    ffn_all = plane_gather(normed_ffn).reshape(count, model)
+    cot_all = plane_gather(cotangent[0]).reshape(count, model)
+
+    def hidden_share(matrix):
+        mine = lax.all_to_all(matrix, "seq", 1, 0, tiled=True)
+        return jnp.concatenate(ring(mine), axis=1)
+
+    gate_weights, up_weights, down_weights = (
+        hidden_share(w_gate),
+        hidden_share(w_up),
+        hidden_share(w_down),
+    )
+    gate_pre = mm(ffn_all, gate_weights)
+    up_pre = mm(ffn_all, up_weights)
+    sigmoid_gate = jax.nn.sigmoid(gate_pre)
+    silu_gate = gate_pre * sigmoid_gate
+    hidden = (silu_gate * up_pre).astype(bf16)
+    grad_hidden = mm(cot_all, down_weights)
+    grad_gate = (
+        grad_hidden * up_pre * sigmoid_gate * (1.0 + gate_pre * (1.0 - sigmoid_gate))
+    ).astype(bf16)
+    grad_up = (grad_hidden * silu_gate).astype(bf16)
+    grad_ffn = (mm_nt(grad_gate, gate_weights) + mm_nt(grad_up, up_weights)).astype(bf16)
+    grad_part = plane_scatter(grad_ffn.reshape(places, rows, model))
+    ffn_out = mm_nt(hidden, down_weights).astype(bf16)
+    output = (residual + plane_scatter(ffn_out.reshape(places, rows, model))).astype(bf16)
+
+    grad_residual = cot_wide + norm_back(residual, inverse_ffn, gain_ffn, grad_part)
+    grad_branch = grad_residual.astype(bf16)
+    grad_narrow_out = mm(grad_branch, up_output)
+    grad_up_output = dot_tn(narrow_out, grad_branch)
+    grad_down_output = dot_tn(grad_narrow_out, att_all.T)
+    grad_att = (
+        mm_nt(output_weights, grad_branch) + mm_nt(down_output, grad_narrow_out)
+    ).astype(bf16)
+    grad_att = lax.all_to_all(
+        grad_att.reshape(places, query_width, rows), "seq", 0, 0, tiled=True
+    )
+
+    def back(spec):
+        return pl.BlockSpec(
+            spec.block_shape, lambda i, *_: spec.index_map(places - 1 - i)
+        )
+
+    grad_pre_t, grad_maps = call(
+        backward_kernel,
+        (places,),
+        [
+            pl.BlockSpec((None, query_width, rows), lambda i, *_: (places - 1 - i, 0, 0)),
+            back(across(query_width)),
+            back(across(query_width)),
+            back(across(group)),
+            back(across(query_width)),
+            back(across(group * maps_height)),
+            back(down(HEAD_SIZE)),
+            back(before_down(HEAD_SIZE)),
+            back(down(maps_height)),
+            back(before_down(maps_height)),
+            back(down(HEAD_SIZE)),
+            back(before_down(HEAD_SIZE)),
+            back(across(HEAD_SIZE)),
+            back(before_across(HEAD_SIZE)),
+            back(across(maps_height)),
+            back(before_across(maps_height)),
+            back(across(value_rows)),
+            back(before_across(value_rows)),
+            pl.BlockSpec(
+                (per_step,) + states_shape[1:], lambda i, *_: (places - 1 - i, 0, 0)
+            ),
+            whole(((group + 1) * HEAD_SIZE, HEAD_SIZE)),
+            whole(((group + 1) * HEAD_SIZE, HEAD_SIZE)),
+            back(across(half)),
+            back(across(half)),
+        ],
+        [back(across(width)), whole(((group + 1) * HEAD_SIZE, HEAD_SIZE))],
+        [shape(width, count), shape((group + 1) * HEAD_SIZE, HEAD_SIZE, dtype=f32)],
+        [
+            pltpu.VMEM((HEAD_SIZE, SUB), f32),
+            pltpu.VMEM((HEAD_SIZE, SUB), f32),
+            pltpu.VMEM((maps_height, SUB), f32),
+            pltpu.VMEM((value_rows, maps_height), f32),
+        ],
+        20 * count * SUB * 2 * group * HEAD_SIZE,
+        count * 8192,
+        32,
+    )(
+        length, grad_att, difference, out_t, denom, q_t, pq_t,
+        keys, keys, key_maps, key_maps, values, values,
+        k_t, k_t, pk_t, pk_t, v_t, v_t,
+        states, maps_ahead, maps_back, cosine, sine,
+    )
+
+    grad_narrow_t = dot_tn(up_block, grad_pre_t).astype(bf16)
+    grad_up_block = mm_nt(grad_pre_t, narrow_t)
+    grad_down_t = mm(grad_narrow_t[: 3 * rank], normed_all)
+    grad_normed = dot_tn(
+        jnp.concatenate([grad_pre_t, grad_narrow_t], axis=0), own_weights_t
+    ).astype(bf16)
+    grad_normed = plane_scatter(grad_normed.reshape(places, rows, model))
+    grad_tokens = (
+        grad_residual + norm_back(inputs_wide, inverse_attn, gain_attn, grad_normed)
+    ).astype(bf16)
+
+    devices = places * lanes
+    ahead = jnp.arange(devices)[None, :] >= (jnp.arange(places) * lanes + lane)[:, None]
+    running = jnp.sum(jnp.where(ahead, losses[:, None], 0.0), axis=0)
+    loss_row = jnp.pad(running[:, None], ((0, 0), (0, model // devices - 1))).reshape(1, model)
+    shared = jnp.concatenate([grad_down_t, grad_down_output, grad_up_output, loss_row], axis=0)
+    shared = jnp.moveaxis(shared.reshape(-1, devices, model // devices), 1, 0)
+    shared = jnp.sum(
+        lax.all_to_all(shared, ("seq", "fsdp"), 0, 0, tiled=True).reshape(shared.shape), axis=0
+    )
+
+    def columns(at):
+        return shared[at * rank : (at + 1) * rank].T
+
+    transfer_loss = shared[5 * rank, :1] / jnp.sum(lengths).astype(f32)
+
+    pieces = [
+        grad_maps[:query_width].reshape(lanes, -1),
+        grad_maps[query_width:].reshape(lanes, -1),
+        grad_up_block[:query_width, :rank].reshape(lanes, -1),
+        grad_up_block[query_width : query_width + HEAD_SIZE, rank : 2 * rank].reshape(lanes, -1),
+        grad_up_block[query_width + HEAD_SIZE :, 2 * rank : 3 * rank].reshape(lanes, -1),
+    ]
+    packed = jnp.concatenate(pieces, axis=1)
+    packed = jnp.sum(lax.all_to_all(packed, "fsdp", 0, 0, tiled=True).reshape(packed.shape), axis=0)
+    ends = [0]
+    for piece in pieces:
+        ends.append(ends[-1] + piece.shape[1])
+    map_query, map_key, up_q, up_k, up_v = (
+        packed[ends[at] : ends[at + 1]].reshape(-1, wide)
+        for at, wide in enumerate((HEAD_SIZE, HEAD_SIZE, rank, rank, rank))
+    )
+    return (
+        output[None],
+        grad_tokens[None],
+        columns(0),
+        up_q,
+        columns(1),
+        up_k,
+        columns(2),
+        up_v,
+        columns(3),
+        columns(4),
+        map_query,
+        map_key,
+        transfer_loss,
+    )
+
 
 def solution(mesh):
     placed = (
@@ -654,8 +1416,12 @@
         P(),
         P("fsdp", "seq", None),
     )
+    sizes = dict(mesh.shape)
+    heads_match = sizes["seq"] == KEY_VALUE_HEADS == 8 and (
+        QUERY_HEADS // KEY_VALUE_HEADS == sizes["fsdp"]
+    )
     return jax.shard_map(
-        local,
+        by_heads if heads_match else local,
         mesh=mesh,
         in_specs=placed,
         out_specs=(

time: 2730 us -> 845 us (0.31)
  waiting for transfers between devices: 1910 us -> 288 us
  matrix products: 479 us -> 131 us
  Pallas kernels: 0 us -> 97.6 us
  starting transfers between devices: 4.69 us -> 92.1 us
  other arithmetic: 135 us -> 48.9 us
  blocking collectives: 64 us -> 0 us
  local copies, waits for them, and re-layouts: 108 us -> 171 us
    unnamed x32 -> x0, waiting for transfers between devices: 965 us -> none
    all_gather x14 -> x0, waiting for transfers between devices: 676 us -> none  [the longest x1 142 us: local(): lax.all_gather(ffn_weights[2], 'seq', axis=0, tiled=True)]
    dot_general x174 -> x18, matrix products: 458 us -> 131 us  [the longest x7 69 us: mm_nt(): lax.dot_general(a, b, (((1,), (1,)), ((), ())), preferred_element_type=jn...]
    reduce_scatter x2 -> x0, waiting for transfers between devices: 266 us -> none  [the longest x1 133 us: local(): lax.psum_scatter(grad_feature_query.reshape(QUERY_HEADS * HEAD_SIZE, HEAD...]
    ppermute x2 -> x59, waiting for transfers between devices: 0.01 us -> 238 us  [the longest x44 123 us: exchanged(): lax.ppermute(value, 'seq', [(place, place ^ bits) for place in range(coun...]
    pallas_call x0 -> x4, Pallas kernels: none -> 97.6 us  [the longest x1 44.4 us: by_heads(): call(teacher_kernel, (places,), [across(query_width), whole((count, HEAD_...]
    ppermute x2 -> x59, starting transfers between devices: 2.57 us -> 56.9 us  [the longest x44 39.1 us: exchanged(): lax.ppermute(value, 'seq', [(place, place ^ bits) for place in range(coun...]
    all_to_all x0 -> x8, waiting for transfers between devices: none -> 50.2 us  [the longest x1 27.1 us: by_heads(): lax.all_to_all(shared, ('seq', 'fsdp'), 0, 0, tiled=True)]
  transfers between devices with their start and end apart: 26 -> 67, of which waited for: 19 -> 24; matrix products, arithmetic and copies ran while one was open for 17% -> 27% of each run, Pallas kernels for 0% -> 8%
where the time goes in v1:
time: 845 us; the launch traced here: 833 us
  waiting for transfers between devices  288 us (34%)
  local copies, waits for them, and re-layouts  171 us (20%)
  matrix products  131 us (16%)
  Pallas kernels  97.6 us (12%)
  starting transfers between devices  92.1 us (11%)
  other arithmetic  48.9 us (6%)
    ppermute x44, waiting for transfers between devices, exchanged(): lax.ppermute(value, 'seq', [(place, place ^ bits) for place in range(coun...  123 us
    ppermute x15, waiting for transfers between devices, ring(): lax.ppermute(found[-1], 'fsdp', [(at, (at + 1) % count) for at in range(c...  114 us
    dot_general x7, matrix products, mm_nt(): lax.dot_general(a, b, (((1,), (1,)), ((), ())), preferred_element_type=jn...  69 us
    dot_general x5, matrix products, mm(): return jnp.dot(a, b, preferred_element_type=jnp.float32)  48.1 us
    unnamed x214, local copies, waits for them, and re-layouts  45 us
    pallas_call x1, Pallas kernels, by_heads(): call(teacher_kernel, (places,), [across(query_width), whole((count, HEAD_...  44.4 us
    ppermute x44, starting transfers between devices, exchanged(): lax.ppermute(value, 'seq', [(place, place ^ bits) for place in range(coun...  39.1 us
    dynamic_update_slice x30, local copies, waits for them, and re-layouts, plane_gather(): lax.dynamic_update_slice_in_dim(whole, found[bits][None], me ^ bits, 0)  39 us
  transfers between devices with their start and end apart: 67, of which 24 were waited for; matrix products, arithmetic and copies ran while one was open for 27% of the time, Pallas kernels for 8%

profile of v1, /device:TPU:0, one launch (start us, length us, event | category | flops | bytes accessed | tf_op | source)
XLA Modules:
  0.0 833.3 jit_solution(9104784798154563021)
XLA Ops:
  2.9 2.5 fusion.13
  5.9 2.5 collective-permute-start.1
  15.4 3.5 all-to-all-start
  25.2 12.9 %all-to-all-done = bf16[8,64,384]{2,1,0:T(8,128)(2,1)S(1)} async-done(((bf16[8,64,384]{2,1,0:T(8,128)(2,1)}), bf16[8,64,384]{2,1,0:T(8,128)(2,1)S(1)}, u32[]{:S(2)}, u32[]{:S(2)}) %all-to-all-start) | async-done | bytes 393248 | tf_op jit(solution)/shard_map/all_to_all | solution.py:1071
  38.1 4.4 all-to-all-start.3
  43.5 4.4 broadcast.94.clone
  54.6 4.5 broadcast.94.clone.2
  61.7 4.2 all-to-all-start.2
  72.4 9.0 %all-to-all-done.2 = bf16[256,8,256]{0,2,1:T(8,128)(2,1)} async-done(((bf16[256,8,256]{0,2,1:T(8,128)(2,1)}), bf16[256,8,256]{0,2,1:T(8,128)(2,1)}, u32[]{:S(2)}, u32[]{:S(2)}) %all-to-all-start.2) | async-done | bytes 1048608 | tf_op jit(solution)/shard_map/all_to_all | solution.py:1247
  81.4 4.2 all-to-all-start.4
  90.5 4.3 broadcast.94.clone.1
  104.4 2.4 bitcast_dynamic-update-slice_fusion.30
  110.7 2.3 bitcast_dynamic-update-slice_fusion.29
  113.0 9.6 %collective-permute-done.44 = bf16[256,2048]{1,0:T(8,128)(2,1)} collective-permute-done((bf16[256,2048]{1,0:T(8,128)(2,1)}, bf16[256,2048]{1,0:T(8,128)(2,1)}, u32[]{:S(2)}, u32[]{:S(2)}) %collective-permute-start.44) | collective-permute-done | bytes 1048608 | tf_op jit(solution)/shard_map/ppermute | solution.py:944
  138.6 2.6 copy.152
  143.0 2.9 collective-permute-done.5
  148.5 6.8 collective-permute-done.48
  162.7 7.1 collective-permute-done.49
  174.7 2.3 bitcast_dynamic-update-slice_fusion.21
  180.5 2.3 bitcast_dynamic-update-slice_fusion.27
  191.1 2.4 bitcast_dynamic-update-slice_fusion.2
  193.5 5.8 collective-permute-done.19
  204.1 12.4 %shard_map.309 = (bf16[256,2048]{1,0:T(8,128)(2,1)S(1)}, bf16[64,2048]{1,0:T(8,128)(2,1)S(1)}, bf16[80,2048]{1,0:T(8,128)(2,1)S(1)}, bf16[2048,64]{1,0:T(8,128)(...) custom-call(bf16[2048,2048]{1,0:T(8,128)(2,1)} %bitcast.8.x_ref, ...), custom_call_target="tpu_custom_call" | custom-call | flops 4294967296 | bytes 16777216 | tf_op jit(solution)/shard_map/pallas_call | solution.py:1133
  216.6 8.1 shard_map.310
  229.7 3.7 all-to-all-start.1
  237.3 2.3 bitcast_dynamic-update-slice_fusion.1
  246.3 15.7 %collective-permute-done.34 = bf16[2048,256]{1,0:T(8,128)(2,1)} collective-permute-done((bf16[2048,256]{1,0:T(8,128)(2,1)}, bf16[2048,256]{1,0:T(8,128)(2,1)}, u32[]{:S(2)}, u32[]{:S(2)}) %collective-permute-start.34) | collective-permute-done | bytes 1048608 | tf_op jit(solution)/shard_map/ppermute | solution.py:983
  262.0 22.5 %collective-permute-done.31 = bf16[2048,256]{1,0:T(8,128)(2,1)} collective-permute-done((bf16[2048,256]{1,0:T(8,128)(2,1)}, bf16[2048,256]{1,0:T(8,128)(2,1)}, u32[]{:S(2)}, u32[]{:S(2)}) %collective-permute-start.31) | collective-permute-done | bytes 1048608 | tf_op jit(solution)/shard_map/ppermute | solution.py:983
  284.5 22.5 %collective-permute-done.37 = bf16[2048,256]{1,0:T(8,128)(2,1)} collective-permute-done((bf16[2048,256]{1,0:T(8,128)(2,1)}, bf16[2048,256]{1,0:T(8,128)(2,1)}, u32[]{:S(2)}, u32[]{:S(2)}) %collective-permute-start.37) | collective-permute-done | bytes 1048608 | tf_op jit(solution)/shard_map/ppermute | solution.py:983
  309.3 6.0 multiply_reduce_fusion.1
  319.8 53.7 %collective-permute-done.38 = bf16[2048,256]{1,0:T(8,128)(2,1)} collective-permute-done((bf16[2048,256]{1,0:T(8,128)(2,1)}, bf16[2048,256]{1,0:T(8,128)(2,1)}, u32[]{:S(2)}, u32[]{:S(2)}) %collective-permute-start.38) | collective-permute-done | bytes 1048608 | tf_op jit(solution)/shard_map/ppermute | solution.py:983
  373.6 14.3 %fusion.41 = f32[2048,1024]{1,0:T(8,128)} fusion(bf16[2048,2048]{1,0:T(8,128)(2,1)} %bitcast.77, bf16[2048,256]{1,0:T(8,128)(2,1)} %collective-permute-done.38, bf16[2048,256]{1,0:T(8,128)(2,1)} %collective-permute-done.37, bf16[2048,256]{1,0:T(8,128)(2,1)} %collective-permute-done.36, bf16[2048,256]{1,0:T(8,128)(2,1)} %bitcast.60), kind=kOutput, calls=%fused_computation.110 | convolution fusion | flops 8606711808 | bytes 20971520 | tf_op jit(solution)/shard_map/dot_general | solution.py:651
  391.8 10.7 %collective-permute-done.27 = bf16[128,2048]{1,0:T(8,128)(2,1)S(1)} collective-permute-done((bf16[128,2048]{1,0:T(8,128)(2,1)S(1)}, bf16[128,2048]{1,0:T(8,128)(2,1)S(1)}, u32[]{:S(2)}, u32[]{:S(2)}) %collective-permute-start.27) | collective-permute-done | bytes 524320 | tf_op jit(solution)/shard_map/ppermute | solution.py:944
  407.0 13.4 %fusion.42 = f32[2048,1024]{1,0:T(8,128)} fusion(bf16[2048,2048]{1,0:T(8,128)(2,1)S(1)} %bitcast.285, bf16[2048,256]{1,0:T(8,128)(2,1)} %collective-permute-done.35, bf16[2048,256]{1,0:T(8,128)(2,1)} %collective-permute-done.34, bf16[2048,256]{1,0:T(8,128)(2,1)} %collective-permute-done.33, bf16[2048,256]{1,0:T(8,128)(2,1)S(1)} %bitcast.303), kind=kOutput, calls=%fused_computation.111 | convolution fusion | flops 8606711808 | bytes 20971520 | tf_op jit(solution)/shard_map/dot_general | solution.py:651
  420.4 13.1 %fusion.43 = f32[2048,1024]{1,0:T(8,128)} fusion(bf16[2048,2048]{1,0:T(8,128)(2,1)S(1)} %bitcast.286, bf16[2048,256]{1,0:T(8,128)(2,1)} %collective-permute-done.32, bf16[2048,256]{1,0:T(8,128)(2,1)} %collective-permute-done.31, bf16[2048,256]{1,0:T(8,128)(2,1)} %collective-permute-done.30, bf16[2048,256]{1,0:T(8,128)(2,1)S(1)} %bitcast.300), kind=kOutput, calls=%fused_computation.112 | convolution fusion | flops 8606711808 | bytes 20971520 | tf_op jit(solution)/shard_map/dot_general | solution.py:651
  433.5 19.9 %fusion.4 = f32[2048,2048]{1,0:T(8,128)} fusion(f32[2048,1024]{1,0:T(8,128)} %fusion.41, f32[2048,1024]{1,0:T(8,128)} %fusion.43, bf16[2048,256]{1,0:T(8,128)(2,1)} %collective-permute-done.35, bf16[2048,256]{1,0:T(8,128)(2,1)} %collective-permute-done.34, bf16[2048,256]{1,0:T(8,128)(2,1)} %collective-permute-done.33, bf16[2048,256]{1,0:T(8,128)(2,1)S(1)} %bitcast.304), kind=kOutput, calls=%fused_computation.14 | convolution fusion | flops 8619294720 | bytes 37748736 | tf_op jit(solution)/shard_map/dot_general | solution.py:655
  453.4 22.2 %add_convert_fusion = bf16[2048,2048]{1,0:T(8,128)(2,1)} fusion(f32[2048,2048]{1,0:T(8,128)} %fusion.4, f32[2048,1024]{1,0:T(8,128)} %fusion.43, f32[2048,1024]{1,0:T(8,128)} %fusion.41, f32[2048,1024]{1,0:T(8,128)} %fusion.42, bf16[2048,256]{1,0:T(8,128)(2,1)} %collective-permute-done.32, bf16[2048,256]{1,0:T(8,128)(2,1)} %collective-permute-done.31, ...), kind=kOutput, calls=%fused_computation | convolution fusion | flops 8636071936 | bytes 54525952 | tf_op jit(solution)/shard_map/dot_general | solution.py:655
  475.6 4.7 dynamic-slice_bitcast_fusion.1
  480.5 18.4 %convolution_convert_fusion.1 = bf16[2048,2048]{1,0:T(8,128)(2,1)} fusion(f32[2048,1024]{1,0:T(8,128)} %fusion.42, f32[2048,1024]{1,0:T(8,128)} %fusion.43, bf16[2048,256]{1,0:T(8,128)(2,1)} %collective-permute-done.38, bf16[2048,256]{1,0:T(8,128)(2,1)} %collective-permute-done.37, bf16[2048,256]{1,0:T(8,128)(2,1)} %collective-permute-done.36, ...), kind=kOutput, calls=%fused_computation.13 | convolution fusion | flops 8623489024 | bytes 29360128 | tf_op jit(solution)/shard_map/dot_general | solution.py:655
  498.9 4.7 dynamic-slice_bitcast_fusion.2
  504.0 5.4 fusion.1
  516.6 5.6 fusion.2
  528.8 10.3 %collective-permute-done.52 = bf16[256,2048]{1,0:T(8,128)(2,1)S(1)} collective-permute-done((bf16[256,2048]{1,0:T(8,128)(2,1)S(1)}, bf16[256,2048]{1,0:T(8,128)(2,1)S(1)}, u32[]{:S(2)}, u32[]{:S(2)}) %collective-permute-start.52) | collective-permute-done | bytes 1048608 | tf_op jit(solution)/shard_map/ppermute | solution.py:944
  539.1 2.5 collective-permute-start.42
  541.6 21.9 %collective-permute-done.53 = bf16[256,2048]{1,0:T(8,128)(2,1)} collective-permute-done((bf16[256,2048]{1,0:T(8,128)(2,1)}, bf16[256,2048]{1,0:T(8,128)(2,1)}, u32[]{:S(2)}, u32[]{:S(2)}) %collective-permute-start.53) | collective-permute-done | bytes 1048608 | tf_op jit(solution)/shard_map/ppermute | solution.py:944
  563.5 2.6 multiply_reduce_fusion
  566.2 18.1 %collective-permute-done.40 = bf16[256,2048]{1,0:T(8,128)(2,1)} collective-permute-done((bf16[256,2048]{1,0:T(8,128)(2,1)}, bf16[256,2048]{1,0:T(8,128)(2,1)}, u32[]{:S(2)}, u32[]{:S(2)}) %collective-permute-start.40) | collective-permute-done | bytes 1048608 | tf_op jit(solution)/shard_map/ppermute | solution.py:944
  584.2 23.1 %collective-permute-done.41 = bf16[256,2048]{1,0:T(8,128)(2,1)} collective-permute-done((bf16[256,2048]{1,0:T(8,128)(2,1)}, bf16[256,2048]{1,0:T(8,128)(2,1)}, u32[]{:S(2)}, u32[]{:S(2)}) %collective-permute-start.41) | collective-permute-done | bytes 1048608 | tf_op jit(solution)/shard_map/ppermute | solution.py:944
  607.3 7.7 subtract_add_fusion
  615.9 6.9 fusion.10
  622.9 4.5 all-to-all-start.5
  629.8 44.4 %shard_map.311 = (f32[256,2048]{1,0:T(8,128)S(1)}, f32[8,2048]{1,0:T(8,128)S(1)}) custom-call(s32[1]{0:T(128)} %dynamic_slice.74.length_ref, bf16[256,2048]{1,0:T(8,128)(2,1)S(1)} %copy-done.13, bf16[2048,64]{1,0:T(8,128)(2,1)S(1)} %copy-done.3, bf16[80,2048]{1,0:T(8,128)(2,1)S(1)} %copy-done.11, bf16[256,2048]{1,0:T(8,128)(2,1)S(1)} %copy-done.32), custom_call_target="tpu_custom_call" | custom-call | flops 4294967296 | bytes 8388608 | tf_op jit(solution)/shard_map/pallas_call | solution.py:1216
  688.2 32.7 %shard_map.312 = (bf16[384,2048]{1,0:T(8,128)(2,1)S(1)}, f32[320,64]{1,0:T(8,128)S(1)}) custom-call(s32[1]{0:T(128)} %dynamic_slice.74.length_ref, bf16[8,256,256]{2,1,0:T(8,128)(2,1)} %all-to-all-done.5.grad_ref, f32[256,2048]{1,0:T(8,128)S(1)} %copy-done.22, f32[256,2048]{1,0:T(8,128)S(1)} %copy-done.20, f32[4,2048]{1,0:T(4,128)S(1)} %copy-done.44, ...), custom_call_target="tpu_custom_call" | custom-call | flops 2684354560 | bytes 16777216 | tf_op jit(solution)/shard_map/pallas_call | solution.py:1287
  721.6 4.9 convolution_convert_fusion
  726.5 2.9 dynamic-slice_bitcast_fusion
  730.9 12.5 %copy.171 = bf16[2048,2048]{1,0:T(8,128)(2,1)} copy(bf16[2048,2048]{0,1:T(8,128)(2,1)} %bitcast.97) | data formatting | bytes 16777216 | tf_op jit(solution)/shard_map/dot_general | solution.py:651
  750.7 4.2 all-to-all-start.7
  754.9 5.4 fusion
  765.5 6.9 fusion.50
  775.8 6.6 all-to-all-start.6
  788.3 27.1 %all-to-all-done.6 = f32[32,1,2624]{2,1,0:T(1,128)} async-done(((f32[32,1,2624]{2,1,0:T(1,128)}), f32[32,1,2624]{2,1,0:T(1,128)}, u32[]{:S(2)}, u32[]{:S(2)}) %all-to-all-start.6) | async-done | bytes 335904 | tf_op jit(solution)/shard_map/all_to_all | solution.py:1353
  815.9 3.2 reduce.5
  824.2 3.0 fusion.20
  827.2 4.5 fusion.40
  (448 shorter events, 190.2 us)
Async XLA Ops:
  5.4 98.4 %collective-permute-start = (bf16[256,2048]{1,0:T(8,128)(2,1)}, bf16[256,2048]{1,0:T(8,128)(2,1)}, u32[]{:S(2)}, u32[]{:S(2)}) collective-permute-start(bf16[256,2048]{1,0:T(8,128)(2,1)} %fusion.13), channel_id=1, source_target_pairs={{0,4},{4,0},{8,12},{12,8},{16,20},{20,16},{24,28},{28,24},{1,5},{5... | collective-permute-start | bytes 3145736 | tf_op jit(solution)/shard_map/ppermute | solution.py:944
  5.9 104.7 %collective-permute-start.1 = (bf16[256,2048]{1,0:T(8,128)(2,1)}, bf16[256,2048]{1,0:T(8,128)(2,1)}, u32[]{:S(2)}, u32[]{:S(2)}) collective-permute-start(bf16[256,2048]{1,0:T(8,128)(2,1)} %fusion.13), channel_id=1, source_target_pairs={{0,8},{4,12},{8,0},{12,4},{16,24},{20,28},{24,16},{28,20},{1,9},{5... | collective-permute-start | bytes 3145736 | tf_op jit(solution)/shard_map/ppermute | solution.py:944
  8.4 122.3 %collective-permute-start.3 = (bf16[256,2048]{1,0:T(8,128)(2,1)}, bf16[256,2048]{1,0:T(8,128)(2,1)}, u32[]{:S(2)}, u32[]{:S(2)}) collective-permute-start(bf16[256,2048]{1,0:T(8,128)(2,1)} %fusion.13), channel_id=1, source_target_pairs={{0,16},{4,20},{8,24},{12,28},{16,0},{20,4},{24,8},{28,12},{1,17},{... | collective-permute-start | bytes 3145736 | tf_op jit(solution)/shard_map/ppermute | solution.py:944
  9.9 50.2 %collective-permute-start.11 = (bf16[64,2048]{1,0:T(8,128)(2,1)}, bf16[64,2048]{1,0:T(8,128)(2,1)}, u32[]{:S(2)}, u32[]{:S(2)}) collective-permute-start(bf16[64,2048]{1,0:T(8,128)(2,1)} %param.29), channel_id=1, source_target_pairs={{0,1},{1,2},{2,3},{3,0},{4,5},{5,6},{6,7},{7,4},{8,9},{9,10},{10,1... | collective-permute-start | bytes 786440 | tf_op jit(solution)/shard_map/ppermute | solution.py:983
  15.4 22.7 %all-to-all-start = ((bf16[8,64,384]{2,1,0:T(8,128)(2,1)}), bf16[8,64,384]{2,1,0:T(8,128)(2,1)S(1)}, u32[]{:S(2)}, u32[]{:S(2)}) async-start(bf16[8,64,384]{2,1,0:T(8,128)(2,1)} %copy.148), calls=%async_computation | async-start | bytes 786432 | tf_op jit(solution)/shard_map/all_to_all | solution.py:1071
  38.1 23.6 %all-to-all-start.3 = ((bf16[256,8,256]{0,2,1:T(8,128)(2,1)}), bf16[256,8,256]{0,2,1:T(8,128)(2,1)}, u32[]{:S(2)}, u32[]{:S(2)}) async-start(bf16[256,8,256]{0,2,1:T(8,128)(2,1)} %bitcast.291), calls=%async_computation.3 | async-start | bytes 2097152 | tf_op jit(solution)/shard_map/all_to_all | solution.py:1247
  60.1 10.7 %collective-permute-start.12 = (bf16[64,2048]{1,0:T(8,128)(2,1)}, bf16[64,2048]{1,0:T(8,128)(2,1)S(1)}, u32[]{:S(2)}, u32[]{:S(2)}) collective-permute-start(bf16[64,2048]{1,0:T(8,128)(2,1)} %collective-permute-done.11), channel_id=1, source_target_pairs={{0,1},{1,2},{2,3},{3,0},{4,5},{5,6},{6,7},{7,4},{8,9},{9,10},{10,1... | collective-permute-start | bytes 786440 | tf_op jit(solution)/shard_map/ppermute | solution.py:983
  61.7 19.7 %all-to-all-start.2 = ((bf16[256,8,256]{0,2,1:T(8,128)(2,1)}), bf16[256,8,256]{0,2,1:T(8,128)(2,1)}, u32[]{:S(2)}, u32[]{:S(2)}) async-start(bf16[256,8,256]{0,2,1:T(8,128)(2,1)} %bitcast.293), calls=%async_computation.2 | async-start | bytes 2097152 | tf_op jit(solution)/shard_map/all_to_all | solution.py:1247
  67.0 18.7 %collective-permute-start.8 = (bf16[8,64,384]{2,1,0:T(8,128)(2,1)S(1)}, bf16[8,64,384]{2,1,0:T(8,128)(2,1)}, u32[]{:S(2)}, u32[]{:S(2)}) collective-permute-start(bf16[8,64,384]{2,1,0:T(8,128)(2,1)S(1)} %all-to-all-done), channel_id=1, source_target_pairs={{0,1},{1,2},{2,3},{3,0},{4,5},{5,6},{6,7},{7,4},{8,9},{9,10},{10,1... | collective-permute-start | bytes 1179656 | tf_op jit(solution)/shard_map/ppermute | solution.py:983
  70.8 17.0 %collective-permute-start.13 = (bf16[64,2048]{1,0:T(8,128)(2,1)S(1)}, bf16[64,2048]{1,0:T(8,128)(2,1)}, u32[]{:S(2)}, u32[]{:S(2)}) collective-permute-start(bf16[64,2048]{1,0:T(8,128)(2,1)S(1)} %collective-permute-done.12), channel_id=1, source_target_pairs={{0,1},{1,2},{2,3},{3,0},{4,5},{5,6},{6,7},{7,4},{8,9},{9,10},{10,1... | collective-permute-start | bytes 786440 | tf_op jit(solution)/shard_map/ppermute | solution.py:983
  81.4 20.1 %all-to-all-start.4 = ((bf16[256,8,256]{0,2,1:T(8,128)(2,1)}), bf16[256,8,256]{0,2,1:T(8,128)(2,1)}, u32[]{:S(2)}, u32[]{:S(2)}) async-start(bf16[256,8,256]{0,2,1:T(8,128)(2,1)} %bitcast.292), calls=%async_computation.4 | async-start | bytes 2097152 | tf_op jit(solution)/shard_map/all_to_all | solution.py:1247
  85.7 21.1 %collective-permute-start.43 = (bf16[256,2048]{1,0:T(8,128)(2,1)}, bf16[256,2048]{1,0:T(8,128)(2,1)}, u32[]{:S(2)}, u32[]{:S(2)}) collective-permute-start(bf16[256,2048]{1,0:T(8,128)(2,1)} %bitcast.295), channel_id=1, source_target_pairs={{0,4},{4,0},{8,12},{12,8},{16,20},{20,16},{24,28},{28,24},{1,5},{5... | collective-permute-start | bytes 3145736 | tf_op jit(solution)/shard_map/ppermute | solution.py:944
  87.8 34.8 %collective-permute-start.44 = (bf16[256,2048]{1,0:T(8,128)(2,1)}, bf16[256,2048]{1,0:T(8,128)(2,1)}, u32[]{:S(2)}, u32[]{:S(2)}) collective-permute-start(bf16[256,2048]{1,0:T(8,128)(2,1)} %bitcast.296), channel_id=1, source_target_pairs={{0,8},{4,12},{8,0},{12,4},{16,24},{20,28},{24,16},{28,20},{1,9},{5... | collective-permute-start | bytes 3145736 | tf_op jit(solution)/shard_map/ppermute | solution.py:944
  103.8 30.5 %collective-permute-start.46 = (bf16[256,2048]{1,0:T(8,128)(2,1)}, bf16[256,2048]{1,0:T(8,128)(2,1)S(1)}, u32[]{:S(2)}, u32[]{:S(2)}) collective-permute-start(bf16[256,2048]{1,0:T(8,128)(2,1)} %bitcast.297), channel_id=1, source_target_pairs={{0,16},{4,20},{8,24},{12,28},{16,0},{20,4},{24,8},{28,12},{1,17},{... | collective-permute-start | bytes 3145736 | tf_op jit(solution)/shard_map/ppermute | solution.py:944
  106.7 16.3 %collective-permute-start.9 = (bf16[8,64,384]{2,1,0:T(8,128)(2,1)}, bf16[8,64,384]{2,1,0:T(8,128)(2,1)S(1)}, u32[]{:S(2)}, u32[]{:S(2)}) collective-permute-start(bf16[8,64,384]{2,1,0:T(8,128)(2,1)} %collective-permute-done.8), channel_id=1, source_target_pairs={{0,1},{1,2},{2,3},{3,0},{4,5},{5,6},{6,7},{7,4},{8,9},{9,10},{10,1... | collective-permute-start | bytes 1179656 | tf_op jit(solution)/shard_map/ppermute | solution.py:983
  110.6 60.0 %collective-permute-start.14 = (bf16[256,2048]{1,0:T(8,128)(2,1)S(1)}, bf16[256,2048]{1,0:T(8,128)(2,1)}, u32[]{:S(2)}, u32[]{:S(2)}) collective-permute-start(bf16[256,2048]{1,0:T(8,128)(2,1)S(1)} %bitcast.288), channel_id=1, source_target_pairs={{0,4},{4,0},{8,12},{12,8},{16,20},{20,16},{24,28},{28,24},{1,5},{5... | collective-permute-start | bytes 3145736 | tf_op jit(solution)/shard_map/ppermute | solution.py:944
  122.6 51.9 %collective-permute-start.15 = (bf16[256,2048]{1,0:T(8,128)(2,1)S(1)}, bf16[256,2048]{1,0:T(8,128)(2,1)}, u32[]{:S(2)}, u32[]{:S(2)}) collective-permute-start(bf16[256,2048]{1,0:T(8,128)(2,1)S(1)} %bitcast.289), channel_id=1, source_target_pairs={{0,8},{4,12},{8,0},{12,4},{16,24},{20,28},{24,16},{28,20},{1,9},{5... | collective-permute-start | bytes 3145736 | tf_op jit(solution)/shard_map/ppermute | solution.py:944
  123.0 14.3 %collective-permute-start.10 = (bf16[8,64,384]{2,1,0:T(8,128)(2,1)S(1)}, bf16[8,64,384]{2,1,0:T(8,128)(2,1)S(1)}, u32[]{:S(2)}, u32[]{:S(2)}) collective-permute-start(bf16[8,64,384]{2,1,0:T(8,128)(2,1)S(1)} %collective-permute-done.9), channel_id=1, source_target_pairs={{0,1},{1,2},{2,3},{3,0},{4,5},{5,6},{6,7},{7,4},{8,9},{9,10},{10,1... | collective-permute-start | bytes 1179656 | tf_op jit(solution)/shard_map/ppermute | solution.py:983
  130.7 15.2 %collective-permute-start.5 = (bf16[128,2048]{1,0:T(8,128)(2,1)}, bf16[128,2048]{1,0:T(8,128)(2,1)}, u32[]{:S(2)}, u32[]{:S(2)}) collective-permute-start(bf16[128,2048]{1,0:T(8,128)(2,1)} %slice.144), channel_id=1, source_target_pairs={{0,16},{4,20},{8,24},{12,28},{16,0},{20,4},{24,8},{28,12},{1,17},{... | collective-permute-start | bytes 1572872 | tf_op jit(solution)/shard_map/ppermute | solution.py:944
  134.3 25.7 %collective-permute-start.6 = (bf16[128,2048]{1,0:T(8,128)(2,1)}, bf16[128,2048]{1,0:T(8,128)(2,1)}, u32[]{:S(2)}, u32[]{:S(2)}) collective-permute-start(bf16[128,2048]{1,0:T(8,128)(2,1)} %slice.145), channel_id=1, source_target_pairs={{0,8},{4,12},{8,0},{12,4},{16,24},{20,28},{24,16},{28,20},{1,9},{5... | collective-permute-start | bytes 1572872 | tf_op jit(solution)/shard_map/ppermute | solution.py:944
  137.3 18.1 %collective-permute-start.48 = (bf16[128,2048]{1,0:T(8,128)(2,1)}, bf16[128,2048]{1,0:T(8,128)(2,1)}, u32[]{:S(2)}, u32[]{:S(2)}) collective-permute-start(bf16[128,2048]{1,0:T(8,128)(2,1)} %slice.150), channel_id=1, source_target_pairs={{0,16},{4,20},{8,24},{12,28},{16,0},{20,4},{24,8},{28,12},{1,17},{... | collective-permute-start | bytes 1572872 | tf_op jit(solution)/shard_map/ppermute | solution.py:944
  145.8 23.9 %collective-permute-start.49 = (bf16[128,2048]{1,0:T(8,128)(2,1)}, bf16[128,2048]{1,0:T(8,128)(2,1)S(1)}, u32[]{:S(2)}, u32[]{:S(2)}) collective-permute-start(bf16[128,2048]{1,0:T(8,128)(2,1)} %slice.151), channel_id=1, source_target_pairs={{0,8},{4,12},{8,0},{12,4},{16,24},{20,28},{24,16},{28,20},{1,9},{5... | collective-permute-start | bytes 1572872 | tf_op jit(solution)/shard_map/ppermute | solution.py:944
  155.4 23.5 %collective-permute-start.17 = (bf16[256,2048]{1,0:T(8,128)(2,1)S(1)}, bf16[256,2048]{1,0:T(8,128)(2,1)S(1)}, u32[]{:S(2)}, u32[]{:S(2)}) collective-permute-start(bf16[256,2048]{1,0:T(8,128)(2,1)S(1)} %bitcast.290), channel_id=1, source_target_pairs={{0,16},{4,20},{8,24},{12,28},{16,0},{20,4},{24,8},{28,12},{1,17},{... | collective-permute-start | bytes 3145736 | tf_op jit(solution)/shard_map/ppermute | solution.py:944
  160.0 73.4 %collective-permute-start.33 = (bf16[2048,256]{1,0:T(8,128)(2,1)}, bf16[2048,256]{1,0:T(8,128)(2,1)}, u32[]{:S(2)}, u32[]{:S(2)}) collective-permute-start(bf16[2048,256]{1,0:T(8,128)(2,1)} %bitcast.302), channel_id=1, source_target_pairs={{0,1},{1,2},{2,3},{3,0},{4,5},{5,6},{6,7},{7,4},{8,9},{9,10},{10,1... | collective-permute-start | bytes 3145736 | tf_op jit(solution)/shard_map/ppermute | solution.py:983
  169.8 9.1 %collective-permute-start.2 = (bf16[256,2048]{1,0:T(8,128)(2,1)}, bf16[256,2048]{1,0:T(8,128)(2,1)S(1)}, u32[]{:S(2)}, u32[]{:S(2)}) collective-permute-start(bf16[256,2048]{1,0:T(8,128)(2,1)} %collective-permute-done.1), channel_id=1, source_target_pairs={{0,4},{4,0},{8,12},{12,8},{16,20},{20,16},{24,28},{28,24},{1,5},{5... | collective-permute-start | bytes 3145736 | tf_op jit(solution)/shard_map/ppermute | solution.py:944
  170.6 63.3 %collective-permute-start.30 = (bf16[2048,256]{1,0:T(8,128)(2,1)}, bf16[2048,256]{1,0:T(8,128)(2,1)}, u32[]{:S(2)}, u32[]{:S(2)}) collective-permute-start(bf16[2048,256]{1,0:T(8,128)(2,1)} %bitcast.299), channel_id=1, source_target_pairs={{0,1},{1,2},{2,3},{3,0},{4,5},{5,6},{6,7},{7,4},{8,9},{9,10},{10,1... | collective-permute-start | bytes 3145736 | tf_op jit(solution)/shard_map/ppermute | solution.py:983
  174.5 8.3 collective-permute-start.4
  178.9 9.4 %collective-permute-start.47 = (bf16[256,2048]{1,0:T(8,128)(2,1)S(1)}, bf16[256,2048]{1,0:T(8,128)(2,1)S(1)}, u32[]{:S(2)}, u32[]{:S(2)}) collective-permute-start(bf16[256,2048]{1,0:T(8,128)(2,1)S(1)} %copy-done.62), channel_id=1, source_target_pairs={{0,4},{4,0},{8,12},{12,8},{16,20},{20,16},{24,28},{28,24},{1,5},{5... | collective-permute-start | bytes 3145736 | tf_op jit(solution)/shard_map/ppermute | solution.py:944
  182.8 19.6 %collective-permute-start.7 = (bf16[256,2048]{1,0:T(8,128)(2,1)S(1)}, bf16[256,2048]{1,0:T(8,128)(2,1)S(1)}, u32[]{:S(2)}, u32[]{:S(2)}) collective-permute-start(bf16[256,2048]{1,0:T(8,128)(2,1)S(1)} %constant_dynamic-update-slice_fusion), channel_id=1, source_target_pairs={{0,4},{4,0},{8,12},{12,8},{16,20},{20,16},{24,28},{28,24},{1,5},{5... | collective-permute-start | bytes 3145736 | tf_op jit(solution)/shard_map/ppermute | solution.py:944
  185.1 14.2 %collective-permute-start.19 = (bf16[128,2048]{1,0:T(8,128)(2,1)S(1)}, bf16[128,2048]{1,0:T(8,128)(2,1)S(1)}, u32[]{:S(2)}, u32[]{:S(2)}) collective-permute-start(bf16[128,2048]{1,0:T(8,128)(2,1)S(1)} %slice.146), channel_id=1, source_target_pairs={{0,16},{4,20},{8,24},{12,28},{16,0},{20,4},{24,8},{28,12},{1,17},{... | collective-permute-start | bytes 1572872 | tf_op jit(solution)/shard_map/ppermute | solution.py:944
  188.3 14.1 %collective-permute-start.20 = (bf16[128,2048]{1,0:T(8,128)(2,1)S(1)}, bf16[128,2048]{1,0:T(8,128)(2,1)S(1)}, u32[]{:S(2)}, u32[]{:S(2)}) collective-permute-start(bf16[128,2048]{1,0:T(8,128)(2,1)S(1)} %slice.147), channel_id=1, source_target_pairs={{0,8},{4,12},{8,0},{12,4},{16,24},{20,28},{24,16},{28,20},{1,9},{5... | collective-permute-start | bytes 1572872 | tf_op jit(solution)/shard_map/ppermute | solution.py:944
  199.3 36.2 %collective-permute-start.36 = (bf16[2048,256]{1,0:T(8,128)(2,1)}, bf16[2048,256]{1,0:T(8,128)(2,1)}, u32[]{:S(2)}, u32[]{:S(2)}) collective-permute-start(bf16[2048,256]{1,0:T(8,128)(2,1)} %bitcast.60), channel_id=1, source_target_pairs={{0,1},{1,2},{2,3},{3,0},{4,5},{5,6},{6,7},{7,4},{8,9},{9,10},{10,1... | collective-permute-start | bytes 3145736 | tf_op jit(solution)/shard_map/ppermute | solution.py:983
  202.4 33.5 %collective-permute-start.50 = (bf16[256,2048]{1,0:T(8,128)(2,1)}, bf16[256,2048]{1,0:T(8,128)(2,1)}, u32[]{:S(2)}, u32[]{:S(2)}) collective-permute-start(bf16[256,2048]{1,0:T(8,128)(2,1)} %constant_dynamic-update-slice_fusion.9), channel_id=1, source_target_pairs={{0,4},{4,0},{8,12},{12,8},{16,20},{20,16},{24,28},{28,24},{1,5},{5... | collective-permute-start | bytes 3145736 | tf_op jit(solution)/shard_map/ppermute | solution.py:944
  202.4 37.2 %collective-permute-start.16 = (bf16[256,2048]{1,0:T(8,128)(2,1)}, bf16[256,2048]{1,0:T(8,128)(2,1)}, u32[]{:S(2)}, u32[]{:S(2)}) collective-permute-start(bf16[256,2048]{1,0:T(8,128)(2,1)} %collective-permute-done.15), channel_id=1, source_target_pairs={{0,4},{4,0},{8,12},{12,8},{16,20},{20,16},{24,28},{28,24},{1,5},{5... | collective-permute-start | bytes 3145736 | tf_op jit(solution)/shard_map/ppermute | solution.py:944
  229.7 78.3 %all-to-all-start.1 = ((bf16[8,256,256]{1,2,0:T(8,128)(2,1)}), bf16[8,256,256]{1,2,0:T(8,128)(2,1)S(1)}, u32[]{:S(2)}, u32[]{:S(2)}) async-start(bf16[8,256,256]{1,2,0:T(8,128)(2,1)} %bitcast.294), calls=%async_computation.1 | async-start | bytes 2097152 | tf_op jit(solution)/shard_map/all_to_all | solution.py:1214
  233.4 10.8 %collective-permute-start.18 = (bf16[256,2048]{1,0:T(8,128)(2,1)}, bf16[256,2048]{1,0:T(8,128)(2,1)S(1)}, u32[]{:S(2)}, u32[]{:S(2)}) collective-permute-start(bf16[256,2048]{1,0:T(8,128)(2,1)} %copy-done.60), channel_id=1, source_target_pairs={{0,4},{4,0},{8,12},{12,8},{16,20},{20,16},{24,28},{28,24},{1,5},{5... | collective-permute-start | bytes 3145736 | tf_op jit(solution)/shard_map/ppermute | solution.py:944
  233.9 28.1 %collective-permute-start.34 = (bf16[2048,256]{1,0:T(8,128)(2,1)}, bf16[2048,256]{1,0:T(8,128)(2,1)}, u32[]{:S(2)}, u32[]{:S(2)}) collective-permute-start(bf16[2048,256]{1,0:T(8,128)(2,1)} %collective-permute-done.33), channel_id=1, source_target_pairs={{0,1},{1,2},{2,3},{3,0},{4,5},{5,6},{6,7},{7,4},{8,9},{9,10},{10,1... | collective-permute-start | bytes 3145736 | tf_op jit(solution)/shard_map/ppermute | solution.py:983
  235.5 49.0 %collective-permute-start.31 = (bf16[2048,256]{1,0:T(8,128)(2,1)}, bf16[2048,256]{1,0:T(8,128)(2,1)}, u32[]{:S(2)}, u32[]{:S(2)}) collective-permute-start(bf16[2048,256]{1,0:T(8,128)(2,1)} %collective-permute-done.30), channel_id=1, source_target_pairs={{0,1},{1,2},{2,3},{3,0},{4,5},{5,6},{6,7},{7,4},{8,9},{9,10},{10,1... | collective-permute-start | bytes 3145736 | tf_op jit(solution)/shard_map/ppermute | solution.py:983
  235.8 71.1 %collective-permute-start.37 = (bf16[2048,256]{1,0:T(8,128)(2,1)}, bf16[2048,256]{1,0:T(8,128)(2,1)}, u32[]{:S(2)}, u32[]{:S(2)}) collective-permute-start(bf16[2048,256]{1,0:T(8,128)(2,1)} %collective-permute-done.36), channel_id=1, source_target_pairs={{0,1},{1,2},{2,3},{3,0},{4,5},{5,6},{6,7},{7,4},{8,9},{9,10},{10,1... | collective-permute-start | bytes 3145736 | tf_op jit(solution)/shard_map/ppermute | solution.py:983
  239.6 67.4 %collective-permute-start.21 = (bf16[256,2048]{1,0:T(8,128)(2,1)}, bf16[256,2048]{1,0:T(8,128)(2,1)S(1)}, u32[]{:S(2)}, u32[]{:S(2)}) collective-permute-start(bf16[256,2048]{1,0:T(8,128)(2,1)} %copy-done.63), channel_id=1, source_target_pairs={{0,4},{4,0},{8,12},{12,8},{16,20},{20,16},{24,28},{28,24},{1,5},{5... | collective-permute-start | bytes 3145736 | tf_op jit(solution)/shard_map/ppermute | solution.py:944
  262.0 145.0 %collective-permute-start.35 = (bf16[2048,256]{1,0:T(8,128)(2,1)}, bf16[2048,256]{1,0:T(8,128)(2,1)}, u32[]{:S(2)}, u32[]{:S(2)}) collective-permute-start(bf16[2048,256]{1,0:T(8,128)(2,1)} %collective-permute-done.34), channel_id=1, source_target_pairs={{0,1},{1,2},{2,3},{3,0},{4,5},{5,6},{6,7},{7,4},{8,9},{9,10},{10,1... | collective-permute-start | bytes 3145736 | tf_op jit(solution)/shard_map/ppermute | solution.py:983
  284.5 135.9 %collective-permute-start.32 = (bf16[2048,256]{1,0:T(8,128)(2,1)}, bf16[2048,256]{1,0:T(8,128)(2,1)}, u32[]{:S(2)}, u32[]{:S(2)}) collective-permute-start(bf16[2048,256]{1,0:T(8,128)(2,1)} %collective-permute-done.31), channel_id=1, source_target_pairs={{0,1},{1,2},{2,3},{3,0},{4,5},{5,6},{6,7},{7,4},{8,9},{9,10},{10,1... | collective-permute-start | bytes 3145736 | tf_op jit(solution)/shard_map/ppermute | solution.py:983
  307.0 66.6 %collective-permute-start.38 = (bf16[2048,256]{1,0:T(8,128)(2,1)}, bf16[2048,256]{1,0:T(8,128)(2,1)}, u32[]{:S(2)}, u32[]{:S(2)}) collective-permute-start(bf16[2048,256]{1,0:T(8,128)(2,1)} %collective-permute-done.37), channel_id=1, source_target_pairs={{0,1},{1,2},{2,3},{3,0},{4,5},{5,6},{6,7},{7,4},{8,9},{9,10},{10,1... | collective-permute-start | bytes 3145736 | tf_op jit(solution)/shard_map/ppermute | solution.py:983
  316.6 71.3 %collective-permute-start.23 = (bf16[256,2048]{1,0:T(8,128)(2,1)S(1)}, bf16[256,2048]{1,0:T(8,128)(2,1)S(1)}, u32[]{:S(2)}, u32[]{:S(2)}) collective-permute-start(bf16[256,2048]{1,0:T(8,128)(2,1)S(1)} %get-tuple-element.113), channel_id=1, source_target_pairs={{0,8},{4,12},{8,0},{12,4},{16,24},{20,28},{24,16},{28,20},{1,9},{5... | collective-permute-start | bytes 3145736 | tf_op jit(solution)/shard_map/ppermute | solution.py:944
  318.4 71.6 %collective-permute-start.25 = (bf16[256,2048]{1,0:T(8,128)(2,1)S(1)}, bf16[256,2048]{1,0:T(8,128)(2,1)S(1)}, u32[]{:S(2)}, u32[]{:S(2)}) collective-permute-start(bf16[256,2048]{1,0:T(8,128)(2,1)S(1)} %get-tuple-element.113), channel_id=1, source_target_pairs={{0,16},{4,20},{8,24},{12,28},{16,0},{20,4},{24,8},{28,12},{1,17},{... | collective-permute-start | bytes 3145736 | tf_op jit(solution)/shard_map/ppermute | solution.py:944
  373.6 18.0 %collective-permute-start.22 = (bf16[256,2048]{1,0:T(8,128)(2,1)S(1)}, bf16[256,2048]{1,0:T(8,128)(2,1)S(1)}, u32[]{:S(2)}, u32[]{:S(2)}) collective-permute-start(bf16[256,2048]{1,0:T(8,128)(2,1)S(1)} %get-tuple-element.113), channel_id=1, source_target_pairs={{0,4},{4,0},{8,12},{12,8},{16,20},{20,16},{24,28},{28,24},{1,5},{5... | collective-permute-start | bytes 3145736 | tf_op jit(solution)/shard_map/ppermute | solution.py:944
  387.9 14.6 %collective-permute-start.27 = (bf16[128,2048]{1,0:T(8,128)(2,1)S(1)}, bf16[128,2048]{1,0:T(8,128)(2,1)S(1)}, u32[]{:S(2)}, u32[]{:S(2)}) collective-permute-start(bf16[128,2048]{1,0:T(8,128)(2,1)S(1)} %slice.148), channel_id=1, source_target_pairs={{0,16},{4,20},{8,24},{12,28},{16,0},{20,4},{24,8},{28,12},{1,17},{... | collective-permute-start | bytes 1572872 | tf_op jit(solution)/shard_map/ppermute | solution.py:944
  390.0 14.1 %collective-permute-start.28 = (bf16[128,2048]{1,0:T(8,128)(2,1)S(1)}, bf16[128,2048]{1,0:T(8,128)(2,1)S(1)}, u32[]{:S(2)}, u32[]{:S(2)}) collective-permute-start(bf16[128,2048]{1,0:T(8,128)(2,1)S(1)} %slice.149), channel_id=1, source_target_pairs={{0,8},{4,12},{8,0},{12,4},{16,24},{20,28},{24,16},{28,20},{1,9},{5... | collective-permute-start | bytes 1572872 | tf_op jit(solution)/shard_map/ppermute | solution.py:944
  391.5 12.7 %collective-permute-start.24 = (bf16[256,2048]{1,0:T(8,128)(2,1)S(1)}, bf16[256,2048]{1,0:T(8,128)(2,1)S(1)}, u32[]{:S(2)}, u32[]{:S(2)}) collective-permute-start(bf16[256,2048]{1,0:T(8,128)(2,1)S(1)} %collective-permute-done.23), channel_id=1, source_target_pairs={{0,4},{4,0},{8,12},{12,8},{16,20},{20,16},{24,28},{28,24},{1,5},{5... | collective-permute-start | bytes 3145736 | tf_op jit(solution)/shard_map/ppermute | solution.py:944
  480.4 23.7 %collective-permute-start.51 = (bf16[4,256,2048]{2,1,0:T(8,128)(2,1)}, bf16[4,256,2048]{2,1,0:T(8,128)(2,1)}, u32[]{:S(2)}, u32[]{:S(2)}) collective-permute-start(bf16[4,256,2048]{2,1,0:T(8,128)(2,1)} %dynamic-slice_bitcast_fusion.1), channel_id=1, source_target_pairs={{0,4},{4,0},{8,12},{12,8},{16,20},{20,16},{24,28},{28,24},{1,5},{5... | collective-permute-start | bytes 12582920 | tf_op jit(solution)/shard_map/ppermute | solution.py:944
  503.7 13.0 %collective-permute-start.39 = (bf16[4,256,2048]{2,1,0:T(8,128)(2,1)}, bf16[4,256,2048]{2,1,0:T(8,128)(2,1)}, u32[]{:S(2)}, u32[]{:S(2)}) collective-permute-start(bf16[4,256,2048]{2,1,0:T(8,128)(2,1)} %dynamic-slice_bitcast_fusion.2), channel_id=1, source_target_pairs={{0,4},{4,0},{8,12},{12,8},{16,20},{20,16},{24,28},{28,24},{1,5},{5... | collective-permute-start | bytes 12582920 | tf_op jit(solution)/shard_map/ppermute | solution.py:944
  513.1 26.0 %collective-permute-start.52 = (bf16[256,2048]{1,0:T(8,128)(2,1)S(1)}, bf16[256,2048]{1,0:T(8,128)(2,1)S(1)}, u32[]{:S(2)}, u32[]{:S(2)}) collective-permute-start(bf16[256,2048]{1,0:T(8,128)(2,1)S(1)} %get-tuple-element.117), channel_id=1, source_target_pairs={{0,8},{4,12},{8,0},{12,4},{16,24},{20,28},{24,16},{28,20},{1,9},{5... | collective-permute-start | bytes 3145736 | tf_op jit(solution)/shard_map/ppermute | solution.py:944
  514.7 48.8 %collective-permute-start.53 = (bf16[256,2048]{1,0:T(8,128)(2,1)}, bf16[256,2048]{1,0:T(8,128)(2,1)}, u32[]{:S(2)}, u32[]{:S(2)}) collective-permute-start(bf16[256,2048]{1,0:T(8,128)(2,1)} %get-tuple-element.119), channel_id=1, source_target_pairs={{0,16},{4,20},{8,24},{12,28},{16,0},{20,4},{24,8},{28,12},{1,17},{... | collective-permute-start | bytes 3145736 | tf_op jit(solution)/shard_map/ppermute | solution.py:944
  516.2 47.3 %collective-permute-start.54 = (bf16[256,2048]{1,0:T(8,128)(2,1)}, bf16[256,2048]{1,0:T(8,128)(2,1)}, u32[]{:S(2)}, u32[]{:S(2)}) collective-permute-start(bf16[256,2048]{1,0:T(8,128)(2,1)} %get-tuple-element.118), channel_id=1, source_target_pairs={{0,24},{4,28},{8,16},{12,20},{16,8},{20,12},{24,0},{28,4},{1,25},{... | collective-permute-start | bytes 3145736 | tf_op jit(solution)/shard_map/ppermute | solution.py:944
  525.9 58.3 %collective-permute-start.40 = (bf16[256,2048]{1,0:T(8,128)(2,1)}, bf16[256,2048]{1,0:T(8,128)(2,1)}, u32[]{:S(2)}, u32[]{:S(2)}) collective-permute-start(bf16[256,2048]{1,0:T(8,128)(2,1)} %get-tuple-element.120), channel_id=1, source_target_pairs={{0,8},{4,12},{8,0},{12,4},{16,24},{20,28},{24,16},{28,20},{1,9},{5... | collective-permute-start | bytes 3145736 | tf_op jit(solution)/shard_map/ppermute | solution.py:944
  527.3 80.0 %collective-permute-start.41 = (bf16[256,2048]{1,0:T(8,128)(2,1)}, bf16[256,2048]{1,0:T(8,128)(2,1)}, u32[]{:S(2)}, u32[]{:S(2)}) collective-permute-start(bf16[256,2048]{1,0:T(8,128)(2,1)} %get-tuple-element.122), channel_id=1, source_target_pairs={{0,16},{4,20},{8,24},{12,28},{16,0},{20,4},{24,8},{28,12},{1,17},{... | collective-permute-start | bytes 3145736 | tf_op jit(solution)/shard_map/ppermute | solution.py:944
  539.1 68.2 %collective-permute-start.42 = (bf16[256,2048]{1,0:T(8,128)(2,1)}, bf16[256,2048]{1,0:T(8,128)(2,1)}, u32[]{:S(2)}, u32[]{:S(2)}) collective-permute-start(bf16[256,2048]{1,0:T(8,128)(2,1)} %get-tuple-element.121), channel_id=1, source_target_pairs={{0,24},{4,28},{8,16},{12,20},{16,8},{20,12},{24,0},{28,4},{1,25},{... | collective-permute-start | bytes 3145736 | tf_op jit(solution)/shard_map/ppermute | solution.py:944
  622.9 53.3 %all-to-all-start.5 = ((bf16[8,256,256]{2,1,0:T(8,128)(2,1)}), bf16[8,256,256]{2,1,0:T(8,128)(2,1)}, u32[]{:S(2)}, u32[]{:S(2)}) async-start(bf16[8,256,256]{2,1,0:T(8,128)(2,1)} %bitcast.305), calls=%async_computation.5 | async-start | bytes 2097152 | tf_op jit(solution)/shard_map/all_to_all | solution.py:1278
  729.3 25.6 %collective-permute-start.55 = (bf16[4,256,2048]{2,1,0:T(8,128)(2,1)}, bf16[4,256,2048]{2,1,0:T(8,128)(2,1)}, u32[]{:S(2)}, u32[]{:S(2)}) collective-permute-start(bf16[4,256,2048]{2,1,0:T(8,128)(2,1)} %dynamic-slice_bitcast_fusion), channel_id=1, source_target_pairs={{0,4},{4,0},{8,12},{12,8},{16,20},{20,16},{24,28},{28,24},{1,5},{5... | collective-permute-start | bytes 12582920 | tf_op jit(solution)/shard_map/ppermute | solution.py:944
  750.7 25.1 %all-to-all-start.7 = ((f32[4,1,5888]{2,1,0:T(1,128)}), f32[4,1,5888]{2,1,0:T(1,128)}, u32[]{:S(2)}, u32[]{:S(2)}) async-start(f32[4,1,5888]{2,1,0:T(1,128)} %copy.178), calls=%async_computation.7 | async-start | bytes 188416 | tf_op jit(solution)/shard_map/all_to_all | solution.py:1369
  762.1 62.1 %collective-permute-start.56 = (bf16[256,2048]{1,0:T(8,128)(2,1)}, bf16[256,2048]{1,0:T(8,128)(2,1)}, u32[]{:S(2)}, u32[]{:S(2)}) collective-permute-start(bf16[256,2048]{1,0:T(8,128)(2,1)} %get-tuple-element.114), channel_id=1, source_target_pairs={{0,8},{4,12},{8,0},{12,4},{16,24},{20,28},{24,16},{28,20},{1,9},{5... | collective-permute-start | bytes 3145736 | tf_op jit(solution)/shard_map/ppermute | solution.py:944
  764.0 60.1 %collective-permute-start.57 = (bf16[256,2048]{1,0:T(8,128)(2,1)}, bf16[256,2048]{1,0:T(8,128)(2,1)}, u32[]{:S(2)}, u32[]{:S(2)}) collective-permute-start(bf16[256,2048]{1,0:T(8,128)(2,1)} %get-tuple-element.116), channel_id=1, source_target_pairs={{0,16},{4,20},{8,24},{12,28},{16,0},{20,4},{24,8},{28,12},{1,17},{... | collective-permute-start | bytes 3145736 | tf_op jit(solution)/shard_map/ppermute | solution.py:944
  765.5 58.6 %collective-permute-start.58 = (bf16[256,2048]{1,0:T(8,128)(2,1)}, bf16[256,2048]{1,0:T(8,128)(2,1)}, u32[]{:S(2)}, u32[]{:S(2)}) collective-permute-start(bf16[256,2048]{1,0:T(8,128)(2,1)} %get-tuple-element.115), channel_id=1, source_target_pairs={{0,24},{4,28},{8,16},{12,20},{16,8},{20,12},{24,0},{28,4},{1,25},{... | collective-permute-start | bytes 3145736 | tf_op jit(solution)/shard_map/ppermute | solution.py:944
  775.8 39.6 %all-to-all-start.6 = ((f32[32,1,2624]{2,1,0:T(1,128)}), f32[32,1,2624]{2,1,0:T(1,128)}, u32[]{:S(2)}, u32[]{:S(2)}) async-start(f32[32,1,2624]{2,1,0:T(1,128)} %reshape.266), calls=%async_computation.6 | async-start | bytes 688128 | tf_op jit(solution)/shard_map/all_to_all | solution.py:1353
  (97 other events, 2479.4 us)

commit v2 on v0

--- a/solution.py
+++ b/solution.py
@@ -1,8 +1,11 @@
+import functools
 import math
 
 import jax
 import jax.numpy as jnp
 from jax import lax
+from jax.experimental import pallas as pl
+from jax.experimental.pallas import tpu as pltpu
 from jax.sharding import PartitionSpec as P
 
 QUERY_HEADS = 32
@@ -15,6 +18,11 @@
 rope_base = 500000.0
 precise = lax.Precision.HIGHEST
 lowest_precision = -1e30
+ONES = 16
+SUB = 128
+VMEM_MIB = 56
+PARTS = 2
+COST = 1.15e9
 
 
 def prefix(x, axis, join, neutral, backward):
@@ -628,6 +636,1445 @@
         transfer_loss,
     )
 
+def halves_rotated(first_half, second_half, cosine, sine):
+    return (
+        first_half * cosine - second_half * sine,
+        second_half * cosine + first_half * sine,
+    )
+
+
+def soft_pair(logits):
+    plus = jnp.exp(logits - jnp.max(logits, axis=0, keepdims=True))
+    minus = jnp.exp(jnp.min(logits, axis=0, keepdims=True) - logits)
+    plus = plus * (1.0 / jnp.sum(plus, axis=0, keepdims=True))
+    minus = minus * (1.0 / jnp.sum(minus, axis=0, keepdims=True))
+    return plus, minus
+
+
+def mm(a, b):
+    return jnp.dot(a, b, preferred_element_type=jnp.float32)
+
+
+def mm_nt(a, b):
+    return lax.dot_general(a, b, (((1,), (1,)), ((), ())), preferred_element_type=jnp.float32)
+
+
+def mm_tn(a, b):
+    return lax.dot_general(a, b, (((0,), (0,)), ((), ())), preferred_element_type=jnp.float32)
+
+
+def split_wide(x):
+    high = x.astype(jnp.bfloat16)
+    low = (x - high.astype(jnp.float32)).astype(jnp.bfloat16)
+    return high, low
+
+
+ANYWHERE = pl.BlockSpec(memory_space=pltpu.HBM)
+
+
+def call(kernel, grid, in_specs, out_specs, out_shape, scratch, flops, moved, scalars=0):
+    spec = pltpu.PrefetchScalarGridSpec(
+        num_scalar_prefetch=scalars,
+        grid=grid,
+        in_specs=in_specs,
+        out_specs=out_specs,
+        scratch_shapes=scratch,
+    )
+    return pl.pallas_call(
+        kernel,
+        grid_spec=spec,
+        out_shape=out_shape,
+        compiler_params=pltpu.CompilerParams(vmem_limit_bytes=VMEM_MIB * 2**20),
+        cost_estimate=pl.CostEstimate(
+            flops=int(COST * moved), bytes_accessed=1, transcendentals=0
+        ),
+    )
+
+
+def spec_whole(*dims):
+    return pl.BlockSpec(dims, lambda i, *_: (0,) * len(dims))
+
+
+def spec_across(height, columns):
+    return pl.BlockSpec((height, columns), lambda i, *_: (0, i))
+
+
+def spec_down(rows, wide):
+    return pl.BlockSpec((rows, wide), lambda i, *_: (i, 0))
+
+
+def spec_block(*dims):
+    return pl.BlockSpec((None,) + dims, lambda i, *_: (i, 0, 0))
+
+
+def spec_placed(spec):
+    return pl.BlockSpec(
+        spec.block_shape,
+        lambda i, place_ref, *_: spec.index_map(lax.bitwise_xor(i, place_ref[0])),
+    )
+
+
+def array(*dims, dtype=jnp.bfloat16):
+    return jax.ShapeDtypeStruct(dims, dtype)
+
+
+def flat(found):
+    return [part for parts in found for part in parts]
+
+
+def grouped(refs, counts):
+    found, start = [], 0
+    for count in counts:
+        found.append(tuple(refs[start : start + count]))
+        start += count
+    return found, refs[start:]
+
+
+def fetch(refs, buffer, sems, at, order=lambda step: step):
+    steps = len(refs)
+
+    def start(step):
+        slot = lax.rem(step, 2)
+        wanted = order(step)
+        for number, parts in enumerate(refs):
+
+            @pl.when(wanted == number)
+            def _():
+                height = buffer.shape[1] // len(parts)
+                for part, ref in enumerate(parts):
+                    pltpu.make_async_copy(
+                        ref, buffer.at[slot, part * height : (part + 1) * height], sems.at[slot]
+                    ).start()
+
+    @pl.when(at == 0)
+    def _():
+        start(at)
+
+    @pl.when(at + 1 < steps)
+    def _():
+        start(at + 1)
+
+    slot = lax.rem(at, 2)
+    pltpu.make_async_copy(buffer.at[slot], buffer.at[slot], sems.at[slot]).wait()
+    return slot
+
+
+def start_columns(refs, span, buffer, sem):
+    first, end = span
+    wide = end - first
+    for chunk, ref in enumerate(refs):
+        pltpu.make_async_copy(
+            ref.at[:, first:end], buffer.at[:, chunk * wide : (chunk + 1) * wide], sem
+        ).start()
+
+
+def chunks_of(ref, order_ref):
+    return [ref.at[order_ref[chunk]] for chunk in range(ref.shape[0])]
+
+
+def wait_whole(buffer, sem):
+    pltpu.make_async_copy(buffer, buffer, sem).wait()
+
+
+def block_shape(blocks):
+    return sum(part.shape[0] for part in blocks[0]), blocks[0][0].shape[1]
+
+
+def fetch_scratch(blocks):
+    rows, wide = block_shape(blocks)
+    return [pltpu.VMEM((2, rows, wide), jnp.bfloat16), pltpu.SemaphoreType.DMA((2,))]
+
+
+def project_kernel(counts, place_ref, *refs):
+    blocks, refs = grouped(refs, counts)
+    (
+        w_ref, down_ref, up_ref, map_ref, cos_ref, sin_ref,
+        q_ref, kt_ref, vt_ref, k_ref, v_ref, pq_ref, pkt_ref, pk_ref, narrow_ref, wt_ref,
+        buffer, sems,
+    ) = refs
+    group = q_ref.shape[0] // HEAD_SIZE
+    half = HEAD_SIZE // 2
+    width = (group + 2) * HEAD_SIZE
+    slot = fetch(blocks, buffer, sems, pl.program_id(0))
+
+    @pl.when(pl.program_id(0) == 0)
+    def _():
+        lanes, places, shard, _ = w_ref.shape
+        for place in range(places):
+            rows = jnp.concatenate([w_ref[lane, place] for lane in range(lanes)], axis=0)
+            columns = slice(place * lanes * shard, (place + 1) * lanes * shard)
+            wt_ref[:width, columns] = jnp.transpose(rows)
+        wt_ref[width:] = down_ref[...]
+
+    full = mm_nt(wt_ref[...], buffer[slot])
+    narrow = full[width:].astype(jnp.bfloat16)
+    narrow_ref[...] = narrow
+    pre = full[:width] + mm(up_ref[...], narrow)
+    cosine, sine = cos_ref[...], sin_ref[...]
+    for head in range(group + 1):
+        base = head * HEAD_SIZE
+        low_half, high_half = halves_rotated(
+            pre[base : base + half], pre[base + half : base + HEAD_SIZE], cosine, sine
+        )
+        wide = jnp.concatenate([low_half, high_half], axis=0)
+        vector = wide.astype(jnp.bfloat16)
+        logits = mm(map_ref[base : base + HEAD_SIZE], vector)
+        plus, minus = soft_pair(logits)
+        maps = jnp.concatenate([plus, minus], axis=0)
+        if head < group:
+            q_ref[base : base + HEAD_SIZE] = vector
+            pq_ref[2 * base : 2 * base + 2 * HEAD_SIZE] = maps.astype(jnp.bfloat16)
+        else:
+            kt_ref[...] = vector
+            k_ref[...] = jnp.transpose(wide).astype(jnp.bfloat16)
+            pkt_ref[...] = maps.astype(jnp.bfloat16)
+            pk_ref[...] = jnp.transpose(maps).astype(jnp.bfloat16)
+    values = pre[width - HEAD_SIZE : width]
+    vt_ref[:HEAD_SIZE] = values.astype(jnp.bfloat16)
+    vt_ref[HEAD_SIZE:] = jnp.ones((ONES, values.shape[1]), jnp.bfloat16)
+    v_ref[...] = jnp.transpose(values).astype(jnp.bfloat16)
+
+
+def project(place_row, blocks, weights, down_block, up_block, maps_ahead, cosine, sine):
+    places = len(blocks)
+    rows, model = block_shape(blocks)
+    count = places * rows
+    width, spare = up_block.shape
+    query_width = width - 2 * HEAD_SIZE
+    group = query_width // HEAD_SIZE
+    maps = 2 * HEAD_SIZE
+    half = HEAD_SIZE // 2
+    counts = [len(found) for found in blocks]
+    outs = [
+        (query_width, False),
+        (HEAD_SIZE, False),
+        (HEAD_SIZE + ONES, False),
+        (HEAD_SIZE, True),
+        (HEAD_SIZE, True),
+        (group * maps, False),
+        (maps, False),
+        (maps, True),
+        (spare, False),
+    ]
+    return call(
+        functools.partial(project_kernel, counts),
+        (places,),
+        [ANYWHERE] * sum(counts)
+        + [
+            spec_whole(*weights.shape),
+            spec_whole(spare, model),
+            spec_whole(width, spare),
+            spec_whole(*maps_ahead.shape),
+            spec_placed(spec_across(half, rows)),
+            spec_placed(spec_across(half, rows)),
+        ],
+        [
+            spec_placed(spec_down(rows, size) if natural else spec_across(size, rows))
+            for size, natural in outs
+        ]
+        + [spec_whole(width + spare, model)],
+        [array(count, size) if natural else array(size, count) for size, natural in outs]
+        + [array(width + spare, model)],
+        fetch_scratch(blocks),
+        0,
+        17,
+        scalars=1,
+    )(place_row, *flat(blocks), weights, down_block, up_block, maps_ahead, cosine, sine)
+
+
+def side_by_side(ref, size, group, columns):
+    return jnp.concatenate(
+        [ref[head * size : (head + 1) * size, columns] for head in range(group)], axis=1
+    )
+
+
+def bands():
+    shape = (WINDOW_KEYS, SUB)
+    query_at = lax.broadcasted_iota(jnp.int32, shape, 1)
+    key_at = lax.broadcasted_iota(jnp.int32, shape, 0)
+    distance = query_at - key_at
+    return (
+        distance < 0,
+        (distance >= 0) & (distance < WINDOW_KEYS),
+        distance >= WINDOW_KEYS,
+        distance >= WINDOW_KEYS,
+    )
+
+
+def forward_kernel(
+    length_ref, q_ref, pq_ref, k_ref, k_before, pk_ref, pk_before, vt_ref, vt_before,
+    att_ref, out_ref, denom_ref, states_ref, weights_ref, state,
+):
+    step = pl.program_id(0)
+    group = q_ref.shape[0] // HEAD_SIZE
+    rows = q_ref.shape[1]
+    quarter = WINDOW_KEYS
+    second, third, third_far, fourth = bands()
+
+    @pl.when(step == 0)
+    def _():
+        state[...] = jnp.zeros_like(state)
+
+    now = state[...]
+    for sub in range(rows // SUB):
+        columns = slice(sub * SUB, (sub + 1) * SUB)
+        queries = side_by_side(q_ref, HEAD_SIZE, group, columns)
+        query_maps = side_by_side(pq_ref, 2 * HEAD_SIZE, group, columns)
+        if sub == 0:
+            keys = jnp.concatenate([k_before[...], k_ref[:SUB]], axis=0)
+            key_maps = jnp.concatenate([pk_before[...], pk_ref[:SUB]], axis=0)
+            values = jnp.concatenate([vt_before[...], vt_ref[:, :SUB]], axis=1)
+        else:
+            around = slice((sub - 1) * SUB, (sub + 1) * SUB)
+            keys, key_maps, values = k_ref[around], pk_ref[around], vt_ref[:, around]
+        scores = mm(keys[quarter:], queries)
+        far = mm(key_maps[: 3 * quarter], query_maps)
+        pieces = []
+        for head in range(group):
+            lanes = slice(head * SUB, (head + 1) * SUB)
+            near = jnp.exp(scores[:, lanes] * (1.0 / math.sqrt(HEAD_SIZE)))
+            away = far[:, lanes]
+            before = jnp.concatenate(
+                [
+                    away[:quarter],
+                    jnp.where(second, near[:quarter], away[quarter : 2 * quarter]),
+                ],
+                axis=0,
+            )
+            if sub == 0:
+                before = jnp.where(step > 0, before, 0.0)
+            pieces.append(
+                jnp.concatenate(
+                    [
+                        before,
+                        jnp.where(
+                            third,
+                            near[quarter : 2 * quarter],
+                            jnp.where(third_far, away[2 * quarter :], 0.0),
+                        ),
+                        jnp.where(fourth, near[2 * quarter :], 0.0),
+                    ],
+                    axis=0,
+                ).astype(jnp.bfloat16)
+            )
+        weights = jnp.concatenate(pieces, axis=1)
+        weights_ref[sub] = weights
+        states_ref[sub] = now
+        high, low = split_wide(now)
+        total = mm(values, weights) + mm(
+            jnp.concatenate([high, low], axis=1),
+            jnp.concatenate([query_maps, query_maps], axis=0),
+        )
+        denom = total[HEAD_SIZE : HEAD_SIZE + 1]
+        out = total[:HEAD_SIZE] * (1.0 / denom)
+        at = step * rows + sub * SUB + lax.broadcasted_iota(jnp.int32, (HEAD_SIZE, SUB), 1)
+        inside = at < length_ref[0]
+        for head in range(group):
+            lanes = slice(head * SUB, (head + 1) * SUB)
+            base = head * HEAD_SIZE
+            out_ref[base : base + HEAD_SIZE, columns] = out[:, lanes]
+            att_ref[base : base + HEAD_SIZE, columns] = jnp.where(
+                inside, out[:, lanes], 0.0
+            ).astype(jnp.bfloat16)
+            denom_ref[head : head + 1, columns] = denom[:, lanes]
+        update = mm(values[:, :SUB], key_maps[:SUB])
+        if sub == 0:
+            update = jnp.where(step > 0, update, 0.0)
+        now = now + update
+    state[...] = now
+
+
+def before_down(rows, wide):
+    per_step = rows // SUB
+    return pl.BlockSpec((SUB, wide), lambda i, *_: (jnp.maximum(per_step * i - 1, 0), 0))
+
+
+def before_across(rows, height):
+    per_step = rows // SUB
+    return pl.BlockSpec((height, SUB), lambda i, *_: (0, jnp.maximum(per_step * i - 1, 0)))
+
+
+def attend(length, q_t, pq_t, keys, key_maps, v_t, rows):
+    query_width, count = q_t.shape
+    group = query_width // HEAD_SIZE
+    places = count // rows
+    per_step = rows // SUB
+    maps = key_maps.shape[1]
+    high = v_t.shape[0]
+    wide = jnp.float32
+    return call(
+        forward_kernel,
+        (places,),
+        [
+            spec_across(query_width, rows),
+            spec_across(group * maps, rows),
+            spec_down(rows, HEAD_SIZE),
+            before_down(rows, HEAD_SIZE),
+            spec_down(rows, maps),
+            before_down(rows, maps),
+            spec_across(high, rows),
+            before_across(rows, high),
+        ],
+        [
+            spec_block(query_width, rows),
+            spec_across(query_width, rows),
+            spec_across(group, rows),
+            pl.BlockSpec((per_step, high, maps), lambda i, *_: (i, 0, 0)),
+            pl.BlockSpec((per_step, 2 * SUB, group * SUB), lambda i, *_: (i, 0, 0)),
+        ],
+        [
+            array(places, query_width, rows),
+            array(query_width, count, dtype=wide),
+            array(group, count, dtype=wide),
+            array(count // SUB, high, maps, dtype=wide),
+            array(count // SUB, 2 * SUB, group * SUB),
+        ],
+        [pltpu.VMEM((high, maps), wide)],
+        0,
+        10,
+        scalars=1,
+    )(length, q_t, pq_t, keys, keys, key_maps, key_maps, v_t, v_t)
+
+
+def teacher_kernel(first, steps, length_ref, q_ref, k_ref, vt_ref, att_ref, *refs):
+    diff_ref, loss_ref = refs[-2:]
+    step = pl.program_id(0)
+    group = q_ref.shape[0] // HEAD_SIZE
+    rows = q_ref.shape[1]
+    scale = 1.0 / math.sqrt(HEAD_SIZE)
+    at = (first + step) * rows + lax.broadcasted_iota(jnp.int32, (HEAD_SIZE, rows), 1)
+    inside = at < length_ref[0]
+    shape = (rows, rows)
+    ahead = lax.broadcasted_iota(jnp.int32, shape, 0) > lax.broadcasted_iota(jnp.int32, shape, 1)
+
+    for blocks in range(first + 1, first + steps + 1):
+
+        @pl.when(first + step == blocks - 1)
+        def _():
+            size = blocks * rows
+            loss = jnp.zeros((1, rows), jnp.float32)
+            for head in range(group):
+                base = head * HEAD_SIZE
+                query = q_ref[base : base + HEAD_SIZE]
+                last = jnp.where(ahead, lowest_precision, mm(k_ref[size - rows : size], query))
+                best = jnp.max(last, axis=0, keepdims=True)
+                if blocks > 1:
+                    early = mm(k_ref[: size - rows], query)
+                    best = jnp.maximum(best, jnp.max(early, axis=0, keepdims=True))
+                total = mm(
+                    vt_ref[:, size - rows : size],
+                    jnp.exp((last - best) * scale).astype(jnp.bfloat16),
+                )
+                if blocks > 1:
+                    total = total + mm(
+                        vt_ref[:, : size - rows],
+                        jnp.exp((early - best) * scale).astype(jnp.bfloat16),
+                    )
+                taught = total[:HEAD_SIZE] * (1.0 / total[HEAD_SIZE : HEAD_SIZE + 1])
+                difference = att_ref[base : base + HEAD_SIZE].astype(jnp.float32) - jnp.where(
+                    inside, taught, 0.0
+                )
+                diff_ref[base : base + HEAD_SIZE] = difference
+                loss = loss + jnp.sum(difference * difference, axis=0, keepdims=True)
+            loss_ref[...] = jnp.broadcast_to(loss, loss_ref.shape)
+
+
+def teach(length, q_t, keys, v_t, att, first, end, before=None):
+    places, query_width, rows = att.shape
+    count = places * rows
+    wide = jnp.float32
+
+    def ahead(spec):
+        return pl.BlockSpec(spec.block_shape, lambda i, *_: spec.index_map(i + first))
+
+    spec = pltpu.PrefetchScalarGridSpec(
+        num_scalar_prefetch=1,
+        grid=(end - first,),
+        in_specs=[
+            ahead(spec_across(query_width, rows)),
+            spec_whole(*keys.shape),
+            spec_whole(*v_t.shape),
+            ahead(spec_block(query_width, rows)),
+        ]
+        + [ANYWHERE] * (2 if before else 0),
+        out_specs=[ahead(spec_across(query_width, rows)), ahead(spec_across(8, rows))],
+    )
+    return pl.pallas_call(
+        functools.partial(teacher_kernel, first, end - first),
+        grid_spec=spec,
+        out_shape=[array(query_width, count, dtype=wide), array(8, count, dtype=wide)],
+        input_output_aliases={5: 0, 6: 1} if before else {},
+        compiler_params=pltpu.CompilerParams(vmem_limit_bytes=VMEM_MIB * 2**20),
+        cost_estimate=pl.CostEstimate(
+            flops=int(COST * 16), bytes_accessed=1, transcendentals=0
+        ),
+    )(length, q_t, keys, v_t, att, *(before or ()))
+
+
+def hidden_kernel(counts, order_ref, *refs):
+    blocks, refs = grouped(refs, counts)
+    *gates, ups, hidden_ref, by_gate_ref, by_up_ref, buffer, sems, both, both_sem = refs
+
+    @pl.when(pl.program_id(0) == 0)
+    def _():
+        unit = ups.shape[2] // PARTS
+        wide = ups.shape[0] * unit
+        for part in range(PARTS):
+            span = part * unit, (part + 1) * unit
+            start_columns(gates, span, both.at[:, part * wide : (part + 1) * wide], both_sem)
+            start = (PARTS + part) * wide
+            start_columns(chunks_of(ups, order_ref), span, both.at[:, start : start + wide], both_sem)
+
+    slot = fetch(blocks, buffer, sems, pl.program_id(0))
+
+    @pl.when(pl.program_id(0) == 0)
+    def _():
+        wait_whole(both, both_sem)
+
+    full = mm(buffer[slot], both[...])
+    wide = full.shape[1] // 2
+    gate, up = full[:, :wide], full[:, wide:]
+    sigmoid = 1.0 / (1.0 + jnp.exp(-gate))
+    silu = gate * sigmoid
+    hidden_ref[...] = (silu * up).astype(jnp.bfloat16)
+    by_gate_ref[...] = (up * (sigmoid + silu * (1.0 - sigmoid))).astype(jnp.bfloat16)
+    by_up_ref[...] = silu.astype(jnp.bfloat16)
+
+
+def hidden_units(order, blocks, gates, ups):
+    rows, model = block_shape(blocks)
+    count = rows * len(blocks)
+    share = ups.shape[0] * ups.shape[2]
+    counts = [len(found) for found in blocks]
+    return call(
+        functools.partial(hidden_kernel, counts),
+        (len(blocks),),
+        [ANYWHERE] * (sum(counts) + 1 + len(gates)),
+        [spec_down(rows, share)] * 3,
+        [array(count, share)] * 3,
+        fetch_scratch(blocks)
+        + [pltpu.VMEM((model, 2 * share), jnp.bfloat16), pltpu.SemaphoreType.DMA],
+        0,
+        25,
+        scalars=1,
+    )(order, *flat(blocks), *gates, ups)
+
+
+def ffn_back_kernel(counts, chunks, part, more, order_ref, *refs):
+    blocks, refs = grouped(refs, counts)
+    *gates, ups, downs, by_gate_ref, by_up_ref = refs[: chunks + 4]
+    before_ref = refs[chunks + 4] if more else None
+    out_ref, buffer, sems, both, both_sem, down, down_sem = refs[-7:]
+
+    @pl.when(pl.program_id(0) == 0)
+    def _():
+        wide = both.shape[1] // 2
+        unit = downs.shape[2]
+        span = part * unit, (part + 1) * unit
+        start_columns(chunks_of(downs, order_ref), (0, unit), down, down_sem)
+        start_columns(gates, span, both.at[:, :wide], both_sem)
+        start_columns(chunks_of(ups, order_ref), span, both.at[:, wide:], both_sem)
+
+    slot = fetch(blocks, buffer, sems, pl.program_id(0))
+
+    @pl.when(pl.program_id(0) == 0)
+    def _():
+        wait_whole(down, down_sem)
+        wait_whole(both, both_sem)
+
+    grad_hidden = mm(buffer[slot], down[...])
+    grad_gate = (grad_hidden * by_gate_ref[...].astype(jnp.float32)).astype(jnp.bfloat16)
+    grad_up = (grad_hidden * by_up_ref[...].astype(jnp.float32)).astype(jnp.bfloat16)
+    total = mm_nt(jnp.concatenate([grad_gate, grad_up], axis=1), both[...])
+    if more:
+        total = total + before_ref[...].astype(jnp.float32)
+    out_ref[...] = total.astype(jnp.bfloat16)
+
+
+def ffn_back(order, blocks, first, each, part, gates, ups, downs, by_gate, by_up, before):
+    rows, model = block_shape(blocks)
+    share = downs.shape[0] * downs.shape[2]
+    counts = [len(found) for found in blocks]
+    more = before is not None
+
+    def rows_of(wide, at=0):
+        return pl.BlockSpec((rows, wide), lambda i, *_: (first + each * i, at))
+
+    return call(
+        functools.partial(ffn_back_kernel, counts, len(gates), part, more),
+        (len(blocks),),
+        [ANYWHERE] * (sum(counts) + len(gates) + 2)
+        + [rows_of(share, part)] * 2
+        + [rows_of(model)] * more,
+        spec_down(rows, model),
+        array(len(blocks) * rows, model),
+        fetch_scratch(blocks)
+        + [pltpu.VMEM((model, 2 * share), jnp.bfloat16), pltpu.SemaphoreType.DMA]
+        + [pltpu.VMEM((model, share), jnp.bfloat16), pltpu.SemaphoreType.DMA],
+        0,
+        3 * len(blocks),
+        scalars=1,
+    )(order, *flat(blocks), *gates, ups, downs, by_gate, by_up, *([before] if more else []))
+
+
+def ffn_out_kernel(place_ref, order_ref, *refs):
+    downs, (hidden_ref, out_ref, down, down_sem) = refs[:PARTS], refs[PARTS:]
+
+    @pl.when(pl.program_id(0) == 0)
+    def _():
+        wide = down.shape[1] // PARTS
+        for part, ref in enumerate(downs):
+            start_columns(
+                chunks_of(ref, order_ref), (0, ref.shape[2]), down.at[:, part * wide : (part + 1) * wide], down_sem
+            )
+        wait_whole(down, down_sem)
+
+    out_ref[...] = mm_nt(hidden_ref[...], down[...]).astype(jnp.bfloat16)
+
+
+def ffn_out(place_row, order, hidden, downs, places):
+    count, share = hidden.shape
+    rows = count // places
+    model = downs[0].shape[1]
+    return call(
+        ffn_out_kernel,
+        (places,),
+        [ANYWHERE] * PARTS + [spec_down(rows, share)],
+        spec_placed(spec_down(rows, model)),
+        array(count, model),
+        [pltpu.VMEM((model, share), jnp.bfloat16), pltpu.SemaphoreType.DMA],
+        0,
+        17,
+        scalars=2,
+    )(place_row, order, *downs, hidden)
+
+
+def backward_kernel(
+    counts, length_ref, place_ref, *refs
+):
+    blocks, refs = grouped(refs, counts)
+    (
+    grad_ref, diff_ref, out_ref, denom_ref, q_ref, pq_ref, weights_ref,
+    v_ref, v_before, kt_ref, kt_before, pkt_ref, pkt_before, vt_ref, vt_before,
+    states_ref, map_ref, back_ref, cos_ref, sin_ref, up_ref, wt_ref,
+    pre_ref, gain_ref, fall_ref, give_ref, keep_ref, key_carry, value_carry, map_carry, later,
+    buffer, sems,
+    ) = refs
+    step = pl.num_programs(0) - 1 - pl.program_id(0)
+    group = q_ref.shape[0] // HEAD_SIZE
+    rows = q_ref.shape[1]
+    half = HEAD_SIZE // 2
+    quarter = WINDOW_KEYS
+    scale = 1.0 / math.sqrt(HEAD_SIZE)
+    second, third, third_far, fourth = bands()
+    short = jnp.bfloat16
+    per_block = grad_ref.shape[2]
+    inner = per_block // SUB
+
+    @pl.when(pl.program_id(0) == 0)
+    def _():
+        gain_ref[...] = jnp.zeros_like(gain_ref)
+        key_carry[...] = jnp.zeros_like(key_carry)
+        value_carry[...] = jnp.zeros_like(value_carry)
+        map_carry[...] = jnp.zeros_like(map_carry)
+        later[...] = jnp.zeros_like(later)
+        fall_ref[...] = jnp.zeros_like(fall_ref)
+
+    carried_keys, carried_values, carried_maps = key_carry[...], value_carry[...], map_carry[...]
+    later_now = later[...]
+    query_parts, map_parts, key_parts, value_parts, key_map_parts = [], [], [], [], []
+    for sub in reversed(range(rows // SUB)):
+        columns = slice(sub * SUB, (sub + 1) * SUB)
+        queries = side_by_side(q_ref, HEAD_SIZE, group, columns)
+        query_maps = side_by_side(pq_ref, 2 * HEAD_SIZE, group, columns)
+        if sub == 0:
+            values = jnp.concatenate([v_before[...], v_ref[:SUB]], axis=0)
+            keys_t = jnp.concatenate([kt_before[...], kt_ref[:, :SUB]], axis=1)
+            key_maps_t = jnp.concatenate([pkt_before[...], pkt_ref[:, :SUB]], axis=1)
+            values_before = vt_before[...]
+        else:
+            around = slice((sub - 1) * SUB, (sub + 1) * SUB)
+            values = v_ref[around]
+            keys_t, key_maps_t = kt_ref[:, around], pkt_ref[:, around]
+            values_before = vt_ref[:, (sub - 1) * SUB : sub * SUB]
+        at = step * rows + sub * SUB + lax.broadcasted_iota(jnp.int32, (HEAD_SIZE, SUB), 1)
+        inside = at < length_ref[0]
+        numers, denoms = [], []
+        for head in range(group):
+            base = head * HEAD_SIZE
+            span = slice(base, base + HEAD_SIZE)
+            place_in = slice(sub % inner * SUB, (sub % inner + 1) * SUB)
+            incoming = grad_ref[sub // inner, span, place_in].astype(jnp.float32) + 2.0 * diff_ref[span, columns]
+            incoming = jnp.where(inside, incoming.astype(short).astype(jnp.float32), 0.0)
+            inverse = 1.0 / denom_ref[head : head + 1, columns]
+            numers.append((incoming * inverse).astype(short))
+            denoms.append(
+                -jnp.sum(incoming * out_ref[span, columns], axis=0, keepdims=True) * inverse
+            )
+        grad_numer = jnp.concatenate(numers, axis=1)
+        grad_denom = jnp.concatenate(denoms, axis=1)
+        rank = lax.broadcasted_iota(jnp.int32, (ONES, group * SUB), 0)
+        denom_high = grad_denom.astype(short).astype(jnp.float32)
+        extra = jnp.where(
+            rank == 0, denom_high, jnp.where(rank == 1, grad_denom - denom_high, 0.0)
+        ).astype(short)
+        grad_both = jnp.concatenate([grad_numer, extra], axis=0)
+        weights = weights_ref[sub]
+        raw = mm(values, grad_numer)
+        scores, fars = [], []
+        for head in range(group):
+            lanes = slice(head * SUB, (head + 1) * SUB)
+            grad_weights = raw[:, lanes] + denoms[head]
+            if sub == 0:
+                kept = jnp.where(step > 0, grad_weights[: 2 * quarter], 0.0)
+                grad_weights = jnp.concatenate([kept, grad_weights[2 * quarter :]], axis=0)
+            by_score = grad_weights[quarter:] * weights[quarter:, lanes].astype(jnp.float32)
+            scores.append(
+                jnp.concatenate(
+                    [
+                        jnp.where(second, by_score[:quarter], 0.0),
+                        jnp.where(third, by_score[quarter : 2 * quarter], 0.0),
+                        jnp.where(fourth, by_score[2 * quarter :], 0.0),
+                    ],
+                    axis=0,
+                ).astype(short)
+            )
+            fars.append(
+                jnp.concatenate(
+                    [
+                        grad_weights[:quarter],
+                        jnp.where(second, 0.0, grad_weights[quarter : 2 * quarter]),
+                        jnp.where(third_far, grad_weights[2 * quarter : 3 * quarter], 0.0),
+                    ],
+                    axis=0,
+                ).astype(short)
+            )
+        grad_scores = jnp.concatenate(scores, axis=1)
+        grad_far = jnp.concatenate(fars, axis=1)
+        state_high, state_low = split_wide(jnp.transpose(states_ref[sub]))
+        query_parts.append(mm(keys_t[:, quarter:], grad_scores) * scale)
+        map_parts.append(
+            mm(key_maps_t[:, : 3 * quarter], grad_far)
+            + mm(
+                jnp.concatenate([state_high, state_low], axis=1),
+                jnp.concatenate([grad_both, grad_both], axis=0),
+            )
+        )
+        grad_keys = mm_nt(queries, grad_scores) * scale
+        grad_values = mm_nt(grad_numer, weights)
+        grad_key_maps = mm_nt(query_maps, grad_far)
+        key_parts.append(carried_keys + grad_keys[:, quarter:])
+        value_parts.append(carried_values + grad_values[:, SUB:])
+        key_map_parts.append(
+            jnp.concatenate(
+                [
+                    carried_maps[:, :quarter] + grad_key_maps[:, 2 * quarter :],
+                    carried_maps[:, quarter:],
+                ],
+                axis=1,
+            )
+        )
+        later_high, later_low = split_wide(jnp.transpose(later_now))
+        carried_keys = jnp.concatenate(
+            [jnp.zeros((HEAD_SIZE, quarter), jnp.float32), grad_keys[:, :quarter]], axis=1
+        )
+        carried_values = grad_values[:, :SUB] + mm(
+            later_now[:HEAD_SIZE].astype(short), key_maps_t[:, :SUB]
+        )
+        carried_maps = grad_key_maps[:, : 2 * quarter] + mm(
+            jnp.concatenate([later_high, later_low], axis=1),
+            jnp.concatenate([values_before, values_before], axis=0),
+        )
+        later_now = later_now + mm_nt(grad_both, query_maps)
+    key_carry[...], value_carry[...], map_carry[...] = carried_keys, carried_values, carried_maps
+    later[...] = later_now
+
+    def joined(parts, lanes=slice(None)):
+        return jnp.concatenate([part[:, lanes] for part in reversed(parts)], axis=1)
+
+    cosine, sine = cos_ref[...], sin_ref[...]
+    for head in range(group + 1):
+        base = head * HEAD_SIZE
+        span = slice(base, base + HEAD_SIZE)
+        lanes = slice(head * SUB, (head + 1) * SUB)
+        if head < group:
+            vector, direct = q_ref[span], joined(query_parts, lanes)
+            grad_maps = joined(map_parts, lanes)
+        else:
+            vector, direct, grad_maps = kt_ref[...], joined(key_parts), joined(key_map_parts)
+        plus, minus = soft_pair(mm(map_ref[span], vector))
+        grad_plus, grad_minus = grad_maps[:HEAD_SIZE], grad_maps[HEAD_SIZE:]
+        grad_logits = plus * (
+            grad_plus - jnp.sum(grad_plus * plus, axis=0, keepdims=True)
+        ) - minus * (grad_minus - jnp.sum(grad_minus * minus, axis=0, keepdims=True))
+        grad_logits = grad_logits.astype(short)
+        gain_ref[span] += mm_nt(vector, grad_logits)
+        total = direct + mm(back_ref[span], grad_logits)
+        low_half, high_half = halves_rotated(total[:half], total[half:], cosine, -sine)
+        pre_ref[base : base + half] = low_half.astype(short)
+        pre_ref[base + half : base + HEAD_SIZE] = high_half.astype(short)
+    width = (group + 2) * HEAD_SIZE
+    pre_ref[width - HEAD_SIZE : width] = joined(value_parts).astype(short)
+    pre_ref[width:] = mm_tn(up_ref[...], pre_ref[:width]).astype(short)
+    per_step = rows // per_block
+
+    def order(at):
+        return (pl.num_programs(0) - 1 - at // per_step) * per_step + lax.rem(at, per_step)
+
+    own_core = lax.rem(place_ref[0], 2)
+    for block in range(rows // per_block):
+        columns = slice(block * per_block, (block + 1) * per_block)
+        here = pre_ref[:, columns]
+        grad_normed = mm_tn(here, wt_ref[...]).astype(short)
+        slot = fetch(
+            blocks,
+            buffer,
+            sems,
+            pl.program_id(0) * (rows // per_block) + block,
+            lambda at: lax.bitwise_xor(order(at), place_ref[0]),
+        )
+        fall_ref[...] += mm(here[width:], buffer[slot])
+
+        @pl.when(own_core == block % 2)
+        def _():
+            keep_ref[...] = grad_normed
+
+        @pl.when(own_core != block % 2)
+        def _():
+            give_ref[...] = grad_normed
+
+
+def heads_back(
+    length, place_row, blocks, grad_att, difference, out_t, denom, q_t, pq_t, weights,
+    values, k_t, pk_t, v_t, states, maps_ahead, maps_back, cosine, sine, up_block, weights_t,
+):
+    places, query_width, per_block = grad_att.shape
+    count = places * per_block
+    rows = 2 * per_block
+    steps = count // rows
+    group = query_width // HEAD_SIZE
+    per_step = rows // SUB
+    counts = [len(found) for found in blocks]
+    width, spare = up_block.shape
+    model = weights_t.shape[1]
+    maps = pk_t.shape[0]
+    high = v_t.shape[0]
+    half = HEAD_SIZE // 2
+
+    def back(spec):
+        return pl.BlockSpec(spec.block_shape, lambda i, *_: spec.index_map(steps - 1 - i))
+
+    def by_chip(i, length_ref, place_ref):
+        return (lax.bitwise_xor(steps - 1 - i, place_ref[0] // 2), 0, 0)
+
+    def leading(*dims):
+        return pl.BlockSpec((per_step,) + dims, lambda i, *_: (i, 0, 0))
+
+    return call(
+        functools.partial(backward_kernel, counts),
+        (steps,),
+        [ANYWHERE] * sum(counts)
+        + [
+            back(pl.BlockSpec((2, query_width, per_block), lambda i, *_: (i, 0, 0))),
+            back(spec_across(query_width, rows)),
+            back(spec_across(query_width, rows)),
+            back(spec_across(group, rows)),
+            back(spec_across(query_width, rows)),
+            back(spec_across(group * maps, rows)),
+            back(leading(2 * SUB, group * SUB)),
+            back(spec_down(rows, HEAD_SIZE)),
+            back(before_down(rows, HEAD_SIZE)),
+            back(spec_across(HEAD_SIZE, rows)),
+            back(before_across(rows, HEAD_SIZE)),
+            back(spec_across(maps, rows)),
+            back(before_across(rows, maps)),
+            back(spec_across(high, rows)),
+            back(before_across(rows, high)),
+            back(leading(high, maps)),
+            spec_whole(*maps_ahead.shape),
+            spec_whole(*maps_back.shape),
+            back(spec_across(half, rows)),
+            back(spec_across(half, rows)),
+            spec_whole(width, spare),
+            spec_whole(width + spare, model),
+        ],
+        [
+            back(spec_across(width + spare, rows)),
+            spec_whole(*maps_back.shape),
+            spec_whole(spare, model),
+            pl.BlockSpec((None, per_block, model), by_chip),
+            pl.BlockSpec((None, per_block, model), by_chip),
+        ],
+        [
+            array(width + spare, count),
+            array(*maps_back.shape, dtype=jnp.float32),
+            array(spare, model, dtype=jnp.float32),
+            array(steps, per_block, model),
+            array(steps, per_block, model),
+        ],
+        [
+            pltpu.VMEM((HEAD_SIZE, SUB), jnp.float32),
+            pltpu.VMEM((HEAD_SIZE, SUB), jnp.float32),
+            pltpu.VMEM((maps, SUB), jnp.float32),
+            pltpu.VMEM((high, maps), jnp.float32),
+        ]
+        + fetch_scratch(blocks),
+        0,
+        30,
+        scalars=2,
+    )(
+        length, place_row, *flat(blocks), grad_att, difference, out_t, denom, q_t, pq_t, weights,
+        values, values, k_t, k_t, pk_t, pk_t, v_t, v_t,
+        states, maps_ahead, maps_back, cosine, sine, up_block, weights_t,
+    )
+
+
+def branch_kernel(
+    counts, place_ref, *refs
+):
+    blocks, refs = grouped(refs, counts)
+    (
+        att_ref, down_ref, up_ref, tokens_ref, gain_ref,
+        residual_ref, normed_ref, inverse_ref, narrow_ref, buffer, sems, total, slim,
+    ) = refs
+    step = pl.program_id(0)
+    slot = fetch(blocks, buffer, sems, step)
+
+    @pl.when(step == 0)
+    def _():
+        total[...] = tokens_ref[...].astype(jnp.float32)
+        slim[...] = jnp.zeros_like(slim)
+
+    total[...] += mm_tn(att_ref[...], buffer[slot])
+    slim[...] += mm_tn(att_ref[...], down_ref[...])
+
+    @pl.when(step == pl.num_programs(0) - 1)
+    def _():
+        narrow = slim[...].astype(jnp.bfloat16)
+        narrow_ref[...] = narrow
+        residual = total[...] + mm_nt(narrow, up_ref[...])
+        residual_ref[...] = residual
+        inverse = lax.rsqrt(jnp.mean(residual * residual, axis=-1, keepdims=True) + epsilon)
+        inverse_ref[...] = jnp.broadcast_to(inverse, inverse_ref.shape)
+        normed_ref[...] = (residual * inverse * gain_ref[...]).astype(jnp.bfloat16)
+
+
+def branch_out(place_row, blocks, att, down_wide, up_wide, tokens, gain):
+    places, query_width, rows = att.shape
+    model = tokens.shape[1]
+    spare = down_wide.shape[1]
+    counts = [len(found) for found in blocks]
+    wide = jnp.float32
+    return call(
+        functools.partial(branch_kernel, counts),
+        (places,),
+        [ANYWHERE] * sum(counts)
+        + [
+            spec_placed(spec_block(query_width, rows)),
+            spec_placed(spec_down(query_width, spare)),
+            spec_whole(model, spare),
+            spec_whole(rows, model),
+            spec_whole(1, model),
+        ],
+        [
+            spec_whole(rows, model),
+            spec_whole(rows, model),
+            spec_whole(rows, 128),
+            spec_whole(rows, spare),
+        ],
+        [
+            array(rows, model, dtype=wide),
+            array(rows, model),
+            array(rows, 128, dtype=wide),
+            array(rows, spare),
+        ],
+        fetch_scratch(blocks)
+        + [pltpu.VMEM((rows, model), wide), pltpu.VMEM((rows, spare), wide)],
+        0,
+        13,
+        scalars=1,
+    )(place_row, *flat(blocks), att, down_wide, up_wide, tokens, gain)
+
+
+def branch_back_kernel(counts, place_ref, *refs):
+    blocks, refs = grouped(refs, counts)
+    (
+        own_ref, from_x, late_x, late_y, from_y, residual_ref, inverse_ref, gain_ref, cot_ref,
+        down_ref, up_ref,
+        grad_att_ref, grad_ref, branch_ref, slim_ref, buffer, sems,
+    ) = refs
+    step = pl.program_id(0)
+    slot = fetch(blocks, buffer, sems, step)
+
+    @pl.when(step == 0)
+    def _():
+        wide = jnp.float32
+        middle = late_x.shape[0]
+        for start, part in enumerate(sums_of(own_ref, from_x, late_x, late_y, from_y)):
+            span = slice(start * middle, (start + 1) * middle)
+            residual, inverse = residual_ref[span], inverse_ref[span, :1]
+            scaled = part * gain_ref[...]
+            mean = jnp.mean(scaled * residual, axis=-1, keepdims=True)
+            grad = (
+                cot_ref[span].astype(wide)
+                + inverse * scaled
+                - residual * (inverse * inverse * inverse * mean)
+            )
+            grad_ref[span] = grad
+            branch_ref[span] = grad.astype(jnp.bfloat16)
+        slim_ref[...] = mm(branch_ref[...], up_ref[...])
+
+    slim = slim_ref[...].astype(jnp.bfloat16)
+    grad_att_ref[...] = (
+        mm_nt(buffer[slot], branch_ref[...]) + mm_nt(down_ref[...], slim)
+    ).astype(jnp.bfloat16)
+
+
+def branch_back(
+    place_row, blocks, sums, residual, inverse, gain, cotangent, down_wide, up_wide
+):
+    places = len(blocks)
+    rows, model = residual.shape
+    query_width = model // places
+    spare = down_wide.shape[1]
+    counts = [len(found) for found in blocks]
+    wide = jnp.float32
+    return call(
+        functools.partial(branch_back_kernel, counts),
+        (places,),
+        [ANYWHERE] * sum(counts)
+        + [spec_whole(*part.shape) for part in sums]
+        + [
+            spec_whole(rows, model),
+            spec_whole(rows, 128),
+            spec_whole(1, model),
+            spec_whole(rows, model),
+            spec_placed(spec_down(query_width, spare)),
+            spec_whole(model, spare),
+        ],
+        [
+            spec_placed(spec_block(query_width, rows)),
+            spec_whole(rows, model),
+            spec_whole(rows, model),
+            spec_whole(rows, spare),
+        ],
+        [
+            array(places, query_width, rows),
+            array(rows, model, dtype=wide),
+            array(rows, model),
+            array(rows, spare, dtype=wide),
+        ],
+        fetch_scratch(blocks),
+        0,
+        15,
+        scalars=1,
+    )(
+        place_row, *flat(blocks), *sums, residual, inverse, gain, cotangent, down_wide, up_wide
+    )
+
+
+def exchanged(value, bits):
+    count = lax.axis_size("seq")
+    return lax.ppermute(value, "seq", [(place, place ^ bits) for place in range(count)])
+
+
+def after(value, *others):
+    return pl.pallas_call(
+        lambda *refs: None,
+        out_shape=jax.ShapeDtypeStruct(value.shape, value.dtype),
+        in_specs=[pl.BlockSpec(memory_space=pl.ANY)] * (1 + len(others)),
+        out_specs=pl.BlockSpec(memory_space=pl.ANY),
+        input_output_aliases={0: 0},
+    )(value, *others)
+
+
+def halves(value):
+    middle = value.shape[0] // 2
+    return value[:middle], value[middle:]
+
+
+def regroup_kernel(*refs):
+    out_ref = refs[-1]
+    for number, ref in enumerate(refs[:-1]):
+        out_ref[number] = ref[...]
+
+
+def regroup(places, *matrices):
+    rows, wide = matrices[0].shape
+    unit = wide // places
+    return call(
+        regroup_kernel,
+        (places,),
+        [spec_across(rows, unit)] * len(matrices),
+        pl.BlockSpec((None, len(matrices), rows, unit), lambda i: (i, 0, 0, 0)),
+        array(places, len(matrices), rows, unit),
+        [],
+        0,
+        6,
+    )(*matrices)
+
+
+def ungroup_kernel(ref, *refs):
+    for number, out_ref in enumerate(refs):
+        out_ref[...] = ref[number]
+
+
+def ungroup(blocks):
+    places, count, rows, unit = blocks.shape
+    return call(
+        ungroup_kernel,
+        (places,),
+        [pl.BlockSpec((None, count, rows, unit), lambda i: (i, 0, 0, 0))],
+        [spec_down(rows, unit)] * count,
+        [array(places * rows, unit)] * count,
+        [],
+        0,
+        6,
+    )(blocks)
+
+
+def gather_first(value):
+    return exchanged(value, 1), exchanged(value, 2), exchanged(value, 4)
+
+
+def gather_rest(value, beside, along_x, along_y, *others):
+    upper, lower = halves(along_x)[0], halves(along_y)[1]
+    if others:
+        upper, lower = after(upper, *others), after(lower, *others)
+    first, second = exchanged(upper, 4), exchanged(lower, 2)
+    return [
+        (value,),
+        (beside,),
+        (along_x,),
+        (exchanged(along_x, 1),),
+        (along_y,),
+        (exchanged(along_y, 1),),
+        (first, second),
+        (exchanged(first, 1), exchanged(second, 1)),
+    ]
+
+
+def plane_gather(value):
+    return gather_rest(value, *gather_first(value))
+
+
+def core_sums_kernel(keep_ref, got_ref, own_ref, to_x, to_y, later_x, later_y):
+    wide, short = jnp.float32, jnp.bfloat16
+    middle = later_x.shape[0]
+
+    def both(bits, span=slice(None)):
+        return keep_ref[bits, span].astype(wide) + got_ref[bits, span].astype(wide)
+
+    upper, lower = slice(0, middle), slice(middle, None)
+    own_ref[...] = both(0)
+    to_x[upper], to_x[lower] = both(3, upper).astype(short), both(1, upper).astype(short)
+    to_y[upper], to_y[lower] = both(3, lower).astype(short), both(2, lower).astype(short)
+    later_x[...] = both(1, lower).astype(short)
+    later_y[...] = both(2, upper).astype(short)
+
+
+def core_sums(keep, got):
+    _, rows, model = keep.shape
+    wide = model // 4
+    block = pl.BlockSpec((4, rows, wide), lambda i: (0, 0, i))
+    return call(
+        core_sums_kernel,
+        (4,),
+        [block] * 2,
+        [spec_across(rows, wide)] * 3 + [spec_across(rows // 2, wide)] * 2,
+        [array(rows, model, dtype=jnp.float32)]
+        + [array(rows, model)] * 2
+        + [array(rows // 2, model)] * 2,
+        [],
+        0,
+        5,
+    )(keep, got)
+
+
+def scatter_first(give, keep):
+    own, to_x, to_y, later_x, later_y = core_sums(keep, exchanged(give, 1))
+    return own, exchanged(to_x, 2), exchanged(to_y, 4), later_x, later_y
+
+
+def scatter_rest(own, from_x, from_y, later_x, later_y, *others):
+    middle = later_x.shape[0]
+    wide, short = jnp.float32, jnp.bfloat16
+    if others:
+        later_x, later_y = after(later_x, *others), after(later_y, *others)
+    late_y = exchanged((later_y.astype(wide) + from_x[:middle].astype(wide)).astype(short), 4)
+    late_x = exchanged((later_x.astype(wide) + from_y[:middle].astype(wide)).astype(short), 2)
+    return own, from_x, late_x, late_y, from_y
+
+
+def sums_of(own_ref, from_x, late_x, late_y, from_y):
+    wide = jnp.float32
+    middle = late_x.shape[0]
+    return (
+        own_ref[:middle] + from_x[middle:].astype(wide) + late_y[...].astype(wide),
+        own_ref[middle:] + late_x[...].astype(wide) + from_y[middle:].astype(wide),
+    )
+
+
+def tokens_back_kernel(
+    own_ref, from_x, late_x, late_y, from_y, tokens_ref, inverse_ref, gain_ref, grad_ref, out_ref
+):
+    middle = late_x.shape[0]
+    for start, part in enumerate(sums_of(own_ref, from_x, late_x, late_y, from_y)):
+        span = slice(start * middle, (start + 1) * middle)
+        values, inverse = tokens_ref[span].astype(jnp.float32), inverse_ref[span, :1]
+        scaled = part * gain_ref[...]
+        mean = jnp.mean(scaled * values, axis=-1, keepdims=True)
+        out_ref[span] = (
+            grad_ref[span] + inverse * scaled - values * (inverse * inverse * inverse * mean)
+        ).astype(jnp.bfloat16)
+
+
+def tokens_back(sums, tokens, inverse, gain, grad):
+    rows, model = tokens.shape
+    return call(
+        tokens_back_kernel,
+        (1,),
+        [spec_whole(*part.shape) for part in (*sums, tokens, inverse, gain, grad)],
+        spec_whole(rows, model),
+        array(rows, model),
+        [],
+        0,
+        6,
+    )(*sums, tokens, inverse, gain, grad)
+
+
+def ring(value):
+    count = lax.axis_size("fsdp")
+    found = [value]
+    for _ in range(count - 1):
+        found.append(ring_step(found[-1]))
+    return found
+
+
+def ring_step(value):
+    count = lax.axis_size("fsdp")
+    return lax.ppermute(value, "fsdp", [(at, (at + 1) % count) for at in range(count)])
+
+
+def by_heads(
+    tokens,
+    lengths,
+    norm_attn,
+    norm_ffn,
+    w_query,
+    key_projection,
+    value_projection,
+    w_output,
+    w_gate,
+    w_up,
+    w_down,
+    down_query,
+    up_query,
+    key_down_matrix,
+    key_up_matrix,
+    value_down_matrix,
+    value_up_matrix,
+    down_output,
+    up_output,
+    feature_query,
+    key_feature_weight,
+    cotangent,
+):
+    places = lax.axis_size("seq")
+    lanes = lax.axis_size("fsdp")
+    rows = tokens.shape[1]
+    model = tokens.shape[2]
+    count = rows * places
+    group = QUERY_HEADS // KEY_VALUE_HEADS
+    query_width = group * HEAD_SIZE
+    width = query_width + 2 * HEAD_SIZE
+    rank = down_query.shape[1]
+    spare = 128
+    place = lax.axis_index("seq")
+    lane = lax.axis_index("fsdp")
+    place_row = place.astype(jnp.int32).reshape(1)
+    length = lax.dynamic_slice_in_dim(lengths, lane, 1)
+    bf16, f32 = jnp.bfloat16, jnp.float32
+    inputs_wide = tokens[0].astype(f32)
+    gain_attn = norm_attn.astype(f32)
+    gain_ffn = norm_ffn.astype(f32).reshape(1, model)
+
+    shard = w_query.shape[0]
+    by_place = jnp.concatenate(
+        [
+            w_query.reshape(shard, places, query_width),
+            key_projection.reshape(shard, places, HEAD_SIZE),
+            value_projection.reshape(shard, places, HEAD_SIZE),
+        ],
+        axis=2,
+    )
+    by_place = lax.all_to_all(jnp.moveaxis(by_place, 1, 0), "seq", 0, 0, tiled=True)
+    own_weights = lax.all_gather(by_place, "fsdp", axis=0)
+
+    inverse_attn = lax.rsqrt(jnp.mean(inputs_wide * inputs_wide, axis=-1, keepdims=True) + epsilon)
+    normed_all = plane_gather((inputs_wide * inverse_attn * gain_attn).astype(bf16))
+    across = normed_all[6]
+    down_block = jnp.concatenate(
+        [
+            down_query.T,
+            key_down_matrix.T,
+            value_down_matrix.T,
+            jnp.zeros((spare - 3 * rank, model), bf16),
+        ],
+        axis=0,
+    )
+
+    output_rows = lax.all_gather(w_output, "fsdp", axis=0)
+    swapped = after(regroup(places, w_gate, w_up, w_down), by_place)
+    swapped = lax.all_to_all(swapped, "seq", 0, 0, tiled=True)
+
+    def own_rows(matrix, size):
+        return lax.dynamic_slice_in_dim(matrix, place * size, size, 0)
+
+    up_own = (
+        own_rows(up_query, query_width),
+        own_rows(key_up_matrix, HEAD_SIZE),
+        own_rows(value_up_matrix, HEAD_SIZE),
+    )
+    up_block = jnp.concatenate(
+        [
+            jnp.pad(part, ((0, 0), (at * rank, spare - (at + 1) * rank)))
+            for at, part in enumerate(up_own)
+        ],
+        axis=0,
+    )
+    maps_back = jnp.concatenate(
+        [own_rows(feature_query, query_width), own_rows(key_feature_weight, HEAD_SIZE)], axis=0
+    )
+    maps_ahead = jnp.swapaxes(
+        maps_back.reshape(group + 1, HEAD_SIZE, HEAD_SIZE), 1, 2
+    ).reshape((group + 1) * HEAD_SIZE, HEAD_SIZE)
+    frequency = rope_base ** (-(jnp.arange(HEAD_SIZE // 2, dtype=f32) * 2.0) / HEAD_SIZE)
+    phase = jnp.arange(count, dtype=jnp.int32).astype(f32)[None, :] * frequency[:, None]
+    cosine, sine = jnp.cos(phase), jnp.sin(phase)
+    down_wide = jnp.pad(down_output, ((0, 0), (0, spare - rank)))
+    up_wide = jnp.pad(up_output, ((0, 0), (0, spare - rank)))
+
+    q_t, k_t, v_t, keys, values, pq_t, pk_t, key_maps, narrow_t, own_weights_t = project(
+        place_row, normed_all, own_weights, down_block, up_block, maps_ahead, cosine, sine
+    )
+    output_rows = after(output_rows.reshape(lanes * shard, model), q_t)
+    output_first = gather_first(output_rows)
+    att, out_t, denom, states, att_weights = attend(
+        length, q_t, pq_t, keys, key_maps, v_t, rows
+    )
+    own_gate, own_up, own_down = ungroup(swapped)
+    up_weights = lax.all_gather(own_up, "fsdp", axis=0)
+    unit = own_down.shape[1] // PARTS
+    down_weights = [
+        lax.all_gather(own_down[:, part * unit : (part + 1) * unit], "fsdp", axis=0)
+        for part in range(PARTS)
+    ]
+    gate_weights = ring(own_gate)
+    chunk_order = lax.rem(lane - jnp.arange(lanes) + lanes, lanes).astype(jnp.int32)
+    output_blocks = gather_rest(output_rows, *output_first, att)
+    att_all = lax.all_to_all(att, "seq", 0, 0, tiled=True)
+    middle = places // 2 + 1
+    taught = teach(
+        after(length, *output_first, gate_weights[1]), q_t, keys, v_t, att, 0, middle
+    )
+    residual, normed_ffn, inverse_ffn, narrow_out = branch_out(
+        after(place_row, taught[1]), output_blocks, att_all, down_wide, up_wide, tokens[0], gain_ffn
+    )
+    ffn_first = gather_first(normed_ffn)
+    difference, loss_rows = teach(
+        after(length, normed_ffn), q_t, keys, v_t, att, middle, places, taught
+    )
+    ffn_all = gather_rest(normed_ffn, *ffn_first, loss_rows)
+    cot_all = plane_gather(after(cotangent[0], *ffn_all[6], gate_weights[2]))
+    losses = jnp.sum(loss_rows[0].reshape(places, rows), axis=1)
+    hidden, by_gate, by_up = hidden_units(chunk_order, ffn_all, gate_weights, up_weights)
+    early = None
+    for part in range(PARTS - 1):
+        early = ffn_back(
+            chunk_order, cot_all, 0, 1, part, gate_weights, up_weights, down_weights[part], by_gate, by_up, early
+        )
+    by_chip = (places // 2, rows, model)
+    last = (PARTS - 1, gate_weights, up_weights, down_weights[-1], by_gate, by_up, early)
+    grad_give = ffn_back(chunk_order, cot_all[1::2], 1, 2, *last)
+    grad_keep = ffn_back(chunk_order, cot_all[0::2], 0, 2, *last)
+    grad_first = scatter_first(grad_give.reshape(by_chip), grad_keep.reshape(by_chip))
+    out_part = ffn_out(after(place_row, grad_first[0]), chunk_order, hidden, down_weights, places)
+
+    grad_sums = scatter_rest(*grad_first, out_part)
+    grad_att, grad_residual, grad_branch, grad_narrow_out = branch_back(
+        place_row,
+        output_blocks, grad_sums, residual, inverse_ffn, gain_ffn, cotangent[0],
+        down_wide, up_wide,
+    )
+    out_sum = lax.psum_scatter(out_part, "seq", scatter_dimension=0, tiled=True)
+    output = (residual + out_sum.astype(f32)).astype(bf16)
+    grad_att = lax.all_to_all(grad_att, "seq", 0, 0, tiled=True)
+    grad_up_output = mm_tn(narrow_out, grad_branch)[:rank]
+    grad_down_output = jnp.einsum(
+        "sft,tr->rsf", att_all, grad_narrow_out[:, :rank].astype(bf16), preferred_element_type=f32
+    ).reshape(rank, model)
+
+    grad_pre_t, grad_maps, grad_down_t, normed_give, normed_keep = heads_back(
+        length, place_row, normed_all, grad_att, difference, out_t, denom,
+        q_t, pq_t, att_weights, values, k_t, pk_t, v_t, states, maps_ahead, maps_back,
+        cosine, sine, up_block, own_weights_t,
+    )
+    normed_sums = scatter_rest(*scatter_first(normed_give, normed_keep))
+    grad_up_block = mm_nt(grad_pre_t[:width], narrow_t)
+    grad_down_t = grad_down_t[: 3 * rank]
+    grad_tokens = tokens_back(
+        normed_sums, tokens[0], jnp.broadcast_to(inverse_attn, (rows, spare)),
+        gain_attn.reshape(1, model), grad_residual,
+    )
+
+    devices = places * lanes
+    ahead = jnp.arange(devices)[None, :] >= (jnp.arange(places) * lanes + lane)[:, None]
+    running = jnp.sum(jnp.where(ahead, losses[:, None], 0.0), axis=0)
+    loss_row = jnp.pad(running[:, None], ((0, 0), (0, model // devices - 1))).reshape(1, model)
+    shared = jnp.concatenate([grad_down_t, grad_down_output, grad_up_output, loss_row], axis=0)
+    shared = after(jnp.moveaxis(shared.reshape(-1, devices, model // devices), 1, 0), normed_sums[0])
+    shared = jnp.sum(
+        lax.all_to_all(shared, ("seq", "fsdp"), 0, 0, tiled=True).reshape(shared.shape), axis=0
+    )
+
+    def columns(at):
+        return shared[at * rank : (at + 1) * rank].T
+
+    transfer_loss = shared[5 * rank, :1] / jnp.sum(lengths).astype(f32)
+
+    pieces = [
+        grad_maps[:query_width].reshape(lanes, -1),
+        grad_maps[query_width:].reshape(lanes, -1),
+        grad_up_block[:query_width, :rank].reshape(lanes, -1),
+        grad_up_block[query_width : query_width + HEAD_SIZE, rank : 2 * rank].reshape(lanes, -1),
+        grad_up_block[query_width + HEAD_SIZE :, 2 * rank : 3 * rank].reshape(lanes, -1),
+    ]
+    packed = after(jnp.concatenate(pieces, axis=1), normed_sums[0])
+    packed = jnp.sum(lax.all_to_all(packed, "fsdp", 0, 0, tiled=True).reshape(packed.shape), axis=0)
+    ends = [0]
+    for piece in pieces:
+        ends.append(ends[-1] + piece.shape[1])
+    map_query, map_key, up_q, up_k, up_v = (
+        packed[ends[at] : ends[at + 1]].reshape(-1, wide)
+        for at, wide in enumerate((HEAD_SIZE, HEAD_SIZE, rank, rank, rank))
+    )
+    return (
+        output[None],
+        grad_tokens[None],
+        columns(0),
+        up_q,
+        columns(1),
+        up_k,
+        columns(2),
+        up_v,
+        columns(3),
+        columns(4),
+        map_query,
+        map_key,
+        transfer_loss,
+    )
+
 
 def solution(mesh):
     placed = (
@@ -654,8 +2101,12 @@
         P(),
         P("fsdp", "seq", None),
     )
+    sizes = dict(mesh.shape)
+    heads_match = sizes["seq"] == KEY_VALUE_HEADS == 8 and (
+        QUERY_HEADS // KEY_VALUE_HEADS == sizes["fsdp"]
+    )
     return jax.shard_map(
-        local,
+        by_heads if heads_match else local,
         mesh=mesh,
         in_specs=placed,
         out_specs=(

time: 2730 us -> 600 us (0.22)
  waiting for transfers between devices: 1910 us -> 186 us
  matrix products: 479 us -> 2.65 us
  Pallas kernels: 0 us -> 240 us
  other arithmetic: 135 us -> 14.2 us
  local copies, waits for them, and re-layouts: 108 us -> 39.4 us
  starting transfers between devices: 4.69 us -> 45.7 us
    unnamed x32 -> x6, waiting for transfers between devices: 965 us -> 0.78 us
    all_gather x14 -> x5, waiting for transfers between devices: 676 us -> 0.07 us  [the longest x2 0.04 us: by_heads(): lax.all_gather(own_down[:, part * unit:(part + 1) * unit], 'fsdp', axis=0)]
    dot_general x174 -> x3, matrix products: 458 us -> 2.65 us  [the longest x1 2 us: mm_nt(): lax.dot_general(a, b, (((1,), (1,)), ((), ())), preferred_element_type=jn...]
    reduce_scatter x2 -> x1, waiting for transfers between devices: 266 us -> 0.01 us  [by_heads(): out_sum = lax.psum_scatter(out_part, 'seq', scatter_dimension=0, tiled=True)]
    pallas_call x0 -> x32, Pallas kernels: none -> 240 us  [the longest x3 50.7 us: ffn_back(): call(functools.partial(ffn_back_kernel, counts, len(gates), part, more),...]
    ppermute x2 -> x49, waiting for transfers between devices: 0.01 us -> 142 us  [the longest x46 121 us: exchanged(): lax.ppermute(value, 'seq', [(place, place ^ bits) for place in range(coun...]
    reduce_sum x22 -> x6, other arithmetic: 59.6 us -> 1.29 us  [the longest x1 0.63 us: by_heads(): transfer_loss = shared[5 * rank, :1] / jnp.sum(lengths).astype(f32)]
    unnamed x1 -> x0, blocking collectives: 46.2 us -> none
  transfers between devices with their start and end apart: 26 -> 59, of which waited for: 19 -> 24; matrix products, arithmetic and copies ran while one was open for 17% -> 8% of each run, Pallas kernels for 0% -> 37%
where the time goes in v2:
time: 600 us; the launch traced here: 592 us
  Pallas kernels  240 us (40%)
  waiting for transfers between devices  186 us (31%)
  starting transfers between devices  45.7 us (8%)
  blocking collectives  44.8 us (7%)
  local copies, waits for them, and re-layouts  39.4 us (7%)
  between operations  19.4 us (3%)
  other arithmetic  14.2 us (2%)
    ppermute x46, waiting for transfers between devices, exchanged(): lax.ppermute(value, 'seq', [(place, place ^ bits) for place in range(coun...  121 us
    pallas_call x3, Pallas kernels, ffn_back(): call(functools.partial(ffn_back_kernel, counts, len(gates), part, more),...  50.7 us
    all_to_all x1, waiting for transfers between devices, by_heads(): swapped = lax.all_to_all(swapped, 'seq', 0, 0, tiled=True)  36.8 us
    all_to_all x1, blocking collectives, by_heads(): grad_att = lax.all_to_all(grad_att, 'seq', 0, 0, tiled=True)  31.4 us
    pallas_call x1, Pallas kernels, heads_back(): call(functools.partial(backward_kernel, counts), (steps,), [ANYWHERE] * s...  30.4 us
    pallas_call x2, Pallas kernels, teach(): pl.pallas_call(functools.partial(teacher_kernel, first, end - first), gri...  28.9 us
    ppermute x46, starting transfers between devices, exchanged(): lax.ppermute(value, 'seq', [(place, place ^ bits) for place in range(coun...  25.8 us
    pallas_call x1, Pallas kernels, hidden_units(): call(functools.partial(hidden_kernel, counts), (len(blocks),), [ANYWHERE]...  25.7 us
  transfers between devices with their start and end apart: 59, of which 24 were waited for; matrix products, arithmetic and copies ran while one was open for 8% of the time, Pallas kernels for 37%

profile of v2, /device:TPU:0, one launch (start us, length us, event | category | flops | bytes accessed | tf_op | source)
XLA Modules:
  0.0 591.9 jit_solution(1155367998767212721)
XLA Ops:
  10.4 13.4 %all_to_all.34.refs_1_ = bf16[8,64,384]{2,1,0:T(8,128)(2,1)} all-to-all(bf16[8,64,384]{2,1,0:T(8,128)(2,1)S(1)} %maximum_bitcast_fusion.1), channel_id=1, replica_groups=mesh['seq'=8,'fsdp'=4] {'seq'}, dimensions={0} | all-to-all | bytes 786432 | tf_op jit(solution)/shard_map/all_to_all | solution.py:1911
  23.8 6.2 %shard_map.311.refs_0_ = bf16[8,3,256,256]{3,2,1,0:T(8,128)(2,1)} custom-call(bf16[256,2048]{1,0:T(8,128)(2,1)} %refs_0_.1, bf16[256,2048]{1,0:T(8,128)(2,1)} %refs_1_.1, bf16[256,2048]{1,0:T(8,128)(2,1)} %refs_2_.1), custom_call_target="tpu_custom_call" | custom-call | flops 6899999744 | bytes 1 | tf_op jit(solution)/shard_map/pallas_call | solution.py:1705
  30.1 4.6 all-to-all-start.1
  35.8 36.8 %all-to-all-done.1.ref = bf16[8,3,256,256]{3,2,1,0:T(8,128)(2,1)} async-done(((bf16[8,3,256,256]{3,2,1,0:T(8,128)(2,1)}), bf16[8,3,256,256]{3,2,1,0:T(8,128)(2,1)}, u32[]{:S(2)}, u32[]{:S(2)}) %all-to-all-start.1) | async-done | bytes 3145760 | tf_op jit(solution)/shard_map/all_to_all | solution.py:1929
  72.6 6.1 %shard_map.313 = (bf16[2048,256]{1,0:T(8,128)(2,1)}, bf16[2048,256]{1,0:T(8,128)(2,1)}, bf16[2048,256]{1,0:T(8,128)(2,1)}) custom-call(bf16[8,3,256,256]{3,2,1,0:T(8,128)(2,1)} %all-to-all-done.1.ref), custom_call_target="tpu_custom_call" | custom-call | flops 6899999744 | bytes 1 | tf_op jit(solution)/shard_map/pallas_call | solution.py:1724
  84.5 19.1 %collective-permute-done.1.refs_2_ = bf16[256,2048]{1,0:T(8,128)(2,1)S(1)} collective-permute-done((bf16[256,2048]{1,0:T(8,128)(2,1)S(1)}, bf16[256,2048]{1,0:T(8,128)(2,1)S(1)}, u32[]{:S(2)}, u32[]{:S(2)}) %collective-permute-start.1) | collective-permute-done | bytes 1048608 | tf_op jit(solution)/shard_map/ppermute | solution.py:1678
  104.1 1.3 collective-permute-done.3.refs_4_
  109.8 6.6 %collective-permute-done.5.refs_6_ = bf16[128,2048]{1,0:T(8,128)(2,1)} collective-permute-done((bf16[128,2048]{1,0:T(8,128)(2,1)S(1)}, bf16[128,2048]{1,0:T(8,128)(2,1)}, u32[]{:S(2)}, u32[]{:S(2)}) %collective-permute-start.5) | collective-permute-done | bytes 524320 | tf_op jit(solution)/shard_map/ppermute | solution.py:1678
  116.4 2.7 collective-permute-done.6.refs_7_
  119.2 1.8 multiply_sine_fusion
  122.1 16.8 %shard_map.309 = (bf16[256,2048]{1,0:T(8,128)(2,1)}, bf16[64,2048]{1,0:T(8,128)(2,1)}, bf16[80,2048]{1,0:T(8,128)(2,1)}, bf16[2048,64]{1,0:T(8,128)(2,1)}, bf16[...) custom-call(s32[1]{0:T(128)} %bitcast.place_ref, ...), custom_call_target="tpu_custom_call" | custom-call | flops 19549999104 | bytes 1 | tf_op jit(solution)/shard_map/pallas_call | solution.py:859
  140.4 1.5 collective-permute-start.11
  141.8 1.6 collective-permute-start.12
  143.5 10.0 %shard_map.315 = (bf16[8,256,256]{2,1,0:T(8,128)(2,1)}, f32[256,2048]{1,0:T(8,128)}, f32[4,2048]{1,0:T(4,128)}, f32[16,80,128]{2,1,0:T(8,128)}, bf16[16,256,512]{2,1,0:T(8,128)(2,1)}) custom-call(s32[1]{0:T(128)} %dynamic_slice.18.length_ref, bf16[256,2048]{1,0:T(8,128)(2,1)} %get-tuple-element.61.refs_1_.q_ref.refs_14_, ...), custom_call_target="tpu_custom_call" | custom-call | flops 11500000256 | bytes 1 | tf_op jit(solution)/shard_map/pallas_call | solution.py:1005
  153.5 11.2 %collective-permute-done.10.refs_2_ = bf16[256,2048]{1,0:T(8,128)(2,1)S(1)} collective-permute-done((bf16[256,2048]{1,0:T(8,128)(2,1)}, bf16[256,2048]{1,0:T(8,128)(2,1)S(1)}, u32[]{:S(2)}, u32[]{:S(2)}) %collective-permute-start.10) | collective-permute-done | bytes 1048608 | tf_op jit(solution)/shard_map/ppermute | solution.py:1678
  167.3 1.7 collective-permute-start.16
  173.4 3.6 all-to-all-start.2
  177.0 2.3 fusion.18
  180.5 11.4 %collective-permute-done.12.refs_4_.refs_11_.refs_6_ = bf16[2048,256]{1,0:T(8,128)(2,1)} collective-permute-done((bf16[2048,256]{1,0:T(8,128)(2,1)}, bf16[2048,256]{1,0:T(8,128)(2,1)}, u32[]{:S(2)}, u32[]{:S(2)}) %collective-permute-start.12) | collective-permute-done | bytes 1048608 | tf_op jit(solution)/shard_map/ppermute | solution.py:1856
  193.1 12.9 %shard_map.316 = (f32[256,2048]{1,0:T(8,128)}, f32[8,2048]{1,0:T(8,128)}) custom-call(s32[1]{0:T(128)} %shard_map.314.length_ref, bf16[256,2048]{1,0:T(8,128)(2,1)} %get-tuple-element.61.refs_1_.q_ref.refs_14_, bf16[2048,64]{1,0:T(8,128)(2,1)} %get-tuple-element.63.k_ref.k_before, bf16[80,2048]{1,0:T(8,128)(2,1)} %get-tuple-element.64.vt_ref.vt_before.refs_23_.refs_24_, ...), custom_call_target="tpu_custom_call" | custom-call | flops 18400000000 | bytes 1 | tf_op jit(solution)/shard_map/pallas_call | solution.py:1102
  207.6 13.0 %shard_map.320 = (f32[256,2048]{1,0:T(8,128)}, bf16[256,2048]{1,0:T(8,128)(2,1)}, f32[256,128]{1,0:T(8,128)}, bf16[256,128]{1,0:T(8,128)(2,1)}) custom-call(s32[1]{0:T(128)} %shard_map.317.place_ref, bf16[256,2048]{1,0:T(8,128)(2,1)} %shard_map.310.refs_0_, bf16[256,2048]{1,0:T(8,128)(2,1)} %collective-permute-done.9.refs_1_, bf16[256,2048]{1,0:T(8,128)(2,1)} %copy-done.6, ...), custom_call_target="tpu_custom_call" | custom-call | flops 14949999616 | bytes 1 | tf_op jit(solution)/shard_map/pallas_call | solution.py:1568
  221.0 1.4 collective-permute-start.21
  222.9 16.0 %shard_map.322 = (f32[256,2048]{1,0:T(8,128)}, f32[8,2048]{1,0:T(8,128)}) custom-call(s32[1]{0:T(128)} %shard_map.321.length_ref, bf16[256,2048]{1,0:T(8,128)(2,1)} %get-tuple-element.61.refs_1_.q_ref.refs_14_, bf16[2048,64]{1,0:T(8,128)(2,1)} %get-tuple-element.63.k_ref.k_before, ...), custom_call_target="tpu_custom_call", output_to_operand_aliasing={{0}: (5, {}), {1}: (6, {})} | custom-call | flops 18400000000 | bytes 1 | tf_op jit(solution)/shard_map/pallas_call | solution.py:1102
  238.8 7.3 %collective-permute-done.19.refs_2_ = bf16[256,2048]{1,0:T(8,128)(2,1)} collective-permute-done((bf16[256,2048]{1,0:T(8,128)(2,1)}, bf16[256,2048]{1,0:T(8,128)(2,1)}, u32[]{:S(2)}, u32[]{:S(2)}) %collective-permute-start.19) | collective-permute-done | bytes 1048608 | tf_op jit(solution)/shard_map/ppermute | solution.py:1678
  246.1 1.9 slice.186.refs_0_
  248.6 1.9 slice.187.refs_0_
  252.4 4.4 collective-permute-done.23.refs_3_.refs_12_.refs_7_
  256.8 4.4 collective-permute-done.20.refs_1_.refs_6_
  261.3 2.3 collective-permute-done.22.refs_2_.refs_7_
  265.4 1.8 collective-permute-start.28
  267.4 19.5 %collective-permute-done.24.refs_2_.refs_1_ = bf16[256,2048]{1,0:T(8,128)(2,1)S(1)} collective-permute-done((bf16[256,2048]{1,0:T(8,128)(2,1)}, bf16[256,2048]{1,0:T(8,128)(2,1)S(1)}, u32[]{:S(2)}, u32[]{:S(2)}) %collective-permute-start.24) | collective-permute-done | bytes 1048608 | tf_op jit(solution)/shard_map/ppermute | solution.py:1678
  288.0 5.0 collective-permute-done.28.refs_13_.refs_8_
  294.1 1.2 collective-permute-start.27
  296.8 9.8 %collective-permute-done.26.refs_6_.refs_3_ = bf16[128,2048]{1,0:T(8,128)(2,1)} collective-permute-done((bf16[128,2048]{1,0:T(8,128)(2,1)S(1)}, bf16[128,2048]{1,0:T(8,128)(2,1)}, u32[]{:S(2)}, u32[]{:S(2)}) %collective-permute-start.26) | collective-permute-done | bytes 524320 | tf_op jit(solution)/shard_map/ppermute | solution.py:1678
  307.4 25.7 %shard_map.326 = (bf16[2048,1024]{1,0:T(8,128)(2,1)}, bf16[2048,1024]{1,0:T(8,128)(2,1)}, bf16[2048,1024]{1,0:T(8,128)(2,1)}) custom-call(s32[4]{0:T(128)} %compare_select_fusion.order_ref, bf16[256,2048]{1,0:T(8,128)(2,1)} %get-tuple-element.70.refs_1_.refs_0_, bf16[256,2048]{1,0:T(8,128)(2,1)} %copy-done.40, ...), custom_call_target="tpu_custom_call" | custom-call | flops 28750000128 | bytes 1 | tf_op jit(solution)/shard_map/pallas_call | solution.py:1149
  334.5 21.9 %shard_map.327.refs_13_ = bf16[2048,2048]{1,0:T(8,128)(2,1)} custom-call(s32[4]{0:T(128)} %compare_select_fusion.order_ref, bf16[256,2048]{1,0:T(8,128)(2,1)} %shard_map.325.refs_0_, bf16[256,2048]{1,0:T(8,128)(2,1)} %copy-done.42, bf16[256,2048]{1,0:T(8,128)(2,1)} %copy-done.23, bf16[256,2048]{1,0:T(8,128)(2,1)} %collective-permute-done.35.refs_3_.refs_1_, ...), custom_call_target="tpu_custom_call" | custom-call | flops 27599998976 | bytes 1 | tf_op jit(solution)/shard_map/pallas_call | solution.py:1203
  356.4 14.4 %shard_map.329 = bf16[1024,2048]{1,0:T(8,128)(2,1)} custom-call(s32[4]{0:T(128)} %compare_select_fusion.order_ref, bf16[256,2048]{1,0:T(8,128)(2,1)} %copy-done.42, bf16[256,2048]{1,0:T(8,128)(2,1)} %collective-permute-done.35.refs_3_.refs_1_, bf16[256,2048]{1,0:T(8,128)(2,1)} %collective-permute-done.36.refs_5_.refs_2_, bf16[128,2048]{1,0:T(8,128)(2,1)} %copy-done.46, ...), custom_call_target="tpu_custom_call" | custom-call | flops 13799999488 | bytes 1 | tf_op jit(solution)/shard_map/pallas_call | solution.py:1203
  371.4 14.4 %shard_map.328 = bf16[1024,2048]{1,0:T(8,128)(2,1)} custom-call(s32[4]{0:T(128)} %compare_select_fusion.order_ref, bf16[256,2048]{1,0:T(8,128)(2,1)} %shard_map.325.refs_0_, bf16[256,2048]{1,0:T(8,128)(2,1)} %copy-done.23, bf16[256,2048]{1,0:T(8,128)(2,1)} %copy-done.24, bf16[128,2048]{1,0:T(8,128)(2,1)} %collective-permute-done.26.refs_6_.refs_3_, ...), custom_call_target="tpu_custom_call" | custom-call | flops 13799999488 | bytes 1 | tf_op jit(solution)/shard_map/pallas_call | solution.py:1203
  385.9 2.0 copy-done.38
  387.8 6.3 %shard_map.330 = (f32[256,2048]{1,0:T(8,128)}, bf16[256,2048]{1,0:T(8,128)(2,1)}, bf16[256,2048]{1,0:T(8,128)(2,1)}, bf16[128,2048]{1,0:T(8,128)(2,1)}, bf16[128,2048]{1,0:T(8,128)(2,1)}) custom-call(bf16[4,256,2048]{2,1,0:T(8,128)(2,1)} %bitcast.81, bf16[4,256,2048]{2,1,0:T(8,128)(2,1)} %copy-done.38), custom_call_target="tpu_custom_call" | custom-call | flops 5750000128 | bytes 1 | tf_op jit(solution)/shard_map/pallas_call | solution.py:1780
  394.1 1.2 collective-permute-start.40
  395.3 1.4 collective-permute-start.41
  397.2 16.3 %shard_map.332.refs_1_ = bf16[2048,2048]{1,0:T(8,128)(2,1)} custom-call(s32[1]{0:T(128)} %shard_map.331.place_ref, s32[4]{0:T(128)} %compare_select_fusion.order_ref, bf16[4,2048,128]{2,1,0:T(8,128)(2,1)} %bitcast.76, bf16[4,2048,128]{2,1,0:T(8,128)(2,1)} %bitcast.79, bf16[2048,1024]{1,0:T(8,128)(2,1)} %get-tuple-element.78.refs_2_), custom_call_target="tpu_custom_call" | custom-call | flops 19549999104 | bytes 1 | tf_op jit(solution)/shard_map/pallas_call | solution.py:1239
  413.6 6.9 %collective-permute-done.41.refs_14_ = bf16[256,2048]{1,0:T(8,128)(2,1)S(1)} collective-permute-done((bf16[256,2048]{1,0:T(8,128)(2,1)}, bf16[256,2048]{1,0:T(8,128)(2,1)S(1)}, u32[]{:S(2)}, u32[]{:S(2)}) %collective-permute-start.41) | collective-permute-done | bytes 1048608 | tf_op jit(solution)/shard_map/ppermute | solution.py:1678
  421.4 1.5 add_convert_fusion.3
  423.9 9.7 %collective-permute-done.42.refs_12_ = bf16[128,2048]{1,0:T(8,128)(2,1)} collective-permute-done((bf16[128,2048]{1,0:T(8,128)(2,1)S(1)}, bf16[128,2048]{1,0:T(8,128)(2,1)}, u32[]{:S(2)}, u32[]{:S(2)}) %collective-permute-start.42) | collective-permute-done | bytes 524320 | tf_op jit(solution)/shard_map/ppermute | solution.py:1678
  433.6 1.8 collective-permute-done.43.refs_13_
  435.5 15.3 %shard_map.335 = (bf16[8,256,256]{2,1,0:T(8,128)(2,1)}, f32[256,2048]{1,0:T(8,128)}, bf16[256,2048]{1,0:T(8,128)(2,1)}, f32[256,128]{1,0:T(8,128)}) custom-call(s32[1]{0:T(128)} %bitcast.place_ref, bf16[256,2048]{1,0:T(8,128)(2,1)} %shard_map.310.refs_0_, bf16[256,2048]{1,0:T(8,128)(2,1)} %collective-permute-done.9.refs_1_, bf16[256,2048]{1,0:T(8,128)(2,1)} %copy-done.6, ...), custom_call_target="tpu_custom_call" | custom-call | flops 17250000896 | bytes 1 | tf_op jit(solution)/shard_map/pallas_call | solution.py:1642
  450.8 31.4 %all_to_all.35.refs_10_ = bf16[8,256,256]{2,1,0:T(8,128)(2,1)} all-to-all(bf16[8,256,256]{2,1,0:T(8,128)(2,1)} %get-tuple-element.84), channel_id=1, replica_groups=mesh['seq'=8,'fsdp'=4] {'seq'}, dimensions={0} | all-to-all | bytes 2097152 | tf_op jit(solution)/shard_map/all_to_all | solution.py:2012
  482.2 30.4 %shard_map.336 = (bf16[512,2048]{1,0:T(8,128)(2,1)}, f32[320,64]{1,0:T(8,128)}, f32[128,2048]{1,0:T(8,128)}, bf16[4,256,2048]{2,1,0:T(8,128)(2,1)}, bf16[4,256,2048]{2,1,0:T(8,128)(2,1)}) custom-call(s32[1]{0:T(128)} %dynamic_slice.18.length_ref, s32[1]{0:T(128)} %bitcast.place_ref, bf16[256,2048]{1,0:T(8,128)(2,1)} %copy-done.13, ...), custom_call_target="tpu_custom_call" | custom-call | flops 34500001792 | bytes 1 | tf_op jit(solution)/shard_map/pallas_call | solution.py:1473
  515.1 2.0 fusion.3
  517.1 3.1 collective-permute-done.44.got_ref
  520.2 6.1 %shard_map.337 = (f32[256,2048]{1,0:T(8,128)}, bf16[256,2048]{1,0:T(8,128)(2,1)}, bf16[256,2048]{1,0:T(8,128)(2,1)}, bf16[128,2048]{1,0:T(8,128)(2,1)}, bf16[128,2048]{1,0:T(8,128)(2,1)}) custom-call(bf16[4,256,2048]{2,1,0:T(8,128)(2,1)} %get-tuple-element.94.keep_ref, bf16[4,256,2048]{2,1,0:T(8,128)(2,1)} %collective-permute-done.44.got_ref), custom_call_target="tpu_custom_call" | custom-call | flops 5750000128 | bytes 1 | tf_op jit(solution)/shard_map/pallas_call | solution.py:1780
  530.4 2.4 reshape.203
  532.7 1.7 copy.134
  534.4 3.4 all-to-all-start.5
  537.8 13.9 %collective-permute-done.46.from_y = bf16[256,2048]{1,0:T(8,128)(2,1)S(1)} collective-permute-done((bf16[256,2048]{1,0:T(8,128)(2,1)}, bf16[256,2048]{1,0:T(8,128)(2,1)S(1)}, u32[]{:S(2)}, u32[]{:S(2)}) %collective-permute-start.46) | collective-permute-done | bytes 1048608 | tf_op jit(solution)/shard_map/ppermute | solution.py:1678
  552.0 3.8 all-to-all-start.4
  555.9 1.2 add_convert_fusion.1
  557.0 1.9 collective-permute-start.48
  564.0 6.2 %all-to-all-done.4 = f32[32,1,2624]{2,1,0:T(1,128)S(1)} async-done(((f32[32,1,2624]{2,1,0:T(1,128)}), f32[32,1,2624]{2,1,0:T(1,128)S(1)}, u32[]{:S(2)}, u32[]{:S(2)}) %all-to-all-start.4) | async-done | bytes 335904 | tf_op jit(solution)/shard_map/all_to_all | solution.py:2038
  570.7 1.5 reduce.5
  575.3 5.7 shard_map.338
  580.9 2.5 fusion.5
  (305 shorter events, 54.7 us)
Async XLA Ops:
  7.2 76.4 %copy-start = (bf16[2048,64]{0,1:T(8,128)(2,1)S(1)}, bf16[2048,64]{0,1:T(8,128)(2,1)}, u32[]{:S(2)}) copy-start(bf16[2048,64]{0,1:T(8,128)(2,1)} %param.41) | copy-start | bytes 786436
  7.2 114.1 %all-gather.13.cloned.1.call-start = ((), (), s32[]{:S(2)}) async-start(), calls=%async_computation.9 | async-start | bytes 1966080 | tf_op jit(solution)/shard_map/all_gather | solution.py:1912
  30.1 42.5 %all-to-all-start.1 = ((bf16[8,3,256,256]{3,2,1,0:T(8,128)(2,1)}), bf16[8,3,256,256]{3,2,1,0:T(8,128)(2,1)}, u32[]{:S(2)}, u32[]{:S(2)}) async-start(bf16[8,3,256,256]{3,2,1,0:T(8,128)(2,1)} %shard_map.312), calls=%async_computation.1 | async-start | bytes 6291456 | tf_op jit(solution)/shard_map/all_to_all | solution.py:1929
  34.7 104.2 %all-gather.11.cloned.1.call-start = ((), (), s32[]{:S(2)}) async-start(), calls=%async_computation.8 | async-start | bytes 1310720 | tf_op jit(solution)/shard_map/all_gather | solution.py:1927
  35.4 272.0 %all-gather.15.cloned.1.call-start = ((), (), s32[]{:S(2)}) async-start(), calls=%async_computation.10 | async-start | bytes 5242880 | tf_op jit(solution)/shard_map/all_gather | solution.py:1967
  35.5 43.2 %copy-start.28 = (f32[2048]{0:T(1024)}, f32[2048]{0:T(1024)S(1)}, u32[]{:S(2)}) copy-start(f32[2048]{0:T(1024)S(1)} %convert_element_type.81) | copy-start | bytes 24580
  79.6 41.7 %copy-start.13 = (bf16[256,2048]{1,0:T(8,128)(2,1)}, bf16[256,2048]{1,0:T(8,128)(2,1)S(1)}, u32[]{:S(2)}) copy-start(bf16[256,2048]{1,0:T(8,128)(2,1)S(1)} %fusion.2.refs_0_) | copy-start | bytes 3145732
  79.6 24.0 %collective-permute-start.1 = (bf16[256,2048]{1,0:T(8,128)(2,1)S(1)}, bf16[256,2048]{1,0:T(8,128)(2,1)S(1)}, u32[]{:S(2)}, u32[]{:S(2)}) collective-permute-start(bf16[256,2048]{1,0:T(8,128)(2,1)S(1)} %fusion.2.refs_0_), channel_id=1, source_target_pairs={{0,8},{4,12},{8,0},{12,4},{16,24},{20,28},{24,16},{28,20},{1,9},{5... | collective-permute-start | bytes 3145736 | tf_op jit(solution)/shard_map/ppermute | solution.py:1678
  80.2 25.2 %collective-permute-start.3 = (bf16[256,2048]{1,0:T(8,128)(2,1)S(1)}, bf16[256,2048]{1,0:T(8,128)(2,1)}, u32[]{:S(2)}, u32[]{:S(2)}) collective-permute-start(bf16[256,2048]{1,0:T(8,128)(2,1)S(1)} %fusion.2.refs_0_), channel_id=1, source_target_pairs={{0,16},{4,20},{8,24},{12,28},{16,0},{20,4},{24,8},{28,12},{1,17},{... | collective-permute-start | bytes 3145736 | tf_op jit(solution)/shard_map/ppermute | solution.py:1678
  80.9 40.1 %collective-permute-start = (bf16[256,2048]{1,0:T(8,128)(2,1)S(1)}, bf16[256,2048]{1,0:T(8,128)(2,1)}, u32[]{:S(2)}, u32[]{:S(2)}) collective-permute-start(bf16[256,2048]{1,0:T(8,128)(2,1)S(1)} %fusion.2.refs_0_), channel_id=1, source_target_pairs={{0,4},{4,0},{8,12},{12,8},{16,20},{20,16},{24,28},{28,24},{1,5},{5... | collective-permute-start | bytes 3145736 | tf_op jit(solution)/shard_map/ppermute | solution.py:1678
  83.7 55.1 %copy-start.18 = (bf16[320,64]{1,0:T(8,128)(2,1)}, bf16[320,64]{1,0:T(8,128)(2,1)S(1)}, u32[]{:S(2)}) copy-start(bf16[320,64]{1,0:T(8,128)(2,1)S(1)} %pad_maximum_fusion.refs_27_) | copy-start | bytes 122884
  103.7 12.8 %collective-permute-start.5 = (bf16[128,2048]{1,0:T(8,128)(2,1)S(1)}, bf16[128,2048]{1,0:T(8,128)(2,1)}, u32[]{:S(2)}, u32[]{:S(2)}) collective-permute-start(bf16[128,2048]{1,0:T(8,128)(2,1)S(1)} %slice.182), channel_id=1, source_target_pairs={{0,16},{4,20},{8,24},{12,28},{16,0},{20,4},{24,8},{28,12},{1,17},{... | collective-permute-start | bytes 1572872 | tf_op jit(solution)/shard_map/ppermute | solution.py:1678
  106.4 12.7 %collective-permute-start.6 = (bf16[128,2048]{1,0:T(8,128)(2,1)S(1)}, bf16[128,2048]{1,0:T(8,128)(2,1)}, u32[]{:S(2)}, u32[]{:S(2)}) collective-permute-start(bf16[128,2048]{1,0:T(8,128)(2,1)S(1)} %slice.183), channel_id=1, source_target_pairs={{0,8},{4,12},{8,0},{12,4},{16,24},{20,28},{24,16},{28,20},{1,9},{5... | collective-permute-start | bytes 1572872 | tf_op jit(solution)/shard_map/ppermute | solution.py:1678
  107.0 14.0 %collective-permute-start.2 = (bf16[256,2048]{1,0:T(8,128)(2,1)S(1)}, bf16[256,2048]{1,0:T(8,128)(2,1)}, u32[]{:S(2)}, u32[]{:S(2)}) collective-permute-start(bf16[256,2048]{1,0:T(8,128)(2,1)S(1)} %collective-permute-done.1.refs_2_), channel_id=1, source_target_pairs={{0,4},{4,0},{8,12},{12,8},{16,20},{20,16},{24,28},{28,24},{1,5},{5... | collective-permute-start | bytes 3145736 | tf_op jit(solution)/shard_map/ppermute | solution.py:1678
  107.0 14.0 %collective-permute-start.4 = (bf16[256,2048]{1,0:T(8,128)(2,1)}, bf16[256,2048]{1,0:T(8,128)(2,1)}, u32[]{:S(2)}, u32[]{:S(2)}) collective-permute-start(bf16[256,2048]{1,0:T(8,128)(2,1)} %collective-permute-done.3.refs_4_), channel_id=1, source_target_pairs={{0,4},{4,0},{8,12},{12,8},{16,20},{20,16},{24,28},{28,24},{1,5},{5... | collective-permute-start | bytes 3145736 | tf_op jit(solution)/shard_map/ppermute | solution.py:1678
  116.4 4.6 collective-permute-start.7
  119.2 2.1 collective-permute-start.8
  138.9 41.5 %collective-permute-start.9 = (bf16[256,2048]{1,0:T(8,128)(2,1)}, bf16[256,2048]{1,0:T(8,128)(2,1)}, u32[]{:S(2)}, u32[]{:S(2)}) collective-permute-start(bf16[256,2048]{1,0:T(8,128)(2,1)} %shard_map.310.refs_0_), channel_id=1, source_target_pairs={{0,4},{4,0},{8,12},{12,8},{16,20},{20,16},{24,28},{28,24},{1,5},{5... | collective-permute-start | bytes 3145736 | tf_op jit(solution)/shard_map/ppermute | solution.py:1678
  139.4 25.4 %collective-permute-start.10 = (bf16[256,2048]{1,0:T(8,128)(2,1)}, bf16[256,2048]{1,0:T(8,128)(2,1)S(1)}, u32[]{:S(2)}, u32[]{:S(2)}) collective-permute-start(bf16[256,2048]{1,0:T(8,128)(2,1)} %shard_map.310.refs_0_), channel_id=1, source_target_pairs={{0,8},{4,12},{8,0},{12,4},{16,24},{20,28},{24,16},{28,20},{1,9},{5... | collective-permute-start | bytes 3145736 | tf_op jit(solution)/shard_map/ppermute | solution.py:1678
  140.4 26.0 %collective-permute-start.11 = (bf16[256,2048]{1,0:T(8,128)(2,1)}, bf16[256,2048]{1,0:T(8,128)(2,1)S(1)}, u32[]{:S(2)}, u32[]{:S(2)}) collective-permute-start(bf16[256,2048]{1,0:T(8,128)(2,1)} %shard_map.310.refs_0_), channel_id=1, source_target_pairs={{0,16},{4,20},{8,24},{12,28},{16,0},{20,4},{24,8},{28,12},{1,17},{... | collective-permute-start | bytes 3145736 | tf_op jit(solution)/shard_map/ppermute | solution.py:1678
  141.8 50.1 %collective-permute-start.12 = (bf16[2048,256]{1,0:T(8,128)(2,1)}, bf16[2048,256]{1,0:T(8,128)(2,1)}, u32[]{:S(2)}, u32[]{:S(2)}) collective-permute-start(bf16[2048,256]{1,0:T(8,128)(2,1)} %get-tuple-element.62.refs_10_.refs_5_), channel_id=1, source_target_pairs={{0,1},{1,2},{2,3},{3,0},{4,5},{5,6},{6,7},{7,4},{8,9},{9,10},{10,1... | collective-permute-start | bytes 3145736 | tf_op jit(solution)/shard_map/ppermute | solution.py:1856
  165.6 26.9 %collective-permute-start.15 = (bf16[128,2048]{1,0:T(8,128)(2,1)}, bf16[128,2048]{1,0:T(8,128)(2,1)}, u32[]{:S(2)}, u32[]{:S(2)}) collective-permute-start(bf16[128,2048]{1,0:T(8,128)(2,1)} %shard_map.318), channel_id=1, source_target_pairs={{0,16},{4,20},{8,24},{12,28},{16,0},{20,4},{24,8},{28,12},{1,17},{... | collective-permute-start | bytes 1572872 | tf_op jit(solution)/shard_map/ppermute | solution.py:1678
  167.3 25.3 %collective-permute-start.16 = (bf16[128,2048]{1,0:T(8,128)(2,1)}, bf16[128,2048]{1,0:T(8,128)(2,1)}, u32[]{:S(2)}, u32[]{:S(2)}) collective-permute-start(bf16[128,2048]{1,0:T(8,128)(2,1)} %shard_map.319), channel_id=1, source_target_pairs={{0,8},{4,12},{8,0},{12,4},{16,24},{20,28},{24,16},{28,20},{1,9},{5... | collective-permute-start | bytes 1572872 | tf_op jit(solution)/shard_map/ppermute | solution.py:1678
  173.4 33.1 %all-to-all-start.2 = ((bf16[8,256,256]{2,1,0:T(8,128)(2,1)}), bf16[8,256,256]{2,1,0:T(8,128)(2,1)S(1)}, u32[]{:S(2)}, u32[]{:S(2)}) async-start(bf16[8,256,256]{2,1,0:T(8,128)(2,1)} %get-tuple-element.67.att_ref.refs_1_), calls=%async_computation.2 | async-start | bytes 2097152 | tf_op jit(solution)/shard_map/all_to_all | solution.py:1976
  177.0 156.2 %all-gather.19.cloned.1.call-start = ((), (), s32[]{:S(2)}) async-start(), calls=%async_computation.12 | async-start | bytes 2621440 | tf_op jit(solution)/shard_map/all_gather | solution.py:1970
  179.4 177.1 %all-gather.17.cloned.1.call-start = ((), (), s32[]{:S(2)}) async-start(), calls=%async_computation.11 | async-start | bytes 2621440 | tf_op jit(solution)/shard_map/all_gather | solution.py:1970
  179.9 26.7 %collective-permute-start.13 = (bf16[256,2048]{1,0:T(8,128)(2,1)S(1)}, bf16[256,2048]{1,0:T(8,128)(2,1)}, u32[]{:S(2)}, u32[]{:S(2)}) collective-permute-start(bf16[256,2048]{1,0:T(8,128)(2,1)S(1)} %collective-permute-done.10.refs_2_), channel_id=1, source_target_pairs={{0,4},{4,0},{8,12},{12,8},{16,20},{20,16},{24,28},{28,24},{1,5},{5... | collective-permute-start | bytes 3145736 | tf_op jit(solution)/shard_map/ppermute | solution.py:1678
  180.4 26.3 %collective-permute-start.14 = (bf16[256,2048]{1,0:T(8,128)(2,1)S(1)}, bf16[256,2048]{1,0:T(8,128)(2,1)}, u32[]{:S(2)}, u32[]{:S(2)}) collective-permute-start(bf16[256,2048]{1,0:T(8,128)(2,1)S(1)} %collective-permute-done.11.refs_3_.refs_4_), channel_id=1, source_target_pairs={{0,4},{4,0},{8,12},{12,8},{16,20},{20,16},{24,28},{28,24},{1,5},{5... | collective-permute-start | bytes 3145736 | tf_op jit(solution)/shard_map/ppermute | solution.py:1678
  192.5 14.1 %collective-permute-start.17 = (bf16[128,2048]{1,0:T(8,128)(2,1)}, bf16[128,2048]{1,0:T(8,128)(2,1)}, u32[]{:S(2)}, u32[]{:S(2)}) collective-permute-start(bf16[128,2048]{1,0:T(8,128)(2,1)} %collective-permute-done.15.refs_6_), channel_id=1, source_target_pairs={{0,4},{4,0},{8,12},{12,8},{16,20},{20,16},{24,28},{28,24},{1,5},{5... | collective-permute-start | bytes 1572872 | tf_op jit(solution)/shard_map/ppermute | solution.py:1678
  192.6 14.0 %collective-permute-start.18 = (bf16[128,2048]{1,0:T(8,128)(2,1)}, bf16[128,2048]{1,0:T(8,128)(2,1)}, u32[]{:S(2)}, u32[]{:S(2)}) collective-permute-start(bf16[128,2048]{1,0:T(8,128)(2,1)} %collective-permute-done.16.refs_7_), channel_id=1, source_target_pairs={{0,4},{4,0},{8,12},{12,8},{16,20},{20,16},{24,28},{28,24},{1,5},{5... | collective-permute-start | bytes 1572872 | tf_op jit(solution)/shard_map/ppermute | solution.py:1678
  206.5 50.3 %collective-permute-start.23 = (bf16[2048,256]{1,0:T(8,128)(2,1)}, bf16[2048,256]{1,0:T(8,128)(2,1)}, u32[]{:S(2)}, u32[]{:S(2)}) collective-permute-start(bf16[2048,256]{1,0:T(8,128)(2,1)} %collective-permute-done.12.refs_4_.refs_11_.refs_6_), channel_id=1, source_target_pairs={{0,1},{1,2},{2,3},{3,0},{4,5},{5,6},{6,7},{7,4},{8,9},{9,10},{10,1... | collective-permute-start | bytes 3145736 | tf_op jit(solution)/shard_map/ppermute | solution.py:1856
  220.6 25.5 %collective-permute-start.19 = (bf16[256,2048]{1,0:T(8,128)(2,1)}, bf16[256,2048]{1,0:T(8,128)(2,1)}, u32[]{:S(2)}, u32[]{:S(2)}) collective-permute-start(bf16[256,2048]{1,0:T(8,128)(2,1)} %get-tuple-element.70.refs_1_.refs_0_), channel_id=1, source_target_pairs={{0,8},{4,12},{8,0},{12,4},{16,24},{20,28},{24,16},{28,20},{1,9},{5... | collective-permute-start | bytes 3145736 | tf_op jit(solution)/shard_map/ppermute | solution.py:1678
  221.0 27.6 %collective-permute-start.21 = (bf16[256,2048]{1,0:T(8,128)(2,1)}, bf16[256,2048]{1,0:T(8,128)(2,1)}, u32[]{:S(2)}, u32[]{:S(2)}) collective-permute-start(bf16[256,2048]{1,0:T(8,128)(2,1)} %get-tuple-element.70.refs_1_.refs_0_), channel_id=1, source_target_pairs={{0,16},{4,20},{8,24},{12,28},{16,0},{20,4},{24,8},{28,12},{1,17},{... | collective-permute-start | bytes 3145736 | tf_op jit(solution)/shard_map/ppermute | solution.py:1678
  248.0 13.3 %collective-permute-start.20 = (bf16[128,2048]{1,0:T(8,128)(2,1)}, bf16[128,2048]{1,0:T(8,128)(2,1)S(1)}, u32[]{:S(2)}, u32[]{:S(2)}) collective-permute-start(bf16[128,2048]{1,0:T(8,128)(2,1)} %shard_map.323), channel_id=1, source_target_pairs={{0,16},{4,20},{8,24},{12,28},{16,0},{20,4},{24,8},{28,12},{1,17},{... | collective-permute-start | bytes 1572872 | tf_op jit(solution)/shard_map/ppermute | solution.py:1678
  250.5 13.1 %collective-permute-start.22 = (bf16[128,2048]{1,0:T(8,128)(2,1)}, bf16[128,2048]{1,0:T(8,128)(2,1)}, u32[]{:S(2)}, u32[]{:S(2)}) collective-permute-start(bf16[128,2048]{1,0:T(8,128)(2,1)} %shard_map.324), channel_id=1, source_target_pairs={{0,8},{4,12},{8,0},{12,4},{16,24},{20,28},{24,16},{28,20},{1,9},{5... | collective-permute-start | bytes 1572872 | tf_op jit(solution)/shard_map/ppermute | solution.py:1678
  263.6 32.5 %copy-start.5 = (bf16[256,2048]{1,0:T(8,128)(2,1)S(1)}, bf16[256,2048]{1,0:T(8,128)(2,1)}, u32[]{:S(2)}) copy-start(bf16[256,2048]{1,0:T(8,128)(2,1)} %shard_map.325.refs_0_) | copy-start | bytes 3145732
  263.6 23.3 %collective-permute-start.24 = (bf16[256,2048]{1,0:T(8,128)(2,1)}, bf16[256,2048]{1,0:T(8,128)(2,1)S(1)}, u32[]{:S(2)}, u32[]{:S(2)}) collective-permute-start(bf16[256,2048]{1,0:T(8,128)(2,1)} %shard_map.325.refs_0_), channel_id=1, source_target_pairs={{0,8},{4,12},{8,0},{12,4},{16,24},{20,28},{24,16},{28,20},{1,9},{5... | collective-permute-start | bytes 3145736 | tf_op jit(solution)/shard_map/ppermute | solution.py:1678
  264.4 22.9 %collective-permute-start.25 = (bf16[256,2048]{1,0:T(8,128)(2,1)}, bf16[256,2048]{1,0:T(8,128)(2,1)S(1)}, u32[]{:S(2)}, u32[]{:S(2)}) collective-permute-start(bf16[256,2048]{1,0:T(8,128)(2,1)} %shard_map.325.refs_0_), channel_id=1, source_target_pairs={{0,16},{4,20},{8,24},{12,28},{16,0},{20,4},{24,8},{28,12},{1,17},{... | collective-permute-start | bytes 3145736 | tf_op jit(solution)/shard_map/ppermute | solution.py:1678
  265.4 22.3 %collective-permute-start.29 = (bf16[256,2048]{1,0:T(8,128)(2,1)S(1)}, bf16[256,2048]{1,0:T(8,128)(2,1)S(1)}, u32[]{:S(2)}, u32[]{:S(2)}) collective-permute-start(bf16[256,2048]{1,0:T(8,128)(2,1)S(1)} %copy-done.10), channel_id=1, source_target_pairs={{0,4},{4,0},{8,12},{12,8},{16,20},{20,16},{24,28},{28,24},{1,5},{5... | collective-permute-start | bytes 3145736 | tf_op jit(solution)/shard_map/ppermute | solution.py:1678
  265.4 27.6 %collective-permute-start.28 = (bf16[2048,256]{1,0:T(8,128)(2,1)}, bf16[2048,256]{1,0:T(8,128)(2,1)S(1)}, u32[]{:S(2)}, u32[]{:S(2)}) collective-permute-start(bf16[2048,256]{1,0:T(8,128)(2,1)} %collective-permute-done.23.refs_3_.refs_12_.refs_7_), channel_id=1, source_target_pairs={{0,1},{1,2},{2,3},{3,0},{4,5},{5,6},{6,7},{7,4},{8,9},{9,10},{10,1... | collective-permute-start | bytes 3145736 | tf_op jit(solution)/shard_map/ppermute | solution.py:1856
  267.2 26.9 %collective-permute-start.30 = (bf16[256,2048]{1,0:T(8,128)(2,1)}, bf16[256,2048]{1,0:T(8,128)(2,1)S(1)}, u32[]{:S(2)}, u32[]{:S(2)}) collective-permute-start(bf16[256,2048]{1,0:T(8,128)(2,1)} %collective-permute-done.19.refs_2_), channel_id=1, source_target_pairs={{0,4},{4,0},{8,12},{12,8},{16,20},{20,16},{24,28},{28,24},{1,5},{5... | collective-permute-start | bytes 3145736 | tf_op jit(solution)/shard_map/ppermute | solution.py:1678
  286.9 9.1 %collective-permute-start.31 = (bf16[256,2048]{1,0:T(8,128)(2,1)}, bf16[256,2048]{1,0:T(8,128)(2,1)}, u32[]{:S(2)}, u32[]{:S(2)}) collective-permute-start(bf16[256,2048]{1,0:T(8,128)(2,1)} %collective-permute-done.21.refs_4_), channel_id=1, source_target_pairs={{0,4},{4,0},{8,12},{12,8},{16,20},{20,16},{24,28},{28,24},{1,5},{5... | collective-permute-start | bytes 3145736 | tf_op jit(solution)/shard_map/ppermute | solution.py:1678
  287.3 8.8 %collective-permute-start.32 = (bf16[128,2048]{1,0:T(8,128)(2,1)}, bf16[128,2048]{1,0:T(8,128)(2,1)}, u32[]{:S(2)}, u32[]{:S(2)}) collective-permute-start(bf16[128,2048]{1,0:T(8,128)(2,1)} %copy-done.17), channel_id=1, source_target_pairs={{0,4},{4,0},{8,12},{12,8},{16,20},{20,16},{24,28},{28,24},{1,5},{5... | collective-permute-start | bytes 1572872 | tf_op jit(solution)/shard_map/ppermute | solution.py:1678
  287.6 9.0 %collective-permute-start.33 = (bf16[128,2048]{1,0:T(8,128)(2,1)}, bf16[128,2048]{1,0:T(8,128)(2,1)}, u32[]{:S(2)}, u32[]{:S(2)}) collective-permute-start(bf16[128,2048]{1,0:T(8,128)(2,1)} %collective-permute-done.22.refs_2_.refs_7_), channel_id=1, source_target_pairs={{0,4},{4,0},{8,12},{12,8},{16,20},{20,16},{24,28},{28,24},{1,5},{5... | collective-permute-start | bytes 1572872 | tf_op jit(solution)/shard_map/ppermute | solution.py:1678
  293.0 13.7 %collective-permute-start.26 = (bf16[128,2048]{1,0:T(8,128)(2,1)S(1)}, bf16[128,2048]{1,0:T(8,128)(2,1)}, u32[]{:S(2)}, u32[]{:S(2)}) collective-permute-start(bf16[128,2048]{1,0:T(8,128)(2,1)S(1)} %slice.188), channel_id=1, source_target_pairs={{0,16},{4,20},{8,24},{12,28},{16,0},{20,4},{24,8},{28,12},{1,17},{... | collective-permute-start | bytes 1572872 | tf_op jit(solution)/shard_map/ppermute | solution.py:1678
  294.1 13.4 %collective-permute-start.27 = (bf16[128,2048]{1,0:T(8,128)(2,1)S(1)}, bf16[128,2048]{1,0:T(8,128)(2,1)}, u32[]{:S(2)}, u32[]{:S(2)}) collective-permute-start(bf16[128,2048]{1,0:T(8,128)(2,1)S(1)} %slice.189), channel_id=1, source_target_pairs={{0,8},{4,12},{8,0},{12,4},{16,24},{20,28},{24,16},{28,20},{1,9},{5... | collective-permute-start | bytes 1572872 | tf_op jit(solution)/shard_map/ppermute | solution.py:1678
  295.8 285.1 %reduce-scatter.2.cloned.1.call-start = ((), (), s32[]{:S(2)}) async-start(), calls=%async_computation.7 | async-start | bytes 9437184 | tf_op jit(solution)/shard_map/reduce_scatter | solution.py:2010
  296.1 37.1 %collective-permute-start.34 = (bf16[256,2048]{1,0:T(8,128)(2,1)S(1)}, bf16[256,2048]{1,0:T(8,128)(2,1)S(1)}, u32[]{:S(2)}, u32[]{:S(2)}) collective-permute-start(bf16[256,2048]{1,0:T(8,128)(2,1)S(1)} %copy-done.5), channel_id=1, source_target_pairs={{0,4},{4,0},{8,12},{12,8},{16,20},{20,16},{24,28},{28,24},{1,5},{5... | collective-permute-start | bytes 3145736 | tf_op jit(solution)/shard_map/ppermute | solution.py:1678
  296.2 37.0 %collective-permute-start.35 = (bf16[256,2048]{1,0:T(8,128)(2,1)}, bf16[256,2048]{1,0:T(8,128)(2,1)}, u32[]{:S(2)}, u32[]{:S(2)}) collective-permute-start(bf16[256,2048]{1,0:T(8,128)(2,1)} %copy-done.23), channel_id=1, source_target_pairs={{0,4},{4,0},{8,12},{12,8},{16,20},{20,16},{24,28},{28,24},{1,5},{5... | collective-permute-start | bytes 3145736 | tf_op jit(solution)/shard_map/ppermute | solution.py:1678
  296.7 36.5 %collective-permute-start.36 = (bf16[256,2048]{1,0:T(8,128)(2,1)}, bf16[256,2048]{1,0:T(8,128)(2,1)}, u32[]{:S(2)}, u32[]{:S(2)}) collective-permute-start(bf16[256,2048]{1,0:T(8,128)(2,1)} %copy-done.24), channel_id=1, source_target_pairs={{0,4},{4,0},{8,12},{12,8},{16,20},{20,16},{24,28},{28,24},{1,5},{5... | collective-permute-start | bytes 3145736 | tf_op jit(solution)/shard_map/ppermute | solution.py:1678
  306.6 26.6 %collective-permute-start.37 = (bf16[128,2048]{1,0:T(8,128)(2,1)}, bf16[128,2048]{1,0:T(8,128)(2,1)S(1)}, u32[]{:S(2)}, u32[]{:S(2)}) collective-permute-start(bf16[128,2048]{1,0:T(8,128)(2,1)} %collective-permute-done.26.refs_6_.refs_3_), channel_id=1, source_target_pairs={{0,4},{4,0},{8,12},{12,8},{16,20},{20,16},{24,28},{28,24},{1,5},{5... | collective-permute-start | bytes 1572872 | tf_op jit(solution)/shard_map/ppermute | solution.py:1678
  307.4 25.8 %collective-permute-start.38 = (bf16[128,2048]{1,0:T(8,128)(2,1)}, bf16[128,2048]{1,0:T(8,128)(2,1)S(1)}, u32[]{:S(2)}, u32[]{:S(2)}) collective-permute-start(bf16[128,2048]{1,0:T(8,128)(2,1)} %collective-permute-done.27.refs_7_.refs_4_), channel_id=1, source_target_pairs={{0,4},{4,0},{8,12},{12,8},{16,20},{20,16},{24,28},{28,24},{1,5},{5... | collective-permute-start | bytes 1572872 | tf_op jit(solution)/shard_map/ppermute | solution.py:1678
  370.9 15.0 %collective-permute-start.39 = (bf16[4,256,2048]{2,1,0:T(8,128)(2,1)}, bf16[4,256,2048]{2,1,0:T(8,128)(2,1)S(1)}, u32[]{:S(2)}, u32[]{:S(2)}) collective-permute-start(bf16[4,256,2048]{2,1,0:T(8,128)(2,1)} %bitcast.74), channel_id=1, source_target_pairs={{0,4},{4,0},{8,12},{12,8},{16,20},{20,16},{24,28},{28,24},{1,5},{5... | collective-permute-start | bytes 12582920 | tf_op jit(solution)/shard_map/ppermute | solution.py:1678
  394.1 27.3 %collective-permute-start.40 = (bf16[256,2048]{1,0:T(8,128)(2,1)}, bf16[256,2048]{1,0:T(8,128)(2,1)S(1)}, u32[]{:S(2)}, u32[]{:S(2)}) collective-permute-start(bf16[256,2048]{1,0:T(8,128)(2,1)} %get-tuple-element.79), channel_id=1, source_target_pairs={{0,8},{4,12},{8,0},{12,4},{16,24},{20,28},{24,16},{28,20},{1,9},{5... | collective-permute-start | bytes 3145736 | tf_op jit(solution)/shard_map/ppermute | solution.py:1678
  395.3 25.2 %collective-permute-start.41 = (bf16[256,2048]{1,0:T(8,128)(2,1)}, bf16[256,2048]{1,0:T(8,128)(2,1)S(1)}, u32[]{:S(2)}, u32[]{:S(2)}) collective-permute-start(bf16[256,2048]{1,0:T(8,128)(2,1)} %get-tuple-element.81), channel_id=1, source_target_pairs={{0,16},{4,20},{8,24},{12,28},{16,0},{20,4},{24,8},{28,12},{1,17},{... | collective-permute-start | bytes 3145736 | tf_op jit(solution)/shard_map/ppermute | solution.py:1678
  420.6 13.0 %collective-permute-start.42 = (bf16[128,2048]{1,0:T(8,128)(2,1)S(1)}, bf16[128,2048]{1,0:T(8,128)(2,1)}, u32[]{:S(2)}, u32[]{:S(2)}) collective-permute-start(bf16[128,2048]{1,0:T(8,128)(2,1)S(1)} %add_convert_fusion.4), channel_id=1, source_target_pairs={{0,8},{4,12},{8,0},{12,4},{16,24},{20,28},{24,16},{28,20},{1,9},{5... | collective-permute-start | bytes 1572872 | tf_op jit(solution)/shard_map/ppermute | solution.py:1678
  422.9 12.6 %collective-permute-start.43 = (bf16[128,2048]{1,0:T(8,128)(2,1)S(1)}, bf16[128,2048]{1,0:T(8,128)(2,1)}, u32[]{:S(2)}, u32[]{:S(2)}) collective-permute-start(bf16[128,2048]{1,0:T(8,128)(2,1)S(1)} %add_convert_fusion.3), channel_id=1, source_target_pairs={{0,16},{4,20},{8,24},{12,28},{16,0},{20,4},{24,8},{28,12},{1,17},{... | collective-permute-start | bytes 1572872 | tf_op jit(solution)/shard_map/ppermute | solution.py:1678
  512.6 7.6 %collective-permute-start.44 = (bf16[4,256,2048]{2,1,0:T(8,128)(2,1)}, bf16[4,256,2048]{2,1,0:T(8,128)(2,1)}, u32[]{:S(2)}, u32[]{:S(2)}) collective-permute-start(bf16[4,256,2048]{2,1,0:T(8,128)(2,1)} %get-tuple-element.95), channel_id=1, source_target_pairs={{0,4},{4,0},{8,12},{12,8},{16,20},{20,16},{24,28},{28,24},{1,5},{5... | collective-permute-start | bytes 12582920 | tf_op jit(solution)/shard_map/ppermute | solution.py:1678
  526.4 25.4 %collective-permute-start.46 = (bf16[256,2048]{1,0:T(8,128)(2,1)}, bf16[256,2048]{1,0:T(8,128)(2,1)S(1)}, u32[]{:S(2)}, u32[]{:S(2)}) collective-permute-start(bf16[256,2048]{1,0:T(8,128)(2,1)} %get-tuple-element.99), channel_id=1, source_target_pairs={{0,16},{4,20},{8,24},{12,28},{16,0},{20,4},{24,8},{28,12},{1,17},{... | collective-permute-start | bytes 3145736 | tf_op jit(solution)/shard_map/ppermute | solution.py:1678
  528.8 27.1 %collective-permute-start.45 = (bf16[256,2048]{1,0:T(8,128)(2,1)}, bf16[256,2048]{1,0:T(8,128)(2,1)}, u32[]{:S(2)}, u32[]{:S(2)}) collective-permute-start(bf16[256,2048]{1,0:T(8,128)(2,1)} %get-tuple-element.97), channel_id=1, source_target_pairs={{0,8},{4,12},{8,0},{12,4},{16,24},{20,28},{24,16},{28,20},{1,9},{5... | collective-permute-start | bytes 3145736 | tf_op jit(solution)/shard_map/ppermute | solution.py:1678
  534.4 17.6 %all-to-all-start.5 = ((f32[4,1,5888]{2,1,0:T(1,128)}), f32[4,1,5888]{2,1,0:T(1,128)S(1)}, u32[]{:S(2)}, u32[]{:S(2)}) async-start(f32[4,1,5888]{2,1,0:T(1,128)} %copy.134), calls=%async_computation.6 | async-start | bytes 188416 | tf_op jit(solution)/shard_map/all_to_all | solution.py:2054
  551.9 22.3 %collective-permute-start.47 = (bf16[128,2048]{1,0:T(8,128)(2,1)S(1)}, bf16[128,2048]{1,0:T(8,128)(2,1)}, u32[]{:S(2)}, u32[]{:S(2)}) collective-permute-start(bf16[128,2048]{1,0:T(8,128)(2,1)S(1)} %add_convert_fusion.2), channel_id=1, source_target_pairs={{0,8},{4,12},{8,0},{12,4},{16,24},{20,28},{24,16},{28,20},{1,9},{5... | collective-permute-start | bytes 1572872 | tf_op jit(solution)/shard_map/ppermute | solution.py:1678
  552.0 18.2 %all-to-all-start.4 = ((f32[32,1,2624]{2,1,0:T(1,128)}), f32[32,1,2624]{2,1,0:T(1,128)S(1)}, u32[]{:S(2)}, u32[]{:S(2)}) async-start(f32[32,1,2624]{2,1,0:T(1,128)} %reshape.203), calls=%async_computation.5 | async-start | bytes 688128 | tf_op jit(solution)/shard_map/all_to_all | solution.py:2038
  557.0 17.3 %collective-permute-start.48 = (bf16[128,2048]{1,0:T(8,128)(2,1)S(1)}, bf16[128,2048]{1,0:T(8,128)(2,1)S(1)}, u32[]{:S(2)}, u32[]{:S(2)}) collective-permute-start(bf16[128,2048]{1,0:T(8,128)(2,1)S(1)} %add_convert_fusion.1), channel_id=1, source_target_pairs={{0,16},{4,20},{8,24},{12,28},{16,0},{20,4},{24,8},{28,12},{1,17},{... | collective-permute-start | bytes 1572872 | tf_op jit(solution)/shard_map/ppermute | solution.py:1678
  (46 other events, 514.7 us)
Sparse Core Ops, SparseCore 0:
  23.9 36.4 all-gather.12
  62.0 26.7 all-gather.10
  90.4 102.5 all-gather.14
  194.5 66.6 all-gather.18
  295.9 43.9 all-gather.16
  424.0 80.9 reduce-scatter.1

commit v3 on v2

--- a/solution.py
+++ b/solution.py
@@ -1180,11 +1180,15 @@
     @pl.when(pl.program_id(0) == 0)
     def _():
         wait_whole(down, down_sem)
-        wait_whole(both, both_sem)
 
     grad_hidden = mm(buffer[slot], down[...])
     grad_gate = (grad_hidden * by_gate_ref[...].astype(jnp.float32)).astype(jnp.bfloat16)
     grad_up = (grad_hidden * by_up_ref[...].astype(jnp.float32)).astype(jnp.bfloat16)
+
+    @pl.when(pl.program_id(0) == 0)
+    def _():
+        wait_whole(both, both_sem)
+
     total = mm_nt(jnp.concatenate([grad_gate, grad_up], axis=1), both[...])
     if more:
         total = total + before_ref[...].astype(jnp.float32)
@@ -1737,11 +1741,13 @@
     return exchanged(value, 1), exchanged(value, 2), exchanged(value, 4)
 
 
-def gather_rest(value, beside, along_x, along_y, *others):
+def gather_rest(value, beside, along_x, along_y, *others, last=()):
     upper, lower = halves(along_x)[0], halves(along_y)[1]
     if others:
         upper, lower = after(upper, *others), after(lower, *others)
     first, second = exchanged(upper, 4), exchanged(lower, 2)
+    if last:
+        first, second = after(first, *last), after(second, *last)
     return [
         (value,),
         (beside,),
@@ -1986,9 +1992,10 @@
         after(length, normed_ffn), q_t, keys, v_t, att, middle, places, taught
     )
     ffn_all = gather_rest(normed_ffn, *ffn_first, loss_rows)
-    cot_all = plane_gather(after(cotangent[0], *ffn_all[6], gate_weights[2]))
+    cot_first = gather_first(after(cotangent[0], *ffn_all[6], gate_weights[2]))
     losses = jnp.sum(loss_rows[0].reshape(places, rows), axis=1)
     hidden, by_gate, by_up = hidden_units(chunk_order, ffn_all, gate_weights, up_weights)
+    cot_all = gather_rest(cotangent[0], *cot_first, last=(hidden,))
     early = None
     for part in range(PARTS - 1):
         early = ffn_back(

time: 600 us -> 592 us (0.987)
  waiting for transfers between devices: 186 us -> 172 us
    ppermute x46, waiting for transfers between devices: 121 us -> 114 us  [exchanged(): lax.ppermute(value, 'seq', [(place, place ^ bits) for place in range(coun...]
    unnamed x119 -> x115, local copies, waits for them, and re-layouts: 12.4 us -> 14.4 us
  transfers between devices with their start and end apart: 59 -> 59, of which waited for: 24 -> 23; matrix products, arithmetic and copies ran while one was open for 8% -> 8% of each run, Pallas kernels for 37% -> 38%
where the time goes in v3:
time: 592 us; the launch traced here: 584 us
  Pallas kernels  242 us (41%)
  waiting for transfers between devices  172 us (29%)
  starting transfers between devices  46.3 us (8%)
  blocking collectives  44.8 us (8%)
  local copies, waits for them, and re-layouts  43.3 us (7%)
  between operations  19.3 us (3%)
  other arithmetic  14.2 us (2%)
    ppermute x46, waiting for transfers between devices, exchanged(): lax.ppermute(value, 'seq', [(place, place ^ bits) for place in range(coun...  114 us
    pallas_call x3, Pallas kernels, ffn_back(): call(functools.partial(ffn_back_kernel, counts, len(gates), part, more),...  52 us
    all_to_all x1, waiting for transfers between devices, by_heads(): swapped = lax.all_to_all(swapped, 'seq', 0, 0, tiled=True)  36.8 us
    all_to_all x1, blocking collectives, by_heads(): grad_att = lax.all_to_all(grad_att, 'seq', 0, 0, tiled=True)  31.4 us
    pallas_call x1, Pallas kernels, heads_back(): call(functools.partial(backward_kernel, counts), (steps,), [ANYWHERE] * s...  30.4 us
    pallas_call x2, Pallas kernels, teach(): pl.pallas_call(functools.partial(teacher_kernel, first, end - first), gri...  28.9 us
    pallas_call x1, Pallas kernels, hidden_units(): call(functools.partial(hidden_kernel, counts), (len(blocks),), [ANYWHERE]...  26 us
    ppermute x46, starting transfers between devices, exchanged(): lax.ppermute(value, 'seq', [(place, place ^ bits) for place in range(coun...  25.9 us
  transfers between devices with their start and end apart: 59, of which 23 were waited for; matrix products, arithmetic and copies ran while one was open for 8% of the time, Pallas kernels for 38%

profile of v3, /device:TPU:0, one launch (start us, length us, event | category | flops | bytes accessed | tf_op | source)
XLA Modules:
  0.0 584.4 jit_solution(5840621828116954235)
XLA Ops:
  10.4 13.4 %all_to_all.34.refs_1_ = bf16[8,64,384]{2,1,0:T(8,128)(2,1)} all-to-all(bf16[8,64,384]{2,1,0:T(8,128)(2,1)S(1)} %maximum_bitcast_fusion.1), channel_id=1, replica_groups=mesh['seq'=8,'fsdp'=4] {'seq'}, dimensions={0} | all-to-all | bytes 786432 | tf_op jit(solution)/shard_map/all_to_all | solution.py:1917
  23.8 6.2 %shard_map.311.refs_0_ = bf16[8,3,256,256]{3,2,1,0:T(8,128)(2,1)} custom-call(bf16[256,2048]{1,0:T(8,128)(2,1)} %refs_0_.1, bf16[256,2048]{1,0:T(8,128)(2,1)} %refs_1_.1, bf16[256,2048]{1,0:T(8,128)(2,1)} %refs_2_.1), custom_call_target="tpu_custom_call" | custom-call | flops 6899999744 | bytes 1 | tf_op jit(solution)/shard_map/pallas_call | solution.py:1709
  30.1 4.6 all-to-all-start.1
  35.8 36.8 %all-to-all-done.1.ref = bf16[8,3,256,256]{3,2,1,0:T(8,128)(2,1)} async-done(((bf16[8,3,256,256]{3,2,1,0:T(8,128)(2,1)}), bf16[8,3,256,256]{3,2,1,0:T(8,128)(2,1)}, u32[]{:S(2)}, u32[]{:S(2)}) %all-to-all-start.1) | async-done | bytes 3145760 | tf_op jit(solution)/shard_map/all_to_all | solution.py:1935
  72.6 6.1 %shard_map.313 = (bf16[2048,256]{1,0:T(8,128)(2,1)}, bf16[2048,256]{1,0:T(8,128)(2,1)}, bf16[2048,256]{1,0:T(8,128)(2,1)}) custom-call(bf16[8,3,256,256]{3,2,1,0:T(8,128)(2,1)} %all-to-all-done.1.ref), custom_call_target="tpu_custom_call" | custom-call | flops 6899999744 | bytes 1 | tf_op jit(solution)/shard_map/pallas_call | solution.py:1728
  84.5 19.1 %collective-permute-done.1.refs_2_ = bf16[256,2048]{1,0:T(8,128)(2,1)S(1)} collective-permute-done((bf16[256,2048]{1,0:T(8,128)(2,1)S(1)}, bf16[256,2048]{1,0:T(8,128)(2,1)S(1)}, u32[]{:S(2)}, u32[]{:S(2)}) %collective-permute-start.1) | collective-permute-done | bytes 1048608 | tf_op jit(solution)/shard_map/ppermute | solution.py:1682
  104.1 1.3 collective-permute-done.3.refs_4_
  109.9 6.6 %collective-permute-done.5.refs_6_ = bf16[128,2048]{1,0:T(8,128)(2,1)} collective-permute-done((bf16[128,2048]{1,0:T(8,128)(2,1)S(1)}, bf16[128,2048]{1,0:T(8,128)(2,1)}, u32[]{:S(2)}, u32[]{:S(2)}) %collective-permute-start.5) | collective-permute-done | bytes 524320 | tf_op jit(solution)/shard_map/ppermute | solution.py:1682
  116.5 2.7 collective-permute-done.6.refs_7_
  119.2 1.8 multiply_sine_fusion
  122.2 16.8 %shard_map.309 = (bf16[256,2048]{1,0:T(8,128)(2,1)}, bf16[64,2048]{1,0:T(8,128)(2,1)}, bf16[80,2048]{1,0:T(8,128)(2,1)}, bf16[2048,64]{1,0:T(8,128)(2,1)}, bf16[...) custom-call(s32[1]{0:T(128)} %bitcast.place_ref, ...), custom_call_target="tpu_custom_call" | custom-call | flops 19549999104 | bytes 1 | tf_op jit(solution)/shard_map/pallas_call | solution.py:859
  139.8 1.8 collective-permute-start.10
  141.6 1.6 collective-permute-start.12
  143.2 10.1 %shard_map.315 = (bf16[8,256,256]{2,1,0:T(8,128)(2,1)}, f32[256,2048]{1,0:T(8,128)}, f32[4,2048]{1,0:T(4,128)}, f32[16,80,128]{2,1,0:T(8,128)}, bf16[16,256,512]{2,1,0:T(8,128)(2,1)}) custom-call(s32[1]{0:T(128)} %dynamic_slice.18.length_ref, bf16[256,2048]{1,0:T(8,128)(2,1)} %get-tuple-element.61.refs_1_.q_ref.refs_14_, ...), custom_call_target="tpu_custom_call" | custom-call | flops 11500000256 | bytes 1 | tf_op jit(solution)/shard_map/pallas_call | solution.py:1005
  153.2 11.5 %collective-permute-done.11.refs_3_.refs_4_ = bf16[256,2048]{1,0:T(8,128)(2,1)S(1)} collective-permute-done((bf16[256,2048]{1,0:T(8,128)(2,1)}, bf16[256,2048]{1,0:T(8,128)(2,1)S(1)}, u32[]{:S(2)}, u32[]{:S(2)}) %collective-permute-start.11) | collective-permute-done | bytes 1048608 | tf_op jit(solution)/shard_map/ppermute | solution.py:1682
  167.6 1.4 collective-permute-start.15
  173.3 3.6 all-to-all-start.2
  177.0 2.3 fusion.18
  180.4 11.6 %collective-permute-done.12.refs_4_.refs_11_.refs_6_ = bf16[2048,256]{1,0:T(8,128)(2,1)} collective-permute-done((bf16[2048,256]{1,0:T(8,128)(2,1)}, bf16[2048,256]{1,0:T(8,128)(2,1)}, u32[]{:S(2)}, u32[]{:S(2)}) %collective-permute-start.12) | collective-permute-done | bytes 1048608 | tf_op jit(solution)/shard_map/ppermute | solution.py:1862
  193.1 12.9 %shard_map.316 = (f32[256,2048]{1,0:T(8,128)}, f32[8,2048]{1,0:T(8,128)}) custom-call(s32[1]{0:T(128)} %shard_map.314.length_ref, bf16[256,2048]{1,0:T(8,128)(2,1)} %get-tuple-element.61.refs_1_.q_ref.refs_14_, bf16[2048,64]{1,0:T(8,128)(2,1)} %get-tuple-element.63.k_ref.k_before, bf16[80,2048]{1,0:T(8,128)(2,1)} %get-tuple-element.64.vt_ref.vt_before.refs_23_.refs_24_, ...), custom_call_target="tpu_custom_call" | custom-call | flops 18400000000 | bytes 1 | tf_op jit(solution)/shard_map/pallas_call | solution.py:1102
  207.6 13.0 %shard_map.320 = (f32[256,2048]{1,0:T(8,128)}, bf16[256,2048]{1,0:T(8,128)(2,1)}, f32[256,128]{1,0:T(8,128)}, bf16[256,128]{1,0:T(8,128)(2,1)}) custom-call(s32[1]{0:T(128)} %shard_map.317.place_ref, bf16[256,2048]{1,0:T(8,128)(2,1)} %shard_map.310.refs_0_, bf16[256,2048]{1,0:T(8,128)(2,1)} %collective-permute-done.9.refs_1_, bf16[256,2048]{1,0:T(8,128)(2,1)} %copy-done.7, ...), custom_call_target="tpu_custom_call" | custom-call | flops 14949999616 | bytes 1 | tf_op jit(solution)/shard_map/pallas_call | solution.py:1572
  221.2 1.2 collective-permute-start.19
  222.9 16.0 %shard_map.322 = (f32[256,2048]{1,0:T(8,128)}, f32[8,2048]{1,0:T(8,128)}) custom-call(s32[1]{0:T(128)} %shard_map.321.length_ref, bf16[256,2048]{1,0:T(8,128)(2,1)} %get-tuple-element.61.refs_1_.q_ref.refs_14_, bf16[2048,64]{1,0:T(8,128)(2,1)} %get-tuple-element.63.k_ref.k_before, ...), custom_call_target="tpu_custom_call", output_to_operand_aliasing={{0}: (5, {}), {1}: (6, {})} | custom-call | flops 18400000000 | bytes 1 | tf_op jit(solution)/shard_map/pallas_call | solution.py:1102
  238.9 7.3 %collective-permute-done.21.refs_4_ = bf16[256,2048]{1,0:T(8,128)(2,1)} collective-permute-done((bf16[256,2048]{1,0:T(8,128)(2,1)}, bf16[256,2048]{1,0:T(8,128)(2,1)}, u32[]{:S(2)}, u32[]{:S(2)}) %collective-permute-start.21) | collective-permute-done | bytes 1048608 | tf_op jit(solution)/shard_map/ppermute | solution.py:1682
  246.2 1.9 slice.187.refs_0_
  248.4 1.9 slice.186.refs_0_
  250.2 1.3 collective-permute-start.20
  252.5 4.4 collective-permute-done.23.refs_3_.refs_12_.refs_7_
  256.9 4.5 collective-permute-done.22.refs_2_.refs_7_
  261.4 1.9 collective-permute-done.20.refs_1_.refs_6_
  265.2 1.2 collective-permute-start.24
  266.4 1.6 collective-permute-start.32
  268.5 19.1 %collective-permute-done.25.refs_4_.refs_2_ = bf16[256,2048]{1,0:T(8,128)(2,1)} collective-permute-done((bf16[256,2048]{1,0:T(8,128)(2,1)}, bf16[256,2048]{1,0:T(8,128)(2,1)}, u32[]{:S(2)}, u32[]{:S(2)}) %collective-permute-start.25) | collective-permute-done | bytes 1048608 | tf_op jit(solution)/shard_map/ppermute | solution.py:1682
  291.8 1.4 collective-permute-start.33
  293.3 1.3 collective-permute-start.26
  295.1 26.0 %shard_map.326 = (bf16[2048,1024]{1,0:T(8,128)(2,1)}, bf16[2048,1024]{1,0:T(8,128)(2,1)}, bf16[2048,1024]{1,0:T(8,128)(2,1)}) custom-call(s32[4]{0:T(128)} %compare_select_fusion.order_ref, bf16[256,2048]{1,0:T(8,128)(2,1)} %get-tuple-element.70.refs_1_.refs_0_, bf16[256,2048]{1,0:T(8,128)(2,1)} %collective-permute-done.27.refs_1_, ...), custom_call_target="tpu_custom_call" | custom-call | flops 28750000128 | bytes 1 | tf_op jit(solution)/shard_map/pallas_call | solution.py:1149
  325.8 22.6 %shard_map.329.refs_13_ = bf16[2048,2048]{1,0:T(8,128)(2,1)} custom-call(s32[4]{0:T(128)} %compare_select_fusion.order_ref, bf16[256,2048]{1,0:T(8,128)(2,1)} %bitcast.55, bf16[256,2048]{1,0:T(8,128)(2,1)} %collective-permute-done.34.refs_1_.refs_0_, bf16[256,2048]{1,0:T(8,128)(2,1)} %collective-permute-done.24.refs_2_.refs_1_, ...), custom_call_target="tpu_custom_call" | custom-call | flops 27599998976 | bytes 1 | tf_op jit(solution)/shard_map/pallas_call | solution.py:1207
  348.5 14.7 %shard_map.331 = bf16[1024,2048]{1,0:T(8,128)(2,1)} custom-call(s32[4]{0:T(128)} %compare_select_fusion.order_ref, bf16[256,2048]{1,0:T(8,128)(2,1)} %collective-permute-done.34.refs_1_.refs_0_, bf16[256,2048]{1,0:T(8,128)(2,1)} %collective-permute-done.35.refs_3_.refs_1_, bf16[256,2048]{1,0:T(8,128)(2,1)} %collective-permute-done.36.refs_5_.refs_2_, ...), custom_call_target="tpu_custom_call" | custom-call | flops 13799999488 | bytes 1 | tf_op jit(solution)/shard_map/pallas_call | solution.py:1207
  363.6 14.7 %shard_map.330 = bf16[1024,2048]{1,0:T(8,128)(2,1)} custom-call(s32[4]{0:T(128)} %compare_select_fusion.order_ref, bf16[256,2048]{1,0:T(8,128)(2,1)} %bitcast.56, bf16[256,2048]{1,0:T(8,128)(2,1)} %collective-permute-done.24.refs_2_.refs_1_, bf16[256,2048]{1,0:T(8,128)(2,1)} %collective-permute-done.25.refs_4_.refs_2_, ...), custom_call_target="tpu_custom_call" | custom-call | flops 13799999488 | bytes 1 | tf_op jit(solution)/shard_map/pallas_call | solution.py:1207
  378.3 2.0 copy-done.39
  380.3 6.2 %shard_map.332 = (f32[256,2048]{1,0:T(8,128)}, bf16[256,2048]{1,0:T(8,128)(2,1)}, bf16[256,2048]{1,0:T(8,128)(2,1)}, bf16[128,2048]{1,0:T(8,128)(2,1)}, bf16[128,2048]{1,0:T(8,128)(2,1)}) custom-call(bf16[4,256,2048]{2,1,0:T(8,128)(2,1)} %bitcast.83, bf16[4,256,2048]{2,1,0:T(8,128)(2,1)} %copy-done.39), custom_call_target="tpu_custom_call" | custom-call | flops 5750000128 | bytes 1 | tf_op jit(solution)/shard_map/pallas_call | solution.py:1786
  388.6 16.3 %shard_map.334.refs_1_ = bf16[2048,2048]{1,0:T(8,128)(2,1)} custom-call(s32[1]{0:T(128)} %shard_map.333.place_ref, s32[4]{0:T(128)} %compare_select_fusion.order_ref, bf16[4,2048,128]{2,1,0:T(8,128)(2,1)} %bitcast.78, bf16[4,2048,128]{2,1,0:T(8,128)(2,1)} %bitcast.81, bf16[2048,1024]{1,0:T(8,128)(2,1)} %get-tuple-element.74.refs_1_.refs_2_), custom_call_target="tpu_custom_call" | custom-call | flops 19549999104 | bytes 1 | tf_op jit(solution)/shard_map/pallas_call | solution.py:1243
  405.0 6.9 %collective-permute-done.40.refs_11_ = bf16[256,2048]{1,0:T(8,128)(2,1)S(1)} collective-permute-done((bf16[256,2048]{1,0:T(8,128)(2,1)}, bf16[256,2048]{1,0:T(8,128)(2,1)S(1)}, u32[]{:S(2)}, u32[]{:S(2)}) %collective-permute-start.40) | collective-permute-done | bytes 1048608 | tf_op jit(solution)/shard_map/ppermute | solution.py:1682
  413.0 1.5 add_convert_fusion.4
  415.3 10.0 %collective-permute-done.43.refs_13_ = bf16[128,2048]{1,0:T(8,128)(2,1)} collective-permute-done((bf16[128,2048]{1,0:T(8,128)(2,1)S(1)}, bf16[128,2048]{1,0:T(8,128)(2,1)}, u32[]{:S(2)}, u32[]{:S(2)}) %collective-permute-start.43) | collective-permute-done | bytes 524320 | tf_op jit(solution)/shard_map/ppermute | solution.py:1682
  425.3 2.2 collective-permute-done.42.refs_12_
  427.6 15.9 %shard_map.337 = (bf16[8,256,256]{2,1,0:T(8,128)(2,1)}, f32[256,2048]{1,0:T(8,128)}, bf16[256,2048]{1,0:T(8,128)(2,1)}, f32[256,128]{1,0:T(8,128)}) custom-call(s32[1]{0:T(128)} %bitcast.place_ref, bf16[256,2048]{1,0:T(8,128)(2,1)} %shard_map.310.refs_0_, bf16[256,2048]{1,0:T(8,128)(2,1)} %collective-permute-done.9.refs_1_, bf16[256,2048]{1,0:T(8,128)(2,1)} %copy-done.7, ...), custom_call_target="tpu_custom_call" | custom-call | flops 17250000896 | bytes 1 | tf_op jit(solution)/shard_map/pallas_call | solution.py:1646
  443.4 31.4 %all_to_all.35.refs_10_ = bf16[8,256,256]{2,1,0:T(8,128)(2,1)} all-to-all(bf16[8,256,256]{2,1,0:T(8,128)(2,1)} %get-tuple-element.84), channel_id=1, replica_groups=mesh['seq'=8,'fsdp'=4] {'seq'}, dimensions={0} | all-to-all | bytes 2097152 | tf_op jit(solution)/shard_map/all_to_all | solution.py:2019
  474.8 30.4 %shard_map.338 = (bf16[512,2048]{1,0:T(8,128)(2,1)}, f32[320,64]{1,0:T(8,128)}, f32[128,2048]{1,0:T(8,128)}, bf16[4,256,2048]{2,1,0:T(8,128)(2,1)}, bf16[4,256,2048]{2,1,0:T(8,128)(2,1)}) custom-call(s32[1]{0:T(128)} %dynamic_slice.18.length_ref, s32[1]{0:T(128)} %bitcast.place_ref, bf16[256,2048]{1,0:T(8,128)(2,1)} %copy-done.13, ...), custom_call_target="tpu_custom_call" | custom-call | flops 34500001792 | bytes 1 | tf_op jit(solution)/shard_map/pallas_call | solution.py:1477
  507.7 2.0 fusion.3
  509.7 3.1 collective-permute-done.44.got_ref
  512.9 6.2 %shard_map.339 = (f32[256,2048]{1,0:T(8,128)}, bf16[256,2048]{1,0:T(8,128)(2,1)}, bf16[256,2048]{1,0:T(8,128)(2,1)}, bf16[128,2048]{1,0:T(8,128)(2,1)}, bf16[128,2048]{1,0:T(8,128)(2,1)}) custom-call(bf16[4,256,2048]{2,1,0:T(8,128)(2,1)} %get-tuple-element.94.keep_ref, bf16[4,256,2048]{2,1,0:T(8,128)(2,1)} %collective-permute-done.44.got_ref), custom_call_target="tpu_custom_call" | custom-call | flops 5750000128 | bytes 1 | tf_op jit(solution)/shard_map/pallas_call | solution.py:1786
  523.1 1.6 copy.136
  524.7 3.9 all-to-all-start.5
  528.6 2.4 reshape.203
  531.0 13.4 %collective-permute-done.45.from_x = bf16[256,2048]{1,0:T(8,128)(2,1)S(1)} collective-permute-done((bf16[256,2048]{1,0:T(8,128)(2,1)}, bf16[256,2048]{1,0:T(8,128)(2,1)S(1)}, u32[]{:S(2)}, u32[]{:S(2)}) %collective-permute-start.45) | collective-permute-done | bytes 1048608 | tf_op jit(solution)/shard_map/ppermute | solution.py:1682
  544.8 4.1 all-to-all-start.4
  549.0 1.2 add_convert_fusion.2
  550.1 1.9 collective-permute-start.47
  557.1 4.6 all-to-all-done.4
  562.2 1.5 reduce.5
  565.7 1.2 collective-permute-done.47.late_x
  567.8 5.7 shard_map.340
  573.4 2.5 fusion.5
  (303 shorter events, 58.8 us)
Async XLA Ops:
  7.2 75.5 %copy-start = (bf16[2048,64]{0,1:T(8,128)(2,1)S(1)}, bf16[2048,64]{0,1:T(8,128)(2,1)}, u32[]{:S(2)}) copy-start(bf16[2048,64]{0,1:T(8,128)(2,1)} %param.41) | copy-start | bytes 786436
  7.2 114.2 %all-gather.13.cloned.1.call-start = ((), (), s32[]{:S(2)}) async-start(), calls=%async_computation.9 | async-start | bytes 1966080 | tf_op jit(solution)/shard_map/all_gather | solution.py:1918
  30.1 42.5 %all-to-all-start.1 = ((bf16[8,3,256,256]{3,2,1,0:T(8,128)(2,1)}), bf16[8,3,256,256]{3,2,1,0:T(8,128)(2,1)}, u32[]{:S(2)}, u32[]{:S(2)}) async-start(bf16[8,3,256,256]{3,2,1,0:T(8,128)(2,1)} %shard_map.312), calls=%async_computation.1 | async-start | bytes 6291456 | tf_op jit(solution)/shard_map/all_to_all | solution.py:1935
  34.7 104.3 %all-gather.11.cloned.1.call-start = ((), (), s32[]{:S(2)}) async-start(), calls=%async_computation.8 | async-start | bytes 1310720 | tf_op jit(solution)/shard_map/all_gather | solution.py:1933
  35.4 259.6 %all-gather.15.cloned.1.call-start = ((), (), s32[]{:S(2)}) async-start(), calls=%async_computation.10 | async-start | bytes 5242880 | tf_op jit(solution)/shard_map/all_gather | solution.py:1973
  35.5 43.2 %copy-start.29 = (f32[2048]{0:T(1024)}, f32[2048]{0:T(1024)S(1)}, u32[]{:S(2)}) copy-start(f32[2048]{0:T(1024)S(1)} %convert_element_type.81) | copy-start | bytes 24580
  79.7 41.7 %copy-start.13 = (bf16[256,2048]{1,0:T(8,128)(2,1)}, bf16[256,2048]{1,0:T(8,128)(2,1)S(1)}, u32[]{:S(2)}) copy-start(bf16[256,2048]{1,0:T(8,128)(2,1)S(1)} %fusion.2.refs_0_) | copy-start | bytes 3145732
  79.7 24.0 %collective-permute-start.1 = (bf16[256,2048]{1,0:T(8,128)(2,1)S(1)}, bf16[256,2048]{1,0:T(8,128)(2,1)S(1)}, u32[]{:S(2)}, u32[]{:S(2)}) collective-permute-start(bf16[256,2048]{1,0:T(8,128)(2,1)S(1)} %fusion.2.refs_0_), channel_id=1, source_target_pairs={{0,8},{4,12},{8,0},{12,4},{16,24},{20,28},{24,16},{28,20},{1,9},{5... | collective-permute-start | bytes 3145736 | tf_op jit(solution)/shard_map/ppermute | solution.py:1682
  80.3 25.2 %collective-permute-start.3 = (bf16[256,2048]{1,0:T(8,128)(2,1)S(1)}, bf16[256,2048]{1,0:T(8,128)(2,1)}, u32[]{:S(2)}, u32[]{:S(2)}) collective-permute-start(bf16[256,2048]{1,0:T(8,128)(2,1)S(1)} %fusion.2.refs_0_), channel_id=1, source_target_pairs={{0,16},{4,20},{8,24},{12,28},{16,0},{20,4},{24,8},{28,12},{1,17},{... | collective-permute-start | bytes 3145736 | tf_op jit(solution)/shard_map/ppermute | solution.py:1682
  80.9 40.1 %collective-permute-start = (bf16[256,2048]{1,0:T(8,128)(2,1)S(1)}, bf16[256,2048]{1,0:T(8,128)(2,1)}, u32[]{:S(2)}, u32[]{:S(2)}) collective-permute-start(bf16[256,2048]{1,0:T(8,128)(2,1)S(1)} %fusion.2.refs_0_), channel_id=1, source_target_pairs={{0,4},{4,0},{8,12},{12,8},{16,20},{20,16},{24,28},{28,24},{1,5},{5... | collective-permute-start | bytes 3145736 | tf_op jit(solution)/shard_map/ppermute | solution.py:1682
  83.8 55.2 %copy-start.21 = (bf16[320,64]{1,0:T(8,128)(2,1)}, bf16[320,64]{1,0:T(8,128)(2,1)S(1)}, u32[]{:S(2)}) copy-start(bf16[320,64]{1,0:T(8,128)(2,1)S(1)} %pad_maximum_fusion.refs_27_) | copy-start | bytes 122884
  103.7 12.8 %collective-permute-start.5 = (bf16[128,2048]{1,0:T(8,128)(2,1)S(1)}, bf16[128,2048]{1,0:T(8,128)(2,1)}, u32[]{:S(2)}, u32[]{:S(2)}) collective-permute-start(bf16[128,2048]{1,0:T(8,128)(2,1)S(1)} %slice.182), channel_id=1, source_target_pairs={{0,16},{4,20},{8,24},{12,28},{16,0},{20,4},{24,8},{28,12},{1,17},{... | collective-permute-start | bytes 1572872 | tf_op jit(solution)/shard_map/ppermute | solution.py:1682
  106.5 12.7 %collective-permute-start.6 = (bf16[128,2048]{1,0:T(8,128)(2,1)S(1)}, bf16[128,2048]{1,0:T(8,128)(2,1)}, u32[]{:S(2)}, u32[]{:S(2)}) collective-permute-start(bf16[128,2048]{1,0:T(8,128)(2,1)S(1)} %slice.183), channel_id=1, source_target_pairs={{0,8},{4,12},{8,0},{12,4},{16,24},{20,28},{24,16},{28,20},{1,9},{5... | collective-permute-start | bytes 1572872 | tf_op jit(solution)/shard_map/ppermute | solution.py:1682
  107.0 14.3 %collective-permute-start.2 = (bf16[256,2048]{1,0:T(8,128)(2,1)S(1)}, bf16[256,2048]{1,0:T(8,128)(2,1)}, u32[]{:S(2)}, u32[]{:S(2)}) collective-permute-start(bf16[256,2048]{1,0:T(8,128)(2,1)S(1)} %collective-permute-done.1.refs_2_), channel_id=1, source_target_pairs={{0,4},{4,0},{8,12},{12,8},{16,20},{20,16},{24,28},{28,24},{1,5},{5... | collective-permute-start | bytes 3145736 | tf_op jit(solution)/shard_map/ppermute | solution.py:1682
  107.0 14.3 %collective-permute-start.4 = (bf16[256,2048]{1,0:T(8,128)(2,1)}, bf16[256,2048]{1,0:T(8,128)(2,1)}, u32[]{:S(2)}, u32[]{:S(2)}) collective-permute-start(bf16[256,2048]{1,0:T(8,128)(2,1)} %collective-permute-done.3.refs_4_), channel_id=1, source_target_pairs={{0,4},{4,0},{8,12},{12,8},{16,20},{20,16},{24,28},{28,24},{1,5},{5... | collective-permute-start | bytes 3145736 | tf_op jit(solution)/shard_map/ppermute | solution.py:1682
  116.5 4.6 collective-permute-start.7
  119.2 2.1 collective-permute-start.8
  139.0 25.7 %collective-permute-start.11 = (bf16[256,2048]{1,0:T(8,128)(2,1)}, bf16[256,2048]{1,0:T(8,128)(2,1)S(1)}, u32[]{:S(2)}, u32[]{:S(2)}) collective-permute-start(bf16[256,2048]{1,0:T(8,128)(2,1)} %shard_map.310.refs_0_), channel_id=1, source_target_pairs={{0,16},{4,20},{8,24},{12,28},{16,0},{20,4},{24,8},{28,12},{1,17},{... | collective-permute-start | bytes 3145736 | tf_op jit(solution)/shard_map/ppermute | solution.py:1682
  139.8 26.9 %collective-permute-start.10 = (bf16[256,2048]{1,0:T(8,128)(2,1)}, bf16[256,2048]{1,0:T(8,128)(2,1)S(1)}, u32[]{:S(2)}, u32[]{:S(2)}) collective-permute-start(bf16[256,2048]{1,0:T(8,128)(2,1)} %shard_map.310.refs_0_), channel_id=1, source_target_pairs={{0,8},{4,12},{8,0},{12,4},{16,24},{20,28},{24,16},{28,20},{1,9},{5... | collective-permute-start | bytes 3145736 | tf_op jit(solution)/shard_map/ppermute | solution.py:1682
  141.6 38.7 %collective-permute-start.9 = (bf16[256,2048]{1,0:T(8,128)(2,1)}, bf16[256,2048]{1,0:T(8,128)(2,1)}, u32[]{:S(2)}, u32[]{:S(2)}) collective-permute-start(bf16[256,2048]{1,0:T(8,128)(2,1)} %shard_map.310.refs_0_), channel_id=1, source_target_pairs={{0,4},{4,0},{8,12},{12,8},{16,20},{20,16},{24,28},{28,24},{1,5},{5... | collective-permute-start | bytes 3145736 | tf_op jit(solution)/shard_map/ppermute | solution.py:1682
  141.6 50.4 %collective-permute-start.12 = (bf16[2048,256]{1,0:T(8,128)(2,1)}, bf16[2048,256]{1,0:T(8,128)(2,1)}, u32[]{:S(2)}, u32[]{:S(2)}) collective-permute-start(bf16[2048,256]{1,0:T(8,128)(2,1)} %get-tuple-element.62.refs_10_.refs_5_), channel_id=1, source_target_pairs={{0,1},{1,2},{2,3},{3,0},{4,5},{5,6},{6,7},{7,4},{8,9},{9,10},{10,1... | collective-permute-start | bytes 3145736 | tf_op jit(solution)/shard_map/ppermute | solution.py:1862
  165.6 26.9 %collective-permute-start.16 = (bf16[128,2048]{1,0:T(8,128)(2,1)}, bf16[128,2048]{1,0:T(8,128)(2,1)}, u32[]{:S(2)}, u32[]{:S(2)}) collective-permute-start(bf16[128,2048]{1,0:T(8,128)(2,1)} %shard_map.319), channel_id=1, source_target_pairs={{0,8},{4,12},{8,0},{12,4},{16,24},{20,28},{24,16},{28,20},{1,9},{5... | collective-permute-start | bytes 1572872 | tf_op jit(solution)/shard_map/ppermute | solution.py:1682
  167.6 25.0 %collective-permute-start.15 = (bf16[128,2048]{1,0:T(8,128)(2,1)}, bf16[128,2048]{1,0:T(8,128)(2,1)}, u32[]{:S(2)}, u32[]{:S(2)}) collective-permute-start(bf16[128,2048]{1,0:T(8,128)(2,1)} %shard_map.318), channel_id=1, source_target_pairs={{0,16},{4,20},{8,24},{12,28},{16,0},{20,4},{24,8},{28,12},{1,17},{... | collective-permute-start | bytes 1572872 | tf_op jit(solution)/shard_map/ppermute | solution.py:1682
  173.3 33.3 %all-to-all-start.2 = ((bf16[8,256,256]{2,1,0:T(8,128)(2,1)}), bf16[8,256,256]{2,1,0:T(8,128)(2,1)S(1)}, u32[]{:S(2)}, u32[]{:S(2)}) async-start(bf16[8,256,256]{2,1,0:T(8,128)(2,1)} %get-tuple-element.67.att_ref.refs_1_), calls=%async_computation.2 | async-start | bytes 2097152 | tf_op jit(solution)/shard_map/all_to_all | solution.py:1982
  176.9 146.4 %all-gather.19.cloned.1.call-start = ((), (), s32[]{:S(2)}) async-start(), calls=%async_computation.12 | async-start | bytes 2621440 | tf_op jit(solution)/shard_map/all_gather | solution.py:1976
  179.2 169.2 %all-gather.17.cloned.1.call-start = ((), (), s32[]{:S(2)}) async-start(), calls=%async_computation.11 | async-start | bytes 2621440 | tf_op jit(solution)/shard_map/all_gather | solution.py:1976
  179.8 26.9 %collective-permute-start.13 = (bf16[256,2048]{1,0:T(8,128)(2,1)S(1)}, bf16[256,2048]{1,0:T(8,128)(2,1)}, u32[]{:S(2)}, u32[]{:S(2)}) collective-permute-start(bf16[256,2048]{1,0:T(8,128)(2,1)S(1)} %collective-permute-done.10.refs_2_), channel_id=1, source_target_pairs={{0,4},{4,0},{8,12},{12,8},{16,20},{20,16},{24,28},{28,24},{1,5},{5... | collective-permute-start | bytes 3145736 | tf_op jit(solution)/shard_map/ppermute | solution.py:1682
  180.3 26.4 %collective-permute-start.14 = (bf16[256,2048]{1,0:T(8,128)(2,1)S(1)}, bf16[256,2048]{1,0:T(8,128)(2,1)}, u32[]{:S(2)}, u32[]{:S(2)}) collective-permute-start(bf16[256,2048]{1,0:T(8,128)(2,1)S(1)} %collective-permute-done.11.refs_3_.refs_4_), channel_id=1, source_target_pairs={{0,4},{4,0},{8,12},{12,8},{16,20},{20,16},{24,28},{28,24},{1,5},{5... | collective-permute-start | bytes 3145736 | tf_op jit(solution)/shard_map/ppermute | solution.py:1682
  192.6 14.1 %collective-permute-start.18 = (bf16[128,2048]{1,0:T(8,128)(2,1)}, bf16[128,2048]{1,0:T(8,128)(2,1)}, u32[]{:S(2)}, u32[]{:S(2)}) collective-permute-start(bf16[128,2048]{1,0:T(8,128)(2,1)} %collective-permute-done.16.refs_7_), channel_id=1, source_target_pairs={{0,4},{4,0},{8,12},{12,8},{16,20},{20,16},{24,28},{28,24},{1,5},{5... | collective-permute-start | bytes 1572872 | tf_op jit(solution)/shard_map/ppermute | solution.py:1682
  192.7 14.0 %collective-permute-start.17 = (bf16[128,2048]{1,0:T(8,128)(2,1)}, bf16[128,2048]{1,0:T(8,128)(2,1)}, u32[]{:S(2)}, u32[]{:S(2)}) collective-permute-start(bf16[128,2048]{1,0:T(8,128)(2,1)} %collective-permute-done.15.refs_6_), channel_id=1, source_target_pairs={{0,4},{4,0},{8,12},{12,8},{16,20},{20,16},{24,28},{28,24},{1,5},{5... | collective-permute-start | bytes 1572872 | tf_op jit(solution)/shard_map/ppermute | solution.py:1682
  206.6 50.4 %collective-permute-start.23 = (bf16[2048,256]{1,0:T(8,128)(2,1)}, bf16[2048,256]{1,0:T(8,128)(2,1)}, u32[]{:S(2)}, u32[]{:S(2)}) collective-permute-start(bf16[2048,256]{1,0:T(8,128)(2,1)} %collective-permute-done.12.refs_4_.refs_11_.refs_6_), channel_id=1, source_target_pairs={{0,1},{1,2},{2,3},{3,0},{4,5},{5,6},{6,7},{7,4},{8,9},{9,10},{10,1... | collective-permute-start | bytes 3145736 | tf_op jit(solution)/shard_map/ppermute | solution.py:1862
  220.7 25.5 %collective-permute-start.21 = (bf16[256,2048]{1,0:T(8,128)(2,1)}, bf16[256,2048]{1,0:T(8,128)(2,1)}, u32[]{:S(2)}, u32[]{:S(2)}) collective-permute-start(bf16[256,2048]{1,0:T(8,128)(2,1)} %get-tuple-element.70.refs_1_.refs_0_), channel_id=1, source_target_pairs={{0,16},{4,20},{8,24},{12,28},{16,0},{20,4},{24,8},{28,12},{1,17},{... | collective-permute-start | bytes 3145736 | tf_op jit(solution)/shard_map/ppermute | solution.py:1682
  221.2 27.1 %collective-permute-start.19 = (bf16[256,2048]{1,0:T(8,128)(2,1)}, bf16[256,2048]{1,0:T(8,128)(2,1)}, u32[]{:S(2)}, u32[]{:S(2)}) collective-permute-start(bf16[256,2048]{1,0:T(8,128)(2,1)} %get-tuple-element.70.refs_1_.refs_0_), channel_id=1, source_target_pairs={{0,8},{4,12},{8,0},{12,4},{16,24},{20,28},{24,16},{28,20},{1,9},{5... | collective-permute-start | bytes 3145736 | tf_op jit(solution)/shard_map/ppermute | solution.py:1682
  248.1 13.3 %collective-permute-start.22 = (bf16[128,2048]{1,0:T(8,128)(2,1)}, bf16[128,2048]{1,0:T(8,128)(2,1)S(1)}, u32[]{:S(2)}, u32[]{:S(2)}) collective-permute-start(bf16[128,2048]{1,0:T(8,128)(2,1)} %shard_map.324), channel_id=1, source_target_pairs={{0,8},{4,12},{8,0},{12,4},{16,24},{20,28},{24,16},{28,20},{1,9},{5... | collective-permute-start | bytes 1572872 | tf_op jit(solution)/shard_map/ppermute | solution.py:1682
  250.2 13.0 %collective-permute-start.20 = (bf16[128,2048]{1,0:T(8,128)(2,1)}, bf16[128,2048]{1,0:T(8,128)(2,1)S(1)}, u32[]{:S(2)}, u32[]{:S(2)}) collective-permute-start(bf16[128,2048]{1,0:T(8,128)(2,1)} %shard_map.323), channel_id=1, source_target_pairs={{0,16},{4,20},{8,24},{12,28},{16,0},{20,4},{24,8},{28,12},{1,17},{... | collective-permute-start | bytes 1572872 | tf_op jit(solution)/shard_map/ppermute | solution.py:1682
  251.5 16.5 %collective-permute-start.27 = (bf16[256,2048]{1,0:T(8,128)(2,1)S(1)}, bf16[256,2048]{1,0:T(8,128)(2,1)}, u32[]{:S(2)}, u32[]{:S(2)}) collective-permute-start(bf16[256,2048]{1,0:T(8,128)(2,1)S(1)} %copy-done.10), channel_id=1, source_target_pairs={{0,4},{4,0},{8,12},{12,8},{16,20},{20,16},{24,28},{28,24},{1,5},{5... | collective-permute-start | bytes 3145736 | tf_op jit(solution)/shard_map/ppermute | solution.py:1682
  264.1 23.5 %collective-permute-start.25 = (bf16[256,2048]{1,0:T(8,128)(2,1)}, bf16[256,2048]{1,0:T(8,128)(2,1)}, u32[]{:S(2)}, u32[]{:S(2)}) collective-permute-start(bf16[256,2048]{1,0:T(8,128)(2,1)} %shard_map.325), channel_id=1, source_target_pairs={{0,16},{4,20},{8,24},{12,28},{16,0},{20,4},{24,8},{28,12},{1,17},{... | collective-permute-start | bytes 3145736 | tf_op jit(solution)/shard_map/ppermute | solution.py:1682
  265.2 23.1 %collective-permute-start.24 = (bf16[256,2048]{1,0:T(8,128)(2,1)}, bf16[256,2048]{1,0:T(8,128)(2,1)}, u32[]{:S(2)}, u32[]{:S(2)}) collective-permute-start(bf16[256,2048]{1,0:T(8,128)(2,1)} %shard_map.325), channel_id=1, source_target_pairs={{0,8},{4,12},{8,0},{12,4},{16,24},{20,28},{24,16},{28,20},{1,9},{5... | collective-permute-start | bytes 3145736 | tf_op jit(solution)/shard_map/ppermute | solution.py:1682
  266.4 24.8 %collective-permute-start.32 = (bf16[2048,256]{1,0:T(8,128)(2,1)}, bf16[2048,256]{1,0:T(8,128)(2,1)}, u32[]{:S(2)}, u32[]{:S(2)}) collective-permute-start(bf16[2048,256]{1,0:T(8,128)(2,1)} %collective-permute-done.23.refs_3_.refs_12_.refs_7_), channel_id=1, source_target_pairs={{0,1},{1,2},{2,3},{3,0},{4,5},{5,6},{6,7},{7,4},{8,9},{9,10},{10,1... | collective-permute-start | bytes 3145736 | tf_op jit(solution)/shard_map/ppermute | solution.py:1862
  268.0 26.6 %collective-permute-start.28 = (bf16[256,2048]{1,0:T(8,128)(2,1)}, bf16[256,2048]{1,0:T(8,128)(2,1)}, u32[]{:S(2)}, u32[]{:S(2)}) collective-permute-start(bf16[256,2048]{1,0:T(8,128)(2,1)} %collective-permute-done.19.refs_2_), channel_id=1, source_target_pairs={{0,4},{4,0},{8,12},{12,8},{16,20},{20,16},{24,28},{28,24},{1,5},{5... | collective-permute-start | bytes 3145736 | tf_op jit(solution)/shard_map/ppermute | solution.py:1682
  268.0 26.6 %collective-permute-start.29 = (bf16[256,2048]{1,0:T(8,128)(2,1)}, bf16[256,2048]{1,0:T(8,128)(2,1)}, u32[]{:S(2)}, u32[]{:S(2)}) collective-permute-start(bf16[256,2048]{1,0:T(8,128)(2,1)} %collective-permute-done.21.refs_4_), channel_id=1, source_target_pairs={{0,4},{4,0},{8,12},{12,8},{16,20},{20,16},{24,28},{28,24},{1,5},{5... | collective-permute-start | bytes 3145736 | tf_op jit(solution)/shard_map/ppermute | solution.py:1682
  287.5 4.3 collective-permute-start.31
  288.3 5.0 collective-permute-start.30
  288.8 284.6 %reduce-scatter.2.cloned.1.call-start = ((), (), s32[]{:S(2)}) async-start(), calls=%async_computation.7 | async-start | bytes 9437184 | tf_op jit(solution)/shard_map/reduce_scatter | solution.py:2017
  291.3 32.0 %collective-permute-start.34 = (bf16[256,2048]{1,0:T(8,128)(2,1)S(1)}, bf16[256,2048]{1,0:T(8,128)(2,1)}, u32[]{:S(2)}, u32[]{:S(2)}) collective-permute-start(bf16[256,2048]{1,0:T(8,128)(2,1)S(1)} %copy-done.5), channel_id=1, source_target_pairs={{0,4},{4,0},{8,12},{12,8},{16,20},{20,16},{24,28},{28,24},{1,5},{5... | collective-permute-start | bytes 3145736 | tf_op jit(solution)/shard_map/ppermute | solution.py:1682
  291.8 29.3 %collective-permute-start.33 = (bf16[128,2048]{1,0:T(8,128)(2,1)S(1)}, bf16[128,2048]{1,0:T(8,128)(2,1)S(1)}, u32[]{:S(2)}, u32[]{:S(2)}) collective-permute-start(bf16[128,2048]{1,0:T(8,128)(2,1)S(1)} %slice.189), channel_id=1, source_target_pairs={{0,8},{4,12},{8,0},{12,4},{16,24},{20,28},{24,16},{28,20},{1,9},{5... | collective-permute-start | bytes 1572872 | tf_op jit(solution)/shard_map/ppermute | solution.py:1682
  293.3 28.8 %collective-permute-start.26 = (bf16[128,2048]{1,0:T(8,128)(2,1)S(1)}, bf16[128,2048]{1,0:T(8,128)(2,1)S(1)}, u32[]{:S(2)}, u32[]{:S(2)}) collective-permute-start(bf16[128,2048]{1,0:T(8,128)(2,1)S(1)} %slice.188), channel_id=1, source_target_pairs={{0,16},{4,20},{8,24},{12,28},{16,0},{20,4},{24,8},{28,12},{1,17},{... | collective-permute-start | bytes 1572872 | tf_op jit(solution)/shard_map/ppermute | solution.py:1682
  294.6 28.7 %collective-permute-start.35 = (bf16[256,2048]{1,0:T(8,128)(2,1)}, bf16[256,2048]{1,0:T(8,128)(2,1)}, u32[]{:S(2)}, u32[]{:S(2)}) collective-permute-start(bf16[256,2048]{1,0:T(8,128)(2,1)} %collective-permute-done.24.refs_2_.refs_1_), channel_id=1, source_target_pairs={{0,4},{4,0},{8,12},{12,8},{16,20},{20,16},{24,28},{28,24},{1,5},{5... | collective-permute-start | bytes 3145736 | tf_op jit(solution)/shard_map/ppermute | solution.py:1682
  294.6 28.7 %collective-permute-start.36 = (bf16[256,2048]{1,0:T(8,128)(2,1)}, bf16[256,2048]{1,0:T(8,128)(2,1)}, u32[]{:S(2)}, u32[]{:S(2)}) collective-permute-start(bf16[256,2048]{1,0:T(8,128)(2,1)} %collective-permute-done.25.refs_4_.refs_2_), channel_id=1, source_target_pairs={{0,4},{4,0},{8,12},{12,8},{16,20},{20,16},{24,28},{28,24},{1,5},{5... | collective-permute-start | bytes 3145736 | tf_op jit(solution)/shard_map/ppermute | solution.py:1682
  322.0 2.1 collective-permute-start.38
  322.9 2.1 collective-permute-start.37
  363.2 15.1 %collective-permute-start.39 = (bf16[4,256,2048]{2,1,0:T(8,128)(2,1)}, bf16[4,256,2048]{2,1,0:T(8,128)(2,1)S(1)}, u32[]{:S(2)}, u32[]{:S(2)}) collective-permute-start(bf16[4,256,2048]{2,1,0:T(8,128)(2,1)} %bitcast.76), channel_id=1, source_target_pairs={{0,4},{4,0},{8,12},{12,8},{16,20},{20,16},{24,28},{28,24},{1,5},{5... | collective-permute-start | bytes 12582920 | tf_op jit(solution)/shard_map/ppermute | solution.py:1682
  386.5 25.4 %collective-permute-start.40 = (bf16[256,2048]{1,0:T(8,128)(2,1)}, bf16[256,2048]{1,0:T(8,128)(2,1)S(1)}, u32[]{:S(2)}, u32[]{:S(2)}) collective-permute-start(bf16[256,2048]{1,0:T(8,128)(2,1)} %get-tuple-element.79), channel_id=1, source_target_pairs={{0,8},{4,12},{8,0},{12,4},{16,24},{20,28},{24,16},{28,20},{1,9},{5... | collective-permute-start | bytes 3145736 | tf_op jit(solution)/shard_map/ppermute | solution.py:1682
  387.4 25.5 %collective-permute-start.41 = (bf16[256,2048]{1,0:T(8,128)(2,1)}, bf16[256,2048]{1,0:T(8,128)(2,1)S(1)}, u32[]{:S(2)}, u32[]{:S(2)}) collective-permute-start(bf16[256,2048]{1,0:T(8,128)(2,1)} %get-tuple-element.81), channel_id=1, source_target_pairs={{0,16},{4,20},{8,24},{12,28},{16,0},{20,4},{24,8},{28,12},{1,17},{... | collective-permute-start | bytes 3145736 | tf_op jit(solution)/shard_map/ppermute | solution.py:1682
  412.0 13.3 %collective-permute-start.43 = (bf16[128,2048]{1,0:T(8,128)(2,1)S(1)}, bf16[128,2048]{1,0:T(8,128)(2,1)}, u32[]{:S(2)}, u32[]{:S(2)}) collective-permute-start(bf16[128,2048]{1,0:T(8,128)(2,1)S(1)} %add_convert_fusion.3), channel_id=1, source_target_pairs={{0,16},{4,20},{8,24},{12,28},{16,0},{20,4},{24,8},{28,12},{1,17},{... | collective-permute-start | bytes 1572872 | tf_op jit(solution)/shard_map/ppermute | solution.py:1682
  414.5 13.0 %collective-permute-start.42 = (bf16[128,2048]{1,0:T(8,128)(2,1)S(1)}, bf16[128,2048]{1,0:T(8,128)(2,1)}, u32[]{:S(2)}, u32[]{:S(2)}) collective-permute-start(bf16[128,2048]{1,0:T(8,128)(2,1)S(1)} %add_convert_fusion.4), channel_id=1, source_target_pairs={{0,8},{4,12},{8,0},{12,4},{16,24},{20,28},{24,16},{28,20},{1,9},{5... | collective-permute-start | bytes 1572872 | tf_op jit(solution)/shard_map/ppermute | solution.py:1682
  474.8 32.4 %copy-start.28 = (bf16[256,128]{1,0:T(8,128)(2,1)S(1)}, bf16[256,128]{1,0:T(8,128)(2,1)}, u32[]{:S(2)}) copy-start(bf16[256,128]{1,0:T(8,128)(2,1)} %get-tuple-element.104) | copy-start | bytes 196612
  505.3 7.6 %collective-permute-start.44 = (bf16[4,256,2048]{2,1,0:T(8,128)(2,1)}, bf16[4,256,2048]{2,1,0:T(8,128)(2,1)}, u32[]{:S(2)}, u32[]{:S(2)}) collective-permute-start(bf16[4,256,2048]{2,1,0:T(8,128)(2,1)} %get-tuple-element.95), channel_id=1, source_target_pairs={{0,4},{4,0},{8,12},{12,8},{16,20},{20,16},{24,28},{28,24},{1,5},{5... | collective-permute-start | bytes 12582920 | tf_op jit(solution)/shard_map/ppermute | solution.py:1682
  519.0 25.4 %collective-permute-start.45 = (bf16[256,2048]{1,0:T(8,128)(2,1)}, bf16[256,2048]{1,0:T(8,128)(2,1)S(1)}, u32[]{:S(2)}, u32[]{:S(2)}) collective-permute-start(bf16[256,2048]{1,0:T(8,128)(2,1)} %get-tuple-element.97), channel_id=1, source_target_pairs={{0,8},{4,12},{8,0},{12,4},{16,24},{20,28},{24,16},{28,20},{1,9},{5... | collective-permute-start | bytes 3145736 | tf_op jit(solution)/shard_map/ppermute | solution.py:1682
  521.3 27.6 %collective-permute-start.46 = (bf16[256,2048]{1,0:T(8,128)(2,1)}, bf16[256,2048]{1,0:T(8,128)(2,1)}, u32[]{:S(2)}, u32[]{:S(2)}) collective-permute-start(bf16[256,2048]{1,0:T(8,128)(2,1)} %get-tuple-element.99), channel_id=1, source_target_pairs={{0,16},{4,20},{8,24},{12,28},{16,0},{20,4},{24,8},{28,12},{1,17},{... | collective-permute-start | bytes 3145736 | tf_op jit(solution)/shard_map/ppermute | solution.py:1682
  524.7 20.1 %all-to-all-start.5 = ((f32[4,1,5888]{2,1,0:T(1,128)}), f32[4,1,5888]{2,1,0:T(1,128)S(1)}, u32[]{:S(2)}, u32[]{:S(2)}) async-start(f32[4,1,5888]{2,1,0:T(1,128)} %copy.136), calls=%async_computation.6 | async-start | bytes 188416 | tf_op jit(solution)/shard_map/all_to_all | solution.py:2061
  544.6 21.2 %collective-permute-start.48 = (bf16[128,2048]{1,0:T(8,128)(2,1)S(1)}, bf16[128,2048]{1,0:T(8,128)(2,1)}, u32[]{:S(2)}, u32[]{:S(2)}) collective-permute-start(bf16[128,2048]{1,0:T(8,128)(2,1)S(1)} %add_convert_fusion.1), channel_id=1, source_target_pairs={{0,16},{4,20},{8,24},{12,28},{16,0},{20,4},{24,8},{28,12},{1,17},{... | collective-permute-start | bytes 1572872 | tf_op jit(solution)/shard_map/ppermute | solution.py:1682
  544.8 16.9 %all-to-all-start.4 = ((f32[32,1,2624]{2,1,0:T(1,128)}), f32[32,1,2624]{2,1,0:T(1,128)S(1)}, u32[]{:S(2)}, u32[]{:S(2)}) async-start(f32[32,1,2624]{2,1,0:T(1,128)} %reshape.203), calls=%async_computation.5 | async-start | bytes 688128 | tf_op jit(solution)/shard_map/all_to_all | solution.py:2045
  550.1 16.8 %collective-permute-start.47 = (bf16[128,2048]{1,0:T(8,128)(2,1)S(1)}, bf16[128,2048]{1,0:T(8,128)(2,1)S(1)}, u32[]{:S(2)}, u32[]{:S(2)}) collective-permute-start(bf16[128,2048]{1,0:T(8,128)(2,1)S(1)} %add_convert_fusion.2), channel_id=1, source_target_pairs={{0,8},{4,12},{8,0},{12,4},{16,24},{20,28},{24,16},{28,20},{1,9},{5... | collective-permute-start | bytes 1572872 | tf_op jit(solution)/shard_map/ppermute | solution.py:1682
  (44 other events, 466.6 us)
Sparse Core Ops, SparseCore 0:
  23.9 36.4 all-gather.12
  62.0 26.7 all-gather.10
  90.4 102.5 all-gather.14
  194.5 66.7 all-gather.18
  288.9 46.3 all-gather.16
  415.4 82.6 reduce-scatter.1

commit v4 on v3

--- a/solution.py
+++ b/solution.py
@@ -1533,34 +1533,50 @@
     )
 
 
-def branch_kernel(
-    counts, place_ref, *refs
-):
+def start_all(blocks, buffer, sems):
+    for number, parts in enumerate(blocks):
+        height = buffer.shape[1] // len(parts)
+        for part, ref in enumerate(parts):
+            pltpu.make_async_copy(
+                ref, buffer.at[number, part * height : (part + 1) * height], sems.at[number]
+            ).start()
+
+
+def all_scratch(blocks):
+    rows, wide = block_shape(blocks)
+    return [
+        pltpu.VMEM((len(blocks), rows, wide), jnp.bfloat16),
+        pltpu.SemaphoreType.DMA((len(blocks),)),
+    ]
+
+
+def placed_rows(ref, place, rows):
+    return ref[pl.ds(pl.multiple_of(place * rows, rows), rows)]
+
+
+def branch_kernel(counts, place_ref, *refs):
     blocks, refs = grouped(refs, counts)
     (
         att_ref, down_ref, up_ref, tokens_ref, gain_ref,
-        residual_ref, normed_ref, inverse_ref, narrow_ref, buffer, sems, total, slim,
+        residual_ref, normed_ref, inverse_ref, narrow_ref, buffer, sems,
     ) = refs
-    step = pl.program_id(0)
-    slot = fetch(blocks, buffer, sems, step)
-
-    @pl.when(step == 0)
-    def _():
-        total[...] = tokens_ref[...].astype(jnp.float32)
-        slim[...] = jnp.zeros_like(slim)
-
-    total[...] += mm_tn(att_ref[...], buffer[slot])
-    slim[...] += mm_tn(att_ref[...], down_ref[...])
-
-    @pl.when(step == pl.num_programs(0) - 1)
-    def _():
-        narrow = slim[...].astype(jnp.bfloat16)
-        narrow_ref[...] = narrow
-        residual = total[...] + mm_nt(narrow, up_ref[...])
-        residual_ref[...] = residual
-        inverse = lax.rsqrt(jnp.mean(residual * residual, axis=-1, keepdims=True) + epsilon)
-        inverse_ref[...] = jnp.broadcast_to(inverse, inverse_ref.shape)
-        normed_ref[...] = (residual * inverse * gain_ref[...]).astype(jnp.bfloat16)
+    start_all(blocks, buffer, sems)
+    width = att_ref.shape[1]
+    total, slim = tokens_ref[...].astype(jnp.float32), None
+    for number in range(len(blocks)):
+        place = lax.bitwise_xor(place_ref[0], number)
+        att = att_ref[place]
+        part = mm_tn(att, placed_rows(down_ref, place, width))
+        slim = part if slim is None else slim + part
+        wait_whole(buffer.at[number], sems.at[number])
+        total = total + mm_tn(att, buffer[number])
+    narrow = slim.astype(jnp.bfloat16)
+    narrow_ref[...] = narrow
+    residual = total + mm_nt(narrow, up_ref[...])
+    residual_ref[...] = residual
+    inverse = lax.rsqrt(jnp.mean(residual * residual, axis=-1, keepdims=True) + epsilon)
+    inverse_ref[...] = jnp.broadcast_to(inverse, inverse_ref.shape)
+    normed_ref[...] = (residual * inverse * gain_ref[...]).astype(jnp.bfloat16)
 
 
 def branch_out(place_row, blocks, att, down_wide, up_wide, tokens, gain):
@@ -1571,15 +1587,9 @@
     wide = jnp.float32
     return call(
         functools.partial(branch_kernel, counts),
-        (places,),
+        (1,),
         [ANYWHERE] * sum(counts)
-        + [
-            spec_placed(spec_block(query_width, rows)),
-            spec_placed(spec_down(query_width, spare)),
-            spec_whole(model, spare),
-            spec_whole(rows, model),
-            spec_whole(1, model),
-        ],
+        + [spec_whole(*part.shape) for part in (att, down_wide, up_wide, tokens, gain)],
         [
             spec_whole(rows, model),
             spec_whole(rows, model),
@@ -1592,8 +1602,7 @@
             array(rows, 128, dtype=wide),
             array(rows, spare),
         ],
-        fetch_scratch(blocks)
-        + [pltpu.VMEM((rows, model), wide), pltpu.VMEM((rows, spare), wide)],
+        all_scratch(blocks),
         0,
         13,
         scalars=1,
@@ -1607,31 +1616,31 @@
         down_ref, up_ref,
         grad_att_ref, grad_ref, branch_ref, slim_ref, buffer, sems,
     ) = refs
-    step = pl.program_id(0)
-    slot = fetch(blocks, buffer, sems, step)
-
-    @pl.when(step == 0)
-    def _():
-        wide = jnp.float32
-        middle = late_x.shape[0]
-        for start, part in enumerate(sums_of(own_ref, from_x, late_x, late_y, from_y)):
-            span = slice(start * middle, (start + 1) * middle)
-            residual, inverse = residual_ref[span], inverse_ref[span, :1]
-            scaled = part * gain_ref[...]
-            mean = jnp.mean(scaled * residual, axis=-1, keepdims=True)
-            grad = (
-                cot_ref[span].astype(wide)
-                + inverse * scaled
-                - residual * (inverse * inverse * inverse * mean)
-            )
-            grad_ref[span] = grad
-            branch_ref[span] = grad.astype(jnp.bfloat16)
-        slim_ref[...] = mm(branch_ref[...], up_ref[...])
-
-    slim = slim_ref[...].astype(jnp.bfloat16)
-    grad_att_ref[...] = (
-        mm_nt(buffer[slot], branch_ref[...]) + mm_nt(down_ref[...], slim)
-    ).astype(jnp.bfloat16)
+    start_all(blocks, buffer, sems)
+    wide = jnp.float32
+    middle = late_x.shape[0]
+    for start, part in enumerate(sums_of(own_ref, from_x, late_x, late_y, from_y)):
+        span = slice(start * middle, (start + 1) * middle)
+        residual, inverse = residual_ref[span], inverse_ref[span, :1]
+        scaled = part * gain_ref[...]
+        mean = jnp.mean(scaled * residual, axis=-1, keepdims=True)
+        grad = (
+            cot_ref[span].astype(wide)
+            + inverse * scaled
+            - residual * (inverse * inverse * inverse * mean)
+        )
+        grad_ref[span] = grad
+        branch_ref[span] = grad.astype(jnp.bfloat16)
+    branch = branch_ref[...]
+    slim = mm(branch, up_ref[...])
+    slim_ref[...] = slim
+    slim = slim.astype(jnp.bfloat16)
+    width = grad_att_ref.shape[1]
+    for number in range(len(blocks)):
+        place = lax.bitwise_xor(place_ref[0], number)
+        part = mm_nt(placed_rows(down_ref, place, width), slim)
+        wait_whole(buffer.at[number], sems.at[number])
+        grad_att_ref[place] = (mm_nt(buffer[number], branch) + part).astype(jnp.bfloat16)
 
 
 def branch_back(
@@ -1643,21 +1652,13 @@
     spare = down_wide.shape[1]
     counts = [len(found) for found in blocks]
     wide = jnp.float32
+    given = (*sums, residual, inverse, gain, cotangent, down_wide, up_wide)
     return call(
         functools.partial(branch_back_kernel, counts),
-        (places,),
-        [ANYWHERE] * sum(counts)
-        + [spec_whole(*part.shape) for part in sums]
-        + [
-            spec_whole(rows, model),
-            spec_whole(rows, 128),
-            spec_whole(1, model),
-            spec_whole(rows, model),
-            spec_placed(spec_down(query_width, spare)),
-            spec_whole(model, spare),
-        ],
+        (1,),
+        [ANYWHERE] * sum(counts) + [spec_whole(*part.shape) for part in given],
         [
-            spec_placed(spec_block(query_width, rows)),
+            spec_whole(places, query_width, rows),
             spec_whole(rows, model),
             spec_whole(rows, model),
             spec_whole(rows, spare),
@@ -1668,13 +1669,11 @@
             array(rows, model),
             array(rows, spare, dtype=wide),
         ],
-        fetch_scratch(blocks),
+        all_scratch(blocks),
         0,
         15,
         scalars=1,
-    )(
-        place_row, *flat(blocks), *sums, residual, inverse, gain, cotangent, down_wide, up_wide
-    )
+    )(place_row, *flat(blocks), *given)
 
 
 def exchanged(value, bits):
@@ -1781,11 +1780,11 @@
 
 def core_sums(keep, got):
     _, rows, model = keep.shape
-    wide = model // 4
+    wide = model // 2
     block = pl.BlockSpec((4, rows, wide), lambda i: (0, 0, i))
     return call(
         core_sums_kernel,
-        (4,),
+        (2,),
         [block] * 2,
         [spec_across(rows, wide)] * 3 + [spec_across(rows // 2, wide)] * 2,
         [array(rows, model, dtype=jnp.float32)]

time: 592 us -> 587 us (level)
  Pallas kernels: 242 us -> 235 us
    pallas_call x4, Pallas kernels: 41.3 us -> 34.5 us  [the longest x1 13.8 us: branch_back(): call(functools.partial(branch_back_kernel, counts), (1,), [ANYWHERE] * su...]
  transfers between devices with their start and end apart: 59 -> 59, of which waited for: 23 -> 24; matrix products, arithmetic and copies ran while one was open for 8% -> 8% of each run, Pallas kernels for 38% -> 37%
where the time goes in v4:
time: 587 us; the launch traced here: 580 us
  Pallas kernels  235 us (40%)
  waiting for transfers between devices  171 us (29%)
  starting transfers between devices  50.1 us (9%)
  blocking collectives  44.6 us (8%)
  local copies, waits for them, and re-layouts  43.5 us (7%)
  between operations  19 us (3%)
  other arithmetic  14.2 us (2%)
    ppermute x46, waiting for transfers between devices, exchanged(): lax.ppermute(value, 'seq', [(place, place ^ bits) for place in range(coun...  109 us
    pallas_call x3, Pallas kernels, ffn_back(): call(functools.partial(ffn_back_kernel, counts, len(gates), part, more),...  52 us
    all_to_all x1, waiting for transfers between devices, by_heads(): swapped = lax.all_to_all(swapped, 'seq', 0, 0, tiled=True)  36.8 us
    all_to_all x1, blocking collectives, by_heads(): grad_att = lax.all_to_all(grad_att, 'seq', 0, 0, tiled=True)  31.2 us
    pallas_call x1, Pallas kernels, heads_back(): call(functools.partial(backward_kernel, counts), (steps,), [ANYWHERE] * s...  30 us
    pallas_call x2, Pallas kernels, teach(): pl.pallas_call(functools.partial(teacher_kernel, first, end - first), gri...  28.9 us
    ppermute x46, starting transfers between devices, exchanged(): lax.ppermute(value, 'seq', [(place, place ^ bits) for place in range(coun...  26.3 us
    pallas_call x1, Pallas kernels, hidden_units(): call(functools.partial(hidden_kernel, counts), (len(blocks),), [ANYWHERE]...  26.2 us
  transfers between devices with their start and end apart: 59, of which 24 were waited for; matrix products, arithmetic and copies ran while one was open for 8% of the time, Pallas kernels for 37%

profile of v4, /device:TPU:0, one launch (start us, length us, event | category | flops | bytes accessed | tf_op | source)
XLA Modules:
  0.0 579.6 jit_solution(12541040353994894972)
XLA Ops:
  10.4 13.4 %all_to_all.34.refs_1_ = bf16[8,64,384]{2,1,0:T(8,128)(2,1)} all-to-all(bf16[8,64,384]{2,1,0:T(8,128)(2,1)S(1)} %maximum_bitcast_fusion.1), channel_id=1, replica_groups=mesh['seq'=8,'fsdp'=4] {'seq'}, dimensions={0} | all-to-all | bytes 786432 | tf_op jit(solution)/shard_map/all_to_all | solution.py:1916
  23.8 6.2 %shard_map.311.refs_0_ = bf16[8,3,256,256]{3,2,1,0:T(8,128)(2,1)} custom-call(bf16[256,2048]{1,0:T(8,128)(2,1)} %refs_0_.1, bf16[256,2048]{1,0:T(8,128)(2,1)} %refs_1_.1, bf16[256,2048]{1,0:T(8,128)(2,1)} %refs_2_.1), custom_call_target="tpu_custom_call" | custom-call | flops 6899999744 | bytes 1 | tf_op jit(solution)/shard_map/pallas_call | solution.py:1708
  30.1 4.6 all-to-all-start.1
  35.8 36.8 %all-to-all-done.1.ref = bf16[8,3,256,256]{3,2,1,0:T(8,128)(2,1)} async-done(((bf16[8,3,256,256]{3,2,1,0:T(8,128)(2,1)}), bf16[8,3,256,256]{3,2,1,0:T(8,128)(2,1)}, u32[]{:S(2)}, u32[]{:S(2)}) %all-to-all-start.1) | async-done | bytes 3145760 | tf_op jit(solution)/shard_map/all_to_all | solution.py:1934
  72.6 6.1 %shard_map.313 = (bf16[2048,256]{1,0:T(8,128)(2,1)}, bf16[2048,256]{1,0:T(8,128)(2,1)}, bf16[2048,256]{1,0:T(8,128)(2,1)}) custom-call(bf16[8,3,256,256]{3,2,1,0:T(8,128)(2,1)} %all-to-all-done.1.ref), custom_call_target="tpu_custom_call" | custom-call | flops 6899999744 | bytes 1 | tf_op jit(solution)/shard_map/pallas_call | solution.py:1727
  84.5 19.1 %collective-permute-done.1.refs_2_ = bf16[256,2048]{1,0:T(8,128)(2,1)S(1)} collective-permute-done((bf16[256,2048]{1,0:T(8,128)(2,1)S(1)}, bf16[256,2048]{1,0:T(8,128)(2,1)S(1)}, u32[]{:S(2)}, u32[]{:S(2)}) %collective-permute-start.1) | collective-permute-done | bytes 1048608 | tf_op jit(solution)/shard_map/ppermute | solution.py:1681
  104.1 1.3 collective-permute-done.3.refs_4_
  109.9 6.6 %collective-permute-done.5.refs_6_ = bf16[128,2048]{1,0:T(8,128)(2,1)} collective-permute-done((bf16[128,2048]{1,0:T(8,128)(2,1)S(1)}, bf16[128,2048]{1,0:T(8,128)(2,1)}, u32[]{:S(2)}, u32[]{:S(2)}) %collective-permute-start.5) | collective-permute-done | bytes 524320 | tf_op jit(solution)/shard_map/ppermute | solution.py:1681
  116.5 2.7 collective-permute-done.6.refs_7_
  119.2 1.8 multiply_sine_fusion
  122.2 16.7 %shard_map.309 = (bf16[256,2048]{1,0:T(8,128)(2,1)}, bf16[64,2048]{1,0:T(8,128)(2,1)}, bf16[80,2048]{1,0:T(8,128)(2,1)}, bf16[2048,64]{1,0:T(8,128)(2,1)}, bf16[...) custom-call(s32[1]{0:T(128)} %bitcast.place_ref, ...), custom_call_target="tpu_custom_call" | custom-call | flops 19549999104 | bytes 1 | tf_op jit(solution)/shard_map/pallas_call | solution.py:859
  139.8 1.8 collective-permute-start.10
  141.6 1.6 collective-permute-start.12
  143.2 10.1 %shard_map.315 = (bf16[8,256,256]{2,1,0:T(8,128)(2,1)}, f32[256,2048]{1,0:T(8,128)}, f32[4,2048]{1,0:T(4,128)}, f32[16,80,128]{2,1,0:T(8,128)}, bf16[16,256,512]{2,1,0:T(8,128)(2,1)}) custom-call(s32[1]{0:T(128)} %dynamic_slice.18.length_ref, bf16[256,2048]{1,0:T(8,128)(2,1)} %get-tuple-element.61.refs_1_.q_ref.refs_14_, ...), custom_call_target="tpu_custom_call" | custom-call | flops 11500000256 | bytes 1 | tf_op jit(solution)/shard_map/pallas_call | solution.py:1005
  153.3 11.5 %collective-permute-done.11.refs_3_.refs_4_ = bf16[256,2048]{1,0:T(8,128)(2,1)S(1)} collective-permute-done((bf16[256,2048]{1,0:T(8,128)(2,1)}, bf16[256,2048]{1,0:T(8,128)(2,1)S(1)}, u32[]{:S(2)}, u32[]{:S(2)}) %collective-permute-start.11) | collective-permute-done | bytes 1048608 | tf_op jit(solution)/shard_map/ppermute | solution.py:1681
  167.6 1.4 collective-permute-start.15
  173.3 3.6 all-to-all-start.2
  177.0 2.3 fusion.18
  180.1 12.0 %collective-permute-done.12.refs_4_.refs_11_.refs_6_ = bf16[2048,256]{1,0:T(8,128)(2,1)} collective-permute-done((bf16[2048,256]{1,0:T(8,128)(2,1)}, bf16[2048,256]{1,0:T(8,128)(2,1)}, u32[]{:S(2)}, u32[]{:S(2)}) %collective-permute-start.12) | collective-permute-done | bytes 1048608 | tf_op jit(solution)/shard_map/ppermute | solution.py:1861
  193.1 12.9 %shard_map.316 = (f32[256,2048]{1,0:T(8,128)}, f32[8,2048]{1,0:T(8,128)}) custom-call(s32[1]{0:T(128)} %shard_map.314.length_ref, bf16[256,2048]{1,0:T(8,128)(2,1)} %get-tuple-element.61.refs_1_.q_ref.refs_14_, bf16[2048,64]{1,0:T(8,128)(2,1)} %get-tuple-element.63.k_ref.k_before, bf16[80,2048]{1,0:T(8,128)(2,1)} %get-tuple-element.64.vt_ref.vt_before.refs_23_.refs_24_, ...), custom_call_target="tpu_custom_call" | custom-call | flops 18400000000 | bytes 1 | tf_op jit(solution)/shard_map/pallas_call | solution.py:1102
  207.6 9.8 %shard_map.320 = (f32[256,2048]{1,0:T(8,128)}, bf16[256,2048]{1,0:T(8,128)(2,1)}, f32[256,128]{1,0:T(8,128)}, bf16[256,128]{1,0:T(8,128)(2,1)}) custom-call(s32[1]{0:T(128)} %shard_map.317.place_ref, bf16[256,2048]{1,0:T(8,128)(2,1)} %shard_map.310.refs_0_, bf16[256,2048]{1,0:T(8,128)(2,1)} %collective-permute-done.9.refs_1_, bf16[256,2048]{1,0:T(8,128)(2,1)} %copy-done.7, ...), custom_call_target="tpu_custom_call" | custom-call | flops 14949999616 | bytes 1 | tf_op jit(solution)/shard_map/pallas_call | solution.py:1588
  219.7 16.0 %shard_map.322 = (f32[256,2048]{1,0:T(8,128)}, f32[8,2048]{1,0:T(8,128)}) custom-call(s32[1]{0:T(128)} %shard_map.321.length_ref, bf16[256,2048]{1,0:T(8,128)(2,1)} %get-tuple-element.61.refs_1_.q_ref.refs_14_, bf16[2048,64]{1,0:T(8,128)(2,1)} %get-tuple-element.63.k_ref.k_before, ...), custom_call_target="tpu_custom_call", output_to_operand_aliasing={{0}: (5, {}), {1}: (6, {})} | custom-call | flops 18400000000 | bytes 1 | tf_op jit(solution)/shard_map/pallas_call | solution.py:1102
  235.7 7.3 %collective-permute-done.21.refs_4_ = bf16[256,2048]{1,0:T(8,128)(2,1)} collective-permute-done((bf16[256,2048]{1,0:T(8,128)(2,1)}, bf16[256,2048]{1,0:T(8,128)(2,1)}, u32[]{:S(2)}, u32[]{:S(2)}) %collective-permute-start.21) | collective-permute-done | bytes 1048608 | tf_op jit(solution)/shard_map/ppermute | solution.py:1681
  242.9 1.9 slice.187.refs_0_
  245.1 1.9 slice.186.refs_0_
  247.0 1.3 collective-permute-start.20
  249.2 7.7 %collective-permute-done.23.refs_3_.refs_12_.refs_7_ = bf16[2048,256]{1,0:T(8,128)(2,1)} collective-permute-done((bf16[2048,256]{1,0:T(8,128)(2,1)}, bf16[2048,256]{1,0:T(8,128)(2,1)}, u32[]{:S(2)}, u32[]{:S(2)}) %collective-permute-start.23) | collective-permute-done | bytes 1048608 | tf_op jit(solution)/shard_map/ppermute | solution.py:1861
  256.9 1.2 collective-permute-done.22.refs_2_.refs_7_
  258.1 1.9 collective-permute-done.20.refs_1_.refs_6_
  261.9 1.2 collective-permute-start.24
  263.1 1.5 collective-permute-start.32
  265.2 19.2 %collective-permute-done.25.refs_4_.refs_2_ = bf16[256,2048]{1,0:T(8,128)(2,1)} collective-permute-done((bf16[256,2048]{1,0:T(8,128)(2,1)}, bf16[256,2048]{1,0:T(8,128)(2,1)}, u32[]{:S(2)}, u32[]{:S(2)}) %collective-permute-start.25) | collective-permute-done | bytes 1048608 | tf_op jit(solution)/shard_map/ppermute | solution.py:1681
  288.2 1.6 collective-permute-done.32.refs_13_.refs_8_
  292.1 26.2 %shard_map.326 = (bf16[2048,1024]{1,0:T(8,128)(2,1)}, bf16[2048,1024]{1,0:T(8,128)(2,1)}, bf16[2048,1024]{1,0:T(8,128)(2,1)}) custom-call(s32[4]{0:T(128)} %compare_select_fusion.order_ref, bf16[256,2048]{1,0:T(8,128)(2,1)} %get-tuple-element.70.refs_1_.refs_0_, bf16[256,2048]{1,0:T(8,128)(2,1)} %collective-permute-done.27.refs_1_, ...), custom_call_target="tpu_custom_call" | custom-call | flops 28750000128 | bytes 1 | tf_op jit(solution)/shard_map/pallas_call | solution.py:1149
  323.0 22.7 %shard_map.329.refs_13_ = bf16[2048,2048]{1,0:T(8,128)(2,1)} custom-call(s32[4]{0:T(128)} %compare_select_fusion.order_ref, bf16[256,2048]{1,0:T(8,128)(2,1)} %bitcast.55, bf16[256,2048]{1,0:T(8,128)(2,1)} %collective-permute-done.34.refs_1_.refs_0_, bf16[256,2048]{1,0:T(8,128)(2,1)} %collective-permute-done.24.refs_2_.refs_1_, ...), custom_call_target="tpu_custom_call" | custom-call | flops 27599998976 | bytes 1 | tf_op jit(solution)/shard_map/pallas_call | solution.py:1207
  345.7 14.7 %shard_map.331 = bf16[1024,2048]{1,0:T(8,128)(2,1)} custom-call(s32[4]{0:T(128)} %compare_select_fusion.order_ref, bf16[256,2048]{1,0:T(8,128)(2,1)} %collective-permute-done.34.refs_1_.refs_0_, bf16[256,2048]{1,0:T(8,128)(2,1)} %collective-permute-done.35.refs_3_.refs_1_, bf16[256,2048]{1,0:T(8,128)(2,1)} %collective-permute-done.36.refs_5_.refs_2_, ...), custom_call_target="tpu_custom_call" | custom-call | flops 13799999488 | bytes 1 | tf_op jit(solution)/shard_map/pallas_call | solution.py:1207
  360.8 14.7 %shard_map.330 = bf16[1024,2048]{1,0:T(8,128)(2,1)} custom-call(s32[4]{0:T(128)} %compare_select_fusion.order_ref, bf16[256,2048]{1,0:T(8,128)(2,1)} %bitcast.56, bf16[256,2048]{1,0:T(8,128)(2,1)} %collective-permute-done.24.refs_2_.refs_1_, bf16[256,2048]{1,0:T(8,128)(2,1)} %collective-permute-done.25.refs_4_.refs_2_, ...), custom_call_target="tpu_custom_call" | custom-call | flops 13799999488 | bytes 1 | tf_op jit(solution)/shard_map/pallas_call | solution.py:1207
  375.5 2.0 copy-done.39
  377.5 5.5 shard_map.332
  383.6 1.5 collective-permute-start.41
  385.6 16.5 %shard_map.334.refs_1_ = bf16[2048,2048]{1,0:T(8,128)(2,1)} custom-call(s32[1]{0:T(128)} %shard_map.333.place_ref, s32[4]{0:T(128)} %compare_select_fusion.order_ref, bf16[4,2048,128]{2,1,0:T(8,128)(2,1)} %bitcast.78, bf16[4,2048,128]{2,1,0:T(8,128)(2,1)} %bitcast.81, bf16[2048,1024]{1,0:T(8,128)(2,1)} %get-tuple-element.74.refs_1_.refs_2_), custom_call_target="tpu_custom_call" | custom-call | flops 19549999104 | bytes 1 | tf_op jit(solution)/shard_map/pallas_call | solution.py:1243
  402.1 6.2 %collective-permute-done.40.refs_11_ = bf16[256,2048]{1,0:T(8,128)(2,1)S(1)} collective-permute-done((bf16[256,2048]{1,0:T(8,128)(2,1)}, bf16[256,2048]{1,0:T(8,128)(2,1)S(1)}, u32[]{:S(2)}, u32[]{:S(2)}) %collective-permute-start.40) | collective-permute-done | bytes 1048608 | tf_op jit(solution)/shard_map/ppermute | solution.py:1681
  409.5 1.5 add_convert_fusion.4
  411.1 1.2 collective-permute-start.42
  412.3 9.4 %collective-permute-done.43.refs_13_ = bf16[128,2048]{1,0:T(8,128)(2,1)} collective-permute-done((bf16[128,2048]{1,0:T(8,128)(2,1)S(1)}, bf16[128,2048]{1,0:T(8,128)(2,1)}, u32[]{:S(2)}, u32[]{:S(2)}) %collective-permute-start.43) | collective-permute-done | bytes 524320 | tf_op jit(solution)/shard_map/ppermute | solution.py:1681
  421.8 2.4 collective-permute-done.42.refs_12_
  424.2 13.8 %shard_map.337 = (bf16[8,256,256]{2,1,0:T(8,128)(2,1)}, f32[256,2048]{1,0:T(8,128)}, bf16[256,2048]{1,0:T(8,128)(2,1)}, f32[256,128]{1,0:T(8,128)}) custom-call(s32[1]{0:T(128)} %bitcast.place_ref, bf16[256,2048]{1,0:T(8,128)(2,1)} %shard_map.310.refs_0_, bf16[256,2048]{1,0:T(8,128)(2,1)} %collective-permute-done.9.refs_1_, bf16[256,2048]{1,0:T(8,128)(2,1)} %copy-done.7, ...), custom_call_target="tpu_custom_call" | custom-call | flops 17250000896 | bytes 1 | tf_op jit(solution)/shard_map/pallas_call | solution.py:1656
  438.1 31.2 %all_to_all.35.refs_10_ = bf16[8,256,256]{2,1,0:T(8,128)(2,1)} all-to-all(bf16[8,256,256]{2,1,0:T(8,128)(2,1)} %get-tuple-element.84), channel_id=1, replica_groups=mesh['seq'=8,'fsdp'=4] {'seq'}, dimensions={0} | all-to-all | bytes 2097152 | tf_op jit(solution)/shard_map/all_to_all | solution.py:2018
  469.2 30.0 %shard_map.338 = (bf16[512,2048]{1,0:T(8,128)(2,1)}, f32[320,64]{1,0:T(8,128)}, f32[128,2048]{1,0:T(8,128)}, bf16[4,256,2048]{2,1,0:T(8,128)(2,1)}, bf16[4,256,2048]{2,1,0:T(8,128)(2,1)}) custom-call(s32[1]{0:T(128)} %dynamic_slice.18.length_ref, s32[1]{0:T(128)} %bitcast.place_ref, bf16[256,2048]{1,0:T(8,128)(2,1)} %copy-done.13, ...), custom_call_target="tpu_custom_call" | custom-call | flops 34500001792 | bytes 1 | tf_op jit(solution)/shard_map/pallas_call | solution.py:1477
  501.7 2.0 fusion.3
  503.7 3.1 collective-permute-done.44.got_ref
  506.9 5.4 shard_map.339
  514.5 1.2 collective-permute-start.46
  516.8 1.6 copy.136
  518.4 5.6 all-to-all-start.5
  524.0 2.4 reshape.203
  526.5 11.2 %collective-permute-done.45.from_x = bf16[256,2048]{1,0:T(8,128)(2,1)S(1)} collective-permute-done((bf16[256,2048]{1,0:T(8,128)(2,1)}, bf16[256,2048]{1,0:T(8,128)(2,1)S(1)}, u32[]{:S(2)}, u32[]{:S(2)}) %collective-permute-start.45) | collective-permute-done | bytes 1048608 | tf_op jit(solution)/shard_map/ppermute | solution.py:1681
  538.5 6.0 %all-to-all-start.4 = ((f32[32,1,2624]{2,1,0:T(1,128)}), f32[32,1,2624]{2,1,0:T(1,128)S(1)}, u32[]{:S(2)}, u32[]{:S(2)}) async-start(f32[32,1,2624]{2,1,0:T(1,128)} %reshape.203), calls=%async_computation.5 | async-start | bytes 688128 | tf_op jit(solution)/shard_map/all_to_all | solution.py:2044
  545.7 1.9 collective-permute-start.47
  552.7 3.0 all-to-all-done.4
  556.1 1.5 reduce.5
  559.6 2.8 collective-permute-done.47.late_x
  563.3 5.7 shard_map.340
  568.9 2.5 fusion.5
  (303 shorter events, 60.2 us)
Async XLA Ops:
  7.2 75.5 %copy-start = (bf16[2048,64]{0,1:T(8,128)(2,1)S(1)}, bf16[2048,64]{0,1:T(8,128)(2,1)}, u32[]{:S(2)}) copy-start(bf16[2048,64]{0,1:T(8,128)(2,1)} %param.41) | copy-start | bytes 786436
  7.2 114.2 %all-gather.13.cloned.1.call-start = ((), (), s32[]{:S(2)}) async-start(), calls=%async_computation.9 | async-start | bytes 1966080 | tf_op jit(solution)/shard_map/all_gather | solution.py:1917
  30.1 42.5 %all-to-all-start.1 = ((bf16[8,3,256,256]{3,2,1,0:T(8,128)(2,1)}), bf16[8,3,256,256]{3,2,1,0:T(8,128)(2,1)}, u32[]{:S(2)}, u32[]{:S(2)}) async-start(bf16[8,3,256,256]{3,2,1,0:T(8,128)(2,1)} %shard_map.312), calls=%async_computation.1 | async-start | bytes 6291456 | tf_op jit(solution)/shard_map/all_to_all | solution.py:1934
  34.7 104.3 %all-gather.11.cloned.1.call-start = ((), (), s32[]{:S(2)}) async-start(), calls=%async_computation.8 | async-start | bytes 1310720 | tf_op jit(solution)/shard_map/all_gather | solution.py:1932
  35.4 256.6 %all-gather.15.cloned.1.call-start = ((), (), s32[]{:S(2)}) async-start(), calls=%async_computation.10 | async-start | bytes 5242880 | tf_op jit(solution)/shard_map/all_gather | solution.py:1972
  35.5 43.2 %copy-start.29 = (f32[2048]{0:T(1024)}, f32[2048]{0:T(1024)S(1)}, u32[]{:S(2)}) copy-start(f32[2048]{0:T(1024)S(1)} %convert_element_type.81) | copy-start | bytes 24580
  79.7 41.7 %copy-start.13 = (bf16[256,2048]{1,0:T(8,128)(2,1)}, bf16[256,2048]{1,0:T(8,128)(2,1)S(1)}, u32[]{:S(2)}) copy-start(bf16[256,2048]{1,0:T(8,128)(2,1)S(1)} %fusion.2.refs_0_) | copy-start | bytes 3145732
  79.7 24.0 %collective-permute-start.1 = (bf16[256,2048]{1,0:T(8,128)(2,1)S(1)}, bf16[256,2048]{1,0:T(8,128)(2,1)S(1)}, u32[]{:S(2)}, u32[]{:S(2)}) collective-permute-start(bf16[256,2048]{1,0:T(8,128)(2,1)S(1)} %fusion.2.refs_0_), channel_id=1, source_target_pairs={{0,8},{4,12},{8,0},{12,4},{16,24},{20,28},{24,16},{28,20},{1,9},{5... | collective-permute-start | bytes 3145736 | tf_op jit(solution)/shard_map/ppermute | solution.py:1681
  80.3 25.2 %collective-permute-start.3 = (bf16[256,2048]{1,0:T(8,128)(2,1)S(1)}, bf16[256,2048]{1,0:T(8,128)(2,1)}, u32[]{:S(2)}, u32[]{:S(2)}) collective-permute-start(bf16[256,2048]{1,0:T(8,128)(2,1)S(1)} %fusion.2.refs_0_), channel_id=1, source_target_pairs={{0,16},{4,20},{8,24},{12,28},{16,0},{20,4},{24,8},{28,12},{1,17},{... | collective-permute-start | bytes 3145736 | tf_op jit(solution)/shard_map/ppermute | solution.py:1681
  80.9 40.1 %collective-permute-start = (bf16[256,2048]{1,0:T(8,128)(2,1)S(1)}, bf16[256,2048]{1,0:T(8,128)(2,1)}, u32[]{:S(2)}, u32[]{:S(2)}) collective-permute-start(bf16[256,2048]{1,0:T(8,128)(2,1)S(1)} %fusion.2.refs_0_), channel_id=1, source_target_pairs={{0,4},{4,0},{8,12},{12,8},{16,20},{20,16},{24,28},{28,24},{1,5},{5... | collective-permute-start | bytes 3145736 | tf_op jit(solution)/shard_map/ppermute | solution.py:1681
  83.8 55.2 %copy-start.21 = (bf16[320,64]{1,0:T(8,128)(2,1)}, bf16[320,64]{1,0:T(8,128)(2,1)S(1)}, u32[]{:S(2)}) copy-start(bf16[320,64]{1,0:T(8,128)(2,1)S(1)} %pad_maximum_fusion.refs_27_) | copy-start | bytes 122884
  103.7 12.8 %collective-permute-start.5 = (bf16[128,2048]{1,0:T(8,128)(2,1)S(1)}, bf16[128,2048]{1,0:T(8,128)(2,1)}, u32[]{:S(2)}, u32[]{:S(2)}) collective-permute-start(bf16[128,2048]{1,0:T(8,128)(2,1)S(1)} %slice.182), channel_id=1, source_target_pairs={{0,16},{4,20},{8,24},{12,28},{16,0},{20,4},{24,8},{28,12},{1,17},{... | collective-permute-start | bytes 1572872 | tf_op jit(solution)/shard_map/ppermute | solution.py:1681
  106.5 12.7 %collective-permute-start.6 = (bf16[128,2048]{1,0:T(8,128)(2,1)S(1)}, bf16[128,2048]{1,0:T(8,128)(2,1)}, u32[]{:S(2)}, u32[]{:S(2)}) collective-permute-start(bf16[128,2048]{1,0:T(8,128)(2,1)S(1)} %slice.183), channel_id=1, source_target_pairs={{0,8},{4,12},{8,0},{12,4},{16,24},{20,28},{24,16},{28,20},{1,9},{5... | collective-permute-start | bytes 1572872 | tf_op jit(solution)/shard_map/ppermute | solution.py:1681
  107.0 14.3 %collective-permute-start.2 = (bf16[256,2048]{1,0:T(8,128)(2,1)S(1)}, bf16[256,2048]{1,0:T(8,128)(2,1)}, u32[]{:S(2)}, u32[]{:S(2)}) collective-permute-start(bf16[256,2048]{1,0:T(8,128)(2,1)S(1)} %collective-permute-done.1.refs_2_), channel_id=1, source_target_pairs={{0,4},{4,0},{8,12},{12,8},{16,20},{20,16},{24,28},{28,24},{1,5},{5... | collective-permute-start | bytes 3145736 | tf_op jit(solution)/shard_map/ppermute | solution.py:1681
  107.0 14.3 %collective-permute-start.4 = (bf16[256,2048]{1,0:T(8,128)(2,1)}, bf16[256,2048]{1,0:T(8,128)(2,1)}, u32[]{:S(2)}, u32[]{:S(2)}) collective-permute-start(bf16[256,2048]{1,0:T(8,128)(2,1)} %collective-permute-done.3.refs_4_), channel_id=1, source_target_pairs={{0,4},{4,0},{8,12},{12,8},{16,20},{20,16},{24,28},{28,24},{1,5},{5... | collective-permute-start | bytes 3145736 | tf_op jit(solution)/shard_map/ppermute | solution.py:1681
  116.5 4.6 collective-permute-start.7
  119.2 2.1 collective-permute-start.8
  139.0 25.8 %collective-permute-start.11 = (bf16[256,2048]{1,0:T(8,128)(2,1)}, bf16[256,2048]{1,0:T(8,128)(2,1)S(1)}, u32[]{:S(2)}, u32[]{:S(2)}) collective-permute-start(bf16[256,2048]{1,0:T(8,128)(2,1)} %shard_map.310.refs_0_), channel_id=1, source_target_pairs={{0,16},{4,20},{8,24},{12,28},{16,0},{20,4},{24,8},{28,12},{1,17},{... | collective-permute-start | bytes 3145736 | tf_op jit(solution)/shard_map/ppermute | solution.py:1681
  139.8 26.9 %collective-permute-start.10 = (bf16[256,2048]{1,0:T(8,128)(2,1)}, bf16[256,2048]{1,0:T(8,128)(2,1)S(1)}, u32[]{:S(2)}, u32[]{:S(2)}) collective-permute-start(bf16[256,2048]{1,0:T(8,128)(2,1)} %shard_map.310.refs_0_), channel_id=1, source_target_pairs={{0,8},{4,12},{8,0},{12,4},{16,24},{20,28},{24,16},{28,20},{1,9},{5... | collective-permute-start | bytes 3145736 | tf_op jit(solution)/shard_map/ppermute | solution.py:1681
  141.6 38.3 %collective-permute-start.9 = (bf16[256,2048]{1,0:T(8,128)(2,1)}, bf16[256,2048]{1,0:T(8,128)(2,1)}, u32[]{:S(2)}, u32[]{:S(2)}) collective-permute-start(bf16[256,2048]{1,0:T(8,128)(2,1)} %shard_map.310.refs_0_), channel_id=1, source_target_pairs={{0,4},{4,0},{8,12},{12,8},{16,20},{20,16},{24,28},{28,24},{1,5},{5... | collective-permute-start | bytes 3145736 | tf_op jit(solution)/shard_map/ppermute | solution.py:1681
  141.6 50.4 %collective-permute-start.12 = (bf16[2048,256]{1,0:T(8,128)(2,1)}, bf16[2048,256]{1,0:T(8,128)(2,1)}, u32[]{:S(2)}, u32[]{:S(2)}) collective-permute-start(bf16[2048,256]{1,0:T(8,128)(2,1)} %get-tuple-element.62.refs_10_.refs_5_), channel_id=1, source_target_pairs={{0,1},{1,2},{2,3},{3,0},{4,5},{5,6},{6,7},{7,4},{8,9},{9,10},{10,1... | collective-permute-start | bytes 3145736 | tf_op jit(solution)/shard_map/ppermute | solution.py:1861
  165.7 26.9 %collective-permute-start.16 = (bf16[128,2048]{1,0:T(8,128)(2,1)}, bf16[128,2048]{1,0:T(8,128)(2,1)}, u32[]{:S(2)}, u32[]{:S(2)}) collective-permute-start(bf16[128,2048]{1,0:T(8,128)(2,1)} %shard_map.319), channel_id=1, source_target_pairs={{0,8},{4,12},{8,0},{12,4},{16,24},{20,28},{24,16},{28,20},{1,9},{5... | collective-permute-start | bytes 1572872 | tf_op jit(solution)/shard_map/ppermute | solution.py:1681
  167.6 25.1 %collective-permute-start.15 = (bf16[128,2048]{1,0:T(8,128)(2,1)}, bf16[128,2048]{1,0:T(8,128)(2,1)}, u32[]{:S(2)}, u32[]{:S(2)}) collective-permute-start(bf16[128,2048]{1,0:T(8,128)(2,1)} %shard_map.318), channel_id=1, source_target_pairs={{0,16},{4,20},{8,24},{12,28},{16,0},{20,4},{24,8},{28,12},{1,17},{... | collective-permute-start | bytes 1572872 | tf_op jit(solution)/shard_map/ppermute | solution.py:1681
  173.3 33.3 %all-to-all-start.2 = ((bf16[8,256,256]{2,1,0:T(8,128)(2,1)}), bf16[8,256,256]{2,1,0:T(8,128)(2,1)S(1)}, u32[]{:S(2)}, u32[]{:S(2)}) async-start(bf16[8,256,256]{2,1,0:T(8,128)(2,1)} %get-tuple-element.67.att_ref.refs_1_), calls=%async_computation.2 | async-start | bytes 2097152 | tf_op jit(solution)/shard_map/all_to_all | solution.py:1981
  176.9 143.5 %all-gather.19.cloned.1.call-start = ((), (), s32[]{:S(2)}) async-start(), calls=%async_computation.12 | async-start | bytes 2621440 | tf_op jit(solution)/shard_map/all_gather | solution.py:1975
  179.3 166.4 %all-gather.17.cloned.1.call-start = ((), (), s32[]{:S(2)}) async-start(), calls=%async_computation.11 | async-start | bytes 2621440 | tf_op jit(solution)/shard_map/all_gather | solution.py:1975
  179.5 27.2 %collective-permute-start.13 = (bf16[256,2048]{1,0:T(8,128)(2,1)S(1)}, bf16[256,2048]{1,0:T(8,128)(2,1)}, u32[]{:S(2)}, u32[]{:S(2)}) collective-permute-start(bf16[256,2048]{1,0:T(8,128)(2,1)S(1)} %collective-permute-done.10.refs_2_), channel_id=1, source_target_pairs={{0,4},{4,0},{8,12},{12,8},{16,20},{20,16},{24,28},{28,24},{1,5},{5... | collective-permute-start | bytes 3145736 | tf_op jit(solution)/shard_map/ppermute | solution.py:1681
  179.9 26.8 %collective-permute-start.14 = (bf16[256,2048]{1,0:T(8,128)(2,1)S(1)}, bf16[256,2048]{1,0:T(8,128)(2,1)}, u32[]{:S(2)}, u32[]{:S(2)}) collective-permute-start(bf16[256,2048]{1,0:T(8,128)(2,1)S(1)} %collective-permute-done.11.refs_3_.refs_4_), channel_id=1, source_target_pairs={{0,4},{4,0},{8,12},{12,8},{16,20},{20,16},{24,28},{28,24},{1,5},{5... | collective-permute-start | bytes 3145736 | tf_op jit(solution)/shard_map/ppermute | solution.py:1681
  192.6 14.1 %collective-permute-start.18 = (bf16[128,2048]{1,0:T(8,128)(2,1)}, bf16[128,2048]{1,0:T(8,128)(2,1)}, u32[]{:S(2)}, u32[]{:S(2)}) collective-permute-start(bf16[128,2048]{1,0:T(8,128)(2,1)} %collective-permute-done.16.refs_7_), channel_id=1, source_target_pairs={{0,4},{4,0},{8,12},{12,8},{16,20},{20,16},{24,28},{28,24},{1,5},{5... | collective-permute-start | bytes 1572872 | tf_op jit(solution)/shard_map/ppermute | solution.py:1681
  192.7 14.0 %collective-permute-start.17 = (bf16[128,2048]{1,0:T(8,128)(2,1)}, bf16[128,2048]{1,0:T(8,128)(2,1)}, u32[]{:S(2)}, u32[]{:S(2)}) collective-permute-start(bf16[128,2048]{1,0:T(8,128)(2,1)} %collective-permute-done.15.refs_6_), channel_id=1, source_target_pairs={{0,4},{4,0},{8,12},{12,8},{16,20},{20,16},{24,28},{28,24},{1,5},{5... | collective-permute-start | bytes 1572872 | tf_op jit(solution)/shard_map/ppermute | solution.py:1681
  206.6 50.3 %collective-permute-start.23 = (bf16[2048,256]{1,0:T(8,128)(2,1)}, bf16[2048,256]{1,0:T(8,128)(2,1)}, u32[]{:S(2)}, u32[]{:S(2)}) collective-permute-start(bf16[2048,256]{1,0:T(8,128)(2,1)} %collective-permute-done.12.refs_4_.refs_11_.refs_6_), channel_id=1, source_target_pairs={{0,1},{1,2},{2,3},{3,0},{4,5},{5,6},{6,7},{7,4},{8,9},{9,10},{10,1... | collective-permute-start | bytes 3145736 | tf_op jit(solution)/shard_map/ppermute | solution.py:1861
  217.4 25.5 %collective-permute-start.21 = (bf16[256,2048]{1,0:T(8,128)(2,1)}, bf16[256,2048]{1,0:T(8,128)(2,1)}, u32[]{:S(2)}, u32[]{:S(2)}) collective-permute-start(bf16[256,2048]{1,0:T(8,128)(2,1)} %get-tuple-element.70.refs_1_.refs_0_), channel_id=1, source_target_pairs={{0,16},{4,20},{8,24},{12,28},{16,0},{20,4},{24,8},{28,12},{1,17},{... | collective-permute-start | bytes 3145736 | tf_op jit(solution)/shard_map/ppermute | solution.py:1681
  218.0 27.1 %collective-permute-start.19 = (bf16[256,2048]{1,0:T(8,128)(2,1)}, bf16[256,2048]{1,0:T(8,128)(2,1)}, u32[]{:S(2)}, u32[]{:S(2)}) collective-permute-start(bf16[256,2048]{1,0:T(8,128)(2,1)} %get-tuple-element.70.refs_1_.refs_0_), channel_id=1, source_target_pairs={{0,8},{4,12},{8,0},{12,4},{16,24},{20,28},{24,16},{28,20},{1,9},{5... | collective-permute-start | bytes 3145736 | tf_op jit(solution)/shard_map/ppermute | solution.py:1681
  244.8 13.3 %collective-permute-start.22 = (bf16[128,2048]{1,0:T(8,128)(2,1)}, bf16[128,2048]{1,0:T(8,128)(2,1)S(1)}, u32[]{:S(2)}, u32[]{:S(2)}) collective-permute-start(bf16[128,2048]{1,0:T(8,128)(2,1)} %shard_map.324), channel_id=1, source_target_pairs={{0,8},{4,12},{8,0},{12,4},{16,24},{20,28},{24,16},{28,20},{1,9},{5... | collective-permute-start | bytes 1572872 | tf_op jit(solution)/shard_map/ppermute | solution.py:1681
  247.0 13.0 %collective-permute-start.20 = (bf16[128,2048]{1,0:T(8,128)(2,1)}, bf16[128,2048]{1,0:T(8,128)(2,1)S(1)}, u32[]{:S(2)}, u32[]{:S(2)}) collective-permute-start(bf16[128,2048]{1,0:T(8,128)(2,1)} %shard_map.323), channel_id=1, source_target_pairs={{0,16},{4,20},{8,24},{12,28},{16,0},{20,4},{24,8},{28,12},{1,17},{... | collective-permute-start | bytes 1572872 | tf_op jit(solution)/shard_map/ppermute | solution.py:1681
  248.3 16.4 %collective-permute-start.27 = (bf16[256,2048]{1,0:T(8,128)(2,1)S(1)}, bf16[256,2048]{1,0:T(8,128)(2,1)}, u32[]{:S(2)}, u32[]{:S(2)}) collective-permute-start(bf16[256,2048]{1,0:T(8,128)(2,1)S(1)} %copy-done.10), channel_id=1, source_target_pairs={{0,4},{4,0},{8,12},{12,8},{16,20},{20,16},{24,28},{28,24},{1,5},{5... | collective-permute-start | bytes 3145736 | tf_op jit(solution)/shard_map/ppermute | solution.py:1681
  260.8 23.6 %collective-permute-start.25 = (bf16[256,2048]{1,0:T(8,128)(2,1)}, bf16[256,2048]{1,0:T(8,128)(2,1)}, u32[]{:S(2)}, u32[]{:S(2)}) collective-permute-start(bf16[256,2048]{1,0:T(8,128)(2,1)} %shard_map.325), channel_id=1, source_target_pairs={{0,16},{4,20},{8,24},{12,28},{16,0},{20,4},{24,8},{28,12},{1,17},{... | collective-permute-start | bytes 3145736 | tf_op jit(solution)/shard_map/ppermute | solution.py:1681
  261.9 23.1 %collective-permute-start.24 = (bf16[256,2048]{1,0:T(8,128)(2,1)}, bf16[256,2048]{1,0:T(8,128)(2,1)}, u32[]{:S(2)}, u32[]{:S(2)}) collective-permute-start(bf16[256,2048]{1,0:T(8,128)(2,1)} %shard_map.325), channel_id=1, source_target_pairs={{0,8},{4,12},{8,0},{12,4},{16,24},{20,28},{24,16},{28,20},{1,9},{5... | collective-permute-start | bytes 3145736 | tf_op jit(solution)/shard_map/ppermute | solution.py:1681
  263.1 26.6 %collective-permute-start.32 = (bf16[2048,256]{1,0:T(8,128)(2,1)}, bf16[2048,256]{1,0:T(8,128)(2,1)}, u32[]{:S(2)}, u32[]{:S(2)}) collective-permute-start(bf16[2048,256]{1,0:T(8,128)(2,1)} %collective-permute-done.23.refs_3_.refs_12_.refs_7_), channel_id=1, source_target_pairs={{0,1},{1,2},{2,3},{3,0},{4,5},{5,6},{6,7},{7,4},{8,9},{9,10},{10,1... | collective-permute-start | bytes 3145736 | tf_op jit(solution)/shard_map/ppermute | solution.py:1861
  264.6 26.9 %collective-permute-start.28 = (bf16[256,2048]{1,0:T(8,128)(2,1)}, bf16[256,2048]{1,0:T(8,128)(2,1)}, u32[]{:S(2)}, u32[]{:S(2)}) collective-permute-start(bf16[256,2048]{1,0:T(8,128)(2,1)} %collective-permute-done.19.refs_2_), channel_id=1, source_target_pairs={{0,4},{4,0},{8,12},{12,8},{16,20},{20,16},{24,28},{28,24},{1,5},{5... | collective-permute-start | bytes 3145736 | tf_op jit(solution)/shard_map/ppermute | solution.py:1681
  264.6 26.9 %collective-permute-start.29 = (bf16[256,2048]{1,0:T(8,128)(2,1)}, bf16[256,2048]{1,0:T(8,128)(2,1)}, u32[]{:S(2)}, u32[]{:S(2)}) collective-permute-start(bf16[256,2048]{1,0:T(8,128)(2,1)} %collective-permute-done.21.refs_4_), channel_id=1, source_target_pairs={{0,4},{4,0},{8,12},{12,8},{16,20},{20,16},{24,28},{28,24},{1,5},{5... | collective-permute-start | bytes 3145736 | tf_op jit(solution)/shard_map/ppermute | solution.py:1681
  284.3 5.4 collective-permute-start.31
  285.0 5.6 collective-permute-start.30
  285.5 283.4 %reduce-scatter.2.cloned.1.call-start = ((), (), s32[]{:S(2)}) async-start(), calls=%async_computation.7 | async-start | bytes 9437184 | tf_op jit(solution)/shard_map/reduce_scatter | solution.py:2016
  289.8 30.7 %collective-permute-start.34 = (bf16[256,2048]{1,0:T(8,128)(2,1)S(1)}, bf16[256,2048]{1,0:T(8,128)(2,1)}, u32[]{:S(2)}, u32[]{:S(2)}) collective-permute-start(bf16[256,2048]{1,0:T(8,128)(2,1)S(1)} %copy-done.5), channel_id=1, source_target_pairs={{0,4},{4,0},{8,12},{12,8},{16,20},{20,16},{24,28},{28,24},{1,5},{5... | collective-permute-start | bytes 3145736 | tf_op jit(solution)/shard_map/ppermute | solution.py:1681
  289.8 28.5 %collective-permute-start.33 = (bf16[128,2048]{1,0:T(8,128)(2,1)S(1)}, bf16[128,2048]{1,0:T(8,128)(2,1)S(1)}, u32[]{:S(2)}, u32[]{:S(2)}) collective-permute-start(bf16[128,2048]{1,0:T(8,128)(2,1)S(1)} %slice.189), channel_id=1, source_target_pairs={{0,8},{4,12},{8,0},{12,4},{16,24},{20,28},{24,16},{28,20},{1,9},{5... | collective-permute-start | bytes 1572872 | tf_op jit(solution)/shard_map/ppermute | solution.py:1681
  290.6 28.5 %collective-permute-start.26 = (bf16[128,2048]{1,0:T(8,128)(2,1)S(1)}, bf16[128,2048]{1,0:T(8,128)(2,1)S(1)}, u32[]{:S(2)}, u32[]{:S(2)}) collective-permute-start(bf16[128,2048]{1,0:T(8,128)(2,1)S(1)} %slice.188), channel_id=1, source_target_pairs={{0,16},{4,20},{8,24},{12,28},{16,0},{20,4},{24,8},{28,12},{1,17},{... | collective-permute-start | bytes 1572872 | tf_op jit(solution)/shard_map/ppermute | solution.py:1681
  291.6 28.9 %collective-permute-start.35 = (bf16[256,2048]{1,0:T(8,128)(2,1)}, bf16[256,2048]{1,0:T(8,128)(2,1)}, u32[]{:S(2)}, u32[]{:S(2)}) collective-permute-start(bf16[256,2048]{1,0:T(8,128)(2,1)} %collective-permute-done.24.refs_2_.refs_1_), channel_id=1, source_target_pairs={{0,4},{4,0},{8,12},{12,8},{16,20},{20,16},{24,28},{28,24},{1,5},{5... | collective-permute-start | bytes 3145736 | tf_op jit(solution)/shard_map/ppermute | solution.py:1681
  291.6 28.8 %collective-permute-start.36 = (bf16[256,2048]{1,0:T(8,128)(2,1)}, bf16[256,2048]{1,0:T(8,128)(2,1)}, u32[]{:S(2)}, u32[]{:S(2)}) collective-permute-start(bf16[256,2048]{1,0:T(8,128)(2,1)} %collective-permute-done.25.refs_4_.refs_2_), channel_id=1, source_target_pairs={{0,4},{4,0},{8,12},{12,8},{16,20},{20,16},{24,28},{28,24},{1,5},{5... | collective-permute-start | bytes 3145736 | tf_op jit(solution)/shard_map/ppermute | solution.py:1681
  319.1 2.1 collective-permute-start.38
  319.9 2.3 collective-permute-start.37
  360.4 15.1 %collective-permute-start.39 = (bf16[4,256,2048]{2,1,0:T(8,128)(2,1)}, bf16[4,256,2048]{2,1,0:T(8,128)(2,1)S(1)}, u32[]{:S(2)}, u32[]{:S(2)}) collective-permute-start(bf16[4,256,2048]{2,1,0:T(8,128)(2,1)} %bitcast.76), channel_id=1, source_target_pairs={{0,4},{4,0},{8,12},{12,8},{16,20},{20,16},{24,28},{28,24},{1,5},{5... | collective-permute-start | bytes 12582920 | tf_op jit(solution)/shard_map/ppermute | solution.py:1681
  382.9 25.4 %collective-permute-start.40 = (bf16[256,2048]{1,0:T(8,128)(2,1)}, bf16[256,2048]{1,0:T(8,128)(2,1)S(1)}, u32[]{:S(2)}, u32[]{:S(2)}) collective-permute-start(bf16[256,2048]{1,0:T(8,128)(2,1)} %get-tuple-element.79), channel_id=1, source_target_pairs={{0,8},{4,12},{8,0},{12,4},{16,24},{20,28},{24,16},{28,20},{1,9},{5... | collective-permute-start | bytes 3145736 | tf_op jit(solution)/shard_map/ppermute | solution.py:1681
  383.6 25.9 %collective-permute-start.41 = (bf16[256,2048]{1,0:T(8,128)(2,1)}, bf16[256,2048]{1,0:T(8,128)(2,1)S(1)}, u32[]{:S(2)}, u32[]{:S(2)}) collective-permute-start(bf16[256,2048]{1,0:T(8,128)(2,1)} %get-tuple-element.81), channel_id=1, source_target_pairs={{0,16},{4,20},{8,24},{12,28},{16,0},{20,4},{24,8},{28,12},{1,17},{... | collective-permute-start | bytes 3145736 | tf_op jit(solution)/shard_map/ppermute | solution.py:1681
  408.5 13.3 %collective-permute-start.43 = (bf16[128,2048]{1,0:T(8,128)(2,1)S(1)}, bf16[128,2048]{1,0:T(8,128)(2,1)}, u32[]{:S(2)}, u32[]{:S(2)}) collective-permute-start(bf16[128,2048]{1,0:T(8,128)(2,1)S(1)} %add_convert_fusion.3), channel_id=1, source_target_pairs={{0,16},{4,20},{8,24},{12,28},{16,0},{20,4},{24,8},{28,12},{1,17},{... | collective-permute-start | bytes 1572872 | tf_op jit(solution)/shard_map/ppermute | solution.py:1681
  411.1 13.2 %collective-permute-start.42 = (bf16[128,2048]{1,0:T(8,128)(2,1)S(1)}, bf16[128,2048]{1,0:T(8,128)(2,1)}, u32[]{:S(2)}, u32[]{:S(2)}) collective-permute-start(bf16[128,2048]{1,0:T(8,128)(2,1)S(1)} %add_convert_fusion.4), channel_id=1, source_target_pairs={{0,8},{4,12},{8,0},{12,4},{16,24},{20,28},{24,16},{28,20},{1,9},{5... | collective-permute-start | bytes 1572872 | tf_op jit(solution)/shard_map/ppermute | solution.py:1681
  469.2 32.0 %copy-start.28 = (bf16[256,128]{1,0:T(8,128)(2,1)S(1)}, bf16[256,128]{1,0:T(8,128)(2,1)}, u32[]{:S(2)}) copy-start(bf16[256,128]{1,0:T(8,128)(2,1)} %get-tuple-element.104) | copy-start | bytes 196612
  499.3 7.6 %collective-permute-start.44 = (bf16[4,256,2048]{2,1,0:T(8,128)(2,1)}, bf16[4,256,2048]{2,1,0:T(8,128)(2,1)}, u32[]{:S(2)}, u32[]{:S(2)}) collective-permute-start(bf16[4,256,2048]{2,1,0:T(8,128)(2,1)} %get-tuple-element.95), channel_id=1, source_target_pairs={{0,4},{4,0},{8,12},{12,8},{16,20},{20,16},{24,28},{28,24},{1,5},{5... | collective-permute-start | bytes 12582920 | tf_op jit(solution)/shard_map/ppermute | solution.py:1681
  512.2 25.4 %collective-permute-start.45 = (bf16[256,2048]{1,0:T(8,128)(2,1)}, bf16[256,2048]{1,0:T(8,128)(2,1)S(1)}, u32[]{:S(2)}, u32[]{:S(2)}) collective-permute-start(bf16[256,2048]{1,0:T(8,128)(2,1)} %get-tuple-element.97), channel_id=1, source_target_pairs={{0,8},{4,12},{8,0},{12,4},{16,24},{20,28},{24,16},{28,20},{1,9},{5... | collective-permute-start | bytes 3145736 | tf_op jit(solution)/shard_map/ppermute | solution.py:1681
  514.5 29.9 %collective-permute-start.46 = (bf16[256,2048]{1,0:T(8,128)(2,1)}, bf16[256,2048]{1,0:T(8,128)(2,1)}, u32[]{:S(2)}, u32[]{:S(2)}) collective-permute-start(bf16[256,2048]{1,0:T(8,128)(2,1)} %get-tuple-element.99), channel_id=1, source_target_pairs={{0,16},{4,20},{8,24},{12,28},{16,0},{20,4},{24,8},{28,12},{1,17},{... | collective-permute-start | bytes 3145736 | tf_op jit(solution)/shard_map/ppermute | solution.py:1681
  518.4 20.1 %all-to-all-start.5 = ((f32[4,1,5888]{2,1,0:T(1,128)}), f32[4,1,5888]{2,1,0:T(1,128)S(1)}, u32[]{:S(2)}, u32[]{:S(2)}) async-start(f32[4,1,5888]{2,1,0:T(1,128)} %copy.136), calls=%async_computation.6 | async-start | bytes 188416 | tf_op jit(solution)/shard_map/all_to_all | solution.py:2060
  537.8 21.9 %collective-permute-start.48 = (bf16[128,2048]{1,0:T(8,128)(2,1)S(1)}, bf16[128,2048]{1,0:T(8,128)(2,1)}, u32[]{:S(2)}, u32[]{:S(2)}) collective-permute-start(bf16[128,2048]{1,0:T(8,128)(2,1)S(1)} %add_convert_fusion.1), channel_id=1, source_target_pairs={{0,16},{4,20},{8,24},{12,28},{16,0},{20,4},{24,8},{28,12},{1,17},{... | collective-permute-start | bytes 1572872 | tf_op jit(solution)/shard_map/ppermute | solution.py:1681
  538.5 17.2 %all-to-all-start.4 = ((f32[32,1,2624]{2,1,0:T(1,128)}), f32[32,1,2624]{2,1,0:T(1,128)S(1)}, u32[]{:S(2)}, u32[]{:S(2)}) async-start(f32[32,1,2624]{2,1,0:T(1,128)} %reshape.203), calls=%async_computation.5 | async-start | bytes 688128 | tf_op jit(solution)/shard_map/all_to_all | solution.py:2044
  545.7 16.8 %collective-permute-start.47 = (bf16[128,2048]{1,0:T(8,128)(2,1)S(1)}, bf16[128,2048]{1,0:T(8,128)(2,1)S(1)}, u32[]{:S(2)}, u32[]{:S(2)}) collective-permute-start(bf16[128,2048]{1,0:T(8,128)(2,1)S(1)} %add_convert_fusion.2), channel_id=1, source_target_pairs={{0,8},{4,12},{8,0},{12,4},{16,24},{20,28},{24,16},{28,20},{1,9},{5... | collective-permute-start | bytes 1572872 | tf_op jit(solution)/shard_map/ppermute | solution.py:1681
  (44 other events, 465.6 us)
Sparse Core Ops, SparseCore 0:
  23.9 36.4 all-gather.12
  62.0 26.7 all-gather.10
  90.4 102.5 all-gather.14
  194.5 66.7 all-gather.18
  285.7 48.1 all-gather.16
  412.4 83.4 reduce-scatter.1

commit v5 on v4

--- a/solution.py
+++ b/solution.py
@@ -22,6 +22,7 @@
 SUB = 128
 VMEM_MIB = 56
 PARTS = 2
+PAIR = 2
 COST = 1.15e9
 
 
@@ -1698,8 +1699,10 @@
 
 def regroup_kernel(*refs):
     out_ref = refs[-1]
+    unit = out_ref.shape[3]
     for number, ref in enumerate(refs[:-1]):
-        out_ref[number] = ref[...]
+        for place in range(out_ref.shape[0]):
+            out_ref[place, number] = ref[:, place * unit : (place + 1) * unit]
 
 
 def regroup(places, *matrices):
@@ -1707,9 +1710,9 @@
     unit = wide // places
     return call(
         regroup_kernel,
-        (places,),
-        [spec_across(rows, unit)] * len(matrices),
-        pl.BlockSpec((None, len(matrices), rows, unit), lambda i: (i, 0, 0, 0)),
+        (places // PAIR,),
+        [spec_across(rows, PAIR * unit)] * len(matrices),
+        pl.BlockSpec((PAIR, len(matrices), rows, unit), lambda i: (i, 0, 0, 0)),
         array(places, len(matrices), rows, unit),
         [],
         0,
@@ -1718,17 +1721,19 @@
 
 
 def ungroup_kernel(ref, *refs):
+    rows = ref.shape[2]
     for number, out_ref in enumerate(refs):
-        out_ref[...] = ref[number]
+        for place in range(ref.shape[0]):
+            out_ref[place * rows : (place + 1) * rows] = ref[place, number]
 
 
 def ungroup(blocks):
     places, count, rows, unit = blocks.shape
     return call(
         ungroup_kernel,
-        (places,),
-        [pl.BlockSpec((None, count, rows, unit), lambda i: (i, 0, 0, 0))],
-        [spec_down(rows, unit)] * count,
+        (places // PAIR,),
+        [pl.BlockSpec((PAIR, count, rows, unit), lambda i: (i, 0, 0, 0))],
+        [spec_down(PAIR * rows, unit)] * count,
         [array(places * rows, unit)] * count,
         [],
         0,

time: 587 us -> 587 us (level)
  starting transfers between devices: 50.1 us -> 56.9 us
  transfers between devices with their start and end apart: 59 -> 59, of which waited for: 24 -> 24; matrix products, arithmetic and copies ran while one was open for 8% -> 8% of each run, Pallas kernels for 37% -> 36%
where the time goes in v5:
time: 587 us; the launch traced here: 580 us
  Pallas kernels  231 us (39%)
  waiting for transfers between devices  168 us (29%)
  starting transfers between devices  56.9 us (10%)
  blocking collectives  44.6 us (8%)
  local copies, waits for them, and re-layouts  43.5 us (7%)
  between operations  19 us (3%)
  other arithmetic  14.2 us (2%)
    ppermute x46, waiting for transfers between devices, exchanged(): lax.ppermute(value, 'seq', [(place, place ^ bits) for place in range(coun...  108 us
    pallas_call x3, Pallas kernels, ffn_back(): call(functools.partial(ffn_back_kernel, counts, len(gates), part, more),...  52 us
    all_to_all x1, waiting for transfers between devices, by_heads(): swapped = lax.all_to_all(swapped, 'seq', 0, 0, tiled=True)  36.8 us
    all_to_all x1, blocking collectives, by_heads(): grad_att = lax.all_to_all(grad_att, 'seq', 0, 0, tiled=True)  31.2 us
    pallas_call x1, Pallas kernels, heads_back(): call(functools.partial(backward_kernel, counts), (steps,), [ANYWHERE] * s...  30 us
    ppermute x46, starting transfers between devices, exchanged(): lax.ppermute(value, 'seq', [(place, place ^ bits) for place in range(coun...  29.9 us
    pallas_call x2, Pallas kernels, teach(): pl.pallas_call(functools.partial(teacher_kernel, first, end - first), gri...  28.9 us
    pallas_call x1, Pallas kernels, hidden_units(): call(functools.partial(hidden_kernel, counts), (len(blocks),), [ANYWHERE]...  26 us
  transfers between devices with their start and end apart: 59, of which 24 were waited for; matrix products, arithmetic and copies ran while one was open for 8% of the time, Pallas kernels for 36%

profile of v5, /device:TPU:0, one launch (start us, length us, event | category | flops | bytes accessed | tf_op | source)
XLA Modules:
  0.0 579.6 jit_solution(8922245733766995550)
XLA Ops:
  10.4 13.4 %all_to_all.34.refs_1_ = bf16[8,64,384]{2,1,0:T(8,128)(2,1)} all-to-all(bf16[8,64,384]{2,1,0:T(8,128)(2,1)S(1)} %maximum_bitcast_fusion.1), channel_id=1, replica_groups=mesh['seq'=8,'fsdp'=4] {'seq'}, dimensions={0} | all-to-all | bytes 786432 | tf_op jit(solution)/shard_map/all_to_all | solution.py:1921
  23.8 4.2 shard_map.311.refs_0_
  28.0 4.6 all-to-all-start.1
  33.8 36.8 %all-to-all-done.1.ref = bf16[8,3,256,256]{3,2,1,0:T(8,128)(2,1)} async-done(((bf16[8,3,256,256]{3,2,1,0:T(8,128)(2,1)}), bf16[8,3,256,256]{3,2,1,0:T(8,128)(2,1)}, u32[]{:S(2)}, u32[]{:S(2)}) %all-to-all-start.1) | async-done | bytes 3145760 | tf_op jit(solution)/shard_map/all_to_all | solution.py:1939
  70.6 4.2 shard_map.313
  80.6 19.1 %collective-permute-done.1.refs_2_ = bf16[256,2048]{1,0:T(8,128)(2,1)S(1)} collective-permute-done((bf16[256,2048]{1,0:T(8,128)(2,1)S(1)}, bf16[256,2048]{1,0:T(8,128)(2,1)S(1)}, u32[]{:S(2)}, u32[]{:S(2)}) %collective-permute-start.1) | collective-permute-done | bytes 1048608 | tf_op jit(solution)/shard_map/ppermute | solution.py:1682
  105.9 6.6 %collective-permute-done.5.refs_6_ = bf16[128,2048]{1,0:T(8,128)(2,1)} collective-permute-done((bf16[128,2048]{1,0:T(8,128)(2,1)S(1)}, bf16[128,2048]{1,0:T(8,128)(2,1)}, u32[]{:S(2)}, u32[]{:S(2)}) %collective-permute-start.5) | collective-permute-done | bytes 524320 | tf_op jit(solution)/shard_map/ppermute | solution.py:1682
  112.5 2.8 collective-permute-done.6.refs_7_
  115.3 1.8 multiply_sine_fusion
  118.3 16.7 %shard_map.309 = (bf16[256,2048]{1,0:T(8,128)(2,1)}, bf16[64,2048]{1,0:T(8,128)(2,1)}, bf16[80,2048]{1,0:T(8,128)(2,1)}, bf16[2048,64]{1,0:T(8,128)(2,1)}, bf16[...) custom-call(s32[1]{0:T(128)} %bitcast.place_ref, ...), custom_call_target="tpu_custom_call" | custom-call | flops 19549999104 | bytes 1 | tf_op jit(solution)/shard_map/pallas_call | solution.py:860
  135.8 1.8 collective-permute-start.10
  137.7 1.6 collective-permute-start.12
  139.2 10.1 %shard_map.315 = (bf16[8,256,256]{2,1,0:T(8,128)(2,1)}, f32[256,2048]{1,0:T(8,128)}, f32[4,2048]{1,0:T(4,128)}, f32[16,80,128]{2,1,0:T(8,128)}, bf16[16,256,512]{2,1,0:T(8,128)(2,1)}) custom-call(s32[1]{0:T(128)} %dynamic_slice.18.length_ref, bf16[256,2048]{1,0:T(8,128)(2,1)} %get-tuple-element.61.refs_1_.q_ref.refs_14_, ...), custom_call_target="tpu_custom_call" | custom-call | flops 11500000256 | bytes 1 | tf_op jit(solution)/shard_map/pallas_call | solution.py:1006
  149.3 11.5 %collective-permute-done.11.refs_3_.refs_4_ = bf16[256,2048]{1,0:T(8,128)(2,1)S(1)} collective-permute-done((bf16[256,2048]{1,0:T(8,128)(2,1)}, bf16[256,2048]{1,0:T(8,128)(2,1)S(1)}, u32[]{:S(2)}, u32[]{:S(2)}) %collective-permute-start.11) | collective-permute-done | bytes 1048608 | tf_op jit(solution)/shard_map/ppermute | solution.py:1682
  169.4 3.6 all-to-all-start.2
  173.1 2.3 fusion.18
  176.2 12.0 %collective-permute-done.12.refs_4_.refs_11_.refs_6_ = bf16[2048,256]{1,0:T(8,128)(2,1)} collective-permute-done((bf16[2048,256]{1,0:T(8,128)(2,1)}, bf16[2048,256]{1,0:T(8,128)(2,1)}, u32[]{:S(2)}, u32[]{:S(2)}) %collective-permute-start.12) | collective-permute-done | bytes 1048608 | tf_op jit(solution)/shard_map/ppermute | solution.py:1866
  189.3 12.9 %shard_map.316 = (f32[256,2048]{1,0:T(8,128)}, f32[8,2048]{1,0:T(8,128)}) custom-call(s32[1]{0:T(128)} %shard_map.314.length_ref, bf16[256,2048]{1,0:T(8,128)(2,1)} %get-tuple-element.61.refs_1_.q_ref.refs_14_, bf16[2048,64]{1,0:T(8,128)(2,1)} %get-tuple-element.63.k_ref.k_before, bf16[80,2048]{1,0:T(8,128)(2,1)} %get-tuple-element.64.vt_ref.vt_before.refs_23_.refs_24_, ...), custom_call_target="tpu_custom_call" | custom-call | flops 18400000000 | bytes 1 | tf_op jit(solution)/shard_map/pallas_call | solution.py:1103
  202.7 2.4 collective-permute-start.23
  206.1 9.8 %shard_map.320 = (f32[256,2048]{1,0:T(8,128)}, bf16[256,2048]{1,0:T(8,128)(2,1)}, f32[256,128]{1,0:T(8,128)}, bf16[256,128]{1,0:T(8,128)(2,1)}) custom-call(s32[1]{0:T(128)} %shard_map.317.place_ref, bf16[256,2048]{1,0:T(8,128)(2,1)} %shard_map.310.refs_0_, bf16[256,2048]{1,0:T(8,128)(2,1)} %collective-permute-done.9.refs_1_, bf16[256,2048]{1,0:T(8,128)(2,1)} %copy-done.7, ...), custom_call_target="tpu_custom_call" | custom-call | flops 14949999616 | bytes 1 | tf_op jit(solution)/shard_map/pallas_call | solution.py:1589
  215.9 1.8 collective-permute-start.21
  217.6 1.5 collective-permute-start.19
  219.6 16.0 %shard_map.322 = (f32[256,2048]{1,0:T(8,128)}, f32[8,2048]{1,0:T(8,128)}) custom-call(s32[1]{0:T(128)} %shard_map.321.length_ref, bf16[256,2048]{1,0:T(8,128)(2,1)} %get-tuple-element.61.refs_1_.q_ref.refs_14_, bf16[2048,64]{1,0:T(8,128)(2,1)} %get-tuple-element.63.k_ref.k_before, ...), custom_call_target="tpu_custom_call", output_to_operand_aliasing={{0}: (5, {}), {1}: (6, {})} | custom-call | flops 18400000000 | bytes 1 | tf_op jit(solution)/shard_map/pallas_call | solution.py:1103
  235.6 5.5 collective-permute-done.21.refs_4_
  241.1 1.9 slice.187.refs_0_
  243.0 1.7 collective-permute-start.22
  244.7 1.9 slice.186.refs_0_
  246.6 1.5 collective-permute-start.20
  249.0 5.4 collective-permute-done.23.refs_3_.refs_12_.refs_7_
  254.5 1.5 collective-permute-done.22.refs_2_.refs_7_
  256.0 3.3 collective-permute-done.20.refs_1_.refs_6_
  260.1 1.5 collective-permute-start.25
  262.1 2.5 collective-permute-start.32
  265.1 18.1 %collective-permute-done.25.refs_4_.refs_2_ = bf16[256,2048]{1,0:T(8,128)(2,1)} collective-permute-done((bf16[256,2048]{1,0:T(8,128)(2,1)}, bf16[256,2048]{1,0:T(8,128)(2,1)}, u32[]{:S(2)}, u32[]{:S(2)}) %collective-permute-start.25) | collective-permute-done | bytes 1048608 | tf_op jit(solution)/shard_map/ppermute | solution.py:1682
  287.6 2.1 collective-permute-done.32.refs_13_.refs_8_
  291.7 26.0 %shard_map.326 = (bf16[2048,1024]{1,0:T(8,128)(2,1)}, bf16[2048,1024]{1,0:T(8,128)(2,1)}, bf16[2048,1024]{1,0:T(8,128)(2,1)}) custom-call(s32[4]{0:T(128)} %compare_select_fusion.order_ref, bf16[256,2048]{1,0:T(8,128)(2,1)} %get-tuple-element.70.refs_1_.refs_0_, bf16[256,2048]{1,0:T(8,128)(2,1)} %collective-permute-done.27.refs_1_, ...), custom_call_target="tpu_custom_call" | custom-call | flops 28750000128 | bytes 1 | tf_op jit(solution)/shard_map/pallas_call | solution.py:1150
  322.5 22.7 %shard_map.329.refs_13_ = bf16[2048,2048]{1,0:T(8,128)(2,1)} custom-call(s32[4]{0:T(128)} %compare_select_fusion.order_ref, bf16[256,2048]{1,0:T(8,128)(2,1)} %bitcast.55, bf16[256,2048]{1,0:T(8,128)(2,1)} %collective-permute-done.34.refs_1_.refs_0_, bf16[256,2048]{1,0:T(8,128)(2,1)} %collective-permute-done.24.refs_2_.refs_1_, ...), custom_call_target="tpu_custom_call" | custom-call | flops 27599998976 | bytes 1 | tf_op jit(solution)/shard_map/pallas_call | solution.py:1208
  345.2 14.7 %shard_map.331 = bf16[1024,2048]{1,0:T(8,128)(2,1)} custom-call(s32[4]{0:T(128)} %compare_select_fusion.order_ref, bf16[256,2048]{1,0:T(8,128)(2,1)} %collective-permute-done.34.refs_1_.refs_0_, bf16[256,2048]{1,0:T(8,128)(2,1)} %collective-permute-done.35.refs_3_.refs_1_, bf16[256,2048]{1,0:T(8,128)(2,1)} %collective-permute-done.36.refs_5_.refs_2_, ...), custom_call_target="tpu_custom_call" | custom-call | flops 13799999488 | bytes 1 | tf_op jit(solution)/shard_map/pallas_call | solution.py:1208
  360.2 14.7 %shard_map.330 = bf16[1024,2048]{1,0:T(8,128)(2,1)} custom-call(s32[4]{0:T(128)} %compare_select_fusion.order_ref, bf16[256,2048]{1,0:T(8,128)(2,1)} %bitcast.56, bf16[256,2048]{1,0:T(8,128)(2,1)} %collective-permute-done.24.refs_2_.refs_1_, bf16[256,2048]{1,0:T(8,128)(2,1)} %collective-permute-done.25.refs_4_.refs_2_, ...), custom_call_target="tpu_custom_call" | custom-call | flops 13799999488 | bytes 1 | tf_op jit(solution)/shard_map/pallas_call | solution.py:1208
  374.9 2.0 copy-done.39
  376.9 5.5 shard_map.332
  383.6 1.5 collective-permute-start.41
  385.6 16.5 %shard_map.334.refs_1_ = bf16[2048,2048]{1,0:T(8,128)(2,1)} custom-call(s32[1]{0:T(128)} %shard_map.333.place_ref, s32[4]{0:T(128)} %compare_select_fusion.order_ref, bf16[4,2048,128]{2,1,0:T(8,128)(2,1)} %bitcast.78, bf16[4,2048,128]{2,1,0:T(8,128)(2,1)} %bitcast.81, bf16[2048,1024]{1,0:T(8,128)(2,1)} %get-tuple-element.74.refs_1_.refs_2_), custom_call_target="tpu_custom_call" | custom-call | flops 19549999104 | bytes 1 | tf_op jit(solution)/shard_map/pallas_call | solution.py:1244
  402.1 5.7 collective-permute-done.40.refs_11_
  408.0 1.5 collective-permute-start.43
  409.5 1.5 add_convert_fusion.4
  412.3 9.1 %collective-permute-done.43.refs_13_ = bf16[128,2048]{1,0:T(8,128)(2,1)} collective-permute-done((bf16[128,2048]{1,0:T(8,128)(2,1)S(1)}, bf16[128,2048]{1,0:T(8,128)(2,1)}, u32[]{:S(2)}, u32[]{:S(2)}) %collective-permute-start.43) | collective-permute-done | bytes 524320 | tf_op jit(solution)/shard_map/ppermute | solution.py:1682
  421.4 2.8 collective-permute-done.42.refs_12_
  424.2 13.8 %shard_map.337 = (bf16[8,256,256]{2,1,0:T(8,128)(2,1)}, f32[256,2048]{1,0:T(8,128)}, bf16[256,2048]{1,0:T(8,128)(2,1)}, f32[256,128]{1,0:T(8,128)}) custom-call(s32[1]{0:T(128)} %bitcast.place_ref, bf16[256,2048]{1,0:T(8,128)(2,1)} %shard_map.310.refs_0_, bf16[256,2048]{1,0:T(8,128)(2,1)} %collective-permute-done.9.refs_1_, bf16[256,2048]{1,0:T(8,128)(2,1)} %copy-done.7, ...), custom_call_target="tpu_custom_call" | custom-call | flops 17250000896 | bytes 1 | tf_op jit(solution)/shard_map/pallas_call | solution.py:1657
  438.1 31.2 %all_to_all.35.refs_10_ = bf16[8,256,256]{2,1,0:T(8,128)(2,1)} all-to-all(bf16[8,256,256]{2,1,0:T(8,128)(2,1)} %get-tuple-element.84), channel_id=1, replica_groups=mesh['seq'=8,'fsdp'=4] {'seq'}, dimensions={0} | all-to-all | bytes 2097152 | tf_op jit(solution)/shard_map/all_to_all | solution.py:2023
  469.3 30.0 %shard_map.338 = (bf16[512,2048]{1,0:T(8,128)(2,1)}, f32[320,64]{1,0:T(8,128)}, f32[128,2048]{1,0:T(8,128)}, bf16[4,256,2048]{2,1,0:T(8,128)(2,1)}, bf16[4,256,2048]{2,1,0:T(8,128)(2,1)}) custom-call(s32[1]{0:T(128)} %dynamic_slice.18.length_ref, s32[1]{0:T(128)} %bitcast.place_ref, bf16[256,2048]{1,0:T(8,128)(2,1)} %copy-done.13, ...), custom_call_target="tpu_custom_call" | custom-call | flops 34500001792 | bytes 1 | tf_op jit(solution)/shard_map/pallas_call | solution.py:1478
  501.7 2.0 fusion.3
  503.7 3.1 collective-permute-done.44.got_ref
  506.9 5.4 shard_map.339
  516.8 1.6 copy.136
  518.4 5.6 all-to-all-start.5
  524.0 2.4 reshape.203
  526.5 11.2 %collective-permute-done.45.from_x = bf16[256,2048]{1,0:T(8,128)(2,1)S(1)} collective-permute-done((bf16[256,2048]{1,0:T(8,128)(2,1)}, bf16[256,2048]{1,0:T(8,128)(2,1)S(1)}, u32[]{:S(2)}, u32[]{:S(2)}) %collective-permute-start.45) | collective-permute-done | bytes 1048608 | tf_op jit(solution)/shard_map/ppermute | solution.py:1682
  538.5 6.0 %all-to-all-start.4 = ((f32[32,1,2624]{2,1,0:T(1,128)}), f32[32,1,2624]{2,1,0:T(1,128)S(1)}, u32[]{:S(2)}, u32[]{:S(2)}) async-start(f32[32,1,2624]{2,1,0:T(1,128)} %reshape.203), calls=%async_computation.5 | async-start | bytes 688128 | tf_op jit(solution)/shard_map/all_to_all | solution.py:2049
  545.7 1.9 collective-permute-start.47
  552.7 3.0 all-to-all-done.4
  559.7 2.8 collective-permute-done.47.late_x
  563.3 5.7 shard_map.340
  569.0 2.5 fusion.5
  (303 shorter events, 64.1 us)
Async XLA Ops:
  7.2 71.6 %copy-start = (bf16[2048,64]{0,1:T(8,128)(2,1)S(1)}, bf16[2048,64]{0,1:T(8,128)(2,1)}, u32[]{:S(2)}) copy-start(bf16[2048,64]{0,1:T(8,128)(2,1)} %param.41) | copy-start | bytes 786436
  7.2 110.2 %all-gather.13.cloned.1.call-start = ((), (), s32[]{:S(2)}) async-start(), calls=%async_computation.9 | async-start | bytes 1966080 | tf_op jit(solution)/shard_map/all_gather | solution.py:1922
  28.0 42.5 %all-to-all-start.1 = ((bf16[8,3,256,256]{3,2,1,0:T(8,128)(2,1)}), bf16[8,3,256,256]{3,2,1,0:T(8,128)(2,1)}, u32[]{:S(2)}, u32[]{:S(2)}) async-start(bf16[8,3,256,256]{3,2,1,0:T(8,128)(2,1)} %shard_map.312), calls=%async_computation.1 | async-start | bytes 6291456 | tf_op jit(solution)/shard_map/all_to_all | solution.py:1939
  32.7 102.4 %all-gather.11.cloned.1.call-start = ((), (), s32[]{:S(2)}) async-start(), calls=%async_computation.8 | async-start | bytes 1310720 | tf_op jit(solution)/shard_map/all_gather | solution.py:1937
  33.4 258.2 %all-gather.15.cloned.1.call-start = ((), (), s32[]{:S(2)}) async-start(), calls=%async_computation.10 | async-start | bytes 5242880 | tf_op jit(solution)/shard_map/all_gather | solution.py:1977
  33.5 41.3 %copy-start.29 = (f32[2048]{0:T(1024)}, f32[2048]{0:T(1024)S(1)}, u32[]{:S(2)}) copy-start(f32[2048]{0:T(1024)S(1)} %convert_element_type.81) | copy-start | bytes 24580
  75.7 41.7 %copy-start.13 = (bf16[256,2048]{1,0:T(8,128)(2,1)}, bf16[256,2048]{1,0:T(8,128)(2,1)S(1)}, u32[]{:S(2)}) copy-start(bf16[256,2048]{1,0:T(8,128)(2,1)S(1)} %fusion.2.refs_0_) | copy-start | bytes 3145732
  75.7 24.0 %collective-permute-start.1 = (bf16[256,2048]{1,0:T(8,128)(2,1)S(1)}, bf16[256,2048]{1,0:T(8,128)(2,1)S(1)}, u32[]{:S(2)}, u32[]{:S(2)}) collective-permute-start(bf16[256,2048]{1,0:T(8,128)(2,1)S(1)} %fusion.2.refs_0_), channel_id=1, source_target_pairs={{0,8},{4,12},{8,0},{12,4},{16,24},{20,28},{24,16},{28,20},{1,9},{5... | collective-permute-start | bytes 3145736 | tf_op jit(solution)/shard_map/ppermute | solution.py:1682
  76.3 25.2 %collective-permute-start.3 = (bf16[256,2048]{1,0:T(8,128)(2,1)S(1)}, bf16[256,2048]{1,0:T(8,128)(2,1)}, u32[]{:S(2)}, u32[]{:S(2)}) collective-permute-start(bf16[256,2048]{1,0:T(8,128)(2,1)S(1)} %fusion.2.refs_0_), channel_id=1, source_target_pairs={{0,16},{4,20},{8,24},{12,28},{16,0},{20,4},{24,8},{28,12},{1,17},{... | collective-permute-start | bytes 3145736 | tf_op jit(solution)/shard_map/ppermute | solution.py:1682
  77.0 40.1 %collective-permute-start = (bf16[256,2048]{1,0:T(8,128)(2,1)S(1)}, bf16[256,2048]{1,0:T(8,128)(2,1)}, u32[]{:S(2)}, u32[]{:S(2)}) collective-permute-start(bf16[256,2048]{1,0:T(8,128)(2,1)S(1)} %fusion.2.refs_0_), channel_id=1, source_target_pairs={{0,4},{4,0},{8,12},{12,8},{16,20},{20,16},{24,28},{28,24},{1,5},{5... | collective-permute-start | bytes 3145736 | tf_op jit(solution)/shard_map/ppermute | solution.py:1682
  79.9 55.1 %copy-start.21 = (bf16[320,64]{1,0:T(8,128)(2,1)}, bf16[320,64]{1,0:T(8,128)(2,1)S(1)}, u32[]{:S(2)}) copy-start(bf16[320,64]{1,0:T(8,128)(2,1)S(1)} %pad_maximum_fusion.refs_27_) | copy-start | bytes 122884
  99.7 12.8 %collective-permute-start.5 = (bf16[128,2048]{1,0:T(8,128)(2,1)S(1)}, bf16[128,2048]{1,0:T(8,128)(2,1)}, u32[]{:S(2)}, u32[]{:S(2)}) collective-permute-start(bf16[128,2048]{1,0:T(8,128)(2,1)S(1)} %slice.182), channel_id=1, source_target_pairs={{0,16},{4,20},{8,24},{12,28},{16,0},{20,4},{24,8},{28,12},{1,17},{... | collective-permute-start | bytes 1572872 | tf_op jit(solution)/shard_map/ppermute | solution.py:1682
  102.5 12.8 %collective-permute-start.6 = (bf16[128,2048]{1,0:T(8,128)(2,1)S(1)}, bf16[128,2048]{1,0:T(8,128)(2,1)}, u32[]{:S(2)}, u32[]{:S(2)}) collective-permute-start(bf16[128,2048]{1,0:T(8,128)(2,1)S(1)} %slice.183), channel_id=1, source_target_pairs={{0,8},{4,12},{8,0},{12,4},{16,24},{20,28},{24,16},{28,20},{1,9},{5... | collective-permute-start | bytes 1572872 | tf_op jit(solution)/shard_map/ppermute | solution.py:1682
  103.0 14.4 %collective-permute-start.2 = (bf16[256,2048]{1,0:T(8,128)(2,1)S(1)}, bf16[256,2048]{1,0:T(8,128)(2,1)}, u32[]{:S(2)}, u32[]{:S(2)}) collective-permute-start(bf16[256,2048]{1,0:T(8,128)(2,1)S(1)} %collective-permute-done.1.refs_2_), channel_id=1, source_target_pairs={{0,4},{4,0},{8,12},{12,8},{16,20},{20,16},{24,28},{28,24},{1,5},{5... | collective-permute-start | bytes 3145736 | tf_op jit(solution)/shard_map/ppermute | solution.py:1682
  103.1 14.4 %collective-permute-start.4 = (bf16[256,2048]{1,0:T(8,128)(2,1)}, bf16[256,2048]{1,0:T(8,128)(2,1)}, u32[]{:S(2)}, u32[]{:S(2)}) collective-permute-start(bf16[256,2048]{1,0:T(8,128)(2,1)} %collective-permute-done.3.refs_4_), channel_id=1, source_target_pairs={{0,4},{4,0},{8,12},{12,8},{16,20},{20,16},{24,28},{28,24},{1,5},{5... | collective-permute-start | bytes 3145736 | tf_op jit(solution)/shard_map/ppermute | solution.py:1682
  112.5 4.6 collective-permute-start.7
  115.3 2.1 collective-permute-start.8
  135.1 25.8 %collective-permute-start.11 = (bf16[256,2048]{1,0:T(8,128)(2,1)}, bf16[256,2048]{1,0:T(8,128)(2,1)S(1)}, u32[]{:S(2)}, u32[]{:S(2)}) collective-permute-start(bf16[256,2048]{1,0:T(8,128)(2,1)} %shard_map.310.refs_0_), channel_id=1, source_target_pairs={{0,16},{4,20},{8,24},{12,28},{16,0},{20,4},{24,8},{28,12},{1,17},{... | collective-permute-start | bytes 3145736 | tf_op jit(solution)/shard_map/ppermute | solution.py:1682
  135.8 26.9 %collective-permute-start.10 = (bf16[256,2048]{1,0:T(8,128)(2,1)}, bf16[256,2048]{1,0:T(8,128)(2,1)S(1)}, u32[]{:S(2)}, u32[]{:S(2)}) collective-permute-start(bf16[256,2048]{1,0:T(8,128)(2,1)} %shard_map.310.refs_0_), channel_id=1, source_target_pairs={{0,8},{4,12},{8,0},{12,4},{16,24},{20,28},{24,16},{28,20},{1,9},{5... | collective-permute-start | bytes 3145736 | tf_op jit(solution)/shard_map/ppermute | solution.py:1682
  137.7 38.3 %collective-permute-start.9 = (bf16[256,2048]{1,0:T(8,128)(2,1)}, bf16[256,2048]{1,0:T(8,128)(2,1)}, u32[]{:S(2)}, u32[]{:S(2)}) collective-permute-start(bf16[256,2048]{1,0:T(8,128)(2,1)} %shard_map.310.refs_0_), channel_id=1, source_target_pairs={{0,4},{4,0},{8,12},{12,8},{16,20},{20,16},{24,28},{28,24},{1,5},{5... | collective-permute-start | bytes 3145736 | tf_op jit(solution)/shard_map/ppermute | solution.py:1682
  137.7 50.5 %collective-permute-start.12 = (bf16[2048,256]{1,0:T(8,128)(2,1)}, bf16[2048,256]{1,0:T(8,128)(2,1)}, u32[]{:S(2)}, u32[]{:S(2)}) collective-permute-start(bf16[2048,256]{1,0:T(8,128)(2,1)} %get-tuple-element.62.refs_10_.refs_5_), channel_id=1, source_target_pairs={{0,1},{1,2},{2,3},{3,0},{4,5},{5,6},{6,7},{7,4},{8,9},{9,10},{10,1... | collective-permute-start | bytes 3145736 | tf_op jit(solution)/shard_map/ppermute | solution.py:1866
  161.8 26.9 %collective-permute-start.16 = (bf16[128,2048]{1,0:T(8,128)(2,1)}, bf16[128,2048]{1,0:T(8,128)(2,1)}, u32[]{:S(2)}, u32[]{:S(2)}) collective-permute-start(bf16[128,2048]{1,0:T(8,128)(2,1)} %shard_map.319), channel_id=1, source_target_pairs={{0,8},{4,12},{8,0},{12,4},{16,24},{20,28},{24,16},{28,20},{1,9},{5... | collective-permute-start | bytes 1572872 | tf_op jit(solution)/shard_map/ppermute | solution.py:1682
  163.7 25.1 %collective-permute-start.15 = (bf16[128,2048]{1,0:T(8,128)(2,1)}, bf16[128,2048]{1,0:T(8,128)(2,1)}, u32[]{:S(2)}, u32[]{:S(2)}) collective-permute-start(bf16[128,2048]{1,0:T(8,128)(2,1)} %shard_map.318), channel_id=1, source_target_pairs={{0,16},{4,20},{8,24},{12,28},{16,0},{20,4},{24,8},{28,12},{1,17},{... | collective-permute-start | bytes 1572872 | tf_op jit(solution)/shard_map/ppermute | solution.py:1682
  169.4 35.7 %all-to-all-start.2 = ((bf16[8,256,256]{2,1,0:T(8,128)(2,1)}), bf16[8,256,256]{2,1,0:T(8,128)(2,1)S(1)}, u32[]{:S(2)}, u32[]{:S(2)}) async-start(bf16[8,256,256]{2,1,0:T(8,128)(2,1)} %get-tuple-element.67.att_ref.refs_1_), calls=%async_computation.2 | async-start | bytes 2097152 | tf_op jit(solution)/shard_map/all_to_all | solution.py:1986
  173.0 146.8 %all-gather.19.cloned.1.call-start = ((), (), s32[]{:S(2)}) async-start(), calls=%async_computation.12 | async-start | bytes 2621440 | tf_op jit(solution)/shard_map/all_gather | solution.py:1980
  175.3 169.9 %all-gather.17.cloned.1.call-start = ((), (), s32[]{:S(2)}) async-start(), calls=%async_computation.11 | async-start | bytes 2621440 | tf_op jit(solution)/shard_map/all_gather | solution.py:1980
  175.6 29.6 %collective-permute-start.13 = (bf16[256,2048]{1,0:T(8,128)(2,1)S(1)}, bf16[256,2048]{1,0:T(8,128)(2,1)}, u32[]{:S(2)}, u32[]{:S(2)}) collective-permute-start(bf16[256,2048]{1,0:T(8,128)(2,1)S(1)} %collective-permute-done.10.refs_2_), channel_id=1, source_target_pairs={{0,4},{4,0},{8,12},{12,8},{16,20},{20,16},{24,28},{28,24},{1,5},{5... | collective-permute-start | bytes 3145736 | tf_op jit(solution)/shard_map/ppermute | solution.py:1682
  176.0 29.1 %collective-permute-start.14 = (bf16[256,2048]{1,0:T(8,128)(2,1)S(1)}, bf16[256,2048]{1,0:T(8,128)(2,1)}, u32[]{:S(2)}, u32[]{:S(2)}) collective-permute-start(bf16[256,2048]{1,0:T(8,128)(2,1)S(1)} %collective-permute-done.11.refs_3_.refs_4_), channel_id=1, source_target_pairs={{0,4},{4,0},{8,12},{12,8},{16,20},{20,16},{24,28},{28,24},{1,5},{5... | collective-permute-start | bytes 3145736 | tf_op jit(solution)/shard_map/ppermute | solution.py:1682
  188.7 16.4 %collective-permute-start.18 = (bf16[128,2048]{1,0:T(8,128)(2,1)}, bf16[128,2048]{1,0:T(8,128)(2,1)}, u32[]{:S(2)}, u32[]{:S(2)}) collective-permute-start(bf16[128,2048]{1,0:T(8,128)(2,1)} %collective-permute-done.16.refs_7_), channel_id=1, source_target_pairs={{0,4},{4,0},{8,12},{12,8},{16,20},{20,16},{24,28},{28,24},{1,5},{5... | collective-permute-start | bytes 1572872 | tf_op jit(solution)/shard_map/ppermute | solution.py:1682
  188.8 16.3 %collective-permute-start.17 = (bf16[128,2048]{1,0:T(8,128)(2,1)}, bf16[128,2048]{1,0:T(8,128)(2,1)}, u32[]{:S(2)}, u32[]{:S(2)}) collective-permute-start(bf16[128,2048]{1,0:T(8,128)(2,1)} %collective-permute-done.15.refs_6_), channel_id=1, source_target_pairs={{0,4},{4,0},{8,12},{12,8},{16,20},{20,16},{24,28},{28,24},{1,5},{5... | collective-permute-start | bytes 1572872 | tf_op jit(solution)/shard_map/ppermute | solution.py:1682
  202.7 51.7 %collective-permute-start.23 = (bf16[2048,256]{1,0:T(8,128)(2,1)}, bf16[2048,256]{1,0:T(8,128)(2,1)}, u32[]{:S(2)}, u32[]{:S(2)}) collective-permute-start(bf16[2048,256]{1,0:T(8,128)(2,1)} %collective-permute-done.12.refs_4_.refs_11_.refs_6_), channel_id=1, source_target_pairs={{0,1},{1,2},{2,3},{3,0},{4,5},{5,6},{6,7},{7,4},{8,9},{9,10},{10,1... | collective-permute-start | bytes 3145736 | tf_op jit(solution)/shard_map/ppermute | solution.py:1866
  215.9 25.2 %collective-permute-start.21 = (bf16[256,2048]{1,0:T(8,128)(2,1)}, bf16[256,2048]{1,0:T(8,128)(2,1)}, u32[]{:S(2)}, u32[]{:S(2)}) collective-permute-start(bf16[256,2048]{1,0:T(8,128)(2,1)} %get-tuple-element.70.refs_1_.refs_0_), channel_id=1, source_target_pairs={{0,16},{4,20},{8,24},{12,28},{16,0},{20,4},{24,8},{28,12},{1,17},{... | collective-permute-start | bytes 3145736 | tf_op jit(solution)/shard_map/ppermute | solution.py:1682
  217.6 27.1 %collective-permute-start.19 = (bf16[256,2048]{1,0:T(8,128)(2,1)}, bf16[256,2048]{1,0:T(8,128)(2,1)}, u32[]{:S(2)}, u32[]{:S(2)}) collective-permute-start(bf16[256,2048]{1,0:T(8,128)(2,1)} %get-tuple-element.70.refs_1_.refs_0_), channel_id=1, source_target_pairs={{0,8},{4,12},{8,0},{12,4},{16,24},{20,28},{24,16},{28,20},{1,9},{5... | collective-permute-start | bytes 3145736 | tf_op jit(solution)/shard_map/ppermute | solution.py:1682
  243.0 13.0 %collective-permute-start.22 = (bf16[128,2048]{1,0:T(8,128)(2,1)}, bf16[128,2048]{1,0:T(8,128)(2,1)S(1)}, u32[]{:S(2)}, u32[]{:S(2)}) collective-permute-start(bf16[128,2048]{1,0:T(8,128)(2,1)} %shard_map.324), channel_id=1, source_target_pairs={{0,8},{4,12},{8,0},{12,4},{16,24},{20,28},{24,16},{28,20},{1,9},{5... | collective-permute-start | bytes 1572872 | tf_op jit(solution)/shard_map/ppermute | solution.py:1682
  246.6 12.7 %collective-permute-start.20 = (bf16[128,2048]{1,0:T(8,128)(2,1)}, bf16[128,2048]{1,0:T(8,128)(2,1)S(1)}, u32[]{:S(2)}, u32[]{:S(2)}) collective-permute-start(bf16[128,2048]{1,0:T(8,128)(2,1)} %shard_map.323), channel_id=1, source_target_pairs={{0,16},{4,20},{8,24},{12,28},{16,0},{20,4},{24,8},{28,12},{1,17},{... | collective-permute-start | bytes 1572872 | tf_op jit(solution)/shard_map/ppermute | solution.py:1682
  248.1 16.5 %collective-permute-start.27 = (bf16[256,2048]{1,0:T(8,128)(2,1)S(1)}, bf16[256,2048]{1,0:T(8,128)(2,1)}, u32[]{:S(2)}, u32[]{:S(2)}) collective-permute-start(bf16[256,2048]{1,0:T(8,128)(2,1)S(1)} %copy-done.10), channel_id=1, source_target_pairs={{0,4},{4,0},{8,12},{12,8},{16,20},{20,16},{24,28},{28,24},{1,5},{5... | collective-permute-start | bytes 3145736 | tf_op jit(solution)/shard_map/ppermute | solution.py:1682
  260.1 23.2 %collective-permute-start.25 = (bf16[256,2048]{1,0:T(8,128)(2,1)}, bf16[256,2048]{1,0:T(8,128)(2,1)}, u32[]{:S(2)}, u32[]{:S(2)}) collective-permute-start(bf16[256,2048]{1,0:T(8,128)(2,1)} %shard_map.325), channel_id=1, source_target_pairs={{0,16},{4,20},{8,24},{12,28},{16,0},{20,4},{24,8},{28,12},{1,17},{... | collective-permute-start | bytes 3145736 | tf_op jit(solution)/shard_map/ppermute | solution.py:1682
  261.6 22.9 %collective-permute-start.24 = (bf16[256,2048]{1,0:T(8,128)(2,1)}, bf16[256,2048]{1,0:T(8,128)(2,1)}, u32[]{:S(2)}, u32[]{:S(2)}) collective-permute-start(bf16[256,2048]{1,0:T(8,128)(2,1)} %shard_map.325), channel_id=1, source_target_pairs={{0,8},{4,12},{8,0},{12,4},{16,24},{20,28},{24,16},{28,20},{1,9},{5... | collective-permute-start | bytes 3145736 | tf_op jit(solution)/shard_map/ppermute | solution.py:1682
  262.1 27.6 %collective-permute-start.32 = (bf16[2048,256]{1,0:T(8,128)(2,1)}, bf16[2048,256]{1,0:T(8,128)(2,1)}, u32[]{:S(2)}, u32[]{:S(2)}) collective-permute-start(bf16[2048,256]{1,0:T(8,128)(2,1)} %collective-permute-done.23.refs_3_.refs_12_.refs_7_), channel_id=1, source_target_pairs={{0,1},{1,2},{2,3},{3,0},{4,5},{5,6},{6,7},{7,4},{8,9},{9,10},{10,1... | collective-permute-start | bytes 3145736 | tf_op jit(solution)/shard_map/ppermute | solution.py:1866
  264.6 26.5 %collective-permute-start.28 = (bf16[256,2048]{1,0:T(8,128)(2,1)}, bf16[256,2048]{1,0:T(8,128)(2,1)}, u32[]{:S(2)}, u32[]{:S(2)}) collective-permute-start(bf16[256,2048]{1,0:T(8,128)(2,1)} %collective-permute-done.19.refs_2_), channel_id=1, source_target_pairs={{0,4},{4,0},{8,12},{12,8},{16,20},{20,16},{24,28},{28,24},{1,5},{5... | collective-permute-start | bytes 3145736 | tf_op jit(solution)/shard_map/ppermute | solution.py:1682
  264.6 26.8 %collective-permute-start.29 = (bf16[256,2048]{1,0:T(8,128)(2,1)}, bf16[256,2048]{1,0:T(8,128)(2,1)}, u32[]{:S(2)}, u32[]{:S(2)}) collective-permute-start(bf16[256,2048]{1,0:T(8,128)(2,1)} %collective-permute-done.21.refs_4_), channel_id=1, source_target_pairs={{0,4},{4,0},{8,12},{12,8},{16,20},{20,16},{24,28},{28,24},{1,5},{5... | collective-permute-start | bytes 3145736 | tf_op jit(solution)/shard_map/ppermute | solution.py:1682
  283.3 6.5 %collective-permute-start.31 = (bf16[128,2048]{1,0:T(8,128)(2,1)}, bf16[128,2048]{1,0:T(8,128)(2,1)S(1)}, u32[]{:S(2)}, u32[]{:S(2)}) collective-permute-start(bf16[128,2048]{1,0:T(8,128)(2,1)} %copy-done.19), channel_id=1, source_target_pairs={{0,4},{4,0},{8,12},{12,8},{16,20},{20,16},{24,28},{28,24},{1,5},{5... | collective-permute-start | bytes 1572872 | tf_op jit(solution)/shard_map/ppermute | solution.py:1682
  284.5 6.1 %collective-permute-start.30 = (bf16[128,2048]{1,0:T(8,128)(2,1)}, bf16[128,2048]{1,0:T(8,128)(2,1)}, u32[]{:S(2)}, u32[]{:S(2)}) collective-permute-start(bf16[128,2048]{1,0:T(8,128)(2,1)} %copy-done.20), channel_id=1, source_target_pairs={{0,4},{4,0},{8,12},{12,8},{16,20},{20,16},{24,28},{28,24},{1,5},{5... | collective-permute-start | bytes 1572872 | tf_op jit(solution)/shard_map/ppermute | solution.py:1682
  285.0 283.9 %reduce-scatter.2.cloned.1.call-start = ((), (), s32[]{:S(2)}) async-start(), calls=%async_computation.7 | async-start | bytes 9437184 | tf_op jit(solution)/shard_map/reduce_scatter | solution.py:2021
  289.8 30.1 %collective-permute-start.34 = (bf16[256,2048]{1,0:T(8,128)(2,1)S(1)}, bf16[256,2048]{1,0:T(8,128)(2,1)}, u32[]{:S(2)}, u32[]{:S(2)}) collective-permute-start(bf16[256,2048]{1,0:T(8,128)(2,1)S(1)} %copy-done.5), channel_id=1, source_target_pairs={{0,4},{4,0},{8,12},{12,8},{16,20},{20,16},{24,28},{28,24},{1,5},{5... | collective-permute-start | bytes 3145736 | tf_op jit(solution)/shard_map/ppermute | solution.py:1682
  289.8 27.9 %collective-permute-start.33 = (bf16[128,2048]{1,0:T(8,128)(2,1)S(1)}, bf16[128,2048]{1,0:T(8,128)(2,1)S(1)}, u32[]{:S(2)}, u32[]{:S(2)}) collective-permute-start(bf16[128,2048]{1,0:T(8,128)(2,1)S(1)} %slice.189), channel_id=1, source_target_pairs={{0,8},{4,12},{8,0},{12,4},{16,24},{20,28},{24,16},{28,20},{1,9},{5... | collective-permute-start | bytes 1572872 | tf_op jit(solution)/shard_map/ppermute | solution.py:1682
  290.6 28.2 %collective-permute-start.26 = (bf16[128,2048]{1,0:T(8,128)(2,1)S(1)}, bf16[128,2048]{1,0:T(8,128)(2,1)S(1)}, u32[]{:S(2)}, u32[]{:S(2)}) collective-permute-start(bf16[128,2048]{1,0:T(8,128)(2,1)S(1)} %slice.188), channel_id=1, source_target_pairs={{0,16},{4,20},{8,24},{12,28},{16,0},{20,4},{24,8},{28,12},{1,17},{... | collective-permute-start | bytes 1572872 | tf_op jit(solution)/shard_map/ppermute | solution.py:1682
  291.1 28.7 %collective-permute-start.35 = (bf16[256,2048]{1,0:T(8,128)(2,1)}, bf16[256,2048]{1,0:T(8,128)(2,1)}, u32[]{:S(2)}, u32[]{:S(2)}) collective-permute-start(bf16[256,2048]{1,0:T(8,128)(2,1)} %collective-permute-done.24.refs_2_.refs_1_), channel_id=1, source_target_pairs={{0,4},{4,0},{8,12},{12,8},{16,20},{20,16},{24,28},{28,24},{1,5},{5... | collective-permute-start | bytes 3145736 | tf_op jit(solution)/shard_map/ppermute | solution.py:1682
  291.4 28.5 %collective-permute-start.36 = (bf16[256,2048]{1,0:T(8,128)(2,1)}, bf16[256,2048]{1,0:T(8,128)(2,1)}, u32[]{:S(2)}, u32[]{:S(2)}) collective-permute-start(bf16[256,2048]{1,0:T(8,128)(2,1)} %collective-permute-done.25.refs_4_.refs_2_), channel_id=1, source_target_pairs={{0,4},{4,0},{8,12},{12,8},{16,20},{20,16},{24,28},{28,24},{1,5},{5... | collective-permute-start | bytes 3145736 | tf_op jit(solution)/shard_map/ppermute | solution.py:1682
  318.5 2.1 collective-permute-start.38
  319.6 2.1 collective-permute-start.37
  359.9 15.0 %collective-permute-start.39 = (bf16[4,256,2048]{2,1,0:T(8,128)(2,1)}, bf16[4,256,2048]{2,1,0:T(8,128)(2,1)S(1)}, u32[]{:S(2)}, u32[]{:S(2)}) collective-permute-start(bf16[4,256,2048]{2,1,0:T(8,128)(2,1)} %bitcast.76), channel_id=1, source_target_pairs={{0,4},{4,0},{8,12},{12,8},{16,20},{20,16},{24,28},{28,24},{1,5},{5... | collective-permute-start | bytes 12582920 | tf_op jit(solution)/shard_map/ppermute | solution.py:1682
  382.4 25.5 %collective-permute-start.40 = (bf16[256,2048]{1,0:T(8,128)(2,1)}, bf16[256,2048]{1,0:T(8,128)(2,1)S(1)}, u32[]{:S(2)}, u32[]{:S(2)}) collective-permute-start(bf16[256,2048]{1,0:T(8,128)(2,1)} %get-tuple-element.79), channel_id=1, source_target_pairs={{0,8},{4,12},{8,0},{12,4},{16,24},{20,28},{24,16},{28,20},{1,9},{5... | collective-permute-start | bytes 3145736 | tf_op jit(solution)/shard_map/ppermute | solution.py:1682
  383.6 25.9 %collective-permute-start.41 = (bf16[256,2048]{1,0:T(8,128)(2,1)}, bf16[256,2048]{1,0:T(8,128)(2,1)S(1)}, u32[]{:S(2)}, u32[]{:S(2)}) collective-permute-start(bf16[256,2048]{1,0:T(8,128)(2,1)} %get-tuple-element.81), channel_id=1, source_target_pairs={{0,16},{4,20},{8,24},{12,28},{16,0},{20,4},{24,8},{28,12},{1,17},{... | collective-permute-start | bytes 3145736 | tf_op jit(solution)/shard_map/ppermute | solution.py:1682
  408.0 13.4 %collective-permute-start.43 = (bf16[128,2048]{1,0:T(8,128)(2,1)S(1)}, bf16[128,2048]{1,0:T(8,128)(2,1)}, u32[]{:S(2)}, u32[]{:S(2)}) collective-permute-start(bf16[128,2048]{1,0:T(8,128)(2,1)S(1)} %add_convert_fusion.3), channel_id=1, source_target_pairs={{0,16},{4,20},{8,24},{12,28},{16,0},{20,4},{24,8},{28,12},{1,17},{... | collective-permute-start | bytes 1572872 | tf_op jit(solution)/shard_map/ppermute | solution.py:1682
  411.1 13.2 %collective-permute-start.42 = (bf16[128,2048]{1,0:T(8,128)(2,1)S(1)}, bf16[128,2048]{1,0:T(8,128)(2,1)}, u32[]{:S(2)}, u32[]{:S(2)}) collective-permute-start(bf16[128,2048]{1,0:T(8,128)(2,1)S(1)} %add_convert_fusion.4), channel_id=1, source_target_pairs={{0,8},{4,12},{8,0},{12,4},{16,24},{20,28},{24,16},{28,20},{1,9},{5... | collective-permute-start | bytes 1572872 | tf_op jit(solution)/shard_map/ppermute | solution.py:1682
  469.3 32.0 %copy-start.28 = (bf16[256,128]{1,0:T(8,128)(2,1)S(1)}, bf16[256,128]{1,0:T(8,128)(2,1)}, u32[]{:S(2)}) copy-start(bf16[256,128]{1,0:T(8,128)(2,1)} %get-tuple-element.104) | copy-start | bytes 196612
  499.3 7.6 %collective-permute-start.44 = (bf16[4,256,2048]{2,1,0:T(8,128)(2,1)}, bf16[4,256,2048]{2,1,0:T(8,128)(2,1)}, u32[]{:S(2)}, u32[]{:S(2)}) collective-permute-start(bf16[4,256,2048]{2,1,0:T(8,128)(2,1)} %get-tuple-element.95), channel_id=1, source_target_pairs={{0,4},{4,0},{8,12},{12,8},{16,20},{20,16},{24,28},{28,24},{1,5},{5... | collective-permute-start | bytes 12582920 | tf_op jit(solution)/shard_map/ppermute | solution.py:1682
  512.3 25.4 %collective-permute-start.45 = (bf16[256,2048]{1,0:T(8,128)(2,1)}, bf16[256,2048]{1,0:T(8,128)(2,1)S(1)}, u32[]{:S(2)}, u32[]{:S(2)}) collective-permute-start(bf16[256,2048]{1,0:T(8,128)(2,1)} %get-tuple-element.97), channel_id=1, source_target_pairs={{0,8},{4,12},{8,0},{12,4},{16,24},{20,28},{24,16},{28,20},{1,9},{5... | collective-permute-start | bytes 3145736 | tf_op jit(solution)/shard_map/ppermute | solution.py:1682
  514.5 29.9 %collective-permute-start.46 = (bf16[256,2048]{1,0:T(8,128)(2,1)}, bf16[256,2048]{1,0:T(8,128)(2,1)}, u32[]{:S(2)}, u32[]{:S(2)}) collective-permute-start(bf16[256,2048]{1,0:T(8,128)(2,1)} %get-tuple-element.99), channel_id=1, source_target_pairs={{0,16},{4,20},{8,24},{12,28},{16,0},{20,4},{24,8},{28,12},{1,17},{... | collective-permute-start | bytes 3145736 | tf_op jit(solution)/shard_map/ppermute | solution.py:1682
  518.4 20.1 %all-to-all-start.5 = ((f32[4,1,5888]{2,1,0:T(1,128)}), f32[4,1,5888]{2,1,0:T(1,128)S(1)}, u32[]{:S(2)}, u32[]{:S(2)}) async-start(f32[4,1,5888]{2,1,0:T(1,128)} %copy.136), calls=%async_computation.6 | async-start | bytes 188416 | tf_op jit(solution)/shard_map/all_to_all | solution.py:2065
  537.8 21.8 %collective-permute-start.48 = (bf16[128,2048]{1,0:T(8,128)(2,1)S(1)}, bf16[128,2048]{1,0:T(8,128)(2,1)}, u32[]{:S(2)}, u32[]{:S(2)}) collective-permute-start(bf16[128,2048]{1,0:T(8,128)(2,1)S(1)} %add_convert_fusion.1), channel_id=1, source_target_pairs={{0,16},{4,20},{8,24},{12,28},{16,0},{20,4},{24,8},{28,12},{1,17},{... | collective-permute-start | bytes 1572872 | tf_op jit(solution)/shard_map/ppermute | solution.py:1682
  538.5 17.2 %all-to-all-start.4 = ((f32[32,1,2624]{2,1,0:T(1,128)}), f32[32,1,2624]{2,1,0:T(1,128)S(1)}, u32[]{:S(2)}, u32[]{:S(2)}) async-start(f32[32,1,2624]{2,1,0:T(1,128)} %reshape.203), calls=%async_computation.5 | async-start | bytes 688128 | tf_op jit(solution)/shard_map/all_to_all | solution.py:2049
  545.7 16.8 %collective-permute-start.47 = (bf16[128,2048]{1,0:T(8,128)(2,1)S(1)}, bf16[128,2048]{1,0:T(8,128)(2,1)S(1)}, u32[]{:S(2)}, u32[]{:S(2)}) collective-permute-start(bf16[128,2048]{1,0:T(8,128)(2,1)S(1)} %add_convert_fusion.2), channel_id=1, source_target_pairs={{0,8},{4,12},{8,0},{12,4},{16,24},{20,28},{24,16},{28,20},{1,9},{5... | collective-permute-start | bytes 1572872 | tf_op jit(solution)/shard_map/ppermute | solution.py:1682
  (44 other events, 467.7 us)
Sparse Core Ops, SparseCore 0:
  23.9 36.4 all-gather.12
  62.0 26.7 all-gather.10
  90.4 102.5 all-gather.14
  194.4 66.7 all-gather.18
  285.1 48.6 all-gather.16
  412.4 83.4 reduce-scatter.1
